TPU v7x, 32 devices: a whole 2x2x4 slice. The times are simulated.
32 devices in a mesh: freq: 8 (over y, x, core), chan: 4 (over z).
Axes of the slice: x: 2, y: 2, z: 4, core: 2. Of those that a mesh axis runs over, the one named last changes fastest.
Arguments:
- factor: bfloat16 [512, 2, 128, 128], P('freq', None, 'chan'), may hold values from -0.2 to 1.2, as said below
- spectrum: bfloat16 [512, 2, 128, 128], P('freq', None, 'chan'), may hold values from -2 to 5, as said below
- guess_scale: float32 [512], P('freq'), may hold values from 0.1 to 0.3
- lag_cutoff: int32 [1], replicated, may hold values from 64 to 255
Outputs:
- new_factor: float32 [512, 2, 128, 128], P('freq', None, None, 'chan')
Inputs may be any that keep to these rules, and one draw needn't show every extreme that they name: The real part of factor is the identity plus independent entries of spread about 0.35 / sqrt(128). At every frequency spectrum is Hermitian: its real part symmetric, its imaginary part antisymmetric with a zero diagonal; it is positive definite.
All inputs are finite; a program needn't handle non-finite values.
Results may differ from a plain program's by a relative error of at most 0.00105.
Values may be sent and summed in bfloat16 or wider, within the bound.
No kernel may reach another device: no remote copies, remote signals or barrier semaphores. Data moves between devices by JAX's collectives and lax.ppermute only.
A program may use at most 128 MiB of HBM per device.

v0:
```python
import functools
import math

import jax
import jax.numpy as jnp
from jax import lax
from jax.experimental import pallas as pl
from jax.experimental.pallas import tpu as pltpu
from jax.sharding import PartitionSpec as P

ITERS = 8
SCALE = 16.0
F32 = jnp.float32
BF16 = jnp.bfloat16
MIB = 1024 * 1024
NN = (((1,), (0,)), ((), ()))
NT = (((1,), (1,)), ((), ()))
TN = (((0,), (0,)), ((), ()))


def dot(left, right, dims=NN):
    return lax.dot_general(left, right, dims, preferred_element_type=F32)


def split(value):
    high = value.astype(BF16)
    return high, (value - high.astype(F32)).astype(BF16)


def cat(parts, axis):
    return jnp.concatenate(parts, axis=axis)


def dot3(left_high, left_low, right_high, right_low, dims=NN):
    rows = left_high.shape[0]
    both = dot(cat([left_high, left_low], 0), right_high, dims)
    return both[:rows] + (both[rows:] + dot(left_high, right_low, dims))


def eye(size):
    rows = lax.broadcasted_iota(jnp.int32, (size, size), 0)
    columns = lax.broadcasted_iota(jnp.int32, (size, size), 1)
    return jnp.where(rows == columns, 1.0, 0.0).astype(F32)


def newton_kernel(scale_ref, psi_ref, out_ref):
    bins = psi_ref.shape[1]
    size = psi_ref.shape[4]
    identity = eye(size)
    state = []
    for item in range(bins):
        re = psi_ref[:, item, 0].reshape(size, size)
        im = psi_ref[:, item, 1].reshape(size, size)
        scale = scale_ref[pl.program_id(0) * bins + item]
        gram = dot(cat([re, im], 0), cat([cat([re, im], 1), cat([im, -re], 1)], 0), TN)
        sym = identity - scale * gram[:, :size]
        anti = -scale * gram[:, size:]
        state.append((sym, anti, None))
    for step in range(ITERS):
        after = []
        for sym, anti, total in state:
            left_high, left_low = split(cat([sym, anti], 1))
            if step == 0:
                total = identity + (sym + anti)
                right = cat([sym + anti, sym - anti], 0)
            elif step < ITERS - 1:
                right = cat([cat([sym + anti, total], 1), cat([sym - anti, total.T], 1)], 0)
            else:
                right = cat([total, total.T], 0)
            product = dot3(left_high, left_low, *split(right))
            if step > 0:
                total = total + product[:, -size:]
            if step < ITERS - 1:
                square = product[:, :size]
                square_t = square.T
                sym = 0.5 * (square + square_t)
                anti = 0.5 * (square - square_t)
            after.append((sym, anti, total))
        state = after
    for item in range(bins):
        total = state[item][2]
        total_t = total.T
        re = psi_ref[:, item, 0].reshape(size, size)
        im = psi_ref[:, item, 1].reshape(size, size)
        scale = scale_ref[pl.program_id(0) * bins + item]
        half = (0.5 * scale) * cat([total + total_t, total - total_t], 1)
        high, low = split(half)
        both = dot(cat([high, low], 0), cat([cat([re, im], 1), cat([-im, re], 1)], 0), NT)
        high, low = split(both[:size] + both[size:])
        out_ref[item, 0] = high
        out_ref[item, 1] = low


def middle_kernel(inverse_ref, packed_ref, out_ref):
    bins, size = inverse_ref.shape[0], inverse_ref.shape[2]
    total_bins = pl.num_programs(0) * bins
    identity = eye(size) * (1.0 / SCALE)
    rows = lax.broadcasted_iota(jnp.int32, (size, size), 0)
    columns = lax.broadcasted_iota(jnp.int32, (size, size), 1)

    def swapped(value):
        return cat([value, cat([value[:, size:], -value[:, :size]], 1)], 0)

    for item in range(bins):
        packed = packed_ref[:, item].reshape(size, size).astype(F32)
        packed_t = packed.T
        re = jnp.where(columns >= rows, packed, packed_t).astype(BF16)
        im = jnp.where(columns == rows, 0.0, jnp.where(columns < rows, packed, -packed_t)).astype(BF16)
        high, low = inverse_ref[item, 0], inverse_ref[item, 1]
        both = dot(cat([high, low], 0), cat([cat([re, im], 1), cat([-im, re], 1)], 0))
        left_high, left_low = split(both[:size] + both[size:])
        middle = dot3(left_high, left_low, swapped(high), swapped(low), NT) * (1.0 / SCALE)
        place = pl.program_id(0) * bins + item
        out_ref[pl.ds(place, size, stride=2 * total_bins), :] = middle[:, :size] + identity
        out_ref[pl.ds(total_bins + place, size, stride=2 * total_bins), :] = middle[:, size:]


def causal_kernel(table_ref, values_ref, out_ref, table_high, table_low):
    count = table_ref.shape[1]
    lanes = values_ref.shape[-1]

    @pl.when(pl.program_id(0) == 0)
    def _():
        for part in range(2):
            high, low = split(table_ref[part])
            table_high[part * count : (part + 1) * count] = high
            table_low[part * count : (part + 1) * count] = low

    values = cat([values_ref[:, 0, part].reshape(count, lanes) for part in range(2)], 1)
    high, low = split(values)
    whole = dot(table_high[...], high) + (dot(table_high[...], low) + dot(table_low[...], high))
    real, imag = whole[:count], whole[count:]
    shape = (out_ref.shape[0], out_ref.shape[3], lanes)
    out_ref[:, 0, 0] = (real[:, :lanes] - imag[:, lanes:]).reshape(shape)
    out_ref[:, 0, 1] = (real[:, lanes:] + imag[:, :lanes]).reshape(shape)


def product_kernel(causal_ref, psi_ref, out_ref):
    bins, size = psi_ref.shape[2], psi_ref.shape[5]
    panels, _, _, rows, _ = out_ref.shape
    columns = panels * rows
    total_bins = causal_ref.shape[0] // (2 * columns)
    base = (pl.program_id(0) * pl.num_programs(1) + pl.program_id(1)) * bins
    for item in range(bins):
        re = psi_ref[0, :, item, 0].reshape(size, size)
        im = psi_ref[0, :, item, 1].reshape(size, size)
        place = base + item
        part_re = causal_ref[pl.ds(place, columns, stride=2 * total_bins), :]
        part_im = causal_ref[pl.ds(total_bins + place, columns, stride=2 * total_bins), :]
        high, low = split(cat([part_re, part_im], 1))
        both = dot(cat([high, low], 0), cat([cat([re, -im], 1), cat([im, re], 1)], 0), NT)
        result = both[:columns] + both[columns:]
        out_ref[:, item, 0] = result[:, :size].reshape(panels, rows, size)
        out_ref[:, item, 1] = result[:, size:].reshape(panels, rows, size)


def projection_table(lag_limit, count, freq_size, pairs):
    own = count // (freq_size * 2 * pairs)
    row = lax.broadcasted_iota(jnp.int32, (count, 1), 0)
    column = lax.broadcasted_iota(jnp.int32, (1, count), 1)
    column_bins = (
        (column // own) % freq_size * (own * 2 * pairs) + column // (own * freq_size) * own + column % own
    )
    holder = row // (2 * own)
    row_bins = (
        holder % freq_size * (own * 2 * pairs)
        + (row // own % 2 * pairs + holder // freq_size) * own
        + row % own
    )
    shift = column_bins - row_bins
    unit = math.pi / count
    half_angle = shift.astype(F32) * unit
    turned = ((2 * lag_limit + 1) * shift) % (2 * count)
    turned = jnp.where(turned >= count, turned - 2 * count, turned)
    last_angle = turned.astype(F32) * unit
    below = jnp.where(shift == 0, 1.0, 2.0 * count * jnp.sin(half_angle))
    real = jnp.where(shift == 0, (lag_limit.astype(F32) + 0.5) / count, jnp.sin(last_angle) / below)
    imag = jnp.where(shift == 0, 0.0, (jnp.cos(half_angle) - jnp.cos(last_angle)) / below)
    return jnp.stack([real, imag])


def params(limit):
    return pltpu.CompilerParams(vmem_limit_bytes=limit * MIB)


def cost(flops, moved):
    return pl.CostEstimate(flops=flops, bytes_accessed=moved, transcendentals=0)


def after(value, *earlier):
    return lax.optimization_barrier((value,) + earlier)[0]


SWAP = ((0, 1), (1, 0))


def shards(freq_size, pairs, factor, spectrum, guess_scale, lag_cutoff):
    chan = ("side", "pair")
    chan_size = 2 * pairs
    group_bins, _, rows, size = factor.shape
    own = group_bins // chan_size
    count = group_bins * freq_size
    step = math.gcd(own, 4)
    column_parts = min(freq_size, rows)
    lane_parts = freq_size // column_parts
    kept = rows // column_parts
    lanes = size // lane_parts
    side, pair = lax.axis_index("side"), lax.axis_index("pair")
    member = side * pairs + pair
    devices = chan_size * freq_size

    panel_block = pl.BlockSpec((chan_size, step, 2, rows, size), lambda i: (0, i, 0, 0, 0))
    inverse_block = pl.BlockSpec((step, 2, size, 2 * size), lambda i: (i, 0, 0, 0))

    factor_own = lax.all_to_all(factor, chan, 0, 0, tiled=True)
    factor_own = factor_own.reshape(chan_size, own, 2, rows, size)
    row_index = lax.broadcasted_iota(jnp.int32, (rows, size), 0) + member * rows
    column_index = lax.broadcasted_iota(jnp.int32, (rows, size), 1)
    packed = jnp.where(column_index >= row_index, spectrum[:, 0], spectrum[:, 1])
    packed = lax.all_to_all(after(packed, factor_own), chan, 0, 0, tiled=True)
    packed = packed.reshape(chan_size, own, rows, size)
    table = projection_table(lag_cutoff[0], count, freq_size, pairs)
    scale = lax.dynamic_slice_in_dim(guess_scale, member * own, own, 0)

    inverse = pl.pallas_call(
        newton_kernel,
        grid=(own // step,),
        in_specs=[pl.BlockSpec(memory_space=pltpu.SMEM), panel_block],
        out_specs=inverse_block,
        out_shape=jax.ShapeDtypeStruct((own, 2, size, 2 * size), BF16),
        compiler_params=params(16),
        cost_estimate=cost(own * 64 * 2 * 4 * size**3, own * 6 * 4 * size * size),
    )(scale, factor_own)
    middle = pl.pallas_call(
        middle_kernel,
        grid=(own // step,),
        in_specs=[
            inverse_block,
            pl.BlockSpec((chan_size, step, rows, size), lambda i: (0, i, 0, 0)),
        ],
        out_specs=pl.BlockSpec((size * 2 * own, size), lambda i: (0, 0)),
        out_shape=jax.ShapeDtypeStruct((size * 2 * own, size), F32),
        compiler_params=params(16),
        cost_estimate=cost(own * 10 * 2 * 4 * size**3, own * 6 * 4 * size * size),
    )(inverse, packed)

    sent = middle.astype(jnp.float16)
    if lane_parts > 1:
        sent = sent.reshape(size, 2, own, lane_parts, lanes).transpose(0, 3, 1, 2, 4)
    sent = sent.reshape(devices, kept, 2, own, lanes)
    arrived = lax.all_to_all(sent, chan + ("freq",), 0, 0, tiled=True)

    across = lax.dynamic_slice_in_dim(factor_own, side * pairs, pairs, 0)
    across = lax.ppermute(after(across, arrived), "side", SWAP)
    far = (1 - side) * pairs
    beside = lax.dynamic_slice_in_dim(factor, (far + 1 - pair) * own, own, 0)
    beside = lax.ppermute(after(beside, arrived), "pair", SWAP)
    here = lax.dynamic_slice_in_dim(factor, (far + pair) * own, own, 0)
    panels = []
    for owner in range(2):
        for panel in range(chan_size):
            near = jnp.where(panel % pairs == pair, here, beside)
            other = jnp.where(panel // pairs == side, near, across[panel % pairs])
            panels.append(jnp.where(owner == side, factor_own[panel], other))
    psi = jnp.stack(panels).reshape(2, chan_size, own, 2, rows, size)

    values = arrived.astype(F32)
    sources, own_rows = devices, own
    if own % 8:
        values = values.transpose(1, 2, 0, 3, 4).reshape(1, kept, 2, count, lanes)
        sources, own_rows = 1, count
    holders, held = pairs * freq_size, 2 * own
    if held % 8:
        holders, held = 1, count
    causal = pl.pallas_call(
        causal_kernel,
        grid=(kept,),
        in_specs=[
            pl.BlockSpec((2, count, count), lambda i: (0, 0, 0)),
            pl.BlockSpec((sources, 1, 2, own_rows, lanes), lambda i: (0, i, 0, 0, 0)),
        ],
        out_specs=pl.BlockSpec((holders, 1, 2, held, lanes), lambda i: (0, i, 0, 0, 0)),
        out_shape=jax.ShapeDtypeStruct((holders, kept, 2, held, lanes), F32),
        scratch_shapes=[pltpu.VMEM((2 * count, count), BF16), pltpu.VMEM((2 * count, count), BF16)],
        compiler_params=params(24),
        cost_estimate=cost(kept * 24 * count * count * lanes, 16 * kept * count * lanes),
    )(table, values)
    causal = causal.astype(jnp.float16)
    if holders == 1:
        causal = causal.reshape(kept, 2, pairs * freq_size, 2 * own, lanes)
        causal = causal.transpose(2, 0, 1, 3, 4)
    back = lax.all_to_all(causal, ("pair", "freq"), 0, 0, tiled=True).astype(F32)
    if lane_parts > 1:
        back = back.reshape(pairs * column_parts, lane_parts, kept, 2, 2 * own, lanes)
        back = back.transpose(0, 2, 3, 4, 1, 5)
    back = back.reshape(pairs * rows * 2 * 2 * own, size)

    steps = own // step
    result = pl.pallas_call(
        product_kernel,
        grid=(2, steps),
        in_specs=[
            pl.BlockSpec(back.shape, lambda i, j: (0, 0)),
            pl.BlockSpec((1, chan_size, step, 2, rows, size), lambda i, j: (i, 0, j, 0, 0, 0)),
        ],
        out_specs=pl.BlockSpec((pairs, step, 2, rows, size), lambda i, j: (0, i * steps + j, 0, 0, 0)),
        out_shape=jax.ShapeDtypeStruct((pairs, 2 * own, 2, rows, size), F32),
        compiler_params=params(16),
        cost_estimate=cost(own * 4 * 4 * size**3, own * 5 * 4 * size * size),
    )(back, psi)
    given = lax.dynamic_index_in_dim(result, 1 - pair, 0, keepdims=False)
    given = lax.ppermute(given.astype(jnp.float16), "pair", SWAP).astype(F32)
    kept_here = lax.dynamic_index_in_dim(result, pair, 0, keepdims=False)
    given = given.reshape(2, 1, own, 2, rows, size)
    kept_here = kept_here.reshape(2, 1, own, 2, rows, size)
    first = jnp.where(pair == 0, kept_here, given)
    second = jnp.where(pair == 0, given, kept_here)
    whole = cat([first, second], 1).reshape(group_bins, 2, rows, size) * SCALE
    return jnp.swapaxes(whole, 2, 3)


def solution(mesh):
    freq_size, pairs = mesh.shape["freq"], mesh.shape["chan"] // 2
    split_mesh = jax.sharding.Mesh(
        mesh.devices.reshape(freq_size, 2, pairs), ("freq", "side", "pair")
    )
    in_specs = (
        P("freq", None, ("side", "pair"), None),
        P("freq", None, ("side", "pair"), None),
        P("freq"),
        P(),
    )
    out_specs = P("freq", None, None, ("side", "pair"))
    body = functools.partial(shards, freq_size, pairs)
    return jax.shard_map(
        body, mesh=split_mesh, in_specs=in_specs, out_specs=out_specs, check_vma=False
    )
```

profile of v0, /device:TPU:0, one launch (start us, length us, event | category | flops | bytes accessed | tf_op | source)
XLA Modules:
  0.0 148.8 jit_solution(2621448460650357434)
XLA Ops:
  0.0 0.0 copy-start.3
  0.0 0.0 copy-start.2
  0.0 6.4 %all-to-all-start = ((bf16[64,2,32,128]{3,2,1,0:T(8,128)(2,1)}), bf16[64,2,32,128]{3,2,1,0:T(8,128)(2,1)S(1)}, u32[]{:S(2)}, u32[]{:S(2)}) async-start(bf16[64,2,32,128]{3,2,1,0:T(8,128)(2,1)} %param.4), calls=%async_computation | async-start | bytes 2097152 | tf_op jit(solution)/shard_map/all_to_all | solution.py:215
  6.5 0.0 copy-done.3
  6.5 0.1 dynamic_slice.19.scale_ref
  6.5 0.1 iota_compare_fusion
  6.6 0.0 copy-done.2
  6.6 0.8 bitcast_select_fusion
  7.5 24.7 %all-to-all-done = bf16[64,2,32,128]{3,2,1,0:T(8,128)(2,1)S(1)} async-done(((bf16[64,2,32,128]{3,2,1,0:T(8,128)(2,1)}), bf16[64,2,32,128]{3,2,1,0:T(8,128)(2,1)S(1)}, u32[]{:S(2)}, u32[]{:S(2)}) %all-to-all-start) | async-done | bytes 1048608 | tf_op jit(solution)/shard_map/all_to_all | solution.py:215
  32.2 3.5 %all-to-all-start.1 = ((bf16[64,32,128]{2,1,0:T(8,128)(2,1)}), bf16[64,32,128]{2,1,0:T(8,128)(2,1)S(1)}, u32[]{:S(2)}, u32[]{:S(2)}) async-start(bf16[64,32,128]{2,1,0:T(8,128)(2,1)} %bitcast_select_fusion), calls=%async_computation.1 | async-start | bytes 1048576 | tf_op jit(solution)/shard_map/all_to_all | solution.py:220
  35.7 13.0 %shard_map.46.inverse_ref = bf16[16,2,128,256]{3,2,1,0:T(8,128)(2,1)S(1)} custom-call(f32[16]{0:T(128)S(1)} %dynamic_slice.19.scale_ref, bf16[4,16,2,32,128]{4,3,2,1,0:T(8,128)(2,1)S(1)} %bitcast.67), custom_call_target="tpu_custom_call" | custom-call | flops 17179869184 | bytes 6291456 | tf_op jit(solution)/shard_map/pallas_call | solution.py:225
  48.7 0.0 copy-start
  48.7 1.3 copy-done
  50.0 0.0 all-to-all-done.1
  50.0 0.0 copy-start.1
  50.0 1.6 %copy-done.1 = bf16[16,2,128,256]{3,2,1,0:T(8,128)(2,1)S(1)} copy-done((bf16[16,2,128,256]{3,2,1,0:T(8,128)(2,1)S(1)}, bf16[16,2,128,256]{3,2,1,0:T(8,128)(2,1)}, u32[]{:S(2)}) %copy-start.1) | copy-done | bytes 2097176
  51.6 4.3 %shard_map.47 = f32[4096,128]{1,0:T(8,128)S(1)} custom-call(bf16[16,2,128,256]{3,2,1,0:T(8,128)(2,1)S(1)} %copy-done.1, bf16[4,16,32,128]{3,2,1,0:T(8,128)(2,1)S(1)} %bitcast.70), custom_call_target="tpu_custom_call" | custom-call | flops 2684354560 | bytes 6291456 | tf_op jit(solution)/shard_map/pallas_call | solution.py:234
  55.9 1.1 convert_element_type.56
  57.1 6.0 %all-to-all-start.2 = ((f16[32,4,2,16,128]{4,3,2,1,0:T(8,128)(2,1)}), f16[32,4,2,16,128]{4,3,2,1,0:T(8,128)(2,1)S(1)}, u32[]{:S(2)}, u32[]{:S(2)}) async-start(f16[32,4,2,16,128]{4,3,2,1,0:T(8,128)(2,1)} %bitcast.6), calls=%async_computation.2 | async-start | bytes 2097152 | tf_op jit(solution)/shard_map/all_to_all | solution.py:251
  63.7 9.3 %fusion.4 = (f32[1,512,512]{2,1,0:T(8,128)S(1)}, f32[1,512,512]{2,1,0:T(8,128)}) fusion(f32[]{:T(128)} %bitcast, s32[512]{0:T(512)S(1)} %get-tuple-element.22, s32[512]{0:T(512)S(1)} %get-tuple-element.21, s32[]{:T(128)} %bitcast.1), kind=kLoop, calls=%fused_computation.14 | loop fusion | flops 7340032 | bytes 2101256 | tf_op jit(solution)/shard_map/jit(_where)/select_n | solution.py:177
  73.0 0.8 constant_dynamic-slice_fusion.1
  73.9 15.4 %all-to-all-done.2 = f16[32,4,2,16,128]{4,3,2,1,0:T(8,128)(2,1)S(1)} async-done(((f16[32,4,2,16,128]{4,3,2,1,0:T(8,128)(2,1)}), f16[32,4,2,16,128]{4,3,2,1,0:T(8,128)(2,1)S(1)}, u32[]{:S(2)}, u32[]{:S(2)}) %all-to-all-start.2) | async-done | bytes 1048608 | tf_op jit(solution)/shard_map/all_to_all | solution.py:251
  89.3 0.8 collective-permute-start.1
  90.1 1.7 %constant_dynamic-slice_fusion.2 = bf16[16,2,32,128]{3,2,1,0:T(8,128)(2,1)} fusion(bf16[64,2,32,128]{3,2,1,0:T(8,128)(2,1)} %param.4, s32[]{:T(128)S(6)} %select_n.396), kind=kLoop, calls=%fused_computation.95 | loop fusion | bytes 524292 | tf_op jit(solution)/shard_map/dynamic_slice | solution.py:256
  91.7 1.4 pad_maximum_fusion.table_ref
  93.1 1.2 collective-permute-start
  94.3 0.3 convert_element_type.57.values_ref
  94.6 4.6 %shard_map.48 = f32[16,4,2,32,128]{4,3,2,1,0:T(8,128)S(1)} custom-call(f32[2,512,512]{2,1,0:T(8,128)S(1)} %pad_maximum_fusion.table_ref, f32[32,4,2,16,128]{4,3,2,1,0:T(8,128)S(1)} %convert_element_type.57.values_ref), custom_call_target="tpu_custom_call" | custom-call | flops 3221225472 | bytes 4194304 | tf_op jit(solution)/shard_map/pallas_call | solution.py:275
  99.1 1.3 convert_element_type.58
  100.4 4.3 %all-to-all-start.3 = ((f16[16,4,2,32,128]{4,3,2,1,0:T(8,128)(2,1)}), f16[16,4,2,32,128]{4,3,2,1,0:T(8,128)(2,1)}, u32[]{:S(2)}, u32[]{:S(2)}) async-start(f16[16,4,2,32,128]{4,3,2,1,0:T(8,128)(2,1)} %convert_element_type.58), calls=%async_computation.3 | async-start | bytes 2097152 | tf_op jit(solution)/shard_map/all_to_all | solution.py:292
  104.7 3.6 %collective-permute-done = bf16[16,2,32,128]{3,2,1,0:T(8,128)(2,1)S(1)} collective-permute-done((bf16[16,2,32,128]{3,2,1,0:T(8,128)(2,1)}, bf16[16,2,32,128]{3,2,1,0:T(8,128)(2,1)S(1)}, u32[]{:S(2)}, u32[]{:S(2)}) %collective-permute-start) | collective-permute-done | bytes 262176 | tf_op jit(solution)/shard_map/ppermute | solution.py:257
  108.4 6.7 %collective-permute-done.1 = bf16[2,16,2,32,128]{4,3,2,1,0:T(8,128)(2,1)} collective-permute-done((bf16[2,16,2,32,128]{4,3,2,1,0:T(8,128)(2,1)}, bf16[2,16,2,32,128]{4,3,2,1,0:T(8,128)(2,1)}, u32[]{:S(2)}, u32[]{:S(2)}) %collective-permute-start.1) | collective-permute-done | bytes 524320 | tf_op jit(solution)/shard_map/ppermute | solution.py:254
  115.0 1.2 bitcast_dynamic-update-slice_fusion.7
  116.3 1.2 bitcast_dynamic-update-slice_fusion.6
  117.5 1.1 bitcast_dynamic-update-slice_fusion.5
  118.6 1.1 bitcast_dynamic-update-slice_fusion.4
  119.7 1.1 bitcast_dynamic-update-slice_fusion.3
  120.8 1.1 bitcast_dynamic-update-slice_fusion.2
  121.9 1.1 bitcast_dynamic-update-slice_fusion.1
  123.0 1.1 bitcast_dynamic-update-slice_fusion
  124.1 3.4 %all-to-all-done.3 = f16[16,4,2,32,128]{4,3,2,1,0:T(8,128)(2,1)} async-done(((f16[16,4,2,32,128]{4,3,2,1,0:T(8,128)(2,1)}), f16[16,4,2,32,128]{4,3,2,1,0:T(8,128)(2,1)}, u32[]{:S(2)}, u32[]{:S(2)}) %all-to-all-start.3) | async-done | bytes 1048608 | tf_op jit(solution)/shard_map/all_to_all | solution.py:292
  127.5 1.4 bitcast_convert_fusion.causal_ref
  128.9 3.4 %shard_map.49 = f32[2,32,2,32,128]{4,3,2,1,0:T(8,128)S(1)} custom-call(f32[4096,128]{1,0:T(8,128)S(1)} %bitcast_convert_fusion.causal_ref, bf16[2,4,16,2,32,128]{5,4,3,2,1,0:T(8,128)(2,1)S(1)} %bitcast.69), custom_call_target="tpu_custom_call" | custom-call | flops 536870912 | bytes 5242880 | tf_op jit(solution)/shard_map/pallas_call | solution.py:299
  132.2 0.3 fusion.16
  132.6 0.1 collective-permute-start.2
  132.6 13.9 %collective-permute-done.2 = f16[32,2,32,128]{3,2,1,0:T(8,128)(2,1)S(1)} collective-permute-done((f16[32,2,32,128]{3,2,1,0:T(8,128)(2,1)S(1)}, f16[32,2,32,128]{3,2,1,0:T(8,128)(2,1)S(1)}, u32[]{:S(2)}, u32[]{:S(2)}) %collective-permute-start.2) | collective-permute-done | bytes 524320 | tf_op jit(solution)/shard_map/ppermute | solution.py:312
  146.5 0.3 convert_select_fusion.1
  146.8 0.4 maximum_multiply_fusion
  147.2 1.6 %copy.6 = f32[2,2,16,2,32,128]{5,4,3,2,1,0:T(8,128)} copy(f32[2,2,16,2,32,128]{5,4,3,2,0,1:T(8,128)S(1)} %maximum_multiply_fusion) | data formatting | bytes 4194304 | tf_op jit(solution)/shard_map/mul | solution.py:318
  (2 shorter events, 0.0 us)
Async XLA Ops:
  0.0 6.5 %copy-start.3 = (f32[64]{0:T(128)S(1)}, f32[64]{0:T(128)}, u32[]{:S(2)}) copy-start(f32[64]{0:T(128)} %param.6) | copy-start | bytes 772
  0.0 6.6 %copy-start.2 = (bf16[64,2,32,128]{3,2,1,0:T(8,128)(2,1)S(1)}, bf16[64,2,32,128]{3,2,1,0:T(8,128)(2,1)}, u32[]{:S(2)}) copy-start(bf16[64,2,32,128]{3,2,1,0:T(8,128)(2,1)} %param.5) | copy-start | bytes 3145732
  0.0 32.2 %all-to-all-start = ((bf16[64,2,32,128]{3,2,1,0:T(8,128)(2,1)}), bf16[64,2,32,128]{3,2,1,0:T(8,128)(2,1)S(1)}, u32[]{:S(2)}, u32[]{:S(2)}) async-start(bf16[64,2,32,128]{3,2,1,0:T(8,128)(2,1)} %param.4), calls=%async_computation | async-start | bytes 2097152 | tf_op jit(solution)/shard_map/all_to_all | solution.py:215
  32.2 17.9 %all-to-all-start.1 = ((bf16[64,32,128]{2,1,0:T(8,128)(2,1)}), bf16[64,32,128]{2,1,0:T(8,128)(2,1)S(1)}, u32[]{:S(2)}, u32[]{:S(2)}) async-start(bf16[64,32,128]{2,1,0:T(8,128)(2,1)} %bitcast_select_fusion), calls=%async_computation.1 | async-start | bytes 1048576 | tf_op jit(solution)/shard_map/all_to_all | solution.py:220
  48.7 1.3 copy-start
  50.0 1.6 %copy-start.1 = (bf16[16,2,128,256]{3,2,1,0:T(8,128)(2,1)S(1)}, bf16[16,2,128,256]{3,2,1,0:T(8,128)(2,1)}, u32[]{:S(2)}) copy-start(bf16[16,2,128,256]{3,2,1,0:T(8,128)(2,1)} %copy-done) | copy-start | bytes 6291460
  57.1 32.2 %all-to-all-start.2 = ((f16[32,4,2,16,128]{4,3,2,1,0:T(8,128)(2,1)}), f16[32,4,2,16,128]{4,3,2,1,0:T(8,128)(2,1)S(1)}, u32[]{:S(2)}, u32[]{:S(2)}) async-start(f16[32,4,2,16,128]{4,3,2,1,0:T(8,128)(2,1)} %bitcast.6), calls=%async_computation.2 | async-start | bytes 2097152 | tf_op jit(solution)/shard_map/all_to_all | solution.py:251
  89.3 25.7 %collective-permute-start.1 = (bf16[2,16,2,32,128]{4,3,2,1,0:T(8,128)(2,1)}, bf16[2,16,2,32,128]{4,3,2,1,0:T(8,128)(2,1)}, u32[]{:S(2)}, u32[]{:S(2)}) collective-permute-start(bf16[2,16,2,32,128]{4,3,2,1,0:T(8,128)(2,1)} %constant_dynamic-slice_fusion.1), channel_id=1, source_target_pairs={{0,2},{2,0},{1,3},{3,1},{4,6},{6,4},{5,7},{7,5},{8,10},{10,8},{9,1... | collective-permute-start | bytes 1572872 | tf_op jit(solution)/shard_map/ppermute | solution.py:254
  93.1 15.2 %collective-permute-start = (bf16[16,2,32,128]{3,2,1,0:T(8,128)(2,1)}, bf16[16,2,32,128]{3,2,1,0:T(8,128)(2,1)S(1)}, u32[]{:S(2)}, u32[]{:S(2)}) collective-permute-start(bf16[16,2,32,128]{3,2,1,0:T(8,128)(2,1)} %constant_dynamic-slice_fusion.2), channel_id=1, source_target_pairs={{0,1},{1,0},{2,3},{3,2},{4,5},{5,4},{6,7},{7,6},{8,9},{9,8},{10,11... | collective-permute-start | bytes 786440 | tf_op jit(solution)/shard_map/ppermute | solution.py:257
  100.4 27.1 %all-to-all-start.3 = ((f16[16,4,2,32,128]{4,3,2,1,0:T(8,128)(2,1)}), f16[16,4,2,32,128]{4,3,2,1,0:T(8,128)(2,1)}, u32[]{:S(2)}, u32[]{:S(2)}) async-start(f16[16,4,2,32,128]{4,3,2,1,0:T(8,128)(2,1)} %convert_element_type.58), calls=%async_computation.3 | async-start | bytes 2097152 | tf_op jit(solution)/shard_map/all_to_all | solution.py:292
  132.6 14.0 %collective-permute-start.2 = (f16[32,2,32,128]{3,2,1,0:T(8,128)(2,1)S(1)}, f16[32,2,32,128]{3,2,1,0:T(8,128)(2,1)S(1)}, u32[]{:S(2)}, u32[]{:S(2)}) collective-permute-start(f16[32,2,32,128]{3,2,1,0:T(8,128)(2,1)S(1)} %get-tuple-element.15), channel_id=1, source_target_pairs={{0,1},{1,0},{2,3},{3,2},{4,5},{5,4},{6,7},{7,6},{8,9},{9,8},{10,11... | collective-permute-start | bytes 1572872 | tf_op jit(solution)/shard_map/ppermute | solution.py:312
where the time goes:
time: 150 us; the launch traced here: 149 us
  waiting for transfers between devices  67.7 us (45%)
  other arithmetic  25.6 us (17%)
  Pallas kernels  25.3 us (17%)
  starting transfers between devices  22.2 us (15%)
  local copies, waits for them, and re-layouts  7.07 us (5%)
    all_to_all x1, waiting for transfers between devices, shards(): factor_own = lax.all_to_all(factor, chan, 0, 0, tiled=True)  24.7 us
    all_to_all x1, waiting for transfers between devices, shards(): arrived = lax.all_to_all(sent, chan + ('freq',), 0, 0, tiled=True)  15.4 us
    ppermute x1, waiting for transfers between devices, shards(): given = lax.ppermute(given.astype(jnp.float16), 'pair', SWAP).astype(F32)  13.9 us
    pallas_call x1, Pallas kernels, shards(): pl.pallas_call(newton_kernel, grid=(own // step,), in_specs=[pl.BlockSpec...  13 us
    select_n x1, other arithmetic, projection_table(): jnp.where(shift == 0, (lag_limit.astype(F32) + 0.5) / count, jnp.sin(last...  9.27 us
    unnamed x7, other arithmetic  7.93 us
    ppermute x1, waiting for transfers between devices, shards(): across = lax.ppermute(after(across, arrived), 'side', SWAP)  6.68 us
    all_to_all x1, starting transfers between devices, shards(): factor_own = lax.all_to_all(factor, chan, 0, 0, tiled=True)  6.45 us
  transfers between devices with their start and end apart: 7, of which 6 were waited for; matrix products, arithmetic and copies ran while one was open for 17% of the time, Pallas kernels for 12%

commit v1 on v0

v1 whole, which is shorter than its diff:
```python
import functools
import math

import jax
import jax.numpy as jnp
from jax import lax
from jax.experimental import pallas as pl
from jax.experimental.pallas import tpu as pltpu
from jax.sharding import PartitionSpec as P

ITERS = 8
SCALE = 16.0
CHUNKS = 2
F32 = jnp.float32
BF16 = jnp.bfloat16
MIB = 1024 * 1024
NN = (((1,), (0,)), ((), ()))
NT = (((1,), (1,)), ((), ()))
TN = (((0,), (0,)), ((), ()))


def dot(left, right, dims=NN):
    return lax.dot_general(left, right, dims, preferred_element_type=F32)


def split(value):
    high = value.astype(BF16)
    return high, (value - high.astype(F32)).astype(BF16)


def cat(parts, axis):
    return jnp.concatenate(parts, axis=axis)


def dot3(left_high, left_low, right_high, right_low, dims=NN):
    rows = left_high.shape[0]
    both = dot(cat([left_high, left_low], 0), right_high, dims)
    return both[:rows] + (both[rows:] + dot(left_high, right_low, dims))


def eye(size):
    rows = lax.broadcasted_iota(jnp.int32, (size, size), 0)
    columns = lax.broadcasted_iota(jnp.int32, (size, size), 1)
    return jnp.where(rows == columns, 1.0, 0.0).astype(F32)


def place_rows(member, panels, out_ref):
    rows = panels[0].shape[-2]
    for index, panel in enumerate(panels):
        start = pl.multiple_of((member ^ index) * rows, rows)
        out_ref[..., pl.ds(start, rows), :] = panel[...]


def newton_kernel(member_ref, scale_ref, own_ref, one_ref, two_ref, three_ref, out_ref, psi_ref):
    bins, _, size, _ = psi_ref.shape
    place_rows(member_ref[0], [own_ref.at[0], one_ref, two_ref, three_ref], psi_ref)
    identity = eye(size)
    state = []
    for item in range(bins):
        re, im = psi_ref[item, 0], psi_ref[item, 1]
        scale = scale_ref[pl.program_id(0) * bins + item]
        gram = dot(cat([re, im], 0), cat([cat([re, im], 1), cat([im, -re], 1)], 0), TN)
        sym = identity - scale * gram[:, :size]
        anti = -scale * gram[:, size:]
        state.append((sym, anti, None))
    for step in range(ITERS):
        after = []
        for sym, anti, total in state:
            left_high, left_low = split(cat([sym, anti], 1))
            if step == 0:
                total = identity + (sym + anti)
                right = cat([sym + anti, sym - anti], 0)
            elif step < ITERS - 1:
                right = cat([cat([sym + anti, total], 1), cat([sym - anti, total.T], 1)], 0)
            else:
                right = cat([total, total.T], 0)
            product = dot3(left_high, left_low, *split(right))
            if step > 0:
                total = total + product[:, -size:]
            if step < ITERS - 1:
                square = product[:, :size]
                square_t = square.T
                sym = 0.5 * (square + square_t)
                anti = 0.5 * (square - square_t)
            after.append((sym, anti, total))
        state = after
    for item in range(bins):
        total = state[item][2]
        total_t = total.T
        re, im = psi_ref[item, 0], psi_ref[item, 1]
        scale = scale_ref[pl.program_id(0) * bins + item]
        half = (0.5 * scale) * cat([total + total_t, total - total_t], 1)
        high, low = split(half)
        both = dot(cat([high, low], 0), cat([cat([re, im], 1), cat([-im, re], 1)], 0), NT)
        high, low = split(both[:size] + both[size:])
        out_ref[item, 0] = high
        out_ref[item, 1] = low


def middle_kernel(member_ref, inverse_ref, own_ref, one_ref, two_ref, three_ref, out_ref, packed_ref):
    bins, size = inverse_ref.shape[0], inverse_ref.shape[2]
    total_bins = pl.num_programs(0) * bins
    place_rows(member_ref[0], [own_ref.at[0], one_ref, two_ref, three_ref], packed_ref)
    identity = eye(size) * (1.0 / SCALE)
    rows = lax.broadcasted_iota(jnp.int32, (size, size), 0)
    columns = lax.broadcasted_iota(jnp.int32, (size, size), 1)

    def swapped(value):
        return cat([value, cat([value[:, size:], -value[:, :size]], 1)], 0)

    for item in range(bins):
        packed = packed_ref[item].astype(F32)
        packed_t = packed.T
        re = jnp.where(columns >= rows, packed, packed_t).astype(BF16)
        im = jnp.where(columns == rows, 0.0, jnp.where(columns < rows, packed, -packed_t)).astype(BF16)
        high, low = inverse_ref[item, 0], inverse_ref[item, 1]
        both = dot(cat([high, low], 0), cat([cat([re, im], 1), cat([-im, re], 1)], 0))
        left_high, left_low = split(both[:size] + both[size:])
        middle = dot3(left_high, left_low, swapped(high), swapped(low), NT) * (1.0 / SCALE)
        place = pl.program_id(0) * bins + item
        out_ref[pl.ds(place, size, stride=2 * total_bins), :] = middle[:, :size] + identity
        out_ref[pl.ds(total_bins + place, size, stride=2 * total_bins), :] = middle[:, size:]


def causal_kernel(real_ref, imag_ref, values_ref, out_ref, table_high, table_low):
    count = real_ref.shape[1]
    lanes = values_ref.shape[-1]

    @pl.when(pl.program_id(0) == 0)
    def _():
        for part, table_ref in enumerate((real_ref, imag_ref)):
            high, low = split(table_ref[...])
            table_high[part * count : (part + 1) * count] = high
            table_low[part * count : (part + 1) * count] = low

    values = cat([values_ref[:, 0, part].reshape(count, lanes) for part in range(2)], 1)
    high, low = split(values)
    whole = dot(table_high[...], high) + (dot(table_high[...], low) + dot(table_low[...], high))
    real, imag = whole[:count], whole[count:]
    shape = (out_ref.shape[0], out_ref.shape[3], lanes)
    out_ref[:, 0, 0] = (real[:, :lanes] - imag[:, lanes:]).reshape(shape)
    out_ref[:, 0, 1] = (real[:, lanes:] + imag[:, :lanes]).reshape(shape)


def product(causal_ref, psi_ref, out_ref, first):
    bins, _, size, _ = psi_ref.shape
    panels, _, _, rows, _ = out_ref.shape
    columns = panels * rows
    total_bins = causal_ref.shape[0] // (2 * columns)
    for item in range(bins):
        re, im = psi_ref[item, 0], psi_ref[item, 1]
        place = first + pl.program_id(0) * bins + item
        part_re = causal_ref[pl.ds(place, columns, stride=2 * total_bins), :]
        part_im = causal_ref[pl.ds(total_bins + place, columns, stride=2 * total_bins), :]
        high, low = split(cat([part_re, part_im], 1))
        both = dot(cat([high, low], 0), cat([cat([re, -im], 1), cat([im, re], 1)], 0), NT)
        result = both[:columns] + both[columns:]
        out_ref[:, item, 0] = result[:, :size].reshape(panels, rows, size)
        out_ref[:, item, 1] = result[:, size:].reshape(panels, rows, size)


def near_kernel(causal_ref, psi_ref, out_ref):
    product(causal_ref, psi_ref, out_ref, 0)


def far_kernel(member_ref, causal_ref, own_ref, one_ref, two_ref, three_ref, out_ref, psi_ref):
    place_rows(member_ref[0], [own_ref.at[0], one_ref, two_ref, three_ref], psi_ref)
    product(causal_ref, psi_ref, out_ref, pl.num_programs(0) * psi_ref.shape[0])


def projection_table(lag_limit, count, freq_size, pairs, side):
    own = count // (freq_size * 2 * pairs)
    row = lax.broadcasted_iota(jnp.int32, (count, 1), 0)
    column = lax.broadcasted_iota(jnp.int32, (1, count), 1)
    column_bins = (
        (column // own) % freq_size * (own * 2 * pairs) + column // (own * freq_size) * own + column % own
    )
    holder = row // (2 * own)
    row_bins = (
        holder % freq_size * (own * 2 * pairs)
        + ((row // own % 2 ^ side) * pairs + holder // freq_size) * own
        + row % own
    )
    shift = column_bins - row_bins
    unit = math.pi / count
    half_angle = shift.astype(F32) * unit
    turned = ((2 * lag_limit + 1) * shift) % (2 * count)
    turned = jnp.where(turned >= count, turned - 2 * count, turned)
    last_angle = turned.astype(F32) * unit
    below = jnp.where(shift == 0, 1.0, 2.0 * count * jnp.sin(half_angle))
    real = jnp.where(shift == 0, (lag_limit.astype(F32) + 0.5) / count, jnp.sin(last_angle) / below)
    imag = jnp.where(shift == 0, 0.0, (jnp.cos(half_angle) - jnp.cos(last_angle)) / below)
    return real, imag


def params(limit):
    return pltpu.CompilerParams(vmem_limit_bytes=limit * MIB)


def cost(flops, moved):
    return pl.CostEstimate(flops=flops, bytes_accessed=moved, transcendentals=0)


def after(value, *earlier):
    return lax.optimization_barrier((value,) + earlier)[0]


SWAP = ((0, 1), (1, 0))
FLIP = ((0, 3), (1, 2), (2, 1), (3, 0))


def swap(value, distance):
    if distance == 1:
        return lax.ppermute(value, "pair", SWAP)
    if distance == 2:
        return lax.ppermute(value, "side", SWAP)
    return lax.ppermute(value, ("side", "pair"), FLIP)


def call(kernel, steps, in_specs, out_specs, out_shape, scratch, flops, moved):
    return pl.pallas_call(
        kernel,
        grid_spec=pltpu.PrefetchScalarGridSpec(
            num_scalar_prefetch=1,
            grid=(steps,),
            in_specs=in_specs,
            out_specs=out_specs,
            scratch_shapes=scratch,
        ),
        out_shape=out_shape,
        compiler_params=params(16),
        cost_estimate=cost(flops, moved),
    )


def shards(freq_size, pairs, factor, spectrum, guess_scale, lag_cutoff):
    chan = ("side", "pair")
    chan_size = 2 * pairs
    group_bins, _, rows, size = factor.shape
    own = group_bins // chan_size
    count = group_bins * freq_size
    chunks = CHUNKS if own % (4 * CHUNKS) == 0 else 1
    part = own // chunks
    step = math.gcd(part, 4)
    column_parts = min(freq_size, rows)
    lane_parts = freq_size // column_parts
    kept = rows // column_parts
    lanes = size // lane_parts
    side, pair = lax.axis_index("side"), lax.axis_index("pair")
    member = side * pairs + pair
    members = member.reshape(1)
    devices = chan_size * freq_size
    distances = range(1, chan_size)

    factors = factor.reshape(chan_size, own, 2, rows, size)

    def rows_for(owner, first, length):
        return lax.dynamic_slice(
            factors, (owner, first, 0, 0, 0), (1, length, 2, rows, size)
        ).reshape(length, 2, rows, size)

    arrived = []
    for chunk in range(chunks):
        pieces = [rows_for(member ^ d, chunk * part, part) for d in distances]
        if arrived:
            pieces = lax.optimization_barrier(tuple(pieces) + tuple(arrived[-1]))[: len(pieces)]
        arrived.append([swap(piece, d) for piece, d in zip(pieces, distances)])
    row_index = lax.broadcasted_iota(jnp.int32, (rows, size), 0) + member * rows
    column_index = lax.broadcasted_iota(jnp.int32, (rows, size), 1)
    packed = jnp.where(column_index >= row_index, spectrum[:, 0], spectrum[:, 1])
    packed = packed.reshape(chan_size, own, rows, size)
    pieces = [lax.dynamic_index_in_dim(packed, member ^ d, 0, keepdims=False) for d in distances]
    pieces = lax.optimization_barrier(tuple(pieces) + tuple(arrived[-1]))[: len(pieces)]
    packed_arrived = [swap(piece, d) for piece, d in zip(pieces, distances)]
    table_re, table_im = projection_table(lag_cutoff[0], count, freq_size, pairs, side)

    local_block = lambda first: pl.BlockSpec(
        (1, step, 2, rows, size), lambda i, m: (m[0], i + first, 0, 0, 0)
    )
    other_block = pl.BlockSpec((step, 2, rows, size), lambda i, m: (i, 0, 0, 0))
    whole_block = pl.BlockSpec((step, 2, size, size), lambda i, m: (i, 0, 0, 0))
    inverse_block = pl.BlockSpec((step, 2, size, 2 * size), lambda i, m: (i, 0, 0, 0))
    inverses, psis, middles = [], [], []
    for chunk in range(chunks):
        scale = lax.dynamic_slice_in_dim(guess_scale, member * own + chunk * part, part, 0)
        inverse, psi = call(
            newton_kernel,
            part // step,
            [pl.BlockSpec(memory_space=pltpu.SMEM), local_block(chunk * part // step)] + [other_block] * 3,
            [inverse_block, whole_block],
            [
                jax.ShapeDtypeStruct((part, 2, size, 2 * size), BF16),
                jax.ShapeDtypeStruct((part, 2, size, size), BF16),
            ],
            [],
            part * 64 * 2 * 4 * size**3,
            part * 6 * 4 * size * size,
        )(members, scale, factors, *arrived[chunk])
        inverses.append(inverse)
        psis.append(psi)
    for chunk in range(chunks):
        first = chunk * part // step
        other = pl.BlockSpec((step, rows, size), lambda i, m, first=first: (i + first, 0, 0))
        middles.append(
            call(
                middle_kernel,
                part // step,
                [
                    inverse_block,
                    pl.BlockSpec(
                        (1, step, rows, size), lambda i, m, first=first: (m[0], i + first, 0, 0)
                    ),
                ]
                + [other] * 3,
                pl.BlockSpec((size * 2 * part, size), lambda i, m: (0, 0)),
                jax.ShapeDtypeStruct((size * 2 * part, size), F32),
                [pltpu.VMEM((step, size, size), BF16)],
                part * 10 * 2 * 4 * size**3,
                part * 6 * 4 * size * size,
            )(members, inverses[chunk], packed, *packed_arrived)
        )
    middles = [value.astype(jnp.float16).reshape(size, 2, part, size) for value in middles]
    sent = cat(middles, 2) if chunks > 1 else middles[0]
    if lane_parts > 1:
        sent = sent.reshape(size, 2, own, lane_parts, lanes).transpose(0, 3, 1, 2, 4)
    sent = sent.reshape(devices, kept, 2, own, lanes)
    gathered = lax.all_to_all(sent, chan + ("freq",), 0, 0, tiled=True)

    across = swap(after(rows_for(member, 0, own), packed_arrived[0]), 2)
    across_pair = cat([piece[0] for piece in arrived], 0) if chunks > 1 else arrived[0][0]
    across_pair = swap(after(across_pair, gathered), 2)
    beside = swap(after(rows_for(member ^ 3, 0, own), packed_arrived[0]), 1)

    values = gathered.astype(F32)
    sources, own_rows = devices, own
    if own % 8:
        values = values.transpose(1, 2, 0, 3, 4).reshape(1, kept, 2, count, lanes)
        sources, own_rows = 1, count
    holders, held = pairs * freq_size, 2 * own
    if held % 8:
        holders, held = 1, count
    table_block = pl.BlockSpec((count, count), lambda i: (0, 0))
    causal = pl.pallas_call(
        causal_kernel,
        grid=(kept,),
        in_specs=[
            table_block,
            table_block,
            pl.BlockSpec((sources, 1, 2, own_rows, lanes), lambda i: (0, i, 0, 0, 0)),
        ],
        out_specs=pl.BlockSpec((holders, 1, 2, held, lanes), lambda i: (0, i, 0, 0, 0)),
        out_shape=jax.ShapeDtypeStruct((holders, kept, 2, held, lanes), F32),
        scratch_shapes=[pltpu.VMEM((2 * count, count), BF16), pltpu.VMEM((2 * count, count), BF16)],
        compiler_params=params(24),
        cost_estimate=cost(kept * 24 * count * count * lanes, 16 * kept * count * lanes),
    )(table_re, table_im, values)
    causal = causal.astype(jnp.float16)
    if holders == 1:
        causal = causal.reshape(kept, 2, pairs * freq_size, 2 * own, lanes)
        causal = causal.transpose(2, 0, 1, 3, 4)
    back = lax.all_to_all(causal, ("pair", "freq"), 0, 0, tiled=True).astype(F32)
    if lane_parts > 1:
        back = back.reshape(pairs * column_parts, lane_parts, kept, 2, 2 * own, lanes)
        back = back.transpose(0, 2, 3, 4, 1, 5)
    back = back.reshape(pairs * rows * 2 * 2 * own, size)

    back_block = pl.BlockSpec(back.shape, lambda i, m: (0, 0))
    result_block = pl.BlockSpec((pairs, step, 2, rows, size), lambda i, m: (0, i, 0, 0, 0))
    result_shape = jax.ShapeDtypeStruct((pairs, own, 2, rows, size), F32)
    flops, moved = own * 2 * 4 * size**3, own * 4 * 4 * size * size
    psi = cat(psis, 0) if chunks > 1 else psis[0]
    near = pl.pallas_call(
        near_kernel,
        grid=(own // step,),
        in_specs=[
            pl.BlockSpec(back.shape, lambda i: (0, 0)),
            pl.BlockSpec((step, 2, size, size), lambda i: (i, 0, 0, 0)),
        ],
        out_specs=pl.BlockSpec((pairs, step, 2, rows, size), lambda i: (0, i, 0, 0, 0)),
        out_shape=result_shape,
        compiler_params=params(16),
        cost_estimate=cost(flops, moved),
    )(back, psi)
    far = call(
        far_kernel,
        own // step,
        [
            back_block,
            pl.BlockSpec((1, step, 2, rows, size), lambda i, m: (m[0] ^ 2, i, 0, 0, 0)),
        ]
        + [other_block] * 3,
        result_block,
        result_shape,
        [pltpu.VMEM((step, 2, size, size), BF16)],
        flops,
        moved,
    )(members, back, factors, beside, across, across_pair)

    blocks = [None] * chan_size
    for distance, result in ((0, near), (2, far)):
        given = lax.dynamic_index_in_dim(result, 1 - pair, 0, keepdims=False)
        blocks[distance] = lax.dynamic_index_in_dim(result, pair, 0, keepdims=False)
        blocks[distance + 1] = swap(given.astype(jnp.float16), 1).astype(F32)
    ordered = []
    for owner in range(chan_size):
        distance = member ^ owner
        low = jnp.where(distance % 2 == 0, blocks[0], blocks[1])
        high = jnp.where(distance % 2 == 0, blocks[2], blocks[3])
        ordered.append(jnp.where(distance < 2, low, high))
    whole = cat(ordered, 0) * SCALE
    return jnp.swapaxes(whole, 2, 3)


def solution(mesh):
    freq_size, pairs = mesh.shape["freq"], mesh.shape["chan"] // 2
    split_mesh = jax.sharding.Mesh(
        mesh.devices.reshape(freq_size, 2, pairs), ("freq", "side", "pair")
    )
    in_specs = (
        P("freq", None, ("side", "pair"), None),
        P("freq", None, ("side", "pair"), None),
        P("freq"),
        P(),
    )
    out_specs = P("freq", None, None, ("side", "pair"))
    body = functools.partial(shards, freq_size, pairs)
    return jax.shard_map(
        body, mesh=split_mesh, in_specs=in_specs, out_specs=out_specs, check_vma=False
    )
```

time: 150 us -> 142 us (0.947)
  starting transfers between devices: 22.2 us -> 31.2 us
  other arithmetic: 25.6 us -> 16.8 us
  waiting for transfers between devices: 67.7 us -> 60.8 us
  local copies, waits for them, and re-layouts: 7.07 us -> 5.17 us
    all_to_all x3 -> x1, waiting for transfers between devices: 40.2 us -> 17.1 us  [shards(): gathered = lax.all_to_all(sent, chan + ('freq',), 0, 0, tiled=True)]
    ppermute x3 -> x14, starting transfers between devices: 2 us -> 21.4 us  [the longest x3 7.99 us: swap(): return lax.ppermute(value, ('side', 'pair'), FLIP)]
    all_to_all x1, waiting for transfers between devices: 3.38 us -> 21.4 us  [shards(): lax.all_to_all(causal, ('pair', 'freq'), 0, 0, tiled=True).astype(F32)]
    all_to_all x3 -> x1, starting transfers between devices: 15.9 us -> 5.32 us  [shards(): gathered = lax.all_to_all(sent, chan + ('freq',), 0, 0, tiled=True)]
    unnamed x7 -> x0, other arithmetic: 7.93 us -> none
    dynamic_slice x3 -> x1, local copies, waits for them, and re-layouts: 2.58 us -> 0.08 us  [shards(): lax.dynamic_slice_in_dim(guess_scale, member * own + chunk * part, part, 0)]
    another operation x2 -> x0, other arithmetic: 2.48 us -> none  [the longest x1 1.39 us: projection_table(): return jnp.stack([real, imag])]
    concatenate x0 -> x3, other arithmetic: none -> 2.19 us  [cat(): return jnp.concatenate(parts, axis=axis)]
  transfers between devices with their start and end apart: 7 -> 16, of which waited for: 6 -> 9; matrix products, arithmetic and copies ran while one was open for 17% -> 9% of each run, Pallas kernels for 12% -> 11%
where the time goes in v1:
time: 142 us; the launch traced here: 141 us
  waiting for transfers between devices  60.8 us (43%)
  starting transfers between devices  31.2 us (22%)
  Pallas kernels  26.4 us (19%)
  other arithmetic  16.8 us (12%)
  local copies, waits for them, and re-layouts  5.17 us (4%)
    all_to_all x1, waiting for transfers between devices, shards(): lax.all_to_all(causal, ('pair', 'freq'), 0, 0, tiled=True).astype(F32)  21.4 us
    all_to_all x1, waiting for transfers between devices, shards(): gathered = lax.all_to_all(sent, chan + ('freq',), 0, 0, tiled=True)  17.1 us
    pallas_call x2, Pallas kernels, shards(): call(newton_kernel, part // step, [pl.BlockSpec(memory_space=pltpu.SMEM),...  13.6 us
    ppermute x6, waiting for transfers between devices, swap(): return lax.ppermute(value, 'pair', SWAP)  11.7 us
    ppermute x5, waiting for transfers between devices, swap(): return lax.ppermute(value, 'side', SWAP)  8.41 us
    select_n x1, other arithmetic, projection_table(): jnp.where(shift == 0, 0.0, (jnp.cos(half_angle) - jnp.cos(last_angle)) /...  8.24 us
    ppermute x3, starting transfers between devices, swap(): return lax.ppermute(value, ('side', 'pair'), FLIP)  7.99 us
    ppermute x5, starting transfers between devices, swap(): return lax.ppermute(value, 'side', SWAP)  6.86 us
  transfers between devices with their start and end apart: 16, of which 9 were waited for; matrix products, arithmetic and copies ran while one was open for 9% of the time, Pallas kernels for 11%

profile of v1, /device:TPU:0, one launch (start us, length us, event | category | flops | bytes accessed | tf_op | source)
XLA Modules:
  0.0 141.3 jit_solution(371134817700999782)
XLA Ops:
  0.0 1.3 dynamic-slice_bitcast_fusion.8
  1.3 0.0 copy-start.5
  1.3 5.1 %collective-permute-start.2 = (bf16[8,2,32,128]{3,2,1,0:T(8,128)(2,1)S(1)}, bf16[8,2,32,128]{3,2,1,0:T(8,128)(2,1)S(1)}, u32[]{:S(2)}, u32[]{:S(2)}) collective-permute-start(bf16[8,2,32,128]{3,2,1,0:T(8,128)(2,1)S(1)} %get-tuple-element.39), channel_id=1, source_target_pairs={{0,3},{1,2},{2,1},{3,0},{4,7},{5,6},{6,5},{7,4},{8,11},{9,10},{10,... | collective-permute-start | bytes 393224 | tf_op jit(solution)/shard_map/ppermute | solution.py:217
  6.4 0.0 collective-permute-start.1
  6.4 0.6 collective-permute-start
  7.0 0.1 iota_compare_fusion
  7.1 1.4 fusion.51
  8.5 0.1 bitcast_select_fusion.own_ref
  8.6 0.0 copy-done.5
  8.6 0.1 fusion.52
  8.7 2.1 %collective-permute-done.2.three_ref = bf16[8,2,32,128]{3,2,1,0:T(8,128)(2,1)S(1)} collective-permute-done((bf16[8,2,32,128]{3,2,1,0:T(8,128)(2,1)S(1)}, bf16[8,2,32,128]{3,2,1,0:T(8,128)(2,1)S(1)}, u32[]{:S(2)}, u32[]{:S(2)}) %collective-permute-start.2) | collective-permute-done | bytes 131104 | tf_op jit(solution)/shard_map/ppermute | solution.py:217
  10.8 6.6 %collective-permute-done.1.two_ref = bf16[8,2,32,128]{3,2,1,0:T(8,128)(2,1)S(1)} collective-permute-done((bf16[8,2,32,128]{3,2,1,0:T(8,128)(2,1)S(1)}, bf16[8,2,32,128]{3,2,1,0:T(8,128)(2,1)S(1)}, u32[]{:S(2)}, u32[]{:S(2)}) %collective-permute-start.1) | collective-permute-done | bytes 131104 | tf_op jit(solution)/shard_map/ppermute | solution.py:216
  17.5 0.0 collective-permute-done.one_ref
  17.5 0.0 collective-permute-start.3
  17.5 3.0 %collective-permute-start.4 = (bf16[8,2,32,128]{3,2,1,0:T(8,128)(2,1)S(1)}, bf16[8,2,32,128]{3,2,1,0:T(8,128)(2,1)S(1)}, u32[]{:S(2)}, u32[]{:S(2)}) collective-permute-start(bf16[8,2,32,128]{3,2,1,0:T(8,128)(2,1)S(1)} %get-tuple-element.20), channel_id=1, source_target_pairs={{0,2},{2,0},{1,3},{3,1},{4,6},{6,4},{5,7},{7,5},{8,10},{10,8},{9,1... | collective-permute-start | bytes 393224 | tf_op jit(solution)/shard_map/ppermute | solution.py:216
  20.5 1.3 collective-permute-start.5
  21.9 0.0 copy-done
  21.9 6.8 %shard_map.46 = (bf16[8,2,128,256]{3,2,1,0:T(8,128)(2,1)S(1)}, bf16[8,2,128,128]{3,2,1,0:T(8,128)(2,1)S(1)}) custom-call(s32[1]{0:T(128)} %bitcast.2.member_ref, f32[8]{0:T(128)S(1)} %get-tuple-element.50.scale_ref, bf16[4,16,2,32,128]{4,3,2,1,0:T(8,128)(2,1)S(1)} %bitcast.54, bf16[8,2,32,128]{3,2,1,0:T(8,128)(2,1)S(1)} %collective-permute-done.one_ref, ...), custom_call_target="tpu_custom_call" | custom-call | flops 8589934592 | bytes 3145728 | tf_op jit(solution)/shard_map/pallas_call | solution.py:286
  28.7 0.0 copy-start.1
  28.7 0.8 copy-done.1
  29.5 0.0 collective-permute-done.3.one_ref
  29.5 0.5 collective-permute-done.4.two_ref
  30.0 0.0 collective-permute-done.5.three_ref
  30.0 2.0 %collective-permute-start.6 = (bf16[16,32,128]{2,1,0:T(8,128)(2,1)S(1)}, bf16[16,32,128]{2,1,0:T(8,128)(2,1)S(1)}, u32[]{:S(2)}, u32[]{:S(2)}) collective-permute-start(bf16[16,32,128]{2,1,0:T(8,128)(2,1)S(1)} %get-tuple-element.22), channel_id=1, source_target_pairs={{0,1},{1,0},{2,3},{3,2},{4,5},{5,4},{6,7},{7,6},{8,9},{9,8},{10,11... | collective-permute-start | bytes 393224 | tf_op jit(solution)/shard_map/ppermute | solution.py:214
  32.0 0.9 collective-permute-start.7
  32.8 1.5 %collective-permute-start.8 = (bf16[16,32,128]{2,1,0:T(8,128)(2,1)S(1)}, bf16[16,32,128]{2,1,0:T(8,128)(2,1)S(1)}, u32[]{:S(2)}, u32[]{:S(2)}) collective-permute-start(bf16[16,32,128]{2,1,0:T(8,128)(2,1)S(1)} %get-tuple-element.24), channel_id=1, source_target_pairs={{0,3},{1,2},{2,1},{3,0},{4,7},{5,6},{6,5},{7,4},{8,11},{9,10},{10,... | collective-permute-start | bytes 393224 | tf_op jit(solution)/shard_map/ppermute | solution.py:217
  34.4 6.8 %shard_map.48 = (bf16[8,2,128,256]{3,2,1,0:T(8,128)(2,1)S(1)}, bf16[8,2,128,128]{3,2,1,0:T(8,128)(2,1)S(1)}) custom-call(s32[1]{0:T(128)} %bitcast.2.member_ref, f32[8]{0:T(128)S(1)} %get-tuple-element.51.scale_ref, bf16[4,16,2,32,128]{4,3,2,1,0:T(8,128)(2,1)S(1)} %bitcast.55, bf16[8,2,32,128]{3,2,1,0:T(8,128)(2,1)S(1)} %collective-permute-done.3.one_ref, ...), custom_call_target="tpu_custom_call" | custom-call | flops 8589934592 | bytes 3145728 | tf_op jit(solution)/shard_map/pallas_call | solution.py:286
  41.2 0.8 copy-done.3
  42.0 0.0 collective-permute-done.6.one_ref
  42.0 1.3 collective-permute-done.7.two_ref
  43.3 0.0 collective-permute-done.8.three_ref
  43.3 1.8 %shard_map.47 = f32[2048,128]{1,0:T(8,128)S(1)} custom-call(s32[1]{0:T(128)} %bitcast.2.member_ref, bf16[8,2,128,256]{3,2,1,0:T(8,128)(2,1)S(1)} %get-tuple-element.18.inverse_ref, bf16[4,16,32,128]{3,2,1,0:T(8,128)(2,1)S(1)} %bitcast_select_fusion.own_ref, bf16[16,32,128]{2,1,0:T(8,128)(2,1)S(1)} %collective-permute-done.6.one_ref, ...), custom_call_target="tpu_custom_call" | custom-call | flops 1342177280 | bytes 3145728 | tf_op jit(solution)/shard_map/pallas_call | solution.py:305
  45.1 0.1 convert_element_type.44
  45.2 1.9 %shard_map.49 = f32[2048,128]{1,0:T(8,128)S(1)} custom-call(s32[1]{0:T(128)} %bitcast.2.member_ref, bf16[8,2,128,256]{3,2,1,0:T(8,128)(2,1)S(1)} %get-tuple-element.25.inverse_ref, bf16[4,16,32,128]{3,2,1,0:T(8,128)(2,1)S(1)} %bitcast_select_fusion.own_ref, bf16[16,32,128]{2,1,0:T(8,128)(2,1)S(1)} %collective-permute-done.6.one_ref, ...), custom_call_target="tpu_custom_call" | custom-call | flops 1342177280 | bytes 3145728 | tf_op jit(solution)/shard_map/pallas_call | solution.py:305
  47.0 0.1 convert_element_type.45
  47.1 1.4 pad_maximum_fusion
  48.5 5.3 %all-to-all-start = ((f16[32,4,2,16,128]{4,3,2,1,0:T(8,128)(2,1)}), f16[32,4,2,16,128]{4,3,2,1,0:T(8,128)(2,1)}, u32[]{:S(2)}, u32[]{:S(2)}) async-start(f16[32,4,2,16,128]{4,3,2,1,0:T(8,128)(2,1)} %pad_maximum_fusion), calls=%async_computation | async-start | bytes 2097152 | tf_op jit(solution)/shard_map/all_to_all | solution.py:327
  54.5 8.2 %fusion.4 = (f32[512,512]{1,0:T(8,128)S(1)}, f32[512,512]{1,0:T(8,128)S(1)}) fusion(s32[512]{0:T(512)S(1)} %get-tuple-element.53, s32[512]{0:T(512)S(1)} %get-tuple-element.52, s32[]{:T(128)} %bitcast.1, f32[]{:T(128)} %bitcast), kind=kLoop, calls=%fused_computation.11 | loop fusion | flops 7340032 | bytes 2101256 | tf_op jit(solution)/shard_map/jit(_where)/select_n | solution.py:192
  62.7 17.1 %all-to-all-done = f16[32,4,2,16,128]{4,3,2,1,0:T(8,128)(2,1)} async-done(((f16[32,4,2,16,128]{4,3,2,1,0:T(8,128)(2,1)}), f16[32,4,2,16,128]{4,3,2,1,0:T(8,128)(2,1)}, u32[]{:S(2)}, u32[]{:S(2)}) %all-to-all-start) | async-done | bytes 1048608 | tf_op jit(solution)/shard_map/all_to_all | solution.py:327
  79.9 1.5 %convert_element_type.46.values_ref = f32[32,4,2,16,128]{4,3,2,1,0:T(8,128)S(1)} convert(f16[32,4,2,16,128]{4,3,2,1,0:T(8,128)(2,1)} %all-to-all-done) | non-fusion elementwise | flops 524288 | bytes 3145728 | tf_op jit(solution)/shard_map/convert_element_type | solution.py:334
  81.3 4.6 %shard_map.50 = f32[16,4,2,32,128]{4,3,2,1,0:T(8,128)S(1)} custom-call(f32[512,512]{1,0:T(8,128)S(1)} %get-tuple-element.49.real_ref, f32[512,512]{1,0:T(8,128)S(1)} %get-tuple-element.48.imag_ref, f32[32,4,2,16,128]{4,3,2,1,0:T(8,128)S(1)} %convert_element_type.46.values_ref), custom_call_target="tpu_custom_call" | custom-call | flops 3221225472 | bytes 4194304 | tf_op jit(solution)/shard_map/pallas_call | solution.py:343
  85.9 1.3 convert_element_type.47
  87.2 4.5 %all-to-all-start.1 = ((f16[16,4,2,32,128]{4,3,2,1,0:T(8,128)(2,1)}), f16[16,4,2,32,128]{4,3,2,1,0:T(8,128)(2,1)}, u32[]{:S(2)}, u32[]{:S(2)}) async-start(f16[16,4,2,32,128]{4,3,2,1,0:T(8,128)(2,1)} %convert_element_type.47), calls=%async_computation.1 | async-start | bytes 2097152 | tf_op jit(solution)/shard_map/all_to_all | solution.py:361
  91.7 0.8 dynamic-slice_bitcast_fusion
  92.5 0.7 pad_maximum_fusion.2
  93.2 0.1 pad_maximum_fusion.1.psi_ref
  93.3 1.8 %collective-permute-start.10 = (bf16[16,2,32,128]{3,2,1,0:T(8,128)(2,1)}, bf16[16,2,32,128]{3,2,1,0:T(8,128)(2,1)S(1)}, u32[]{:S(2)}, u32[]{:S(2)}) collective-permute-start(bf16[16,2,32,128]{3,2,1,0:T(8,128)(2,1)} %get-tuple-element.28), channel_id=1, source_target_pairs={{0,1},{1,0},{2,3},{3,2},{4,5},{5,4},{6,7},{7,6},{8,9},{9,8},{10,11... | collective-permute-start | bytes 786440 | tf_op jit(solution)/shard_map/ppermute | solution.py:214
  95.2 1.0 collective-permute-start.11
  96.2 1.9 %collective-permute-start.12 = (bf16[16,2,32,128]{3,2,1,0:T(8,128)(2,1)}, bf16[16,2,32,128]{3,2,1,0:T(8,128)(2,1)}, u32[]{:S(2)}, u32[]{:S(2)}) collective-permute-start(bf16[16,2,32,128]{3,2,1,0:T(8,128)(2,1)} %pad_maximum_fusion.2), channel_id=1, source_target_pairs={{0,2},{2,0},{1,3},{3,1},{4,6},{6,4},{5,7},{7,5},{8,10},{10,8},{9,1... | collective-permute-start | bytes 786440 | tf_op jit(solution)/shard_map/ppermute | solution.py:216
  98.1 21.4 %all-to-all-done.1 = f16[16,4,2,32,128]{4,3,2,1,0:T(8,128)(2,1)} async-done(((f16[16,4,2,32,128]{4,3,2,1,0:T(8,128)(2,1)}), f16[16,4,2,32,128]{4,3,2,1,0:T(8,128)(2,1)}, u32[]{:S(2)}, u32[]{:S(2)}) %all-to-all-start.1) | async-done | bytes 1048608 | tf_op jit(solution)/shard_map/all_to_all | solution.py:361
  119.5 1.4 bitcast_convert_fusion.causal_ref
  120.9 1.6 %shard_map.51 = f32[2,16,2,32,128]{4,3,2,1,0:T(8,128)S(1)} custom-call(f32[4096,128]{1,0:T(8,128)S(1)} %bitcast_convert_fusion.causal_ref, bf16[16,2,128,128]{3,2,1,0:T(8,128)(2,1)S(1)} %pad_maximum_fusion.1.psi_ref), custom_call_target="tpu_custom_call" | custom-call | flops 268435456 | bytes 4194304 | tf_op jit(solution)/shard_map/pallas_call | solution.py:372
  122.5 0.3 collective-permute-done.10.one_ref
  122.7 0.0 collective-permute-done.11.two_ref
  122.7 0.0 collective-permute-done.12.three_ref
  122.7 3.0 %shard_map.52 = f32[2,16,2,32,128]{4,3,2,1,0:T(8,128)S(1)} custom-call(s32[1]{0:T(128)} %bitcast.2.member_ref, f32[4096,128]{1,0:T(8,128)S(1)} %bitcast_convert_fusion.causal_ref, bf16[4,16,2,32,128]{4,3,2,1,0:T(8,128)(2,1)S(1)} %bitcast.57, bf16[16,2,32,128]{3,2,1,0:T(8,128)(2,1)S(1)} %collective-permute-done.10.one_ref, ...), custom_call_target="tpu_custom_call" | custom-call | flops 268435456 | bytes 4194304 | tf_op jit(solution)/shard_map/pallas_call | solution.py:384
  125.8 0.1 fusion.22
  125.8 0.1 fusion.21
  125.9 1.2 collective-permute-start.9
  127.0 0.9 collective-permute-start.13
  128.0 7.2 %collective-permute-done.9 = f16[16,2,32,128]{3,2,1,0:T(8,128)(2,1)S(1)} collective-permute-done((f16[16,2,32,128]{3,2,1,0:T(8,128)(2,1)S(1)}, f16[16,2,32,128]{3,2,1,0:T(8,128)(2,1)S(1)}, u32[]{:S(2)}, u32[]{:S(2)}) %collective-permute-start.9) | collective-permute-done | bytes 262176 | tf_op jit(solution)/shard_map/ppermute | solution.py:214
  135.2 4.2 %collective-permute-done.13 = f16[16,2,32,128]{3,2,1,0:T(8,128)(2,1)S(1)} collective-permute-done((f16[16,2,32,128]{3,2,1,0:T(8,128)(2,1)S(1)}, f16[16,2,32,128]{3,2,1,0:T(8,128)(2,1)S(1)}, u32[]{:S(2)}, u32[]{:S(2)}) %collective-permute-start.13) | collective-permute-done | bytes 262176 | tf_op jit(solution)/shard_map/ppermute | solution.py:214
  139.4 0.3 fusion.17
  139.8 1.6 %fusion = f32[64,2,128,32]{2,3,1,0:T(8,128)} fusion(f32[16,2,32,128]{3,2,1,0:T(8,128)S(1)} %get-tuple-element.34, f32[16,2,32,128]{3,2,1,0:T(8,128)S(1)} %get-tuple-element.33, f32[16,2,32,128]{3,2,1,0:T(8,128)S(1)} %get-tuple-element.32, f32[16,2,32,128]{3,2,1,0:T(8,128)S(1)} %get-tuple-element.31), kind=kLoop, calls=%fused_computation.2 | loop fusion | flops 2097152 | bytes 4194304 | tf_op jit(solution)/shard_map/transpose | solution.py:411
  (9 shorter events, 0.1 us)
Async XLA Ops:
  1.3 7.3 %copy-start.5 = (f32[64]{0:T(128)S(1)}, f32[64]{0:T(128)}, u32[]{:S(2)}) copy-start(f32[64]{0:T(128)} %param.6) | copy-start | bytes 772
  1.3 9.5 %collective-permute-start.2 = (bf16[8,2,32,128]{3,2,1,0:T(8,128)(2,1)S(1)}, bf16[8,2,32,128]{3,2,1,0:T(8,128)(2,1)S(1)}, u32[]{:S(2)}, u32[]{:S(2)}) collective-permute-start(bf16[8,2,32,128]{3,2,1,0:T(8,128)(2,1)S(1)} %get-tuple-element.39), channel_id=1, source_target_pairs={{0,3},{1,2},{2,1},{3,0},{4,7},{5,6},{6,5},{7,4},{8,11},{9,10},{10,... | collective-permute-start | bytes 393224 | tf_op jit(solution)/shard_map/ppermute | solution.py:217
  6.4 11.1 %collective-permute-start.1 = (bf16[8,2,32,128]{3,2,1,0:T(8,128)(2,1)S(1)}, bf16[8,2,32,128]{3,2,1,0:T(8,128)(2,1)S(1)}, u32[]{:S(2)}, u32[]{:S(2)}) collective-permute-start(bf16[8,2,32,128]{3,2,1,0:T(8,128)(2,1)S(1)} %get-tuple-element.43), channel_id=1, source_target_pairs={{0,2},{2,0},{1,3},{3,1},{4,6},{6,4},{5,7},{7,5},{8,10},{10,8},{9,1... | collective-permute-start | bytes 393224 | tf_op jit(solution)/shard_map/ppermute | solution.py:216
  6.4 11.1 %collective-permute-start = (bf16[8,2,32,128]{3,2,1,0:T(8,128)(2,1)S(1)}, bf16[8,2,32,128]{3,2,1,0:T(8,128)(2,1)S(1)}, u32[]{:S(2)}, u32[]{:S(2)}) collective-permute-start(bf16[8,2,32,128]{3,2,1,0:T(8,128)(2,1)S(1)} %get-tuple-element.44), channel_id=1, source_target_pairs={{0,1},{1,0},{2,3},{3,2},{4,5},{5,4},{6,7},{7,6},{8,9},{9,8},{10,11... | collective-permute-start | bytes 393224 | tf_op jit(solution)/shard_map/ppermute | solution.py:214
  7.1 14.7 %copy-start = (bf16[64,2,32,128]{3,2,1,0:T(8,128)(2,1)S(1)}, bf16[64,2,32,128]{3,2,1,0:T(8,128)(2,1)}, u32[]{:S(2)}) copy-start(bf16[64,2,32,128]{3,2,1,0:T(8,128)(2,1)} %param.4) | copy-start | bytes 3145732
  17.5 12.0 %collective-permute-start.3 = (bf16[8,2,32,128]{3,2,1,0:T(8,128)(2,1)S(1)}, bf16[8,2,32,128]{3,2,1,0:T(8,128)(2,1)S(1)}, u32[]{:S(2)}, u32[]{:S(2)}) collective-permute-start(bf16[8,2,32,128]{3,2,1,0:T(8,128)(2,1)S(1)} %get-tuple-element.19), channel_id=1, source_target_pairs={{0,1},{1,0},{2,3},{3,2},{4,5},{5,4},{6,7},{7,6},{8,9},{9,8},{10,11... | collective-permute-start | bytes 393224 | tf_op jit(solution)/shard_map/ppermute | solution.py:214
  17.5 12.5 %collective-permute-start.4 = (bf16[8,2,32,128]{3,2,1,0:T(8,128)(2,1)S(1)}, bf16[8,2,32,128]{3,2,1,0:T(8,128)(2,1)S(1)}, u32[]{:S(2)}, u32[]{:S(2)}) collective-permute-start(bf16[8,2,32,128]{3,2,1,0:T(8,128)(2,1)S(1)} %get-tuple-element.20), channel_id=1, source_target_pairs={{0,2},{2,0},{1,3},{3,1},{4,6},{6,4},{5,7},{7,5},{8,10},{10,8},{9,1... | collective-permute-start | bytes 393224 | tf_op jit(solution)/shard_map/ppermute | solution.py:216
  20.5 9.5 %collective-permute-start.5 = (bf16[8,2,32,128]{3,2,1,0:T(8,128)(2,1)S(1)}, bf16[8,2,32,128]{3,2,1,0:T(8,128)(2,1)S(1)}, u32[]{:S(2)}, u32[]{:S(2)}) collective-permute-start(bf16[8,2,32,128]{3,2,1,0:T(8,128)(2,1)S(1)} %get-tuple-element.21), channel_id=1, source_target_pairs={{0,3},{1,2},{2,1},{3,0},{4,7},{5,6},{6,5},{7,4},{8,11},{9,10},{10,... | collective-permute-start | bytes 393224 | tf_op jit(solution)/shard_map/ppermute | solution.py:217
  28.7 0.8 copy-start.1
  30.0 12.0 %collective-permute-start.6 = (bf16[16,32,128]{2,1,0:T(8,128)(2,1)S(1)}, bf16[16,32,128]{2,1,0:T(8,128)(2,1)S(1)}, u32[]{:S(2)}, u32[]{:S(2)}) collective-permute-start(bf16[16,32,128]{2,1,0:T(8,128)(2,1)S(1)} %get-tuple-element.22), channel_id=1, source_target_pairs={{0,1},{1,0},{2,3},{3,2},{4,5},{5,4},{6,7},{7,6},{8,9},{9,8},{10,11... | collective-permute-start | bytes 393224 | tf_op jit(solution)/shard_map/ppermute | solution.py:214
  32.0 11.3 %collective-permute-start.7 = (bf16[16,32,128]{2,1,0:T(8,128)(2,1)S(1)}, bf16[16,32,128]{2,1,0:T(8,128)(2,1)S(1)}, u32[]{:S(2)}, u32[]{:S(2)}) collective-permute-start(bf16[16,32,128]{2,1,0:T(8,128)(2,1)S(1)} %get-tuple-element.23), channel_id=1, source_target_pairs={{0,2},{2,0},{1,3},{3,1},{4,6},{6,4},{5,7},{7,5},{8,10},{10,8},{9,1... | collective-permute-start | bytes 393224 | tf_op jit(solution)/shard_map/ppermute | solution.py:216
  32.8 10.4 %collective-permute-start.8 = (bf16[16,32,128]{2,1,0:T(8,128)(2,1)S(1)}, bf16[16,32,128]{2,1,0:T(8,128)(2,1)S(1)}, u32[]{:S(2)}, u32[]{:S(2)}) collective-permute-start(bf16[16,32,128]{2,1,0:T(8,128)(2,1)S(1)} %get-tuple-element.24), channel_id=1, source_target_pairs={{0,3},{1,2},{2,1},{3,0},{4,7},{5,6},{6,5},{7,4},{8,11},{9,10},{10,... | collective-permute-start | bytes 393224 | tf_op jit(solution)/shard_map/ppermute | solution.py:217
  41.2 0.8 copy-start.3
  48.5 31.4 %all-to-all-start = ((f16[32,4,2,16,128]{4,3,2,1,0:T(8,128)(2,1)}), f16[32,4,2,16,128]{4,3,2,1,0:T(8,128)(2,1)}, u32[]{:S(2)}, u32[]{:S(2)}) async-start(f16[32,4,2,16,128]{4,3,2,1,0:T(8,128)(2,1)} %pad_maximum_fusion), calls=%async_computation | async-start | bytes 2097152 | tf_op jit(solution)/shard_map/all_to_all | solution.py:327
  87.2 6.1 %copy-start.2 = (bf16[8,2,128,128]{3,2,1,0:T(8,128)(2,1)S(1)}, bf16[8,2,128,128]{3,2,1,0:T(8,128)(2,1)}, u32[]{:S(2)}) copy-start(bf16[8,2,128,128]{3,2,1,0:T(8,128)(2,1)} %copy-done.1) | copy-start | bytes 1572868
  87.2 6.1 %copy-start.4 = (bf16[8,2,128,128]{3,2,1,0:T(8,128)(2,1)S(1)}, bf16[8,2,128,128]{3,2,1,0:T(8,128)(2,1)}, u32[]{:S(2)}) copy-start(bf16[8,2,128,128]{3,2,1,0:T(8,128)(2,1)} %copy-done.3) | copy-start | bytes 1572868
  87.2 32.4 %all-to-all-start.1 = ((f16[16,4,2,32,128]{4,3,2,1,0:T(8,128)(2,1)}), f16[16,4,2,32,128]{4,3,2,1,0:T(8,128)(2,1)}, u32[]{:S(2)}, u32[]{:S(2)}) async-start(f16[16,4,2,32,128]{4,3,2,1,0:T(8,128)(2,1)} %convert_element_type.47), calls=%async_computation.1 | async-start | bytes 2097152 | tf_op jit(solution)/shard_map/all_to_all | solution.py:361
  93.3 29.4 %collective-permute-start.10 = (bf16[16,2,32,128]{3,2,1,0:T(8,128)(2,1)}, bf16[16,2,32,128]{3,2,1,0:T(8,128)(2,1)S(1)}, u32[]{:S(2)}, u32[]{:S(2)}) collective-permute-start(bf16[16,2,32,128]{3,2,1,0:T(8,128)(2,1)} %get-tuple-element.28), channel_id=1, source_target_pairs={{0,1},{1,0},{2,3},{3,2},{4,5},{5,4},{6,7},{7,6},{8,9},{9,8},{10,11... | collective-permute-start | bytes 786440 | tf_op jit(solution)/shard_map/ppermute | solution.py:214
  95.2 27.6 %collective-permute-start.11 = (bf16[16,2,32,128]{3,2,1,0:T(8,128)(2,1)}, bf16[16,2,32,128]{3,2,1,0:T(8,128)(2,1)}, u32[]{:S(2)}, u32[]{:S(2)}) collective-permute-start(bf16[16,2,32,128]{3,2,1,0:T(8,128)(2,1)} %get-tuple-element.29), channel_id=1, source_target_pairs={{0,2},{2,0},{1,3},{3,1},{4,6},{6,4},{5,7},{7,5},{8,10},{10,8},{9,1... | collective-permute-start | bytes 786440 | tf_op jit(solution)/shard_map/ppermute | solution.py:216
  96.2 26.6 %collective-permute-start.12 = (bf16[16,2,32,128]{3,2,1,0:T(8,128)(2,1)}, bf16[16,2,32,128]{3,2,1,0:T(8,128)(2,1)}, u32[]{:S(2)}, u32[]{:S(2)}) collective-permute-start(bf16[16,2,32,128]{3,2,1,0:T(8,128)(2,1)} %pad_maximum_fusion.2), channel_id=1, source_target_pairs={{0,2},{2,0},{1,3},{3,1},{4,6},{6,4},{5,7},{7,5},{8,10},{10,8},{9,1... | collective-permute-start | bytes 786440 | tf_op jit(solution)/shard_map/ppermute | solution.py:216
  125.9 9.3 %collective-permute-start.9 = (f16[16,2,32,128]{3,2,1,0:T(8,128)(2,1)S(1)}, f16[16,2,32,128]{3,2,1,0:T(8,128)(2,1)S(1)}, u32[]{:S(2)}, u32[]{:S(2)}) collective-permute-start(f16[16,2,32,128]{3,2,1,0:T(8,128)(2,1)S(1)} %fusion.21), channel_id=1, source_target_pairs={{0,1},{1,0},{2,3},{3,2},{4,5},{5,4},{6,7},{7,6},{8,9},{9,8},{10,11... | collective-permute-start | bytes 786440 | tf_op jit(solution)/shard_map/ppermute | solution.py:214
  127.0 12.4 %collective-permute-start.13 = (f16[16,2,32,128]{3,2,1,0:T(8,128)(2,1)S(1)}, f16[16,2,32,128]{3,2,1,0:T(8,128)(2,1)S(1)}, u32[]{:S(2)}, u32[]{:S(2)}) collective-permute-start(f16[16,2,32,128]{3,2,1,0:T(8,128)(2,1)S(1)} %fusion.22), channel_id=1, source_target_pairs={{0,1},{1,0},{2,3},{3,2},{4,5},{5,4},{6,7},{7,6},{8,9},{9,8},{10,11... | collective-permute-start | bytes 786440 | tf_op jit(solution)/shard_map/ppermute | solution.py:214

commit v2 on v1

--- a/solution.py
+++ b/solution.py
@@ -142,46 +142,40 @@
     out_ref[:, 0, 1] = (real[:, lanes:] + imag[:, :lanes]).reshape(shape)
 
 
-def product(causal_ref, psi_ref, out_ref, first):
+def product(member_ref, causal_ref, psi_ref, out_ref, distance):
     bins, _, size, _ = psi_ref.shape
-    panels, _, _, rows, _ = out_ref.shape
-    columns = panels * rows
-    total_bins = causal_ref.shape[0] // (2 * columns)
+    rows = out_ref.shape[2]
+    total_bins = causal_ref.shape[0] // (2 * rows)
+    first = (member_ref[0] ^ distance) * (pl.num_programs(0) * bins) + pl.program_id(0) * bins
     for item in range(bins):
         re, im = psi_ref[item, 0], psi_ref[item, 1]
-        place = first + pl.program_id(0) * bins + item
-        part_re = causal_ref[pl.ds(place, columns, stride=2 * total_bins), :]
-        part_im = causal_ref[pl.ds(total_bins + place, columns, stride=2 * total_bins), :]
+        place = first + item
+        part_re = causal_ref[pl.ds(place, rows, stride=2 * total_bins), :]
+        part_im = causal_ref[pl.ds(total_bins + place, rows, stride=2 * total_bins), :]
         high, low = split(cat([part_re, part_im], 1))
         both = dot(cat([high, low], 0), cat([cat([re, -im], 1), cat([im, re], 1)], 0), NT)
-        result = both[:columns] + both[columns:]
-        out_ref[:, item, 0] = result[:, :size].reshape(panels, rows, size)
-        out_ref[:, item, 1] = result[:, size:].reshape(panels, rows, size)
-
-
-def near_kernel(causal_ref, psi_ref, out_ref):
-    product(causal_ref, psi_ref, out_ref, 0)
-
-
-def far_kernel(member_ref, causal_ref, own_ref, one_ref, two_ref, three_ref, out_ref, psi_ref):
+        result = (both[:rows] + both[rows:]) * SCALE
+        out_ref[item, 0] = result[:, :size]
+        out_ref[item, 1] = result[:, size:]
+
+
+def near_kernel(member_ref, causal_ref, psi_ref, out_ref):
+    product(member_ref, causal_ref, psi_ref, out_ref, 0)
+
+
+def far_kernel(distance, member_ref, causal_ref, own_ref, one_ref, two_ref, three_ref, done_ref, out_ref, psi_ref):
     place_rows(member_ref[0], [own_ref.at[0], one_ref, two_ref, three_ref], psi_ref)
-    product(causal_ref, psi_ref, out_ref, pl.num_programs(0) * psi_ref.shape[0])
-
-
-def projection_table(lag_limit, count, freq_size, pairs, side):
+    product(member_ref, causal_ref, psi_ref, out_ref, distance)
+
+
+def projection_table(lag_limit, count, freq_size, pairs):
     own = count // (freq_size * 2 * pairs)
     row = lax.broadcasted_iota(jnp.int32, (count, 1), 0)
     column = lax.broadcasted_iota(jnp.int32, (1, count), 1)
     column_bins = (
         (column // own) % freq_size * (own * 2 * pairs) + column // (own * freq_size) * own + column % own
     )
-    holder = row // (2 * own)
-    row_bins = (
-        holder % freq_size * (own * 2 * pairs)
-        + ((row // own % 2 ^ side) * pairs + holder // freq_size) * own
-        + row % own
-    )
-    shift = column_bins - row_bins
+    shift = column_bins - row
     unit = math.pi / count
     half_angle = shift.astype(F32) * unit
     turned = ((2 * lag_limit + 1) * shift) % (2 * count)
@@ -217,7 +211,7 @@
     return lax.ppermute(value, ("side", "pair"), FLIP)
 
 
-def call(kernel, steps, in_specs, out_specs, out_shape, scratch, flops, moved):
+def call(kernel, steps, in_specs, out_specs, out_shape, scratch, flops, moved, aliases={}):
     return pl.pallas_call(
         kernel,
         grid_spec=pltpu.PrefetchScalarGridSpec(
@@ -228,6 +222,7 @@
             scratch_shapes=scratch,
         ),
         out_shape=out_shape,
+        input_output_aliases=aliases,
         compiler_params=params(16),
         cost_estimate=cost(flops, moved),
     )
@@ -259,7 +254,7 @@
             factors, (owner, first, 0, 0, 0), (1, length, 2, rows, size)
         ).reshape(length, 2, rows, size)
 
-    arrived = []
+    arrived, beside = [], []
     for chunk in range(chunks):
         pieces = [rows_for(member ^ d, chunk * part, part) for d in distances]
         if arrived:
@@ -271,8 +266,10 @@
     packed = packed.reshape(chan_size, own, rows, size)
     pieces = [lax.dynamic_index_in_dim(packed, member ^ d, 0, keepdims=False) for d in distances]
     pieces = lax.optimization_barrier(tuple(pieces) + tuple(arrived[-1]))[: len(pieces)]
+    beside.append(swap(after(rows_for(member, 0, own), arrived[0][2]), 1))
+    beside.append(swap(after(rows_for(member ^ 2, 0, own), arrived[-1][2]), 1))
     packed_arrived = [swap(piece, d) for piece, d in zip(pieces, distances)]
-    table_re, table_im = projection_table(lag_cutoff[0], count, freq_size, pairs, side)
+    table_re, table_im = projection_table(lag_cutoff[0], count, freq_size, pairs)
 
     local_block = lambda first: pl.BlockSpec(
         (1, step, 2, rows, size), lambda i, m: (m[0], i + first, 0, 0, 0)
@@ -326,17 +323,22 @@
     sent = sent.reshape(devices, kept, 2, own, lanes)
     gathered = lax.all_to_all(sent, chan + ("freq",), 0, 0, tiled=True)
 
-    across = swap(after(rows_for(member, 0, own), packed_arrived[0]), 2)
-    across_pair = cat([piece[0] for piece in arrived], 0) if chunks > 1 else arrived[0][0]
-    across_pair = swap(after(across_pair, gathered), 2)
-    beside = swap(after(rows_for(member ^ 3, 0, own), packed_arrived[0]), 1)
+    def both_chunks(distance):
+        pieces = [piece[distance - 1] for piece in arrived]
+        return cat(pieces, 0) if chunks > 1 else pieces[0]
+
+    across = [swap(after(rows_for(member, 0, own), packed_arrived[2]), 2)]
+    across += [swap(after(rows_for(member ^ 1, 0, own), packed_arrived[2]), 2)]
+    beside += [swap(after(rows_for(member ^ 3, 0, own), packed_arrived[2]), 1)]
+    rest = [swap(after(both_chunks(d), packed_arrived[2]), 1) for d in (2, 3)]
+    passed = [swap(value, 1) for value in across]
 
     values = gathered.astype(F32)
     sources, own_rows = devices, own
     if own % 8:
         values = values.transpose(1, 2, 0, 3, 4).reshape(1, kept, 2, count, lanes)
         sources, own_rows = 1, count
-    holders, held = pairs * freq_size, 2 * own
+    holders, held = freq_size, group_bins
     if held % 8:
         holders, held = 1, count
     table_block = pl.BlockSpec((count, count), lambda i: (0, 0))
@@ -356,58 +358,52 @@
     )(table_re, table_im, values)
     causal = causal.astype(jnp.float16)
     if holders == 1:
-        causal = causal.reshape(kept, 2, pairs * freq_size, 2 * own, lanes)
+        causal = causal.reshape(kept, 2, freq_size, group_bins, lanes)
         causal = causal.transpose(2, 0, 1, 3, 4)
-    back = lax.all_to_all(causal, ("pair", "freq"), 0, 0, tiled=True).astype(F32)
+    back = lax.all_to_all(causal, "freq", 0, 0, tiled=True).astype(F32)
     if lane_parts > 1:
-        back = back.reshape(pairs * column_parts, lane_parts, kept, 2, 2 * own, lanes)
+        back = back.reshape(column_parts, lane_parts, kept, 2, group_bins, lanes)
         back = back.transpose(0, 2, 3, 4, 1, 5)
-    back = back.reshape(pairs * rows * 2 * 2 * own, size)
-
+    back = back.reshape(rows * 2 * group_bins, size)
+
+    steps = own // step
     back_block = pl.BlockSpec(back.shape, lambda i, m: (0, 0))
-    result_block = pl.BlockSpec((pairs, step, 2, rows, size), lambda i, m: (0, i, 0, 0, 0))
-    result_shape = jax.ShapeDtypeStruct((pairs, own, 2, rows, size), F32)
-    flops, moved = own * 2 * 4 * size**3, own * 4 * 4 * size * size
+    result_shape = jax.ShapeDtypeStruct((group_bins, 2, rows, size), F32)
+    flops, moved = own * 4 * size**3, own * 4 * 4 * size * size
     psi = cat(psis, 0) if chunks > 1 else psis[0]
-    near = pl.pallas_call(
-        near_kernel,
-        grid=(own // step,),
-        in_specs=[
-            pl.BlockSpec(back.shape, lambda i: (0, 0)),
-            pl.BlockSpec((step, 2, size, size), lambda i: (i, 0, 0, 0)),
-        ],
-        out_specs=pl.BlockSpec((pairs, step, 2, rows, size), lambda i: (0, i, 0, 0, 0)),
-        out_shape=result_shape,
-        compiler_params=params(16),
-        cost_estimate=cost(flops, moved),
-    )(back, psi)
-    far = call(
-        far_kernel,
-        own // step,
-        [
-            back_block,
-            pl.BlockSpec((1, step, 2, rows, size), lambda i, m: (m[0] ^ 2, i, 0, 0, 0)),
-        ]
-        + [other_block] * 3,
-        result_block,
-        result_shape,
-        [pltpu.VMEM((step, 2, size, size), BF16)],
-        flops,
-        moved,
-    )(members, back, factors, beside, across, across_pair)
-
-    blocks = [None] * chan_size
-    for distance, result in ((0, near), (2, far)):
-        given = lax.dynamic_index_in_dim(result, 1 - pair, 0, keepdims=False)
-        blocks[distance] = lax.dynamic_index_in_dim(result, pair, 0, keepdims=False)
-        blocks[distance + 1] = swap(given.astype(jnp.float16), 1).astype(F32)
-    ordered = []
-    for owner in range(chan_size):
-        distance = member ^ owner
-        low = jnp.where(distance % 2 == 0, blocks[0], blocks[1])
-        high = jnp.where(distance % 2 == 0, blocks[2], blocks[3])
-        ordered.append(jnp.where(distance < 2, low, high))
-    whole = cat(ordered, 0) * SCALE
+
+    def result_block(distance):
+        return pl.BlockSpec(
+            (step, 2, rows, size), lambda i, m: ((m[0] ^ distance) * steps + i, 0, 0, 0)
+        )
+
+    whole = call(
+        near_kernel, steps, [back_block, whole_block], result_block(0), result_shape, [], flops, moved
+    )(members, back, psi)
+    for distance, one, two, three in (
+        (1, beside[0], rest[1], rest[0]),
+        (2, beside[2], across[0], passed[1]),
+        (3, beside[1], across[1], passed[0]),
+    ):
+        whole = call(
+            functools.partial(far_kernel, distance),
+            steps,
+            [
+                back_block,
+                pl.BlockSpec(
+                    (1, step, 2, rows, size),
+                    lambda i, m, distance=distance: (m[0] ^ distance, i, 0, 0, 0),
+                ),
+            ]
+            + [other_block] * 3
+            + [pl.BlockSpec(memory_space=pl.ANY)],
+            result_block(distance),
+            result_shape,
+            [pltpu.VMEM((step, 2, size, size), BF16)],
+            flops,
+            moved,
+            {6: 0},
+        )(members, back, factors, one, two, three, whole)
     return jnp.swapaxes(whole, 2, 3)
 
 

time: 142 us -> 150 us (1.056)
  Pallas kernels: 26.4 us -> 35.1 us
  other arithmetic: 16.8 us -> 14.8 us
    all_to_all x1, waiting for transfers between devices: 21.4 us -> 0.01 us  [shards(): back = lax.all_to_all(causal, 'freq', 0, 0, tiled=True).astype(F32)]
    ppermute x6 -> x10, waiting for transfers between devices: 11.7 us -> 31.1 us  [swap(): return lax.ppermute(value, 'pair', SWAP)]
    pallas_call x2 -> x4, Pallas kernels: 4.57 us -> 13.3 us  [the longest x3 11 us: shards(): call(functools.partial(far_kernel, distance), steps, [back_block, pl.Bloc...]
    transpose x1 -> x0, other arithmetic: 1.55 us -> none  [shards(): return jnp.swapaxes(whole, 2, 3)]
    unnamed x12 -> x28, local copies, waits for them, and re-layouts: 1.59 us -> 3 us
    ppermute x6 -> x10, starting transfers between devices: 6.55 us -> 7.49 us  [swap(): return lax.ppermute(value, 'pair', SWAP)]
  transfers between devices with their start and end apart: 16 -> 20, of which waited for: 9 -> 12; matrix products, arithmetic and copies ran while one was open for 9% -> 9% of each run, Pallas kernels for 11% -> 16%
where the time goes in v2:
time: 150 us
  waiting for transfers between devices  60.1 us (40%)
  Pallas kernels  35.1 us (23%)
  starting transfers between devices  32.1 us (21%)
  other arithmetic  14.8 us (10%)
  local copies, waits for them, and re-layouts  6.66 us (4%)
    ppermute x10, waiting for transfers between devices, swap(): return lax.ppermute(value, 'pair', SWAP)  31.1 us
    all_to_all x1, waiting for transfers between devices, shards(): gathered = lax.all_to_all(sent, chan + ('freq',), 0, 0, tiled=True)  17.2 us
    pallas_call x2, Pallas kernels, shards(): call(newton_kernel, part // step, [pl.BlockSpec(memory_space=pltpu.SMEM),...  13.6 us
    pallas_call x3, Pallas kernels, shards(): call(functools.partial(far_kernel, distance), steps, [back_block, pl.Bloc...  11 us
    ppermute x5, waiting for transfers between devices, swap(): return lax.ppermute(value, 'side', SWAP)  9.59 us
    select_n x1, other arithmetic, projection_table(): jnp.where(shift == 0, 0.0, (jnp.cos(half_angle) - jnp.cos(last_angle)) /...  8.18 us
    ppermute x3, starting transfers between devices, swap(): return lax.ppermute(value, ('side', 'pair'), FLIP)  7.99 us
    ppermute x10, starting transfers between devices, swap(): return lax.ppermute(value, 'pair', SWAP)  7.49 us
  transfers between devices with their start and end apart: 20, of which 12 were waited for; matrix products, arithmetic and copies ran while one was open for 9% of the time, Pallas kernels for 16%

profile of v2, /device:TPU:0, one launch (start us, length us, event | category | flops | bytes accessed | tf_op | source)
XLA Modules:
  0.0 149.6 jit_solution(6910514962315512408)
XLA Ops:
  0.0 1.3 dynamic-slice_bitcast_fusion.10
  1.3 0.0 copy-start.13
  1.3 5.1 %collective-permute-start.2 = (bf16[8,2,32,128]{3,2,1,0:T(8,128)(2,1)S(1)}, bf16[8,2,32,128]{3,2,1,0:T(8,128)(2,1)S(1)}, u32[]{:S(2)}, u32[]{:S(2)}) collective-permute-start(bf16[8,2,32,128]{3,2,1,0:T(8,128)(2,1)S(1)} %get-tuple-element.45), channel_id=1, source_target_pairs={{0,3},{1,2},{2,1},{3,0},{4,7},{5,6},{6,5},{7,4},{8,11},{9,10},{10,... | collective-permute-start | bytes 393224 | tf_op jit(solution)/shard_map/ppermute | solution.py:211
  6.4 0.6 collective-permute-start
  7.0 0.1 iota_compare_fusion
  7.1 1.4 fusion.18
  8.5 0.1 bitcast_select_fusion.own_ref
  8.6 0.1 fusion.19
  8.7 2.1 %collective-permute-done.2.three_ref = bf16[8,2,32,128]{3,2,1,0:T(8,128)(2,1)S(1)} collective-permute-done((bf16[8,2,32,128]{3,2,1,0:T(8,128)(2,1)S(1)}, bf16[8,2,32,128]{3,2,1,0:T(8,128)(2,1)S(1)}, u32[]{:S(2)}, u32[]{:S(2)}) %collective-permute-start.2) | collective-permute-done | bytes 131104 | tf_op jit(solution)/shard_map/ppermute | solution.py:211
  10.8 6.6 %collective-permute-done.1.two_ref = bf16[8,2,32,128]{3,2,1,0:T(8,128)(2,1)S(1)} collective-permute-done((bf16[8,2,32,128]{3,2,1,0:T(8,128)(2,1)S(1)}, bf16[8,2,32,128]{3,2,1,0:T(8,128)(2,1)S(1)}, u32[]{:S(2)}, u32[]{:S(2)}) %collective-permute-start.1) | collective-permute-done | bytes 131104 | tf_op jit(solution)/shard_map/ppermute | solution.py:210
  17.5 3.0 %collective-permute-start.4 = (bf16[8,2,32,128]{3,2,1,0:T(8,128)(2,1)S(1)}, bf16[8,2,32,128]{3,2,1,0:T(8,128)(2,1)S(1)}, u32[]{:S(2)}, u32[]{:S(2)}) collective-permute-start(bf16[8,2,32,128]{3,2,1,0:T(8,128)(2,1)S(1)} %get-tuple-element.24), channel_id=1, source_target_pairs={{0,2},{2,0},{1,3},{3,1},{4,6},{6,4},{5,7},{7,5},{8,10},{10,8},{9,1... | collective-permute-start | bytes 393224 | tf_op jit(solution)/shard_map/ppermute | solution.py:210
  20.5 1.3 collective-permute-start.5
  21.9 6.8 %shard_map.46 = (bf16[8,2,128,256]{3,2,1,0:T(8,128)(2,1)S(1)}, bf16[8,2,128,128]{3,2,1,0:T(8,128)(2,1)S(1)}) custom-call(s32[1]{0:T(128)} %bitcast.member_ref, f32[8]{0:T(128)S(1)} %get-tuple-element.56.scale_ref, bf16[4,16,2,32,128]{4,3,2,1,0:T(8,128)(2,1)S(1)} %bitcast.43, bf16[8,2,32,128]{3,2,1,0:T(8,128)(2,1)S(1)} %collective-permute-done.one_ref, ...), custom_call_target="tpu_custom_call" | custom-call | flops 8589934592 | bytes 3145728 | tf_op jit(solution)/shard_map/pallas_call | solution.py:283
  28.7 0.8 copy-done.1
  29.5 0.0 collective-permute-done.3.one_ref
  29.5 0.5 collective-permute-done.4.two_ref
  30.0 0.0 collective-permute-done.5.three_ref
  30.0 2.0 %collective-permute-start.6 = (bf16[16,32,128]{2,1,0:T(8,128)(2,1)S(1)}, bf16[16,32,128]{2,1,0:T(8,128)(2,1)S(1)}, u32[]{:S(2)}, u32[]{:S(2)}) collective-permute-start(bf16[16,32,128]{2,1,0:T(8,128)(2,1)S(1)} %get-tuple-element.26), channel_id=1, source_target_pairs={{0,1},{1,0},{2,3},{3,2},{4,5},{5,4},{6,7},{7,6},{8,9},{9,8},{10,11... | collective-permute-start | bytes 393224 | tf_op jit(solution)/shard_map/ppermute | solution.py:208
  32.0 1.0 collective-permute-start.7
  32.9 1.5 %collective-permute-start.8 = (bf16[16,32,128]{2,1,0:T(8,128)(2,1)S(1)}, bf16[16,32,128]{2,1,0:T(8,128)(2,1)S(1)}, u32[]{:S(2)}, u32[]{:S(2)}) collective-permute-start(bf16[16,32,128]{2,1,0:T(8,128)(2,1)S(1)} %get-tuple-element.28), channel_id=1, source_target_pairs={{0,3},{1,2},{2,1},{3,0},{4,7},{5,6},{6,5},{7,4},{8,11},{9,10},{10,... | collective-permute-start | bytes 393224 | tf_op jit(solution)/shard_map/ppermute | solution.py:211
  34.4 6.8 %shard_map.48 = (bf16[8,2,128,256]{3,2,1,0:T(8,128)(2,1)S(1)}, bf16[8,2,128,128]{3,2,1,0:T(8,128)(2,1)S(1)}) custom-call(s32[1]{0:T(128)} %bitcast.member_ref, f32[8]{0:T(128)S(1)} %get-tuple-element.57.scale_ref, bf16[4,16,2,32,128]{4,3,2,1,0:T(8,128)(2,1)S(1)} %bitcast.44, bf16[8,2,32,128]{3,2,1,0:T(8,128)(2,1)S(1)} %collective-permute-done.3.one_ref, ...), custom_call_target="tpu_custom_call" | custom-call | flops 8589934592 | bytes 3145728 | tf_op jit(solution)/shard_map/pallas_call | solution.py:283
  41.3 0.8 copy-done.3
  42.1 1.2 collective-permute-done.7.two_ref
  43.3 0.0 collective-permute-done.8.three_ref
  43.3 1.8 %shard_map.47 = f32[2048,128]{1,0:T(8,128)S(1)} custom-call(s32[1]{0:T(128)} %bitcast.member_ref, bf16[8,2,128,256]{3,2,1,0:T(8,128)(2,1)S(1)} %get-tuple-element.22.inverse_ref, bf16[4,16,32,128]{3,2,1,0:T(8,128)(2,1)S(1)} %bitcast_select_fusion.own_ref, bf16[16,32,128]{2,1,0:T(8,128)(2,1)S(1)} %collective-permute-done.6.one_ref, ...), custom_call_target="tpu_custom_call" | custom-call | flops 1342177280 | bytes 3145728 | tf_op jit(solution)/shard_map/pallas_call | solution.py:302
  45.1 0.1 convert_element_type.30
  45.2 1.8 %shard_map.49 = f32[2048,128]{1,0:T(8,128)S(1)} custom-call(s32[1]{0:T(128)} %bitcast.member_ref, bf16[8,2,128,256]{3,2,1,0:T(8,128)(2,1)S(1)} %get-tuple-element.29.inverse_ref, bf16[4,16,32,128]{3,2,1,0:T(8,128)(2,1)S(1)} %bitcast_select_fusion.own_ref, bf16[16,32,128]{2,1,0:T(8,128)(2,1)S(1)} %collective-permute-done.6.one_ref, ...), custom_call_target="tpu_custom_call" | custom-call | flops 1342177280 | bytes 3145728 | tf_op jit(solution)/shard_map/pallas_call | solution.py:302
  47.0 0.1 convert_element_type.31
  47.1 1.4 pad_maximum_fusion
  48.5 5.3 %all-to-all-start = ((f16[32,4,2,16,128]{4,3,2,1,0:T(8,128)(2,1)}), f16[32,4,2,16,128]{4,3,2,1,0:T(8,128)(2,1)}, u32[]{:S(2)}, u32[]{:S(2)}) async-start(f16[32,4,2,16,128]{4,3,2,1,0:T(8,128)(2,1)} %pad_maximum_fusion), calls=%async_computation | async-start | bytes 2097152 | tf_op jit(solution)/shard_map/all_to_all | solution.py:324
  54.5 8.2 %divide_select_fusion = (f32[512,512]{1,0:T(8,128)S(1)}, f32[512,512]{1,0:T(8,128)S(1)}) fusion(s32[512]{0:T(512)S(1)} %fusion.12, s32[]{:T(128)} %bitcast.2, f32[]{:T(128)} %bitcast.1), kind=kLoop, calls=%fused_computation.10 | loop fusion | flops 7340032 | bytes 2099208 | tf_op jit(solution)/shard_map/jit(_where)/select_n | solution.py:186
  62.7 17.2 %all-to-all-done = f16[32,4,2,16,128]{4,3,2,1,0:T(8,128)(2,1)} async-done(((f16[32,4,2,16,128]{4,3,2,1,0:T(8,128)(2,1)}), f16[32,4,2,16,128]{4,3,2,1,0:T(8,128)(2,1)}, u32[]{:S(2)}, u32[]{:S(2)}) %all-to-all-start) | async-done | bytes 1048608 | tf_op jit(solution)/shard_map/all_to_all | solution.py:324
  79.9 1.5 convert_element_type.32.values_ref
  81.4 4.6 %shard_map.50 = f32[8,4,2,64,128]{4,3,2,1,0:T(8,128)S(1)} custom-call(f32[512,512]{1,0:T(8,128)S(1)} %get-tuple-element.55.real_ref, f32[512,512]{1,0:T(8,128)S(1)} %get-tuple-element.54.imag_ref, f32[32,4,2,16,128]{4,3,2,1,0:T(8,128)S(1)} %convert_element_type.32.values_ref), custom_call_target="tpu_custom_call" | custom-call | flops 3221225472 | bytes 4194304 | tf_op jit(solution)/shard_map/pallas_call | solution.py:345
  85.9 1.2 convert_element_type.33
  87.2 4.4 %all-to-all-start.1 = ((f16[8,4,2,64,128]{4,3,2,1,0:T(8,128)(2,1)}), f16[8,4,2,64,128]{4,3,2,1,0:T(8,128)(2,1)}, u32[]{:S(2)}, u32[]{:S(2)}) async-start(f16[8,4,2,64,128]{4,3,2,1,0:T(8,128)(2,1)} %convert_element_type.33), calls=%async_computation.1 | async-start | bytes 2097152 | tf_op jit(solution)/shard_map/all_to_all | solution.py:363
  91.6 0.9 dynamic-slice_bitcast_fusion
  92.5 0.8 collective-permute-start.15
  93.3 1.3 collective-permute-start.16
  94.6 0.8 collective-permute-start.10
  95.4 2.2 %collective-permute-start.11 = (bf16[16,2,32,128]{3,2,1,0:T(8,128)(2,1)S(1)}, bf16[16,2,32,128]{3,2,1,0:T(8,128)(2,1)}, u32[]{:S(2)}, u32[]{:S(2)}) collective-permute-start(bf16[16,2,32,128]{3,2,1,0:T(8,128)(2,1)S(1)} %get-tuple-element.34), channel_id=1, source_target_pairs={{0,2},{2,0},{1,3},{3,1},{4,6},{6,4},{5,7},{7,5},{8,10},{10,8},{9,1... | collective-permute-start | bytes 786440 | tf_op jit(solution)/shard_map/ppermute | solution.py:210
  97.5 0.8 collective-permute-start.9
  98.3 0.7 pad_maximum_fusion.3
  99.0 0.1 pad_maximum_fusion.1.psi_ref
  99.1 11.9 %collective-permute-done.15.one_ref = bf16[16,2,32,128]{3,2,1,0:T(8,128)(2,1)S(1)} collective-permute-done((bf16[16,2,32,128]{3,2,1,0:T(8,128)(2,1)S(1)}, bf16[16,2,32,128]{3,2,1,0:T(8,128)(2,1)S(1)}, u32[]{:S(2)}, u32[]{:S(2)}) %collective-permute-start.15) | collective-permute-done | bytes 262176 | tf_op jit(solution)/shard_map/ppermute | solution.py:208
  111.0 0.7 copy-done.5
  111.7 0.0 collective-permute-start.17
  111.7 4.9 %collective-permute-done.16.two_ref = bf16[16,2,32,128]{3,2,1,0:T(8,128)(2,1)S(1)} collective-permute-done((bf16[16,2,32,128]{3,2,1,0:T(8,128)(2,1)S(1)}, bf16[16,2,32,128]{3,2,1,0:T(8,128)(2,1)S(1)}, u32[]{:S(2)}, u32[]{:S(2)}) %collective-permute-start.16) | collective-permute-done | bytes 262176 | tf_op jit(solution)/shard_map/ppermute | solution.py:208
  116.6 0.7 copy-done.7
  117.3 0.0 collective-permute-start.13
  117.3 0.0 collective-permute-done.10.two_ref
  117.3 2.0 %collective-permute-start.14 = (bf16[16,2,32,128]{3,2,1,0:T(8,128)(2,1)S(1)}, bf16[16,2,32,128]{3,2,1,0:T(8,128)(2,1)}, u32[]{:S(2)}, u32[]{:S(2)}) collective-permute-start(bf16[16,2,32,128]{3,2,1,0:T(8,128)(2,1)S(1)} %collective-permute-done.10.two_ref), channel_id=1, source_target_pairs={{0,1},{1,0},{2,3},{3,2},{4,5},{5,4},{6,7},{7,6},{8,9},{9,8},{10,11... | collective-permute-start | bytes 786440 | tf_op jit(solution)/shard_map/ppermute | solution.py:208
  119.3 1.3 collective-permute-done.11.two_ref
  120.6 0.0 collective-permute-start.12
  120.6 0.0 all-to-all-done.1
  120.6 1.4 bitcast_convert_fusion.causal_ref
  122.0 2.2 %shard_map.51.done_ref = f32[64,2,32,128]{3,2,1,0:T(8,128)} custom-call(s32[1]{0:T(128)} %bitcast.member_ref, f32[4096,128]{1,0:T(8,128)S(1)} %bitcast_convert_fusion.causal_ref, bf16[16,2,128,128]{3,2,1,0:T(8,128)(2,1)S(1)} %pad_maximum_fusion.1.psi_ref), custom_call_target="tpu_custom_call" | custom-call | flops 134217728 | bytes 4194304 | tf_op jit(solution)/shard_map/pallas_call | solution.py:380
  124.2 5.6 %collective-permute-done.17.three_ref = bf16[16,2,32,128]{3,2,1,0:T(8,128)(2,1)} collective-permute-done((bf16[16,2,32,128]{3,2,1,0:T(8,128)(2,1)}, bf16[16,2,32,128]{3,2,1,0:T(8,128)(2,1)}, u32[]{:S(2)}, u32[]{:S(2)}) %collective-permute-start.17) | collective-permute-done | bytes 262176 | tf_op jit(solution)/shard_map/ppermute | solution.py:208
  129.8 3.7 %shard_map.52.done_ref = f32[64,2,32,128]{3,2,1,0:T(8,128)} custom-call(s32[1]{0:T(128)} %bitcast.member_ref, f32[4096,128]{1,0:T(8,128)S(1)} %bitcast_convert_fusion.causal_ref, bf16[4,16,2,32,128]{4,3,2,1,0:T(8,128)(2,1)S(1)} %bitcast.46, bf16[16,2,32,128]{3,2,1,0:T(8,128)(2,1)S(1)} %copy-done.6, ...), custom_call_target="tpu_custom_call", output_to_operand_aliasing={{}: (6, {})} | custom-call | flops 134217728 | bytes 4194304 | tf_op jit(solution)/shard_map/pallas_call | solution.py:388
  133.5 1.9 %collective-permute-done.13.one_ref = bf16[16,2,32,128]{3,2,1,0:T(8,128)(2,1)S(1)} collective-permute-done((bf16[16,2,32,128]{3,2,1,0:T(8,128)(2,1)}, bf16[16,2,32,128]{3,2,1,0:T(8,128)(2,1)S(1)}, u32[]{:S(2)}, u32[]{:S(2)}) %collective-permute-start.13) | collective-permute-done | bytes 262176 | tf_op jit(solution)/shard_map/ppermute | solution.py:208
  135.3 5.7 %collective-permute-done.14.three_ref = bf16[16,2,32,128]{3,2,1,0:T(8,128)(2,1)} collective-permute-done((bf16[16,2,32,128]{3,2,1,0:T(8,128)(2,1)S(1)}, bf16[16,2,32,128]{3,2,1,0:T(8,128)(2,1)}, u32[]{:S(2)}, u32[]{:S(2)}) %collective-permute-start.14) | collective-permute-done | bytes 262176 | tf_op jit(solution)/shard_map/ppermute | solution.py:208
  141.0 3.7 %shard_map.53.done_ref = f32[64,2,32,128]{3,2,1,0:T(8,128)} custom-call(s32[1]{0:T(128)} %bitcast.member_ref, f32[4096,128]{1,0:T(8,128)S(1)} %bitcast_convert_fusion.causal_ref, bf16[4,16,2,32,128]{4,3,2,1,0:T(8,128)(2,1)S(1)} %bitcast.47, bf16[16,2,32,128]{3,2,1,0:T(8,128)(2,1)S(1)} %collective-permute-done.13.one_ref, ...), custom_call_target="tpu_custom_call", output_to_operand_aliasing={{}: (6, {})} | custom-call | flops 134217728 | bytes 4194304 | tf_op jit(solution)/shard_map/pallas_call | solution.py:388
  144.8 1.2 collective-permute-done.12.three_ref
  146.0 3.6 %shard_map.54 = f32[64,2,32,128]{3,2,1,0:T(8,128)} custom-call(s32[1]{0:T(128)} %bitcast.member_ref, f32[4096,128]{1,0:T(8,128)S(1)} %bitcast_convert_fusion.causal_ref, bf16[4,16,2,32,128]{4,3,2,1,0:T(8,128)(2,1)S(1)} %bitcast.48, bf16[16,2,32,128]{3,2,1,0:T(8,128)(2,1)} %collective-permute-done.9.one_ref, ...), custom_call_target="tpu_custom_call", output_to_operand_aliasing={{}: (6, {})} | custom-call | flops 134217728 | bytes 4194304 | tf_op jit(solution)/shard_map/pallas_call | solution.py:388
  (32 shorter events, 0.1 us)
Async XLA Ops:
  1.3 7.3 %copy-start.13 = (f32[64]{0:T(128)S(1)}, f32[64]{0:T(128)}, u32[]{:S(2)}) copy-start(f32[64]{0:T(128)} %param.6) | copy-start | bytes 772
  1.3 9.5 %collective-permute-start.2 = (bf16[8,2,32,128]{3,2,1,0:T(8,128)(2,1)S(1)}, bf16[8,2,32,128]{3,2,1,0:T(8,128)(2,1)S(1)}, u32[]{:S(2)}, u32[]{:S(2)}) collective-permute-start(bf16[8,2,32,128]{3,2,1,0:T(8,128)(2,1)S(1)} %get-tuple-element.45), channel_id=1, source_target_pairs={{0,3},{1,2},{2,1},{3,0},{4,7},{5,6},{6,5},{7,4},{8,11},{9,10},{10,... | collective-permute-start | bytes 393224 | tf_op jit(solution)/shard_map/ppermute | solution.py:211
  6.4 11.1 %collective-permute-start.1 = (bf16[8,2,32,128]{3,2,1,0:T(8,128)(2,1)S(1)}, bf16[8,2,32,128]{3,2,1,0:T(8,128)(2,1)S(1)}, u32[]{:S(2)}, u32[]{:S(2)}) collective-permute-start(bf16[8,2,32,128]{3,2,1,0:T(8,128)(2,1)S(1)} %get-tuple-element.49), channel_id=1, source_target_pairs={{0,2},{2,0},{1,3},{3,1},{4,6},{6,4},{5,7},{7,5},{8,10},{10,8},{9,1... | collective-permute-start | bytes 393224 | tf_op jit(solution)/shard_map/ppermute | solution.py:210
  6.4 11.1 %collective-permute-start = (bf16[8,2,32,128]{3,2,1,0:T(8,128)(2,1)S(1)}, bf16[8,2,32,128]{3,2,1,0:T(8,128)(2,1)S(1)}, u32[]{:S(2)}, u32[]{:S(2)}) collective-permute-start(bf16[8,2,32,128]{3,2,1,0:T(8,128)(2,1)S(1)} %get-tuple-element.50), channel_id=1, source_target_pairs={{0,1},{1,0},{2,3},{3,2},{4,5},{5,4},{6,7},{7,6},{8,9},{9,8},{10,11... | collective-permute-start | bytes 393224 | tf_op jit(solution)/shard_map/ppermute | solution.py:208
  7.1 14.7 %copy-start = (bf16[64,2,32,128]{3,2,1,0:T(8,128)(2,1)S(1)}, bf16[64,2,32,128]{3,2,1,0:T(8,128)(2,1)}, u32[]{:S(2)}) copy-start(bf16[64,2,32,128]{3,2,1,0:T(8,128)(2,1)} %param.4) | copy-start | bytes 3145732
  17.5 12.0 %collective-permute-start.3 = (bf16[8,2,32,128]{3,2,1,0:T(8,128)(2,1)S(1)}, bf16[8,2,32,128]{3,2,1,0:T(8,128)(2,1)S(1)}, u32[]{:S(2)}, u32[]{:S(2)}) collective-permute-start(bf16[8,2,32,128]{3,2,1,0:T(8,128)(2,1)S(1)} %get-tuple-element.23), channel_id=1, source_target_pairs={{0,1},{1,0},{2,3},{3,2},{4,5},{5,4},{6,7},{7,6},{8,9},{9,8},{10,11... | collective-permute-start | bytes 393224 | tf_op jit(solution)/shard_map/ppermute | solution.py:208
  17.5 12.5 %collective-permute-start.4 = (bf16[8,2,32,128]{3,2,1,0:T(8,128)(2,1)S(1)}, bf16[8,2,32,128]{3,2,1,0:T(8,128)(2,1)S(1)}, u32[]{:S(2)}, u32[]{:S(2)}) collective-permute-start(bf16[8,2,32,128]{3,2,1,0:T(8,128)(2,1)S(1)} %get-tuple-element.24), channel_id=1, source_target_pairs={{0,2},{2,0},{1,3},{3,1},{4,6},{6,4},{5,7},{7,5},{8,10},{10,8},{9,1... | collective-permute-start | bytes 393224 | tf_op jit(solution)/shard_map/ppermute | solution.py:210
  20.5 9.5 %collective-permute-start.5 = (bf16[8,2,32,128]{3,2,1,0:T(8,128)(2,1)S(1)}, bf16[8,2,32,128]{3,2,1,0:T(8,128)(2,1)S(1)}, u32[]{:S(2)}, u32[]{:S(2)}) collective-permute-start(bf16[8,2,32,128]{3,2,1,0:T(8,128)(2,1)S(1)} %get-tuple-element.25), channel_id=1, source_target_pairs={{0,3},{1,2},{2,1},{3,0},{4,7},{5,6},{6,5},{7,4},{8,11},{9,10},{10,... | collective-permute-start | bytes 393224 | tf_op jit(solution)/shard_map/ppermute | solution.py:211
  28.7 0.8 copy-start.1
  30.0 11.3 %copy-start.9 = (bf16[8,2,32,128]{3,2,1,0:T(8,128)(2,1)}, bf16[8,2,32,128]{3,2,1,0:T(8,128)(2,1)S(1)}, u32[]{:S(2)}) copy-start(bf16[8,2,32,128]{3,2,1,0:T(8,128)(2,1)S(1)} %collective-permute-done.4.two_ref) | copy-start | bytes 393220
  30.0 11.3 %copy-start.11 = (bf16[8,2,32,128]{3,2,1,0:T(8,128)(2,1)}, bf16[8,2,32,128]{3,2,1,0:T(8,128)(2,1)S(1)}, u32[]{:S(2)}) copy-start(bf16[8,2,32,128]{3,2,1,0:T(8,128)(2,1)S(1)} %collective-permute-done.5.three_ref) | copy-start | bytes 393220
  30.0 12.1 %collective-permute-start.6 = (bf16[16,32,128]{2,1,0:T(8,128)(2,1)S(1)}, bf16[16,32,128]{2,1,0:T(8,128)(2,1)S(1)}, u32[]{:S(2)}, u32[]{:S(2)}) collective-permute-start(bf16[16,32,128]{2,1,0:T(8,128)(2,1)S(1)} %get-tuple-element.26), channel_id=1, source_target_pairs={{0,1},{1,0},{2,3},{3,2},{4,5},{5,4},{6,7},{7,6},{8,9},{9,8},{10,11... | collective-permute-start | bytes 393224 | tf_op jit(solution)/shard_map/ppermute | solution.py:208
  32.0 11.3 %collective-permute-start.7 = (bf16[16,32,128]{2,1,0:T(8,128)(2,1)S(1)}, bf16[16,32,128]{2,1,0:T(8,128)(2,1)S(1)}, u32[]{:S(2)}, u32[]{:S(2)}) collective-permute-start(bf16[16,32,128]{2,1,0:T(8,128)(2,1)S(1)} %get-tuple-element.27), channel_id=1, source_target_pairs={{0,2},{2,0},{1,3},{3,1},{4,6},{6,4},{5,7},{7,5},{8,10},{10,8},{9,1... | collective-permute-start | bytes 393224 | tf_op jit(solution)/shard_map/ppermute | solution.py:210
  32.9 10.4 %collective-permute-start.8 = (bf16[16,32,128]{2,1,0:T(8,128)(2,1)S(1)}, bf16[16,32,128]{2,1,0:T(8,128)(2,1)S(1)}, u32[]{:S(2)}, u32[]{:S(2)}) collective-permute-start(bf16[16,32,128]{2,1,0:T(8,128)(2,1)S(1)} %get-tuple-element.28), channel_id=1, source_target_pairs={{0,3},{1,2},{2,1},{3,0},{4,7},{5,6},{6,5},{7,4},{8,11},{9,10},{10,... | collective-permute-start | bytes 393224 | tf_op jit(solution)/shard_map/ppermute | solution.py:211
  41.3 0.8 copy-start.3
  48.5 31.4 %all-to-all-start = ((f16[32,4,2,16,128]{4,3,2,1,0:T(8,128)(2,1)}), f16[32,4,2,16,128]{4,3,2,1,0:T(8,128)(2,1)}, u32[]{:S(2)}, u32[]{:S(2)}) async-start(f16[32,4,2,16,128]{4,3,2,1,0:T(8,128)(2,1)} %pad_maximum_fusion), calls=%async_computation | async-start | bytes 2097152 | tf_op jit(solution)/shard_map/all_to_all | solution.py:324
  87.2 6.1 %copy-start.12 = (bf16[8,2,32,128]{3,2,1,0:T(8,128)(2,1)S(1)}, bf16[8,2,32,128]{3,2,1,0:T(8,128)(2,1)}, u32[]{:S(2)}) copy-start(bf16[8,2,32,128]{3,2,1,0:T(8,128)(2,1)} %copy-done.11) | copy-start | bytes 393220
  87.2 11.1 %copy-start.10 = (bf16[8,2,32,128]{3,2,1,0:T(8,128)(2,1)S(1)}, bf16[8,2,32,128]{3,2,1,0:T(8,128)(2,1)}, u32[]{:S(2)}) copy-start(bf16[8,2,32,128]{3,2,1,0:T(8,128)(2,1)} %copy-done.9) | copy-start | bytes 393220
  87.2 33.5 %all-to-all-start.1 = ((f16[8,4,2,64,128]{4,3,2,1,0:T(8,128)(2,1)}), f16[8,4,2,64,128]{4,3,2,1,0:T(8,128)(2,1)}, u32[]{:S(2)}, u32[]{:S(2)}) async-start(f16[8,4,2,64,128]{4,3,2,1,0:T(8,128)(2,1)} %convert_element_type.33), calls=%async_computation.1 | async-start | bytes 2097152 | tf_op jit(solution)/shard_map/all_to_all | solution.py:363
  91.5 7.5 %copy-start.2 = (bf16[8,2,128,128]{3,2,1,0:T(8,128)(2,1)S(1)}, bf16[8,2,128,128]{3,2,1,0:T(8,128)(2,1)}, u32[]{:S(2)}) copy-start(bf16[8,2,128,128]{3,2,1,0:T(8,128)(2,1)} %copy-done.1) | copy-start | bytes 1572868
  91.5 7.5 %copy-start.4 = (bf16[8,2,128,128]{3,2,1,0:T(8,128)(2,1)S(1)}, bf16[8,2,128,128]{3,2,1,0:T(8,128)(2,1)}, u32[]{:S(2)}) copy-start(bf16[8,2,128,128]{3,2,1,0:T(8,128)(2,1)} %copy-done.3) | copy-start | bytes 1572868
  92.5 18.5 %collective-permute-start.15 = (bf16[16,2,32,128]{3,2,1,0:T(8,128)(2,1)S(1)}, bf16[16,2,32,128]{3,2,1,0:T(8,128)(2,1)S(1)}, u32[]{:S(2)}, u32[]{:S(2)}) collective-permute-start(bf16[16,2,32,128]{3,2,1,0:T(8,128)(2,1)S(1)} %get-tuple-element.34), channel_id=1, source_target_pairs={{0,1},{1,0},{2,3},{3,2},{4,5},{5,4},{6,7},{7,6},{8,9},{9,8},{10,11... | collective-permute-start | bytes 786440 | tf_op jit(solution)/shard_map/ppermute | solution.py:208
  93.3 23.3 %collective-permute-start.16 = (bf16[16,2,32,128]{3,2,1,0:T(8,128)(2,1)S(1)}, bf16[16,2,32,128]{3,2,1,0:T(8,128)(2,1)S(1)}, u32[]{:S(2)}, u32[]{:S(2)}) collective-permute-start(bf16[16,2,32,128]{3,2,1,0:T(8,128)(2,1)S(1)} %pad_maximum_fusion.2), channel_id=1, source_target_pairs={{0,1},{1,0},{2,3},{3,2},{4,5},{5,4},{6,7},{7,6},{8,9},{9,8},{10,11... | collective-permute-start | bytes 786440 | tf_op jit(solution)/shard_map/ppermute | solution.py:208
  94.6 22.7 %collective-permute-start.10 = (bf16[16,2,32,128]{3,2,1,0:T(8,128)(2,1)S(1)}, bf16[16,2,32,128]{3,2,1,0:T(8,128)(2,1)S(1)}, u32[]{:S(2)}, u32[]{:S(2)}) collective-permute-start(bf16[16,2,32,128]{3,2,1,0:T(8,128)(2,1)S(1)} %get-tuple-element.31), channel_id=1, source_target_pairs={{0,2},{2,0},{1,3},{3,1},{4,6},{6,4},{5,7},{7,5},{8,10},{10,8},{9,1... | collective-permute-start | bytes 786440 | tf_op jit(solution)/shard_map/ppermute | solution.py:210
  95.4 25.3 %collective-permute-start.11 = (bf16[16,2,32,128]{3,2,1,0:T(8,128)(2,1)S(1)}, bf16[16,2,32,128]{3,2,1,0:T(8,128)(2,1)}, u32[]{:S(2)}, u32[]{:S(2)}) collective-permute-start(bf16[16,2,32,128]{3,2,1,0:T(8,128)(2,1)S(1)} %get-tuple-element.34), channel_id=1, source_target_pairs={{0,2},{2,0},{1,3},{3,1},{4,6},{6,4},{5,7},{7,5},{8,10},{10,8},{9,1... | collective-permute-start | bytes 786440 | tf_op jit(solution)/shard_map/ppermute | solution.py:210
  97.5 47.2 %collective-permute-start.9 = (bf16[16,2,32,128]{3,2,1,0:T(8,128)(2,1)}, bf16[16,2,32,128]{3,2,1,0:T(8,128)(2,1)}, u32[]{:S(2)}, u32[]{:S(2)}) collective-permute-start(bf16[16,2,32,128]{3,2,1,0:T(8,128)(2,1)} %get-tuple-element.30), channel_id=1, source_target_pairs={{0,1},{1,0},{2,3},{3,2},{4,5},{5,4},{6,7},{7,6},{8,9},{9,8},{10,11... | collective-permute-start | bytes 786440 | tf_op jit(solution)/shard_map/ppermute | solution.py:208
  111.0 0.7 copy-start.5
  111.7 18.1 %collective-permute-start.17 = (bf16[16,2,32,128]{3,2,1,0:T(8,128)(2,1)}, bf16[16,2,32,128]{3,2,1,0:T(8,128)(2,1)}, u32[]{:S(2)}, u32[]{:S(2)}) collective-permute-start(bf16[16,2,32,128]{3,2,1,0:T(8,128)(2,1)} %pad_maximum_fusion.3), channel_id=1, source_target_pairs={{0,1},{1,0},{2,3},{3,2},{4,5},{5,4},{6,7},{7,6},{8,9},{9,8},{10,11... | collective-permute-start | bytes 786440 | tf_op jit(solution)/shard_map/ppermute | solution.py:208
  116.6 0.7 copy-start.7
  117.3 18.0 %collective-permute-start.13 = (bf16[16,2,32,128]{3,2,1,0:T(8,128)(2,1)}, bf16[16,2,32,128]{3,2,1,0:T(8,128)(2,1)S(1)}, u32[]{:S(2)}, u32[]{:S(2)}) collective-permute-start(bf16[16,2,32,128]{3,2,1,0:T(8,128)(2,1)} %get-tuple-element.33), channel_id=1, source_target_pairs={{0,1},{1,0},{2,3},{3,2},{4,5},{5,4},{6,7},{7,6},{8,9},{9,8},{10,11... | collective-permute-start | bytes 786440 | tf_op jit(solution)/shard_map/ppermute | solution.py:208
  117.3 23.7 %collective-permute-start.14 = (bf16[16,2,32,128]{3,2,1,0:T(8,128)(2,1)S(1)}, bf16[16,2,32,128]{3,2,1,0:T(8,128)(2,1)}, u32[]{:S(2)}, u32[]{:S(2)}) collective-permute-start(bf16[16,2,32,128]{3,2,1,0:T(8,128)(2,1)S(1)} %collective-permute-done.10.two_ref), channel_id=1, source_target_pairs={{0,1},{1,0},{2,3},{3,2},{4,5},{5,4},{6,7},{7,6},{8,9},{9,8},{10,11... | collective-permute-start | bytes 786440 | tf_op jit(solution)/shard_map/ppermute | solution.py:208
  120.6 25.4 %collective-permute-start.12 = (bf16[16,2,32,128]{3,2,1,0:T(8,128)(2,1)}, bf16[16,2,32,128]{3,2,1,0:T(8,128)(2,1)S(1)}, u32[]{:S(2)}, u32[]{:S(2)}) collective-permute-start(bf16[16,2,32,128]{3,2,1,0:T(8,128)(2,1)} %collective-permute-done.11.two_ref), channel_id=1, source_target_pairs={{0,1},{1,0},{2,3},{3,2},{4,5},{5,4},{6,7},{7,6},{8,9},{9,8},{10,11... | collective-permute-start | bytes 786440 | tf_op jit(solution)/shard_map/ppermute | solution.py:208
  122.0 7.8 %copy-start.6 = (bf16[16,2,32,128]{3,2,1,0:T(8,128)(2,1)S(1)}, bf16[16,2,32,128]{3,2,1,0:T(8,128)(2,1)}, u32[]{:S(2)}) copy-start(bf16[16,2,32,128]{3,2,1,0:T(8,128)(2,1)} %copy-done.5) | copy-start | bytes 786436
  122.0 7.8 %copy-start.8 = (bf16[16,2,32,128]{3,2,1,0:T(8,128)(2,1)S(1)}, bf16[16,2,32,128]{3,2,1,0:T(8,128)(2,1)}, u32[]{:S(2)}) copy-start(bf16[16,2,32,128]{3,2,1,0:T(8,128)(2,1)} %copy-done.7) | copy-start | bytes 786436

commit v3 on v1

v3 whole, which is shorter than its diff:
```python
import functools
import math

import jax
import jax.numpy as jnp
from jax import lax
from jax.experimental import pallas as pl
from jax.experimental.pallas import tpu as pltpu
from jax.sharding import PartitionSpec as P

ITERS = 8
SCALE = 16.0
CHUNKS = 2
F32 = jnp.float32
BF16 = jnp.bfloat16
MIB = 1024 * 1024
NN = (((1,), (0,)), ((), ()))
NT = (((1,), (1,)), ((), ()))
TN = (((0,), (0,)), ((), ()))


def dot(left, right, dims=NN):
    return lax.dot_general(left, right, dims, preferred_element_type=F32)


def split(value):
    high = value.astype(BF16)
    return high, (value - high.astype(F32)).astype(BF16)


def cat(parts, axis):
    return jnp.concatenate(parts, axis=axis)


def dot3(left_high, left_low, right_high, right_low, dims=NN):
    rows = left_high.shape[0]
    both = dot(cat([left_high, left_low], 0), right_high, dims)
    return both[:rows] + (both[rows:] + dot(left_high, right_low, dims))


def eye(size):
    rows = lax.broadcasted_iota(jnp.int32, (size, size), 0)
    columns = lax.broadcasted_iota(jnp.int32, (size, size), 1)
    return jnp.where(rows == columns, 1.0, 0.0).astype(F32)


def place_rows(member, panels, out_ref):
    rows = panels[0].shape[-2]
    for index, panel in enumerate(panels):
        start = pl.multiple_of((member ^ index) * rows, rows)
        out_ref[..., pl.ds(start, rows), :] = panel[...]


def newton_kernel(member_ref, scale_ref, own_ref, one_ref, two_ref, three_ref, out_ref, psi_ref):
    bins, _, size, _ = psi_ref.shape
    place_rows(member_ref[0], [own_ref.at[0], one_ref, two_ref, three_ref], psi_ref)
    identity = eye(size)
    state = []
    for item in range(bins):
        re, im = psi_ref[item, 0], psi_ref[item, 1]
        scale = scale_ref[pl.program_id(0) * bins + item]
        gram = dot(cat([re, im], 0), cat([cat([re, im], 1), cat([im, -re], 1)], 0), TN)
        sym = identity - scale * gram[:, :size]
        anti = -scale * gram[:, size:]
        state.append((sym, anti, None))
    for step in range(ITERS):
        after = []
        for sym, anti, total in state:
            left_high, left_low = split(cat([sym, anti], 1))
            if step == 0:
                total = identity + (sym + anti)
                right = cat([sym + anti, sym - anti], 0)
            elif step < ITERS - 1:
                right = cat([cat([sym + anti, total], 1), cat([sym - anti, total.T], 1)], 0)
            else:
                right = cat([total, total.T], 0)
            product = dot3(left_high, left_low, *split(right))
            if step > 0:
                total = total + product[:, -size:]
            if step < ITERS - 1:
                square = product[:, :size]
                square_t = square.T
                sym = 0.5 * (square + square_t)
                anti = 0.5 * (square - square_t)
            after.append((sym, anti, total))
        state = after
    for item in range(bins):
        total = state[item][2]
        total_t = total.T
        re, im = psi_ref[item, 0], psi_ref[item, 1]
        scale = scale_ref[pl.program_id(0) * bins + item]
        half = (0.5 * scale) * cat([total + total_t, total - total_t], 1)
        high, low = split(half)
        both = dot(cat([high, low], 0), cat([cat([re, im], 1), cat([-im, re], 1)], 0), NT)
        high, low = split(both[:size] + both[size:])
        out_ref[item, 0] = high
        out_ref[item, 1] = low


def middle_kernel(member_ref, inverse_ref, own_ref, one_ref, two_ref, three_ref, out_ref, packed_ref):
    bins, size = inverse_ref.shape[0], inverse_ref.shape[2]
    total_bins = pl.num_programs(0) * bins
    place_rows(member_ref[0], [own_ref.at[0], one_ref, two_ref, three_ref], packed_ref)
    identity = eye(size)
    rows = lax.broadcasted_iota(jnp.int32, (size, size), 0)
    columns = lax.broadcasted_iota(jnp.int32, (size, size), 1)
    for item in range(bins):
        packed = packed_ref[item].astype(F32)
        packed_t = packed.T
        re = jnp.where(columns >= rows, packed, packed_t).astype(BF16)
        im = jnp.where(columns == rows, 0.0, jnp.where(columns < rows, packed, -packed_t)).astype(BF16)
        high, low = inverse_ref[item, 0], inverse_ref[item, 1]
        both = dot(cat([high, low], 0), cat([cat([re, im], 1), cat([-im, re], 1)], 0))
        left = both[:size] + both[size:]
        left_re, left_im = left[:, :size], left[:, size:]
        left_high, left_low = split(cat([left_re + left_im, left_im - left_re], 1))
        middle = dot3(left_high, left_low, high, low, NT)
        place = pl.program_id(0) * bins + item
        out_ref[pl.ds(place, size, stride=total_bins), :] = (middle + identity) * (1.0 / SCALE)


def causal_kernel(real_ref, imag_ref, values_ref, *refs):
    *out_refs, table_high, table_low = refs
    count = real_ref.shape[1]
    sources, kept, own, lanes = values_ref.shape

    @pl.when(pl.program_id(0) == 0)
    def _():
        for part, table_ref in enumerate((real_ref, imag_ref)):
            high, low = split(table_ref[...])
            table_high[part * count : (part + 1) * count] = high
            table_low[part * count : (part + 1) * count] = low

    values = cat([values_ref[:, item].reshape(count, lanes) for item in range(kept)], 1)
    high, low = split(values)
    whole = dot(table_high[...], high) + (dot(table_high[...], low) + dot(table_low[...], high))
    for item in range(kept):
        for part in range(2):
            piece = whole[part * count : (part + 1) * count, item * lanes : (item + 1) * lanes]
            piece = piece.reshape(sources, own, lanes)
            step = own // len(out_refs)
            for chunk, out_ref in enumerate(out_refs):
                out_ref[:, item, part] = piece[:, chunk * step : (chunk + 1) * step]


def product_kernel(causal_ref, psi_ref, out_ref):
    bins, _, size, _ = psi_ref.shape
    total_bins = causal_ref.shape[0] // (2 * size)
    shape = (out_ref.shape[0], out_ref.shape[3], size)
    for item in range(bins):
        re, im = psi_ref[item, 0], psi_ref[item, 1]
        place = pl.program_id(0) * bins + item
        part_re = causal_ref[pl.ds(place, size, stride=2 * total_bins), :]
        part_im = causal_ref[pl.ds(total_bins + place, size, stride=2 * total_bins), :]
        added, taken = part_re + part_im, part_re - part_im
        high, low = split(0.5 * cat([taken.T + added, added.T - taken], 1))
        both = dot(cat([high, low], 0), cat([cat([re, -im], 1), cat([im, re], 1)], 0), NT)
        result = both[:size] + both[size:]
        out_ref[:, item, 0] = result[:, :size].reshape(shape)
        out_ref[:, item, 1] = result[:, size:].reshape(shape)


def projection_table(lag_limit, count, freq_size, pairs, chunks):
    own = count // (freq_size * 2 * pairs)

    def bins(index):
        part = own // chunks
        group, holder, inner = index // own % freq_size, index // (own * freq_size), index % own
        return (group * chunks + inner // part) * (part * 2 * pairs) + holder * part + inner % part

    row = lax.broadcasted_iota(jnp.int32, (count, 1), 0)
    column = lax.broadcasted_iota(jnp.int32, (1, count), 1)
    shift = bins(column) - bins(row)
    unit = math.pi / count
    half_angle = shift.astype(F32) * unit
    turned = ((2 * lag_limit + 1) * shift) % (2 * count)
    turned = jnp.where(turned >= count, turned - 2 * count, turned)
    last_angle = turned.astype(F32) * unit
    below = jnp.where(shift == 0, 1.0, 2.0 * count * jnp.sin(half_angle))
    real = jnp.where(shift == 0, (lag_limit.astype(F32) + 0.5) / count, jnp.sin(last_angle) / below)
    imag = jnp.where(shift == 0, 0.0, (jnp.cos(half_angle) - jnp.cos(last_angle)) / below)
    return real, imag


def params(limit):
    return pltpu.CompilerParams(vmem_limit_bytes=limit * MIB)


def cost(flops, moved):
    return pl.CostEstimate(flops=flops, bytes_accessed=moved, transcendentals=0)


def after(value, *earlier):
    return lax.optimization_barrier((value,) + earlier)[0]


SWAP = ((0, 1), (1, 0))
FLIP = ((0, 3), (1, 2), (2, 1), (3, 0))


def swap(value, distance):
    if distance == 1:
        return lax.ppermute(value, "pair", SWAP)
    if distance == 2:
        return lax.ppermute(value, "side", SWAP)
    return lax.ppermute(value, ("side", "pair"), FLIP)


def call(kernel, steps, in_specs, out_specs, out_shape, scratch, flops, moved):
    return pl.pallas_call(
        kernel,
        grid_spec=pltpu.PrefetchScalarGridSpec(
            num_scalar_prefetch=1,
            grid=(steps,),
            in_specs=in_specs,
            out_specs=out_specs,
            scratch_shapes=scratch,
        ),
        out_shape=out_shape,
        compiler_params=params(16),
        cost_estimate=cost(flops, moved),
    )


def shards(freq_size, pairs, factor, spectrum, guess_scale, lag_cutoff):
    chan = ("side", "pair")
    chan_size = 2 * pairs
    group_bins, _, rows, size = factor.shape
    own = group_bins // chan_size
    count = group_bins * freq_size
    chunks = CHUNKS if own % (4 * CHUNKS) == 0 else 1
    part = own // chunks
    step = math.gcd(part, 4)
    column_parts = min(freq_size, rows)
    lane_parts = freq_size // column_parts
    kept = rows // column_parts
    lanes = size // lane_parts
    side, pair = lax.axis_index("side"), lax.axis_index("pair")
    member = side * pairs + pair
    members = member.reshape(1)
    devices = chan_size * freq_size
    distances = range(1, chan_size)

    factors = factor.reshape(chunks, chan_size, part, 2, rows, size)

    arrived = []
    for chunk in range(chunks):
        pieces = [
            lax.dynamic_index_in_dim(factors[chunk], member ^ d, 0, keepdims=False)
            for d in distances
        ]
        if arrived:
            pieces = lax.optimization_barrier(tuple(pieces) + tuple(arrived[-1]))[: len(pieces)]
        arrived.append([swap(piece, d) for piece, d in zip(pieces, distances)])
    row_index = lax.broadcasted_iota(jnp.int32, (rows, size), 0) + member * rows
    column_index = lax.broadcasted_iota(jnp.int32, (rows, size), 1)
    packed = jnp.where(column_index >= row_index, spectrum[:, 0], spectrum[:, 1])
    packed = packed.reshape(chunks, chan_size, part, rows, size)
    pieces = [
        lax.dynamic_index_in_dim(packed, member ^ d, 1, keepdims=False).reshape(own, rows, size)
        for d in distances
    ]
    pieces = lax.optimization_barrier(tuple(pieces) + tuple(arrived[-1]))[: len(pieces)]
    packed_arrived = [swap(piece, d) for piece, d in zip(pieces, distances)]
    table_re, table_im = projection_table(lag_cutoff[0], count, freq_size, pairs, chunks)

    local_block = lambda chunk: pl.BlockSpec(
        (pl.squeezed, 1, step, 2, rows, size), lambda i, m: (chunk, m[0], i, 0, 0, 0)
    )
    other_block = pl.BlockSpec((step, 2, rows, size), lambda i, m: (i, 0, 0, 0))
    whole_block = pl.BlockSpec((step, 2, size, size), lambda i, m: (i, 0, 0, 0))
    inverse_block = pl.BlockSpec((step, 2, size, 2 * size), lambda i, m: (i, 0, 0, 0))
    inverses, psis, middles = [], [], []
    for chunk in range(chunks):
        scale = lax.dynamic_slice_in_dim(guess_scale, (chunk * chan_size + member) * part, part, 0)
        inverse, psi = call(
            newton_kernel,
            part // step,
            [pl.BlockSpec(memory_space=pltpu.SMEM), local_block(chunk)] + [other_block] * 3,
            [inverse_block, whole_block],
            [
                jax.ShapeDtypeStruct((part, 2, size, 2 * size), BF16),
                jax.ShapeDtypeStruct((part, 2, size, size), BF16),
            ],
            [],
            part * 64 * 2 * 4 * size**3,
            part * 6 * 4 * size * size,
        )(members, scale, factors, *arrived[chunk])
        inverses.append(inverse)
        psis.append(psi)
    for chunk in range(chunks):
        first = chunk * part // step
        other = pl.BlockSpec((step, rows, size), lambda i, m, first=first: (i + first, 0, 0))
        middles.append(
            call(
                middle_kernel,
                part // step,
                [
                    inverse_block,
                    pl.BlockSpec(
                        (pl.squeezed, 1, step, rows, size),
                        lambda i, m, chunk=chunk: (chunk, m[0], i, 0, 0),
                    ),
                ]
                + [other] * 3,
                pl.BlockSpec((size * part, size), lambda i, m: (0, 0)),
                jax.ShapeDtypeStruct((size * part, size), F32),
                [pltpu.VMEM((step, size, size), BF16)],
                part * 10 * 2 * 4 * size**3,
                part * 6 * 4 * size * size,
            )(members, inverses[chunk], packed, *packed_arrived)
        )
    middles = [value.astype(jnp.float16).reshape(size, part, size) for value in middles]
    sent = cat(middles, 1) if chunks > 1 else middles[0]
    if lane_parts > 1:
        sent = sent.reshape(size, own, lane_parts, lanes).transpose(0, 2, 1, 3)
    sent = sent.reshape(devices, kept, own, lanes)
    values = lax.all_to_all(sent, chan + ("freq",), 0, 0, tiled=True).astype(F32)
    sources, own_rows, parts = devices, own, chunks
    if own % 8:
        values = values.transpose(1, 0, 2, 3).reshape(1, kept, count, lanes)
        sources, own_rows = 1, count
    twice = math.gcd(kept, 2)
    table_block = pl.BlockSpec((count, count), lambda i: (0, 0))
    causal = pl.pallas_call(
        causal_kernel,
        grid=(kept // twice,),
        in_specs=[
            table_block,
            table_block,
            pl.BlockSpec((sources, twice, own_rows, lanes), lambda i: (0, i, 0, 0)),
        ],
        out_specs=[
            pl.BlockSpec((sources, twice, 2, own_rows // chunks, lanes), lambda i: (0, i, 0, 0, 0))
        ]
        * chunks,
        out_shape=[jax.ShapeDtypeStruct((sources, kept, 2, own_rows // chunks, lanes), F32)] * chunks,
        scratch_shapes=[pltpu.VMEM((2 * count, count), BF16), pltpu.VMEM((2 * count, count), BF16)],
        compiler_params=params(24),
        cost_estimate=cost(kept * 12 * count * count * lanes, 12 * kept * count * lanes),
    )(table_re, table_im, values)

    blocks = []
    for chunk in range(chunks):
        back = causal[chunk].astype(jnp.float16)
        if own % 8:
            back = back.reshape(kept, 2, devices, own, lanes).transpose(2, 0, 1, 3, 4)
        if blocks:
            back = after(back, backs)
        back = lax.all_to_all(back, chan + ("freq",), 0, 0, tiled=True)
        backs = back
        if blocks:
            back = after(back, *blocks[-1][1:])
        back = back.astype(F32)
        if lane_parts > 1:
            back = back.reshape(chan_size * column_parts, lane_parts, kept, 2, part, lanes)
            back = back.transpose(0, 2, 3, 4, 1, 5)
        back = back.reshape(size * 2 * part, size)
        result = pl.pallas_call(
            product_kernel,
            grid=(part // step,),
            in_specs=[
                pl.BlockSpec(back.shape, lambda i: (0, 0)),
                pl.BlockSpec((step, 2, size, size), lambda i: (i, 0, 0, 0)),
            ],
            out_specs=pl.BlockSpec((chan_size, step, 2, rows, size), lambda i: (0, i, 0, 0, 0)),
            out_shape=jax.ShapeDtypeStruct((chan_size, part, 2, rows, size), F32),
            compiler_params=params(16),
            cost_estimate=cost(part * 4 * 4 * size**3, part * 5 * 4 * size * size),
        )(back, psis[chunk])
        panels = [
            lax.dynamic_index_in_dim(result, member ^ d, 0, keepdims=False) for d in range(chan_size)
        ]
        blocks.append(panels[:1] + [swap(panels[d].astype(jnp.float16), d) for d in distances])
    ordered = []
    for chunk in range(chunks):
        pieces = [piece.astype(F32) for piece in blocks[chunk]]
        owners = []
        for owner in range(chan_size):
            distance = member ^ owner
            low = jnp.where(distance % 2 == 0, pieces[0], pieces[1])
            high = jnp.where(distance % 2 == 0, pieces[2], pieces[3])
            owners.append(jnp.where(distance < 2, low, high) * SCALE)
        if chunk < chunks - 1:
            owners = [lax.optimization_barrier(cat(owners, 0))]
        ordered += owners
    return jnp.swapaxes(cat(ordered, 0), 2, 3)


def solution(mesh):
    freq_size, pairs = mesh.shape["freq"], mesh.shape["chan"] // 2
    split_mesh = jax.sharding.Mesh(
        mesh.devices.reshape(freq_size, 2, pairs), ("freq", "side", "pair")
    )
    in_specs = (
        P("freq", None, ("side", "pair"), None),
        P("freq", None, ("side", "pair"), None),
        P("freq"),
        P(),
    )
    out_specs = P("freq", None, None, ("side", "pair"))
    body = functools.partial(shards, freq_size, pairs)
    return jax.shard_map(
        body, mesh=split_mesh, in_specs=in_specs, out_specs=out_specs, check_vma=False
    )
```

time: 142 us -> 142 us (level)
  other arithmetic: 16.8 us -> 12.3 us
  starting transfers between devices: 31.2 us -> 35.6 us
  Pallas kernels: 26.4 us -> 23.1 us
  waiting for transfers between devices: 60.8 us -> 63.2 us
    ppermute x5, waiting for transfers between devices: 8.41 us -> 38.8 us  [swap(): return lax.ppermute(value, 'side', SWAP)]
    all_to_all x2 -> x3, waiting for transfers between devices: 38.5 us -> 21.1 us  [the longest x2 14.6 us: shards(): back = lax.all_to_all(back, chan + ('freq',), 0, 0, tiled=True)]
    ppermute x6 -> x5, waiting for transfers between devices: 11.7 us -> 3.3 us  [swap(): return lax.ppermute(value, 'pair', SWAP)]
    ppermute x6 -> x5, starting transfers between devices: 6.55 us -> 9.97 us  [swap(): return lax.ppermute(value, 'pair', SWAP)]
    pallas_call x5, Pallas kernels: 12.8 us -> 9.43 us  [the longest x2 4.92 us: shards(): call(middle_kernel, part // step, [inverse_block, pl.BlockSpec((pl.squeez...]
    ppermute x3 -> x5, waiting for transfers between devices: 2.14 us -> 0.01 us  [swap(): return lax.ppermute(value, ('side', 'pair'), FLIP)]
    reshape x2 -> x0, local copies, waits for them, and re-layouts: 2.1 us -> none  [rows_for(): return lax.dynamic_slice(factors, (owner, first, 0, 0, 0), (1, length, 2,...]
    all_to_all x2 -> x3, starting transfers between devices: 9.79 us -> 11.7 us  [the longest x2 6.37 us: shards(): back = lax.all_to_all(back, chan + ('freq',), 0, 0, tiled=True)]
  transfers between devices with their start and end apart: 16 -> 18, of which waited for: 9 -> 9; matrix products, arithmetic and copies ran while one was open for 9% -> 8% of each run, Pallas kernels for 11% -> 10%
where the time goes in v3:
time: 142 us; the launch traced here: 141 us
  waiting for transfers between devices  63.2 us (45%)
  starting transfers between devices  35.6 us (25%)
  Pallas kernels  23.1 us (16%)
  other arithmetic  12.3 us (9%)
  local copies, waits for them, and re-layouts  6.11 us (4%)
    ppermute x5, waiting for transfers between devices, swap(): return lax.ppermute(value, 'side', SWAP)  38.8 us
    all_to_all x2, waiting for transfers between devices, shards(): back = lax.all_to_all(back, chan + ('freq',), 0, 0, tiled=True)  14.6 us
    pallas_call x2, Pallas kernels, shards(): call(newton_kernel, part // step, [pl.BlockSpec(memory_space=pltpu.SMEM),...  13.6 us
    ppermute x5, starting transfers between devices, swap(): return lax.ppermute(value, 'pair', SWAP)  9.97 us
    select_n x1, other arithmetic, projection_table(): jnp.where(shift == 0, 0.0, (jnp.cos(half_angle) - jnp.cos(last_angle)) /...  8.24 us
    ppermute x5, starting transfers between devices, swap(): return lax.ppermute(value, 'side', SWAP)  7.17 us
    ppermute x5, starting transfers between devices, swap(): return lax.ppermute(value, ('side', 'pair'), FLIP)  6.82 us
    all_to_all x1, waiting for transfers between devices, shards(): lax.all_to_all(sent, chan + ('freq',), 0, 0, tiled=True).astype(F32)  6.46 us
  transfers between devices with their start and end apart: 18, of which 9 were waited for; matrix products, arithmetic and copies ran while one was open for 8% of the time, Pallas kernels for 10%

profile of v3, /device:TPU:0, one launch (start us, length us, event | category | flops | bytes accessed | tf_op | source)
XLA Modules:
  0.0 141.3 jit_solution(1537301049099836939)
XLA Ops:
  0.0 1.4 fusion.60
  1.4 0.8 dynamic-slice_bitcast_fusion.3
  2.1 3.0 %collective-permute-start = (bf16[8,2,32,128]{3,2,1,0:T(8,128)(2,1)}, bf16[8,2,32,128]{3,2,1,0:T(8,128)(2,1)S(1)}, u32[]{:S(2)}, u32[]{:S(2)}) collective-permute-start(bf16[8,2,32,128]{3,2,1,0:T(8,128)(2,1)} %get-tuple-element.52), channel_id=1, source_target_pairs={{0,1},{1,0},{2,3},{3,2},{4,5},{5,4},{6,7},{7,6},{8,9},{9,8},{10,11... | collective-permute-start | bytes 393224 | tf_op jit(solution)/shard_map/ppermute | solution.py:203
  5.2 2.6 %collective-permute-start.1 = (bf16[8,2,32,128]{3,2,1,0:T(8,128)(2,1)}, bf16[8,2,32,128]{3,2,1,0:T(8,128)(2,1)S(1)}, u32[]{:S(2)}, u32[]{:S(2)}) collective-permute-start(bf16[8,2,32,128]{3,2,1,0:T(8,128)(2,1)} %get-tuple-element.51), channel_id=1, source_target_pairs={{0,2},{2,0},{1,3},{3,1},{4,6},{6,4},{5,7},{7,5},{8,10},{10,8},{9,1... | collective-permute-start | bytes 393224 | tf_op jit(solution)/shard_map/ppermute | solution.py:205
  7.8 0.7 dynamic-slice_bitcast_fusion
  8.5 0.1 iota_compare_fusion
  8.6 0.1 fusion.59
  8.7 0.0 copy-start.7
  8.7 0.1 broadcast_select_fusion.own_ref
  8.8 0.1 fusion.61
  8.9 1.5 %collective-permute-done.one_ref = bf16[8,2,32,128]{3,2,1,0:T(8,128)(2,1)S(1)} collective-permute-done((bf16[8,2,32,128]{3,2,1,0:T(8,128)(2,1)}, bf16[8,2,32,128]{3,2,1,0:T(8,128)(2,1)S(1)}, u32[]{:S(2)}, u32[]{:S(2)}) %collective-permute-start) | collective-permute-done | bytes 131104 | tf_op jit(solution)/shard_map/ppermute | solution.py:203
  10.4 7.9 %collective-permute-done.1.two_ref = bf16[8,2,32,128]{3,2,1,0:T(8,128)(2,1)S(1)} collective-permute-done((bf16[8,2,32,128]{3,2,1,0:T(8,128)(2,1)}, bf16[8,2,32,128]{3,2,1,0:T(8,128)(2,1)S(1)}, u32[]{:S(2)}, u32[]{:S(2)}) %collective-permute-start.1) | collective-permute-done | bytes 131104 | tf_op jit(solution)/shard_map/ppermute | solution.py:205
  18.3 2.0 %collective-permute-start.3 = (bf16[8,2,32,128]{3,2,1,0:T(8,128)(2,1)S(1)}, bf16[8,2,32,128]{3,2,1,0:T(8,128)(2,1)S(1)}, u32[]{:S(2)}, u32[]{:S(2)}) collective-permute-start(bf16[8,2,32,128]{3,2,1,0:T(8,128)(2,1)S(1)} %copy-done.9), channel_id=1, source_target_pairs={{0,1},{1,0},{2,3},{3,2},{4,5},{5,4},{6,7},{7,6},{8,9},{9,8},{10,11... | collective-permute-start | bytes 393224 | tf_op jit(solution)/shard_map/ppermute | solution.py:203
  20.3 1.1 collective-permute-start.4
  21.4 1.5 %collective-permute-start.5 = (bf16[8,2,32,128]{3,2,1,0:T(8,128)(2,1)S(1)}, bf16[8,2,32,128]{3,2,1,0:T(8,128)(2,1)S(1)}, u32[]{:S(2)}, u32[]{:S(2)}) collective-permute-start(bf16[8,2,32,128]{3,2,1,0:T(8,128)(2,1)S(1)} %copy-done.7), channel_id=1, source_target_pairs={{0,3},{1,2},{2,1},{3,0},{4,7},{5,6},{6,5},{7,4},{8,11},{9,10},{10,... | collective-permute-start | bytes 393224 | tf_op jit(solution)/shard_map/ppermute | solution.py:206
  22.8 6.8 %shard_map.46 = (bf16[8,2,128,256]{3,2,1,0:T(8,128)(2,1)S(1)}, bf16[8,2,128,128]{3,2,1,0:T(8,128)(2,1)S(1)}) custom-call(s32[1]{0:T(128)} %bitcast.2.member_ref, f32[8]{0:T(128)S(1)} %get-tuple-element.58.scale_ref, bf16[2,4,8,2,32,128]{5,4,3,2,1,0:T(8,128)(2,1)S(1)} %bitcast.54, bf16[8,2,32,128]{3,2,1,0:T(8,128)(2,1)S(1)} %collective-permute-done.one_ref, ...), custom_call_target="tpu_custom_call" | custom-call | flops 8589934592 | bytes 3145728 | tf_op jit(solution)/shard_map/pallas_call | solution.py:276
  29.7 0.8 copy-done.3
  30.5 0.0 collective-permute-done.3.one_ref
  30.5 1.6 %collective-permute-done.4.two_ref = bf16[8,2,32,128]{3,2,1,0:T(8,128)(2,1)S(1)} collective-permute-done((bf16[8,2,32,128]{3,2,1,0:T(8,128)(2,1)S(1)}, bf16[8,2,32,128]{3,2,1,0:T(8,128)(2,1)S(1)}, u32[]{:S(2)}, u32[]{:S(2)}) %collective-permute-start.4) | collective-permute-done | bytes 131104 | tf_op jit(solution)/shard_map/ppermute | solution.py:205
  32.0 0.0 collective-permute-done.5.three_ref
  32.0 2.0 %collective-permute-start.6 = (bf16[16,32,128]{2,1,0:T(8,128)(2,1)S(1)}, bf16[16,32,128]{2,1,0:T(8,128)(2,1)S(1)}, u32[]{:S(2)}, u32[]{:S(2)}) collective-permute-start(bf16[16,32,128]{2,1,0:T(8,128)(2,1)S(1)} %bitcast.64), channel_id=1, source_target_pairs={{0,1},{1,0},{2,3},{3,2},{4,5},{5,4},{6,7},{7,6},{8,9},{9,8},{10,11... | collective-permute-start | bytes 393224 | tf_op jit(solution)/shard_map/ppermute | solution.py:203
  34.0 1.0 collective-permute-start.7
  35.0 1.5 %collective-permute-start.8 = (bf16[16,32,128]{2,1,0:T(8,128)(2,1)S(1)}, bf16[16,32,128]{2,1,0:T(8,128)(2,1)S(1)}, u32[]{:S(2)}, u32[]{:S(2)}) collective-permute-start(bf16[16,32,128]{2,1,0:T(8,128)(2,1)S(1)} %bitcast.62), channel_id=1, source_target_pairs={{0,3},{1,2},{2,1},{3,0},{4,7},{5,6},{6,5},{7,4},{8,11},{9,10},{10,... | collective-permute-start | bytes 393224 | tf_op jit(solution)/shard_map/ppermute | solution.py:206
  36.4 6.8 %shard_map.48 = (bf16[8,2,128,256]{3,2,1,0:T(8,128)(2,1)S(1)}, bf16[8,2,128,128]{3,2,1,0:T(8,128)(2,1)S(1)}) custom-call(s32[1]{0:T(128)} %bitcast.2.member_ref, f32[8]{0:T(128)S(1)} %get-tuple-element.59.scale_ref, bf16[2,4,8,2,32,128]{5,4,3,2,1,0:T(8,128)(2,1)S(1)} %bitcast.55, bf16[8,2,32,128]{3,2,1,0:T(8,128)(2,1)S(1)} %collective-permute-done.3.one_ref, ...), custom_call_target="tpu_custom_call" | custom-call | flops 8589934592 | bytes 3145728 | tf_op jit(solution)/shard_map/pallas_call | solution.py:276
  43.3 2.8 %collective-permute-done.7.two_ref = bf16[16,32,128]{2,1,0:T(8,128)(2,1)S(1)} collective-permute-done((bf16[16,32,128]{2,1,0:T(8,128)(2,1)S(1)}, bf16[16,32,128]{2,1,0:T(8,128)(2,1)S(1)}, u32[]{:S(2)}, u32[]{:S(2)}) %collective-permute-start.7) | collective-permute-done | bytes 131104 | tf_op jit(solution)/shard_map/ppermute | solution.py:205
  46.1 2.5 %shard_map.47 = f32[1024,128]{1,0:T(8,128)S(1)} custom-call(s32[1]{0:T(128)} %bitcast.2.member_ref, bf16[8,2,128,256]{3,2,1,0:T(8,128)(2,1)S(1)} %get-tuple-element.19.inverse_ref, bf16[2,4,8,32,128]{4,3,2,1,0:T(8,128)(2,1)S(1)} %broadcast_select_fusion.own_ref, bf16[16,32,128]{2,1,0:T(8,128)(2,1)S(1)} %collective-permute-done.6.one_ref, ...), custom_call_target="tpu_custom_call" | custom-call | flops 1342177280 | bytes 3145728 | tf_op jit(solution)/shard_map/pallas_call | solution.py:295
  48.6 2.5 %shard_map.49 = f32[1024,128]{1,0:T(8,128)S(1)} custom-call(s32[1]{0:T(128)} %bitcast.2.member_ref, bf16[8,2,128,256]{3,2,1,0:T(8,128)(2,1)S(1)} %get-tuple-element.26.inverse_ref, bf16[2,4,8,32,128]{4,3,2,1,0:T(8,128)(2,1)S(1)} %broadcast_select_fusion.own_ref, bf16[16,32,128]{2,1,0:T(8,128)(2,1)S(1)} %collective-permute-done.6.one_ref, ...), custom_call_target="tpu_custom_call" | custom-call | flops 1342177280 | bytes 3145728 | tf_op jit(solution)/shard_map/pallas_call | solution.py:295
  51.1 1.0 pad_maximum_fusion.1
  52.1 5.3 %all-to-all-start = ((f16[32,4,16,128]{3,2,1,0:T(8,128)(2,1)}), f16[32,4,16,128]{3,2,1,0:T(8,128)(2,1)S(1)}, u32[]{:S(2)}, u32[]{:S(2)}) async-start(f16[32,4,16,128]{3,2,1,0:T(8,128)(2,1)} %pad_maximum_fusion.1), calls=%async_computation | async-start | bytes 1048576 | tf_op jit(solution)/shard_map/all_to_all | solution.py:318
  58.1 8.2 %fusion.3 = (f32[512,512]{1,0:T(8,128)S(1)}, f32[512,512]{1,0:T(8,128)S(1)}) fusion(s32[512]{0:T(512)S(1)} %fusion.51, s32[]{:T(128)} %bitcast.1, f32[]{:T(128)} %bitcast), kind=kLoop, calls=%fused_computation.9 | loop fusion | flops 7340032 | bytes 2099208 | tf_op jit(solution)/shard_map/jit(_where)/select_n | solution.py:181
  66.3 6.5 %all-to-all-done = f16[32,4,16,128]{3,2,1,0:T(8,128)(2,1)S(1)} async-done(((f16[32,4,16,128]{3,2,1,0:T(8,128)(2,1)}), f16[32,4,16,128]{3,2,1,0:T(8,128)(2,1)S(1)}, u32[]{:S(2)}, u32[]{:S(2)}) %all-to-all-start) | async-done | bytes 524320 | tf_op jit(solution)/shard_map/all_to_all | solution.py:318
  72.8 0.1 convert_element_type.90.values_ref
  72.9 2.5 %shard_map.50 = (f32[32,4,2,8,128]{4,3,2,1,0:T(8,128)S(1)}, f32[32,4,2,8,128]{4,3,2,1,0:T(8,128)S(1)}) custom-call(f32[512,512]{1,0:T(8,128)S(1)} %get-tuple-element.57.real_ref, f32[512,512]{1,0:T(8,128)S(1)} %get-tuple-element.56.imag_ref, f32[32,4,16,128]{3,2,1,0:T(8,128)S(1)} %convert_element_type.90.values_ref), custom_call_target="tpu_custom_call" | custom-call | flops 1610612736 | bytes 3145728 | tf_op jit(solution)/shard_map/pallas_call | solution.py:325
  75.4 0.9 convert_element_type.91
  76.3 3.1 %all-to-all-start.1 = ((f16[32,4,2,8,128]{4,3,2,1,0:T(8,128)(2,1)}), f16[32,4,2,8,128]{4,3,2,1,0:T(8,128)(2,1)S(1)}, u32[]{:S(2)}, u32[]{:S(2)}) async-start(f16[32,4,2,8,128]{4,3,2,1,0:T(8,128)(2,1)} %convert_element_type.91), calls=%async_computation.1 | async-start | bytes 1048576 | tf_op jit(solution)/shard_map/all_to_all | solution.py:350
  79.4 0.9 convert_element_type.101
  80.3 14.6 %all-to-all-done.1 = f16[32,4,2,8,128]{4,3,2,1,0:T(8,128)(2,1)S(1)} async-done(((f16[32,4,2,8,128]{4,3,2,1,0:T(8,128)(2,1)}), f16[32,4,2,8,128]{4,3,2,1,0:T(8,128)(2,1)S(1)}, u32[]{:S(2)}, u32[]{:S(2)}) %all-to-all-start.1) | async-done | bytes 524320 | tf_op jit(solution)/shard_map/all_to_all | solution.py:350
  94.9 3.3 %all-to-all-start.2 = ((f16[32,4,2,8,128]{4,3,2,1,0:T(8,128)(2,1)}), f16[32,4,2,8,128]{4,3,2,1,0:T(8,128)(2,1)S(1)}, u32[]{:S(2)}, u32[]{:S(2)}) async-start(f16[32,4,2,8,128]{4,3,2,1,0:T(8,128)(2,1)} %convert_element_type.101), calls=%async_computation.2 | async-start | bytes 1048576 | tf_op jit(solution)/shard_map/all_to_all | solution.py:350
  98.2 0.1 bitcast_convert_fusion.1.causal_ref
  98.3 1.0 shard_map.51
  99.3 0.1 fusion.37
  99.5 2.5 %collective-permute-start.10 = (f16[8,2,32,128]{3,2,1,0:T(8,128)(2,1)S(1)}, f16[8,2,32,128]{3,2,1,0:T(8,128)(2,1)S(1)}, u32[]{:S(2)}, u32[]{:S(2)}) collective-permute-start(f16[8,2,32,128]{3,2,1,0:T(8,128)(2,1)S(1)} %get-tuple-element.40), channel_id=1, source_target_pairs={{0,2},{2,0},{1,3},{3,1},{4,6},{6,4},{5,7},{7,5},{8,10},{10,8},{9,1... | collective-permute-start | bytes 393224 | tf_op jit(solution)/shard_map/ppermute | solution.py:205
  102.0 1.5 %collective-permute-start.11 = (f16[8,2,32,128]{3,2,1,0:T(8,128)(2,1)S(1)}, f16[8,2,32,128]{3,2,1,0:T(8,128)(2,1)S(1)}, u32[]{:S(2)}, u32[]{:S(2)}) collective-permute-start(f16[8,2,32,128]{3,2,1,0:T(8,128)(2,1)S(1)} %get-tuple-element.41), channel_id=1, source_target_pairs={{0,3},{1,2},{2,1},{3,0},{4,7},{5,6},{6,5},{7,4},{8,11},{9,10},{10,... | collective-permute-start | bytes 393224 | tf_op jit(solution)/shard_map/ppermute | solution.py:206
  103.4 0.1 collective-permute-start.9
  103.5 18.4 %collective-permute-done.10 = f16[8,2,32,128]{3,2,1,0:T(8,128)(2,1)S(1)} collective-permute-done((f16[8,2,32,128]{3,2,1,0:T(8,128)(2,1)S(1)}, f16[8,2,32,128]{3,2,1,0:T(8,128)(2,1)S(1)}, u32[]{:S(2)}, u32[]{:S(2)}) %collective-permute-start.10) | collective-permute-done | bytes 131104 | tf_op jit(solution)/shard_map/ppermute | solution.py:205
  121.9 0.0 collective-permute-done.11
  121.9 0.0 collective-permute-done.9
  121.9 0.2 fusion.17
  122.1 0.1 pad_maximum_fusion
  122.2 0.1 bitcast_convert_fusion.causal_ref
  122.3 0.8 copy-done.2
  123.1 1.0 shard_map.52
  124.1 0.1 fusion.40
  124.2 3.0 %collective-permute-start.12 = (f16[8,2,32,128]{3,2,1,0:T(8,128)(2,1)S(1)}, f16[8,2,32,128]{3,2,1,0:T(8,128)(2,1)S(1)}, u32[]{:S(2)}, u32[]{:S(2)}) collective-permute-start(f16[8,2,32,128]{3,2,1,0:T(8,128)(2,1)S(1)} %get-tuple-element.39), channel_id=1, source_target_pairs={{0,1},{1,0},{2,3},{3,2},{4,5},{5,4},{6,7},{7,6},{8,9},{9,8},{10,11... | collective-permute-start | bytes 393224 | tf_op jit(solution)/shard_map/ppermute | solution.py:203
  127.2 2.4 %collective-permute-start.14 = (f16[8,2,32,128]{3,2,1,0:T(8,128)(2,1)S(1)}, f16[8,2,32,128]{3,2,1,0:T(8,128)(2,1)S(1)}, u32[]{:S(2)}, u32[]{:S(2)}) collective-permute-start(f16[8,2,32,128]{3,2,1,0:T(8,128)(2,1)S(1)} %get-tuple-element.38), channel_id=1, source_target_pairs={{0,3},{1,2},{2,1},{3,0},{4,7},{5,6},{6,5},{7,4},{8,11},{9,10},{10,... | collective-permute-start | bytes 393224 | tf_op jit(solution)/shard_map/ppermute | solution.py:206
  129.6 0.1 constant_dynamic-update-slice_fusion
  129.7 1.8 %collective-permute-done.12 = f16[8,2,32,128]{3,2,1,0:T(8,128)(2,1)S(1)} collective-permute-done((f16[8,2,32,128]{3,2,1,0:T(8,128)(2,1)S(1)}, f16[8,2,32,128]{3,2,1,0:T(8,128)(2,1)S(1)}, u32[]{:S(2)}, u32[]{:S(2)}) %collective-permute-start.12) | collective-permute-done | bytes 131104 | tf_op jit(solution)/shard_map/ppermute | solution.py:203
  131.5 8.1 %collective-permute-done.13 = f16[8,2,32,128]{3,2,1,0:T(8,128)(2,1)S(1)} collective-permute-done((f16[8,2,32,128]{3,2,1,0:T(8,128)(2,1)S(1)}, f16[8,2,32,128]{3,2,1,0:T(8,128)(2,1)S(1)}, u32[]{:S(2)}, u32[]{:S(2)}) %collective-permute-start.13) | collective-permute-done | bytes 131104 | tf_op jit(solution)/shard_map/ppermute | solution.py:205
  139.6 0.1 fusion.26
  139.7 0.1 fusion.29
  139.8 0.1 fusion.32
  139.9 0.1 fusion.35
  140.0 0.0 copy-start.6
  140.0 1.3 copy-done.6
  (29 shorter events, 0.2 us)
Async XLA Ops:
  0.0 8.6 %copy-start.5 = (bf16[64,2,32,128]{3,2,1,0:T(8,128)(2,1)S(1)}, bf16[64,2,32,128]{3,2,1,0:T(8,128)(2,1)}, u32[]{:S(2)}) copy-start(bf16[64,2,32,128]{3,2,1,0:T(8,128)(2,1)} %param.5) | copy-start | bytes 3145732
  2.1 8.3 %collective-permute-start = (bf16[8,2,32,128]{3,2,1,0:T(8,128)(2,1)}, bf16[8,2,32,128]{3,2,1,0:T(8,128)(2,1)S(1)}, u32[]{:S(2)}, u32[]{:S(2)}) collective-permute-start(bf16[8,2,32,128]{3,2,1,0:T(8,128)(2,1)} %get-tuple-element.52), channel_id=1, source_target_pairs={{0,1},{1,0},{2,3},{3,2},{4,5},{5,4},{6,7},{7,6},{8,9},{9,8},{10,11... | collective-permute-start | bytes 393224 | tf_op jit(solution)/shard_map/ppermute | solution.py:203
  5.2 13.1 %collective-permute-start.1 = (bf16[8,2,32,128]{3,2,1,0:T(8,128)(2,1)}, bf16[8,2,32,128]{3,2,1,0:T(8,128)(2,1)S(1)}, u32[]{:S(2)}, u32[]{:S(2)}) collective-permute-start(bf16[8,2,32,128]{3,2,1,0:T(8,128)(2,1)} %get-tuple-element.51), channel_id=1, source_target_pairs={{0,2},{2,0},{1,3},{3,1},{4,6},{6,4},{5,7},{7,5},{8,10},{10,8},{9,1... | collective-permute-start | bytes 393224 | tf_op jit(solution)/shard_map/ppermute | solution.py:205
  7.8 10.5 %collective-permute-start.2 = (bf16[8,2,32,128]{3,2,1,0:T(8,128)(2,1)}, bf16[8,2,32,128]{3,2,1,0:T(8,128)(2,1)S(1)}, u32[]{:S(2)}, u32[]{:S(2)}) collective-permute-start(bf16[8,2,32,128]{3,2,1,0:T(8,128)(2,1)} %get-tuple-element.50), channel_id=1, source_target_pairs={{0,3},{1,2},{2,1},{3,0},{4,7},{5,6},{6,5},{7,4},{8,11},{9,10},{10,... | collective-permute-start | bytes 393224 | tf_op jit(solution)/shard_map/ppermute | solution.py:206
  7.8 1.0 copy-start.10
  8.6 14.2 %copy-start = (bf16[64,2,32,128]{3,2,1,0:T(8,128)(2,1)S(1)}, bf16[64,2,32,128]{3,2,1,0:T(8,128)(2,1)}, u32[]{:S(2)}) copy-start(bf16[64,2,32,128]{3,2,1,0:T(8,128)(2,1)} %param.4) | copy-start | bytes 3145732
  8.7 9.6 %copy-start.9 = (bf16[8,2,32,128]{3,2,1,0:T(8,128)(2,1)S(1)}, bf16[8,2,32,128]{3,2,1,0:T(8,128)(2,1)}, u32[]{:S(2)}) copy-start(bf16[8,2,32,128]{3,2,1,0:T(8,128)(2,1)} %get-tuple-element.20) | copy-start | bytes 393220
  8.7 11.6 %copy-start.8 = (bf16[8,2,32,128]{3,2,1,0:T(8,128)(2,1)S(1)}, bf16[8,2,32,128]{3,2,1,0:T(8,128)(2,1)}, u32[]{:S(2)}) copy-start(bf16[8,2,32,128]{3,2,1,0:T(8,128)(2,1)} %get-tuple-element.21) | copy-start | bytes 393220
  8.7 12.7 %copy-start.7 = (bf16[8,2,32,128]{3,2,1,0:T(8,128)(2,1)S(1)}, bf16[8,2,32,128]{3,2,1,0:T(8,128)(2,1)}, u32[]{:S(2)}) copy-start(bf16[8,2,32,128]{3,2,1,0:T(8,128)(2,1)} %get-tuple-element.22) | copy-start | bytes 393220
  18.3 12.2 %collective-permute-start.3 = (bf16[8,2,32,128]{3,2,1,0:T(8,128)(2,1)S(1)}, bf16[8,2,32,128]{3,2,1,0:T(8,128)(2,1)S(1)}, u32[]{:S(2)}, u32[]{:S(2)}) collective-permute-start(bf16[8,2,32,128]{3,2,1,0:T(8,128)(2,1)S(1)} %copy-done.9), channel_id=1, source_target_pairs={{0,1},{1,0},{2,3},{3,2},{4,5},{5,4},{6,7},{7,6},{8,9},{9,8},{10,11... | collective-permute-start | bytes 393224 | tf_op jit(solution)/shard_map/ppermute | solution.py:203
  20.3 11.7 %collective-permute-start.4 = (bf16[8,2,32,128]{3,2,1,0:T(8,128)(2,1)S(1)}, bf16[8,2,32,128]{3,2,1,0:T(8,128)(2,1)S(1)}, u32[]{:S(2)}, u32[]{:S(2)}) collective-permute-start(bf16[8,2,32,128]{3,2,1,0:T(8,128)(2,1)S(1)} %copy-done.8), channel_id=1, source_target_pairs={{0,2},{2,0},{1,3},{3,1},{4,6},{6,4},{5,7},{7,5},{8,10},{10,8},{9,1... | collective-permute-start | bytes 393224 | tf_op jit(solution)/shard_map/ppermute | solution.py:205
  21.4 10.7 %collective-permute-start.5 = (bf16[8,2,32,128]{3,2,1,0:T(8,128)(2,1)S(1)}, bf16[8,2,32,128]{3,2,1,0:T(8,128)(2,1)S(1)}, u32[]{:S(2)}, u32[]{:S(2)}) collective-permute-start(bf16[8,2,32,128]{3,2,1,0:T(8,128)(2,1)S(1)} %copy-done.7), channel_id=1, source_target_pairs={{0,3},{1,2},{2,1},{3,0},{4,7},{5,6},{6,5},{7,4},{8,11},{9,10},{10,... | collective-permute-start | bytes 393224 | tf_op jit(solution)/shard_map/ppermute | solution.py:206
  29.7 0.8 copy-start.3
  32.0 11.2 %collective-permute-start.6 = (bf16[16,32,128]{2,1,0:T(8,128)(2,1)S(1)}, bf16[16,32,128]{2,1,0:T(8,128)(2,1)S(1)}, u32[]{:S(2)}, u32[]{:S(2)}) collective-permute-start(bf16[16,32,128]{2,1,0:T(8,128)(2,1)S(1)} %bitcast.64), channel_id=1, source_target_pairs={{0,1},{1,0},{2,3},{3,2},{4,5},{5,4},{6,7},{7,6},{8,9},{9,8},{10,11... | collective-permute-start | bytes 393224 | tf_op jit(solution)/shard_map/ppermute | solution.py:203
  34.0 12.1 %collective-permute-start.7 = (bf16[16,32,128]{2,1,0:T(8,128)(2,1)S(1)}, bf16[16,32,128]{2,1,0:T(8,128)(2,1)S(1)}, u32[]{:S(2)}, u32[]{:S(2)}) collective-permute-start(bf16[16,32,128]{2,1,0:T(8,128)(2,1)S(1)} %bitcast.63), channel_id=1, source_target_pairs={{0,2},{2,0},{1,3},{3,1},{4,6},{6,4},{5,7},{7,5},{8,10},{10,8},{9,1... | collective-permute-start | bytes 393224 | tf_op jit(solution)/shard_map/ppermute | solution.py:205
  35.0 11.1 %collective-permute-start.8 = (bf16[16,32,128]{2,1,0:T(8,128)(2,1)S(1)}, bf16[16,32,128]{2,1,0:T(8,128)(2,1)S(1)}, u32[]{:S(2)}, u32[]{:S(2)}) collective-permute-start(bf16[16,32,128]{2,1,0:T(8,128)(2,1)S(1)} %bitcast.62), channel_id=1, source_target_pairs={{0,3},{1,2},{2,1},{3,0},{4,7},{5,6},{6,5},{7,4},{8,11},{9,10},{10,... | collective-permute-start | bytes 393224 | tf_op jit(solution)/shard_map/ppermute | solution.py:206
  43.3 5.3 %copy-start.1 = (bf16[8,2,128,128]{3,2,1,0:T(8,128)(2,1)}, bf16[8,2,128,128]{3,2,1,0:T(8,128)(2,1)S(1)}, u32[]{:S(2)}) copy-start(bf16[8,2,128,128]{3,2,1,0:T(8,128)(2,1)S(1)} %get-tuple-element.32.psi_ref) | copy-start | bytes 1572868
  52.1 20.7 %all-to-all-start = ((f16[32,4,16,128]{3,2,1,0:T(8,128)(2,1)}), f16[32,4,16,128]{3,2,1,0:T(8,128)(2,1)S(1)}, u32[]{:S(2)}, u32[]{:S(2)}) async-start(f16[32,4,16,128]{3,2,1,0:T(8,128)(2,1)} %pad_maximum_fusion.1), calls=%async_computation | async-start | bytes 1048576 | tf_op jit(solution)/shard_map/all_to_all | solution.py:318
  76.3 18.6 %all-to-all-start.1 = ((f16[32,4,2,8,128]{4,3,2,1,0:T(8,128)(2,1)}), f16[32,4,2,8,128]{4,3,2,1,0:T(8,128)(2,1)S(1)}, u32[]{:S(2)}, u32[]{:S(2)}) async-start(f16[32,4,2,8,128]{4,3,2,1,0:T(8,128)(2,1)} %convert_element_type.91), calls=%async_computation.1 | async-start | bytes 1048576 | tf_op jit(solution)/shard_map/all_to_all | solution.py:350
  79.3 19.0 %copy-start.4 = (bf16[8,2,128,128]{3,2,1,0:T(8,128)(2,1)S(1)}, bf16[8,2,128,128]{3,2,1,0:T(8,128)(2,1)}, u32[]{:S(2)}) copy-start(bf16[8,2,128,128]{3,2,1,0:T(8,128)(2,1)} %copy-done.3) | copy-start | bytes 1572868
  94.9 27.3 %all-to-all-start.2 = ((f16[32,4,2,8,128]{4,3,2,1,0:T(8,128)(2,1)}), f16[32,4,2,8,128]{4,3,2,1,0:T(8,128)(2,1)S(1)}, u32[]{:S(2)}, u32[]{:S(2)}) async-start(f16[32,4,2,8,128]{4,3,2,1,0:T(8,128)(2,1)} %convert_element_type.101), calls=%async_computation.2 | async-start | bytes 1048576 | tf_op jit(solution)/shard_map/all_to_all | solution.py:350
  99.5 22.4 %collective-permute-start.10 = (f16[8,2,32,128]{3,2,1,0:T(8,128)(2,1)S(1)}, f16[8,2,32,128]{3,2,1,0:T(8,128)(2,1)S(1)}, u32[]{:S(2)}, u32[]{:S(2)}) collective-permute-start(f16[8,2,32,128]{3,2,1,0:T(8,128)(2,1)S(1)} %get-tuple-element.40), channel_id=1, source_target_pairs={{0,2},{2,0},{1,3},{3,1},{4,6},{6,4},{5,7},{7,5},{8,10},{10,8},{9,1... | collective-permute-start | bytes 393224 | tf_op jit(solution)/shard_map/ppermute | solution.py:205
  102.0 19.9 %collective-permute-start.11 = (f16[8,2,32,128]{3,2,1,0:T(8,128)(2,1)S(1)}, f16[8,2,32,128]{3,2,1,0:T(8,128)(2,1)S(1)}, u32[]{:S(2)}, u32[]{:S(2)}) collective-permute-start(f16[8,2,32,128]{3,2,1,0:T(8,128)(2,1)S(1)} %get-tuple-element.41), channel_id=1, source_target_pairs={{0,3},{1,2},{2,1},{3,0},{4,7},{5,6},{6,5},{7,4},{8,11},{9,10},{10,... | collective-permute-start | bytes 393224 | tf_op jit(solution)/shard_map/ppermute | solution.py:206
  103.4 18.4 %collective-permute-start.9 = (f16[8,2,32,128]{3,2,1,0:T(8,128)(2,1)S(1)}, f16[8,2,32,128]{3,2,1,0:T(8,128)(2,1)S(1)}, u32[]{:S(2)}, u32[]{:S(2)}) collective-permute-start(f16[8,2,32,128]{3,2,1,0:T(8,128)(2,1)S(1)} %get-tuple-element.42), channel_id=1, source_target_pairs={{0,1},{1,0},{2,3},{3,2},{4,5},{5,4},{6,7},{7,6},{8,9},{9,8},{10,11... | collective-permute-start | bytes 393224 | tf_op jit(solution)/shard_map/ppermute | solution.py:203
  122.1 1.0 copy-start.2
  124.2 7.3 %collective-permute-start.12 = (f16[8,2,32,128]{3,2,1,0:T(8,128)(2,1)S(1)}, f16[8,2,32,128]{3,2,1,0:T(8,128)(2,1)S(1)}, u32[]{:S(2)}, u32[]{:S(2)}) collective-permute-start(f16[8,2,32,128]{3,2,1,0:T(8,128)(2,1)S(1)} %get-tuple-element.39), channel_id=1, source_target_pairs={{0,1},{1,0},{2,3},{3,2},{4,5},{5,4},{6,7},{7,6},{8,9},{9,8},{10,11... | collective-permute-start | bytes 393224 | tf_op jit(solution)/shard_map/ppermute | solution.py:203
  127.2 12.4 %collective-permute-start.13 = (f16[8,2,32,128]{3,2,1,0:T(8,128)(2,1)S(1)}, f16[8,2,32,128]{3,2,1,0:T(8,128)(2,1)S(1)}, u32[]{:S(2)}, u32[]{:S(2)}) collective-permute-start(f16[8,2,32,128]{3,2,1,0:T(8,128)(2,1)S(1)} %get-tuple-element.37), channel_id=1, source_target_pairs={{0,2},{2,0},{1,3},{3,1},{4,6},{6,4},{5,7},{7,5},{8,10},{10,8},{9,1... | collective-permute-start | bytes 393224 | tf_op jit(solution)/shard_map/ppermute | solution.py:205
  127.2 12.4 %collective-permute-start.14 = (f16[8,2,32,128]{3,2,1,0:T(8,128)(2,1)S(1)}, f16[8,2,32,128]{3,2,1,0:T(8,128)(2,1)S(1)}, u32[]{:S(2)}, u32[]{:S(2)}) collective-permute-start(f16[8,2,32,128]{3,2,1,0:T(8,128)(2,1)S(1)} %get-tuple-element.38), channel_id=1, source_target_pairs={{0,3},{1,2},{2,1},{3,0},{4,7},{5,6},{6,5},{7,4},{8,11},{9,10},{10,... | collective-permute-start | bytes 393224 | tf_op jit(solution)/shard_map/ppermute | solution.py:206
  140.0 1.3 copy-start.6

commit v4 on v1

--- a/solution.py
+++ b/solution.py
@@ -51,7 +51,8 @@
         out_ref[..., pl.ds(start, rows), :] = panel[...]
 
 
-def newton_kernel(member_ref, scale_ref, own_ref, one_ref, two_ref, three_ref, out_ref, psi_ref):
+def newton_kernel(member_ref, scale_ref, own_ref, one_ref, two_ref, three_ref, *refs):
+    out_ref, psi_ref = refs[-2:]
     bins, _, size, _ = psi_ref.shape
     place_rows(member_ref[0], [own_ref.at[0], one_ref, two_ref, three_ref], psi_ref)
     identity = eye(size)
@@ -142,30 +143,24 @@
     out_ref[:, 0, 1] = (real[:, lanes:] + imag[:, :lanes]).reshape(shape)
 
 
-def product(causal_ref, psi_ref, out_ref, first):
+def place_kernel(member_ref, own_ref, one_ref, two_ref, three_ref, out_ref):
+    place_rows(member_ref[0], [own_ref.at[0], one_ref, two_ref, three_ref], out_ref)
+
+
+def product_kernel(first, member_ref, causal_ref, psi_ref, out_ref):
     bins, _, size, _ = psi_ref.shape
-    panels, _, _, rows, _ = out_ref.shape
-    columns = panels * rows
-    total_bins = causal_ref.shape[0] // (2 * columns)
+    rows = out_ref.shape[2]
+    total_bins = causal_ref.shape[0] // (2 * rows)
     for item in range(bins):
         re, im = psi_ref[item, 0], psi_ref[item, 1]
         place = first + pl.program_id(0) * bins + item
-        part_re = causal_ref[pl.ds(place, columns, stride=2 * total_bins), :]
-        part_im = causal_ref[pl.ds(total_bins + place, columns, stride=2 * total_bins), :]
+        part_re = causal_ref[pl.ds(place, rows, stride=2 * total_bins), :]
+        part_im = causal_ref[pl.ds(total_bins + place, rows, stride=2 * total_bins), :]
         high, low = split(cat([part_re, part_im], 1))
         both = dot(cat([high, low], 0), cat([cat([re, -im], 1), cat([im, re], 1)], 0), NT)
-        result = both[:columns] + both[columns:]
-        out_ref[:, item, 0] = result[:, :size].reshape(panels, rows, size)
-        out_ref[:, item, 1] = result[:, size:].reshape(panels, rows, size)
-
-
-def near_kernel(causal_ref, psi_ref, out_ref):
-    product(causal_ref, psi_ref, out_ref, 0)
-
-
-def far_kernel(member_ref, causal_ref, own_ref, one_ref, two_ref, three_ref, out_ref, psi_ref):
-    place_rows(member_ref[0], [own_ref.at[0], one_ref, two_ref, three_ref], psi_ref)
-    product(causal_ref, psi_ref, out_ref, pl.num_programs(0) * psi_ref.shape[0])
+        result = both[:rows] + both[rows:]
+        out_ref[item, 0] = result[:, :size]
+        out_ref[item, 1] = result[:, size:]
 
 
 def projection_table(lag_limit, count, freq_size, pairs, side):
@@ -217,7 +212,7 @@
     return lax.ppermute(value, ("side", "pair"), FLIP)
 
 
-def call(kernel, steps, in_specs, out_specs, out_shape, scratch, flops, moved):
+def call(kernel, steps, in_specs, out_specs, out_shape, scratch, flops, moved, aliases={}):
     return pl.pallas_call(
         kernel,
         grid_spec=pltpu.PrefetchScalarGridSpec(
@@ -228,6 +223,7 @@
             scratch_shapes=scratch,
         ),
         out_shape=out_shape,
+        input_output_aliases=aliases,
         compiler_params=params(16),
         cost_estimate=cost(flops, moved),
     )
@@ -280,56 +276,64 @@
     other_block = pl.BlockSpec((step, 2, rows, size), lambda i, m: (i, 0, 0, 0))
     whole_block = pl.BlockSpec((step, 2, size, size), lambda i, m: (i, 0, 0, 0))
     inverse_block = pl.BlockSpec((step, 2, size, 2 * size), lambda i, m: (i, 0, 0, 0))
-    inverses, psis, middles = [], [], []
+    state = []
     for chunk in range(chunks):
         scale = lax.dynamic_slice_in_dim(guess_scale, member * own + chunk * part, part, 0)
-        inverse, psi = call(
+        offset = chunk * part // step
+        state = call(
             newton_kernel,
             part // step,
-            [pl.BlockSpec(memory_space=pltpu.SMEM), local_block(chunk * part // step)] + [other_block] * 3,
-            [inverse_block, whole_block],
+            [pl.BlockSpec(memory_space=pltpu.SMEM), local_block(offset)]
+            + [other_block] * 3
+            + [pl.BlockSpec(memory_space=pl.ANY)] * len(state),
             [
-                jax.ShapeDtypeStruct((part, 2, size, 2 * size), BF16),
-                jax.ShapeDtypeStruct((part, 2, size, size), BF16),
+                pl.BlockSpec(
+                    (step, 2, size, 2 * size), lambda i, m, offset=offset: (i + offset, 0, 0, 0)
+                ),
+                pl.BlockSpec(
+                    (step, 2, size, size), lambda i, m, offset=offset: (i + offset, 0, 0, 0)
+                ),
+            ],
+            [
+                jax.ShapeDtypeStruct((own, 2, size, 2 * size), BF16),
+                jax.ShapeDtypeStruct((own, 2, size, size), BF16),
             ],
             [],
             part * 64 * 2 * 4 * size**3,
             part * 6 * 4 * size * size,
-        )(members, scale, factors, *arrived[chunk])
-        inverses.append(inverse)
-        psis.append(psi)
-    for chunk in range(chunks):
-        first = chunk * part // step
-        other = pl.BlockSpec((step, rows, size), lambda i, m, first=first: (i + first, 0, 0))
-        middles.append(
-            call(
-                middle_kernel,
-                part // step,
-                [
-                    inverse_block,
-                    pl.BlockSpec(
-                        (1, step, rows, size), lambda i, m, first=first: (m[0], i + first, 0, 0)
-                    ),
-                ]
-                + [other] * 3,
-                pl.BlockSpec((size * 2 * part, size), lambda i, m: (0, 0)),
-                jax.ShapeDtypeStruct((size * 2 * part, size), F32),
-                [pltpu.VMEM((step, size, size), BF16)],
-                part * 10 * 2 * 4 * size**3,
-                part * 6 * 4 * size * size,
-            )(members, inverses[chunk], packed, *packed_arrived)
-        )
-    middles = [value.astype(jnp.float16).reshape(size, 2, part, size) for value in middles]
-    sent = cat(middles, 2) if chunks > 1 else middles[0]
+            {6 + index: index for index in range(len(state))},
+        )(members, scale, factors, *arrived[chunk], *state)
+    inverse, psi = state
+
+    def local_rows(chunk):
+        return lax.dynamic_slice(
+            factors, (member, chunk * part, 0, 0, 0), (1, part, 2, rows, size)
+        ).reshape(part, 2, rows, size)
+
+    across = [swap(after(local_rows(0), packed_arrived[2]), 2)]
+    other = pl.BlockSpec((step, rows, size), lambda i, m: (i, 0, 0))
+    middle = call(
+        middle_kernel,
+        own // step,
+        [inverse_block, pl.BlockSpec((1, step, rows, size), lambda i, m: (m[0], i, 0, 0))]
+        + [other] * 3,
+        pl.BlockSpec((size * 2 * own, size), lambda i, m: (0, 0)),
+        jax.ShapeDtypeStruct((size * 2 * own, size), F32),
+        [pltpu.VMEM((step, size, size), BF16)],
+        own * 40 * 2 * 4 * size**3,
+        own * 6 * 4 * size * size,
+    )(members, inverse, packed, *packed_arrived)
+    sent = after(middle, across[0]).astype(jnp.float16)
     if lane_parts > 1:
         sent = sent.reshape(size, 2, own, lane_parts, lanes).transpose(0, 3, 1, 2, 4)
     sent = sent.reshape(devices, kept, 2, own, lanes)
     gathered = lax.all_to_all(sent, chan + ("freq",), 0, 0, tiled=True)
 
-    across = swap(after(rows_for(member, 0, own), packed_arrived[0]), 2)
-    across_pair = cat([piece[0] for piece in arrived], 0) if chunks > 1 else arrived[0][0]
-    across_pair = swap(after(across_pair, gathered), 2)
-    beside = swap(after(rows_for(member ^ 3, 0, own), packed_arrived[0]), 1)
+    beside = swap(after(rows_for(member ^ 3, 0, own), packed_arrived[2]), 1)
+    gathered = after(gathered, beside)
+    across += [swap(after(local_rows(chunk), gathered), 2) for chunk in range(1, chunks)]
+    first = cat([piece[0] for piece in arrived], 0) if chunks > 1 else arrived[0][0]
+    across_pair = swap(after(first, gathered), 2)
 
     values = gathered.astype(F32)
     sources, own_rows = devices, own
@@ -352,9 +356,9 @@
         out_shape=jax.ShapeDtypeStruct((holders, kept, 2, held, lanes), F32),
         scratch_shapes=[pltpu.VMEM((2 * count, count), BF16), pltpu.VMEM((2 * count, count), BF16)],
         compiler_params=params(24),
-        cost_estimate=cost(kept * 24 * count * count * lanes, 16 * kept * count * lanes),
+        cost_estimate=cost(kept * 96 * count * count * lanes, 16 * kept * count * lanes),
     )(table_re, table_im, values)
-    causal = causal.astype(jnp.float16)
+    causal = after(causal, *across[1:]).astype(jnp.float16)
     if holders == 1:
         causal = causal.reshape(kept, 2, pairs * freq_size, 2 * own, lanes)
         causal = causal.transpose(2, 0, 1, 3, 4)
@@ -364,43 +368,38 @@
         back = back.transpose(0, 2, 3, 4, 1, 5)
     back = back.reshape(pairs * rows * 2 * 2 * own, size)
 
-    back_block = pl.BlockSpec(back.shape, lambda i, m: (0, 0))
-    result_block = pl.BlockSpec((pairs, step, 2, rows, size), lambda i, m: (0, i, 0, 0, 0))
-    result_shape = jax.ShapeDtypeStruct((pairs, own, 2, rows, size), F32)
-    flops, moved = own * 2 * 4 * size**3, own * 4 * 4 * size * size
-    psi = cat(psis, 0) if chunks > 1 else psis[0]
-    near = pl.pallas_call(
-        near_kernel,
-        grid=(own // step,),
-        in_specs=[
-            pl.BlockSpec(back.shape, lambda i: (0, 0)),
-            pl.BlockSpec((step, 2, size, size), lambda i: (i, 0, 0, 0)),
-        ],
-        out_specs=pl.BlockSpec((pairs, step, 2, rows, size), lambda i: (0, i, 0, 0, 0)),
-        out_shape=result_shape,
-        compiler_params=params(16),
-        cost_estimate=cost(flops, moved),
-    )(back, psi)
+    across = cat(across, 0) if chunks > 1 else across[0]
+    steps = own // step
     far = call(
-        far_kernel,
-        own // step,
-        [
-            back_block,
-            pl.BlockSpec((1, step, 2, rows, size), lambda i, m: (m[0] ^ 2, i, 0, 0, 0)),
-        ]
+        place_kernel,
+        steps,
+        [pl.BlockSpec((1, step, 2, rows, size), lambda i, m: (m[0] ^ 2, i, 0, 0, 0))]
         + [other_block] * 3,
-        result_block,
-        result_shape,
-        [pltpu.VMEM((step, 2, size, size), BF16)],
-        flops,
-        moved,
-    )(members, back, factors, beside, across, across_pair)
+        whole_block,
+        jax.ShapeDtypeStruct((own, 2, size, size), BF16),
+        [],
+        own,
+        own * 4 * 4 * size * size,
+    )(members, factors, beside, across, across_pair)
+
+    def products(column_panel, distance, factor_rows):
+        return call(
+            functools.partial(product_kernel, distance * own // 2),
+            steps,
+            [pl.BlockSpec((back.shape[0] // pairs, size), lambda i, m: (m[0], 0)), whole_block],
+            other_block,
+            jax.ShapeDtypeStruct((own, 2, rows, size), F32),
+            [],
+            own * 8 * size**3,
+            own * 4 * 4 * size * size,
+        )(column_panel.reshape(1), back, factor_rows)
 
     blocks = [None] * chan_size
-    for distance, result in ((0, near), (2, far)):
-        given = lax.dynamic_index_in_dim(result, 1 - pair, 0, keepdims=False)
-        blocks[distance] = lax.dynamic_index_in_dim(result, pair, 0, keepdims=False)
-        blocks[distance + 1] = swap(given.astype(jnp.float16), 1).astype(F32)
+    for distance, factor_rows in ((0, psi), (2, far)):
+        given = products(1 - pair, distance, factor_rows).astype(jnp.float16)
+        blocks[distance + 1] = swap(given, 1).astype(F32)
+    for distance, factor_rows in ((0, psi), (2, far)):
+        blocks[distance] = products(pair, distance, factor_rows)
     ordered = []
     for owner in range(chan_size):
         distance = member ^ owner

time: 142 us -> 145 us (1.021)
  starting transfers between devices: 31.2 us -> 34.5 us
  waiting for transfers between devices: 60.8 us -> 59.3 us
    ppermute x5 -> x6, waiting for transfers between devices: 8.41 us -> 29.7 us  [swap(): return lax.ppermute(value, 'side', SWAP)]
    all_to_all x1, waiting for transfers between devices: 21.4 us -> 3.96 us  [shards(): lax.all_to_all(causal, ('pair', 'freq'), 0, 0, tiled=True).astype(F32)]
    all_to_all x1, waiting for transfers between devices: 17.1 us -> 2.41 us  [shards(): gathered = lax.all_to_all(sent, chan + ('freq',), 0, 0, tiled=True)]
    ppermute x6, waiting for transfers between devices: 11.7 us -> 22.7 us  [swap(): return lax.ppermute(value, 'pair', SWAP)]
    ppermute x5 -> x6, starting transfers between devices: 6.86 us -> 12.4 us  [swap(): return lax.ppermute(value, 'side', SWAP)]
    ppermute x3, starting transfers between devices: 7.99 us -> 2.93 us  [swap(): return lax.ppermute(value, ('side', 'pair'), FLIP)]
    ppermute x6, starting transfers between devices: 6.55 us -> 10.6 us  [swap(): return lax.ppermute(value, 'pair', SWAP)]
    convert_element_type x5 -> x4, other arithmetic: 1.53 us -> 3.94 us  [the longest x2 1.57 us: shards(): given = products(1 - pair, distance, factor_rows).astype(jnp.float16)]
  transfers between devices with their start and end apart: 16 -> 17, of which waited for: 9 -> 12; matrix products, arithmetic and copies ran while one was open for 9% -> 7% of each run, Pallas kernels for 11% -> 18%
where the time goes in v4:
time: 145 us; the launch traced here: 144 us
  waiting for transfers between devices  59.3 us (41%)
  starting transfers between devices  34.5 us (24%)
  Pallas kernels  27.3 us (19%)
  other arithmetic  18.1 us (12%)
  local copies, waits for them, and re-layouts  4.28 us (3%)
    ppermute x6, waiting for transfers between devices, swap(): return lax.ppermute(value, 'side', SWAP)  29.7 us
    ppermute x6, waiting for transfers between devices, swap(): return lax.ppermute(value, 'pair', SWAP)  22.7 us
    pallas_call x2, Pallas kernels, shards(): call(newton_kernel, part // step, [pl.BlockSpec(memory_space=pltpu.SMEM),...  13.6 us
    ppermute x6, starting transfers between devices, swap(): return lax.ppermute(value, 'side', SWAP)  12.4 us
    ppermute x6, starting transfers between devices, swap(): return lax.ppermute(value, 'pair', SWAP)  10.6 us
    select_n x1, other arithmetic, projection_table(): jnp.where(shift == 0, 0.0, (jnp.cos(half_angle) - jnp.cos(last_angle)) /...  8.23 us
    pallas_call x4, Pallas kernels, products(): call(functools.partial(product_kernel, distance * own // 2), steps, [pl.B...  4.69 us
    pallas_call x1, Pallas kernels, shards(): pl.pallas_call(causal_kernel, grid=(kept,), in_specs=[table_block, table_...  4.54 us
  transfers between devices with their start and end apart: 17, of which 12 were waited for; matrix products, arithmetic and copies ran while one was open for 7% of the time, Pallas kernels for 18%

profile of v4, /device:TPU:0, one launch (start us, length us, event | category | flops | bytes accessed | tf_op | source)
XLA Modules:
  0.0 144.4 jit_solution(2013072208671653529)
XLA Ops:
  0.0 2.3 %dynamic-slice_bitcast_fusion.1 = (bf16[8,2,32,128]{3,2,1,0:T(8,128)(2,1)}, bf16[8,2,32,128]{3,2,1,0:T(8,128)(2,1)}, bf16[8,2,32,128]{3,2,1,0:T(8,128)(2,1)}, bf...) fusion(bf16[4,16,2,32,128]{4,3,2,1,0:T(8,128)(2,1)} %bitcast.42, ...), kind=kLoop, calls=%fused_computation.41 | loop fusion | bytes 2097168 | tf_op jit(solution)/shard_map/reshape | solution.py:311
  2.3 3.1 %collective-permute-start = (bf16[8,2,32,128]{3,2,1,0:T(8,128)(2,1)}, bf16[8,2,32,128]{3,2,1,0:T(8,128)(2,1)S(1)}, u32[]{:S(2)}, u32[]{:S(2)}) collective-permute-start(bf16[8,2,32,128]{3,2,1,0:T(8,128)(2,1)} %get-tuple-element.47), channel_id=1, source_target_pairs={{0,1},{1,0},{2,3},{3,2},{4,5},{5,4},{6,7},{7,6},{8,9},{9,8},{10,11... | collective-permute-start | bytes 393224 | tf_op jit(solution)/shard_map/ppermute | solution.py:209
  5.4 2.6 %collective-permute-start.1 = (bf16[8,2,32,128]{3,2,1,0:T(8,128)(2,1)}, bf16[8,2,32,128]{3,2,1,0:T(8,128)(2,1)S(1)}, u32[]{:S(2)}, u32[]{:S(2)}) collective-permute-start(bf16[8,2,32,128]{3,2,1,0:T(8,128)(2,1)} %get-tuple-element.46), channel_id=1, source_target_pairs={{0,2},{2,0},{1,3},{3,1},{4,6},{6,4},{5,7},{7,5},{8,10},{10,8},{9,1... | collective-permute-start | bytes 393224 | tf_op jit(solution)/shard_map/ppermute | solution.py:211
  8.0 0.0 collective-permute-start.2
  8.0 0.1 iota_compare_fusion
  8.1 0.1 fusion.49
  8.2 0.1 bitcast_select_fusion.own_ref
  8.3 0.1 fusion.50
  8.4 2.3 %collective-permute-done.one_ref = bf16[8,2,32,128]{3,2,1,0:T(8,128)(2,1)S(1)} collective-permute-done((bf16[8,2,32,128]{3,2,1,0:T(8,128)(2,1)}, bf16[8,2,32,128]{3,2,1,0:T(8,128)(2,1)S(1)}, u32[]{:S(2)}, u32[]{:S(2)}) %collective-permute-start) | collective-permute-done | bytes 131104 | tf_op jit(solution)/shard_map/ppermute | solution.py:209
  10.6 7.9 %collective-permute-done.1.two_ref = bf16[8,2,32,128]{3,2,1,0:T(8,128)(2,1)S(1)} collective-permute-done((bf16[8,2,32,128]{3,2,1,0:T(8,128)(2,1)}, bf16[8,2,32,128]{3,2,1,0:T(8,128)(2,1)S(1)}, u32[]{:S(2)}, u32[]{:S(2)}) %collective-permute-start.1) | collective-permute-done | bytes 131104 | tf_op jit(solution)/shard_map/ppermute | solution.py:211
  18.5 0.0 collective-permute-done.2.three_ref
  18.5 2.0 %collective-permute-start.3 = (bf16[8,2,32,128]{3,2,1,0:T(8,128)(2,1)S(1)}, bf16[8,2,32,128]{3,2,1,0:T(8,128)(2,1)S(1)}, u32[]{:S(2)}, u32[]{:S(2)}) collective-permute-start(bf16[8,2,32,128]{3,2,1,0:T(8,128)(2,1)S(1)} %copy-done.11), channel_id=1, source_target_pairs={{0,1},{1,0},{2,3},{3,2},{4,5},{5,4},{6,7},{7,6},{8,9},{9,8},{10,11... | collective-permute-start | bytes 393224 | tf_op jit(solution)/shard_map/ppermute | solution.py:209
  20.5 0.0 copy-done.10
  20.5 1.1 collective-permute-start.4
  21.6 1.5 %collective-permute-start.5 = (bf16[8,2,32,128]{3,2,1,0:T(8,128)(2,1)S(1)}, bf16[8,2,32,128]{3,2,1,0:T(8,128)(2,1)S(1)}, u32[]{:S(2)}, u32[]{:S(2)}) collective-permute-start(bf16[8,2,32,128]{3,2,1,0:T(8,128)(2,1)S(1)} %copy-done.9), channel_id=1, source_target_pairs={{0,3},{1,2},{2,1},{3,0},{4,7},{5,6},{6,5},{7,4},{8,11},{9,10},{10,... | collective-permute-start | bytes 393224 | tf_op jit(solution)/shard_map/ppermute | solution.py:212
  23.1 6.8 %shard_map.46 = (bf16[16,2,128,256]{3,2,1,0:T(8,128)(2,1)S(1)}, bf16[16,2,128,128]{3,2,1,0:T(8,128)(2,1)S(1)}) custom-call(s32[1]{0:T(128)} %bitcast.3.member_ref, f32[8]{0:T(128)S(1)} %get-tuple-element.58.scale_ref, bf16[4,16,2,32,128]{4,3,2,1,0:T(8,128)(2,1)S(1)} %bitcast.43, bf16[8,2,32,128]{3,2,1,0:T(8,128)(2,1)S(1)} %collective-permute-done.one_ref, ...), custom_call_target="tpu_custom_call" | custom-call | flops 8589934592 | bytes 3145728 | tf_op jit(solution)/shard_map/pallas_call | solution.py:283
  29.9 0.0 collective-permute-done.3.one_ref
  29.9 2.3 %collective-permute-done.4.two_ref = bf16[8,2,32,128]{3,2,1,0:T(8,128)(2,1)S(1)} collective-permute-done((bf16[8,2,32,128]{3,2,1,0:T(8,128)(2,1)S(1)}, bf16[8,2,32,128]{3,2,1,0:T(8,128)(2,1)S(1)}, u32[]{:S(2)}, u32[]{:S(2)}) %collective-permute-start.4) | collective-permute-done | bytes 131104 | tf_op jit(solution)/shard_map/ppermute | solution.py:211
  32.3 0.0 collective-permute-done.5.three_ref
  32.3 2.0 %collective-permute-start.6 = (bf16[16,32,128]{2,1,0:T(8,128)(2,1)S(1)}, bf16[16,32,128]{2,1,0:T(8,128)(2,1)S(1)}, u32[]{:S(2)}, u32[]{:S(2)}) collective-permute-start(bf16[16,32,128]{2,1,0:T(8,128)(2,1)S(1)} %get-tuple-element.28), channel_id=1, source_target_pairs={{0,1},{1,0},{2,3},{3,2},{4,5},{5,4},{6,7},{7,6},{8,9},{9,8},{10,11... | collective-permute-start | bytes 393224 | tf_op jit(solution)/shard_map/ppermute | solution.py:209
  34.2 1.0 collective-permute-start.7
  35.2 1.5 %collective-permute-start.8 = (bf16[16,32,128]{2,1,0:T(8,128)(2,1)S(1)}, bf16[16,32,128]{2,1,0:T(8,128)(2,1)S(1)}, u32[]{:S(2)}, u32[]{:S(2)}) collective-permute-start(bf16[16,32,128]{2,1,0:T(8,128)(2,1)S(1)} %get-tuple-element.30), channel_id=1, source_target_pairs={{0,3},{1,2},{2,1},{3,0},{4,7},{5,6},{6,5},{7,4},{8,11},{9,10},{10,... | collective-permute-start | bytes 393224 | tf_op jit(solution)/shard_map/ppermute | solution.py:212
  36.7 6.8 %shard_map.47 = (bf16[16,2,128,256]{3,2,1,0:T(8,128)(2,1)S(1)}, bf16[16,2,128,128]{3,2,1,0:T(8,128)(2,1)S(1)}) custom-call(s32[1]{0:T(128)} %bitcast.3.member_ref, f32[8]{0:T(128)S(1)} %get-tuple-element.59.scale_ref, bf16[4,16,2,32,128]{4,3,2,1,0:T(8,128)(2,1)S(1)} %bitcast.44, ...), custom_call_target="tpu_custom_call", output_to_operand_aliasing={{0}: (6, {}), {1}: (7, {})} | custom-call | flops 8589934592 | bytes 3145728 | tf_op jit(solution)/shard_map/pallas_call | solution.py:283
  43.5 0.0 copy-done.4
  43.5 0.0 copy-start.1
  43.5 1.0 copy-done.1
  44.5 0.4 collective-permute-done.8.three_ref
  44.9 0.0 copy-done.8
  44.9 4.5 %collective-permute-start.9 = (bf16[8,2,32,128]{3,2,1,0:T(8,128)(2,1)S(1)}, bf16[8,2,32,128]{3,2,1,0:T(8,128)(2,1)S(1)}, u32[]{:S(2)}, u32[]{:S(2)}) collective-permute-start(bf16[8,2,32,128]{3,2,1,0:T(8,128)(2,1)S(1)} %copy-done.8), channel_id=1, source_target_pairs={{0,2},{2,0},{1,3},{3,1},{4,6},{6,4},{5,7},{7,5},{8,10},{10,8},{9,1... | collective-permute-start | bytes 393224 | tf_op jit(solution)/shard_map/ppermute | solution.py:211
  49.5 0.0 collective-permute-done.6.one_ref
  49.5 0.0 collective-permute-done.7.two_ref
  49.5 4.3 %shard_map.48 = f32[4096,128]{1,0:T(8,128)S(1)} custom-call(s32[1]{0:T(128)} %bitcast.3.member_ref, bf16[16,2,128,256]{3,2,1,0:T(8,128)(2,1)S(1)} %get-tuple-element.27.inverse_ref, bf16[4,16,32,128]{3,2,1,0:T(8,128)(2,1)S(1)} %bitcast_select_fusion.own_ref, bf16[16,32,128]{2,1,0:T(8,128)(2,1)S(1)} %collective-permute-done.6.one_ref, ...), custom_call_target="tpu_custom_call" | custom-call | flops 10737418240 | bytes 6291456 | tf_op jit(solution)/shard_map/pallas_call | solution.py:315
  53.8 1.1 collective-permute-done.9
  54.9 1.1 convert_element_type.35
  56.0 4.0 %all-to-all-start = ((f16[32,4,2,16,128]{4,3,2,1,0:T(8,128)(2,1)}), f16[32,4,2,16,128]{4,3,2,1,0:T(8,128)(2,1)}, u32[]{:S(2)}, u32[]{:S(2)}) async-start(f16[32,4,2,16,128]{4,3,2,1,0:T(8,128)(2,1)} %bitcast.17), calls=%async_computation | async-start | bytes 2097152 | tf_op jit(solution)/shard_map/all_to_all | solution.py:330
  60.8 1.6 %collective-permute-start.10 = (bf16[16,2,32,128]{3,2,1,0:T(8,128)(2,1)S(1)}, bf16[16,2,32,128]{3,2,1,0:T(8,128)(2,1)S(1)}, u32[]{:S(2)}, u32[]{:S(2)}) collective-permute-start(bf16[16,2,32,128]{3,2,1,0:T(8,128)(2,1)S(1)} %dynamic-slice_bitcast_fusion), channel_id=1, source_target_pairs={{0,1},{1,0},{2,3},{3,2},{4,5},{5,4},{6,7},{7,6},{8,9},{9,8},{10,11... | collective-permute-start | bytes 786440 | tf_op jit(solution)/shard_map/ppermute | solution.py:209
  62.4 8.2 %fusion.4 = (f32[512,512]{1,0:T(8,128)S(1)}, f32[512,512]{1,0:T(8,128)S(1)}) fusion(s32[512]{0:T(512)S(1)} %get-tuple-element.61, s32[512]{0:T(512)S(1)} %get-tuple-element.60, s32[]{:T(128)} %bitcast.2, f32[]{:T(128)} %bitcast.1), kind=kLoop, calls=%fused_computation.11 | loop fusion | flops 7340032 | bytes 2101256 | tf_op jit(solution)/shard_map/jit(_where)/select_n | solution.py:187
  70.6 13.1 %collective-permute-done.10.one_ref = bf16[16,2,32,128]{3,2,1,0:T(8,128)(2,1)S(1)} collective-permute-done((bf16[16,2,32,128]{3,2,1,0:T(8,128)(2,1)S(1)}, bf16[16,2,32,128]{3,2,1,0:T(8,128)(2,1)S(1)}, u32[]{:S(2)}, u32[]{:S(2)}) %collective-permute-start.10) | collective-permute-done | bytes 262176 | tf_op jit(solution)/shard_map/ppermute | solution.py:209
  83.7 2.4 %all-to-all-done = f16[32,4,2,16,128]{4,3,2,1,0:T(8,128)(2,1)} async-done(((f16[32,4,2,16,128]{4,3,2,1,0:T(8,128)(2,1)}), f16[32,4,2,16,128]{4,3,2,1,0:T(8,128)(2,1)}, u32[]{:S(2)}, u32[]{:S(2)}) %all-to-all-start) | async-done | bytes 1048608 | tf_op jit(solution)/shard_map/all_to_all | solution.py:330
  86.1 1.5 %convert_element_type.36.values_ref = f32[32,4,2,16,128]{4,3,2,1,0:T(8,128)S(1)} convert(f16[32,4,2,16,128]{4,3,2,1,0:T(8,128)(2,1)} %all-to-all-done) | non-fusion elementwise | flops 524288 | bytes 3145728 | tf_op jit(solution)/shard_map/convert_element_type | solution.py:338
  87.7 1.5 %collective-permute-start.11 = (bf16[8,2,32,128]{3,2,1,0:T(8,128)(2,1)S(1)}, bf16[8,2,32,128]{3,2,1,0:T(8,128)(2,1)S(1)}, u32[]{:S(2)}, u32[]{:S(2)}) collective-permute-start(bf16[8,2,32,128]{3,2,1,0:T(8,128)(2,1)S(1)} %copy-done.7), channel_id=1, source_target_pairs={{0,2},{2,0},{1,3},{3,1},{4,6},{6,4},{5,7},{7,5},{8,10},{10,8},{9,1... | collective-permute-start | bytes 393224 | tf_op jit(solution)/shard_map/ppermute | solution.py:211
  89.1 4.5 %shard_map.49 = f32[16,4,2,32,128]{4,3,2,1,0:T(8,128)S(1)} custom-call(f32[512,512]{1,0:T(8,128)S(1)} %get-tuple-element.57.real_ref, f32[512,512]{1,0:T(8,128)S(1)} %get-tuple-element.56.imag_ref, f32[32,4,2,16,128]{4,3,2,1,0:T(8,128)S(1)} %convert_element_type.36.values_ref), custom_call_target="tpu_custom_call" | custom-call | flops 12884901888 | bytes 4194304 | tf_op jit(solution)/shard_map/pallas_call | solution.py:347
  93.7 2.5 %collective-permute-done.11 = bf16[8,2,32,128]{3,2,1,0:T(8,128)(2,1)S(1)} collective-permute-done((bf16[8,2,32,128]{3,2,1,0:T(8,128)(2,1)S(1)}, bf16[8,2,32,128]{3,2,1,0:T(8,128)(2,1)S(1)}, u32[]{:S(2)}, u32[]{:S(2)}) %collective-permute-start.11) | collective-permute-done | bytes 131104 | tf_op jit(solution)/shard_map/ppermute | solution.py:211
  96.2 0.6 copy-done.14
  96.8 1.3 convert_element_type.37
  98.1 4.5 %all-to-all-start.1 = ((f16[16,4,2,32,128]{4,3,2,1,0:T(8,128)(2,1)}), f16[16,4,2,32,128]{4,3,2,1,0:T(8,128)(2,1)}, u32[]{:S(2)}, u32[]{:S(2)}) async-start(f16[16,4,2,32,128]{4,3,2,1,0:T(8,128)(2,1)} %convert_element_type.37), calls=%async_computation.1 | async-start | bytes 2097152 | tf_op jit(solution)/shard_map/all_to_all | solution.py:365
  102.6 1.7 %collective-permute-start.13 = (bf16[16,2,32,128]{3,2,1,0:T(8,128)(2,1)S(1)}, bf16[16,2,32,128]{3,2,1,0:T(8,128)(2,1)S(1)}, u32[]{:S(2)}, u32[]{:S(2)}) collective-permute-start(bf16[16,2,32,128]{3,2,1,0:T(8,128)(2,1)S(1)} %pad_maximum_fusion.1), channel_id=1, source_target_pairs={{0,2},{2,0},{1,3},{3,1},{4,6},{6,4},{5,7},{7,5},{8,10},{10,8},{9,1... | collective-permute-start | bytes 786440 | tf_op jit(solution)/shard_map/ppermute | solution.py:211
  104.4 15.9 %collective-permute-done.13.three_ref = bf16[16,2,32,128]{3,2,1,0:T(8,128)(2,1)S(1)} collective-permute-done((bf16[16,2,32,128]{3,2,1,0:T(8,128)(2,1)S(1)}, bf16[16,2,32,128]{3,2,1,0:T(8,128)(2,1)S(1)}, u32[]{:S(2)}, u32[]{:S(2)}) %collective-permute-start.13) | collective-permute-done | bytes 262176 | tf_op jit(solution)/shard_map/ppermute | solution.py:211
  120.2 0.1 shard_map.52.psi_ref
  120.4 4.0 %all-to-all-done.1 = f16[16,4,2,32,128]{4,3,2,1,0:T(8,128)(2,1)} async-done(((f16[16,4,2,32,128]{4,3,2,1,0:T(8,128)(2,1)}), f16[16,4,2,32,128]{4,3,2,1,0:T(8,128)(2,1)}, u32[]{:S(2)}, u32[]{:S(2)}) %all-to-all-start.1) | async-done | bytes 1048608 | tf_op jit(solution)/shard_map/all_to_all | solution.py:365
  124.4 1.4 bitcast_convert_fusion.causal_ref
  125.7 1.2 shard_map.54
  126.9 0.8 convert_element_type.40
  127.7 0.0 collective-permute-start.14
  127.7 1.2 shard_map.51
  128.9 0.8 convert_element_type.38
  129.7 2.0 %collective-permute-start.12 = (f16[16,2,32,128]{3,2,1,0:T(8,128)(2,1)}, f16[16,2,32,128]{3,2,1,0:T(8,128)(2,1)}, u32[]{:S(2)}, u32[]{:S(2)}) collective-permute-start(f16[16,2,32,128]{3,2,1,0:T(8,128)(2,1)} %convert_element_type.38), channel_id=1, source_target_pairs={{0,1},{1,0},{2,3},{3,2},{4,5},{5,4},{6,7},{7,6},{8,9},{9,8},{10,11... | collective-permute-start | bytes 786440 | tf_op jit(solution)/shard_map/ppermute | solution.py:209
  131.7 1.2 shard_map.53
  132.9 0.1 copy-done.3
  132.9 1.2 shard_map.50
  134.1 3.1 %collective-permute-done.14 = f16[16,2,32,128]{3,2,1,0:T(8,128)(2,1)S(1)} collective-permute-done((f16[16,2,32,128]{3,2,1,0:T(8,128)(2,1)}, f16[16,2,32,128]{3,2,1,0:T(8,128)(2,1)S(1)}, u32[]{:S(2)}, u32[]{:S(2)}) %collective-permute-start.14) | collective-permute-done | bytes 262176 | tf_op jit(solution)/shard_map/ppermute | solution.py:209
  137.1 4.4 %collective-permute-done.12 = f16[16,2,32,128]{3,2,1,0:T(8,128)(2,1)} collective-permute-done((f16[16,2,32,128]{3,2,1,0:T(8,128)(2,1)}, f16[16,2,32,128]{3,2,1,0:T(8,128)(2,1)}, u32[]{:S(2)}, u32[]{:S(2)}) %collective-permute-start.12) | collective-permute-done | bytes 262176 | tf_op jit(solution)/shard_map/ppermute | solution.py:209
  141.5 1.3 fusion.17
  142.8 1.6 %fusion = f32[64,2,128,32]{2,3,1,0:T(8,128)} fusion(f32[16,2,32,128]{3,2,1,0:T(8,128)S(1)} %get-tuple-element.40, f32[16,2,32,128]{3,2,1,0:T(8,128)S(1)} %get-tuple-element.41, f32[16,2,32,128]{3,2,1,0:T(8,128)S(1)} %get-tuple-element.42, f32[16,2,32,128]{3,2,1,0:T(8,128)S(1)} %get-tuple-element.39), kind=kLoop, calls=%fused_computation.2 | loop fusion | flops 2097152 | bytes 4194304 | tf_op jit(solution)/shard_map/transpose | solution.py:410
  (33 shorter events, 0.2 us)
Async XLA Ops:
  0.0 8.1 %copy-start.6 = (bf16[64,2,32,128]{3,2,1,0:T(8,128)(2,1)S(1)}, bf16[64,2,32,128]{3,2,1,0:T(8,128)(2,1)}, u32[]{:S(2)}) copy-start(bf16[64,2,32,128]{3,2,1,0:T(8,128)(2,1)} %param.5) | copy-start | bytes 3145732
  2.3 5.9 %copy-start.16 = (f32[64]{0:T(128)S(1)}, f32[64]{0:T(128)}, u32[]{:S(2)}) copy-start(f32[64]{0:T(128)} %param.6) | copy-start | bytes 772
  2.3 8.3 %collective-permute-start = (bf16[8,2,32,128]{3,2,1,0:T(8,128)(2,1)}, bf16[8,2,32,128]{3,2,1,0:T(8,128)(2,1)S(1)}, u32[]{:S(2)}, u32[]{:S(2)}) collective-permute-start(bf16[8,2,32,128]{3,2,1,0:T(8,128)(2,1)} %get-tuple-element.47), channel_id=1, source_target_pairs={{0,1},{1,0},{2,3},{3,2},{4,5},{5,4},{6,7},{7,6},{8,9},{9,8},{10,11... | collective-permute-start | bytes 393224 | tf_op jit(solution)/shard_map/ppermute | solution.py:209
  5.4 13.1 %collective-permute-start.1 = (bf16[8,2,32,128]{3,2,1,0:T(8,128)(2,1)}, bf16[8,2,32,128]{3,2,1,0:T(8,128)(2,1)S(1)}, u32[]{:S(2)}, u32[]{:S(2)}) collective-permute-start(bf16[8,2,32,128]{3,2,1,0:T(8,128)(2,1)} %get-tuple-element.46), channel_id=1, source_target_pairs={{0,2},{2,0},{1,3},{3,1},{4,6},{6,4},{5,7},{7,5},{8,10},{10,8},{9,1... | collective-permute-start | bytes 393224 | tf_op jit(solution)/shard_map/ppermute | solution.py:211
  8.0 10.6 %collective-permute-start.2 = (bf16[8,2,32,128]{3,2,1,0:T(8,128)(2,1)}, bf16[8,2,32,128]{3,2,1,0:T(8,128)(2,1)S(1)}, u32[]{:S(2)}, u32[]{:S(2)}) collective-permute-start(bf16[8,2,32,128]{3,2,1,0:T(8,128)(2,1)} %get-tuple-element.45), channel_id=1, source_target_pairs={{0,3},{1,2},{2,1},{3,0},{4,7},{5,6},{6,5},{7,4},{8,11},{9,10},{10,... | collective-permute-start | bytes 393224 | tf_op jit(solution)/shard_map/ppermute | solution.py:212
  8.1 15.0 %copy-start = (bf16[64,2,32,128]{3,2,1,0:T(8,128)(2,1)S(1)}, bf16[64,2,32,128]{3,2,1,0:T(8,128)(2,1)}, u32[]{:S(2)}) copy-start(bf16[64,2,32,128]{3,2,1,0:T(8,128)(2,1)} %param.4) | copy-start | bytes 3145732
  8.2 10.4 %copy-start.11 = (bf16[8,2,32,128]{3,2,1,0:T(8,128)(2,1)S(1)}, bf16[8,2,32,128]{3,2,1,0:T(8,128)(2,1)}, u32[]{:S(2)}) copy-start(bf16[8,2,32,128]{3,2,1,0:T(8,128)(2,1)} %get-tuple-element.22) | copy-start | bytes 393220
  8.2 12.3 %copy-start.10 = (bf16[8,2,32,128]{3,2,1,0:T(8,128)(2,1)S(1)}, bf16[8,2,32,128]{3,2,1,0:T(8,128)(2,1)}, u32[]{:S(2)}) copy-start(bf16[8,2,32,128]{3,2,1,0:T(8,128)(2,1)} %get-tuple-element.23) | copy-start | bytes 393220
  8.2 13.4 %copy-start.9 = (bf16[8,2,32,128]{3,2,1,0:T(8,128)(2,1)S(1)}, bf16[8,2,32,128]{3,2,1,0:T(8,128)(2,1)}, u32[]{:S(2)}) copy-start(bf16[8,2,32,128]{3,2,1,0:T(8,128)(2,1)} %get-tuple-element.24) | copy-start | bytes 393220
  18.5 11.4 %collective-permute-start.3 = (bf16[8,2,32,128]{3,2,1,0:T(8,128)(2,1)S(1)}, bf16[8,2,32,128]{3,2,1,0:T(8,128)(2,1)S(1)}, u32[]{:S(2)}, u32[]{:S(2)}) collective-permute-start(bf16[8,2,32,128]{3,2,1,0:T(8,128)(2,1)S(1)} %copy-done.11), channel_id=1, source_target_pairs={{0,1},{1,0},{2,3},{3,2},{4,5},{5,4},{6,7},{7,6},{8,9},{9,8},{10,11... | collective-permute-start | bytes 393224 | tf_op jit(solution)/shard_map/ppermute | solution.py:209
  20.5 11.7 %collective-permute-start.4 = (bf16[8,2,32,128]{3,2,1,0:T(8,128)(2,1)S(1)}, bf16[8,2,32,128]{3,2,1,0:T(8,128)(2,1)S(1)}, u32[]{:S(2)}, u32[]{:S(2)}) collective-permute-start(bf16[8,2,32,128]{3,2,1,0:T(8,128)(2,1)S(1)} %copy-done.10), channel_id=1, source_target_pairs={{0,2},{2,0},{1,3},{3,1},{4,6},{6,4},{5,7},{7,5},{8,10},{10,8},{9,1... | collective-permute-start | bytes 393224 | tf_op jit(solution)/shard_map/ppermute | solution.py:211
  21.6 10.7 %collective-permute-start.5 = (bf16[8,2,32,128]{3,2,1,0:T(8,128)(2,1)S(1)}, bf16[8,2,32,128]{3,2,1,0:T(8,128)(2,1)S(1)}, u32[]{:S(2)}, u32[]{:S(2)}) collective-permute-start(bf16[8,2,32,128]{3,2,1,0:T(8,128)(2,1)S(1)} %copy-done.9), channel_id=1, source_target_pairs={{0,3},{1,2},{2,1},{3,0},{4,7},{5,6},{6,5},{7,4},{8,11},{9,10},{10,... | collective-permute-start | bytes 393224 | tf_op jit(solution)/shard_map/ppermute | solution.py:212
  29.9 13.6 %copy-start.4 = (bf16[8,2,32,128]{3,2,1,0:T(8,128)(2,1)}, bf16[8,2,32,128]{3,2,1,0:T(8,128)(2,1)S(1)}, u32[]{:S(2)}) copy-start(bf16[8,2,32,128]{3,2,1,0:T(8,128)(2,1)S(1)} %collective-permute-done.3.one_ref) | copy-start | bytes 393220
  32.3 17.2 %collective-permute-start.6 = (bf16[16,32,128]{2,1,0:T(8,128)(2,1)S(1)}, bf16[16,32,128]{2,1,0:T(8,128)(2,1)S(1)}, u32[]{:S(2)}, u32[]{:S(2)}) collective-permute-start(bf16[16,32,128]{2,1,0:T(8,128)(2,1)S(1)} %get-tuple-element.28), channel_id=1, source_target_pairs={{0,1},{1,0},{2,3},{3,2},{4,5},{5,4},{6,7},{7,6},{8,9},{9,8},{10,11... | collective-permute-start | bytes 393224 | tf_op jit(solution)/shard_map/ppermute | solution.py:209
  34.2 15.2 %collective-permute-start.7 = (bf16[16,32,128]{2,1,0:T(8,128)(2,1)S(1)}, bf16[16,32,128]{2,1,0:T(8,128)(2,1)S(1)}, u32[]{:S(2)}, u32[]{:S(2)}) collective-permute-start(bf16[16,32,128]{2,1,0:T(8,128)(2,1)S(1)} %get-tuple-element.29), channel_id=1, source_target_pairs={{0,2},{2,0},{1,3},{3,1},{4,6},{6,4},{5,7},{7,5},{8,10},{10,8},{9,1... | collective-permute-start | bytes 393224 | tf_op jit(solution)/shard_map/ppermute | solution.py:211
  35.2 9.7 %collective-permute-start.8 = (bf16[16,32,128]{2,1,0:T(8,128)(2,1)S(1)}, bf16[16,32,128]{2,1,0:T(8,128)(2,1)S(1)}, u32[]{:S(2)}, u32[]{:S(2)}) collective-permute-start(bf16[16,32,128]{2,1,0:T(8,128)(2,1)S(1)} %get-tuple-element.30), channel_id=1, source_target_pairs={{0,3},{1,2},{2,1},{3,0},{4,7},{5,6},{6,5},{7,4},{8,11},{9,10},{10,... | collective-permute-start | bytes 393224 | tf_op jit(solution)/shard_map/ppermute | solution.py:212
  36.7 8.3 %copy-start.8 = (bf16[8,2,32,128]{3,2,1,0:T(8,128)(2,1)S(1)}, bf16[8,2,32,128]{3,2,1,0:T(8,128)(2,1)}, u32[]{:S(2)}) copy-start(bf16[8,2,32,128]{3,2,1,0:T(8,128)(2,1)} %get-tuple-element.31) | copy-start | bytes 393220
  43.5 1.0 copy-start.1
  44.9 10.0 %collective-permute-start.9 = (bf16[8,2,32,128]{3,2,1,0:T(8,128)(2,1)S(1)}, bf16[8,2,32,128]{3,2,1,0:T(8,128)(2,1)S(1)}, u32[]{:S(2)}, u32[]{:S(2)}) collective-permute-start(bf16[8,2,32,128]{3,2,1,0:T(8,128)(2,1)S(1)} %copy-done.8), channel_id=1, source_target_pairs={{0,2},{2,0},{1,3},{3,1},{4,6},{6,4},{5,7},{7,5},{8,10},{10,8},{9,1... | collective-permute-start | bytes 393224 | tf_op jit(solution)/shard_map/ppermute | solution.py:211
  54.9 1.1 copy-start.12
  56.0 30.1 %all-to-all-start = ((f16[32,4,2,16,128]{4,3,2,1,0:T(8,128)(2,1)}), f16[32,4,2,16,128]{4,3,2,1,0:T(8,128)(2,1)}, u32[]{:S(2)}, u32[]{:S(2)}) async-start(f16[32,4,2,16,128]{4,3,2,1,0:T(8,128)(2,1)} %bitcast.17), calls=%async_computation | async-start | bytes 2097152 | tf_op jit(solution)/shard_map/all_to_all | solution.py:330
  60.8 22.9 %collective-permute-start.10 = (bf16[16,2,32,128]{3,2,1,0:T(8,128)(2,1)S(1)}, bf16[16,2,32,128]{3,2,1,0:T(8,128)(2,1)S(1)}, u32[]{:S(2)}, u32[]{:S(2)}) collective-permute-start(bf16[16,2,32,128]{3,2,1,0:T(8,128)(2,1)S(1)} %dynamic-slice_bitcast_fusion), channel_id=1, source_target_pairs={{0,1},{1,0},{2,3},{3,2},{4,5},{5,4},{6,7},{7,6},{8,9},{9,8},{10,11... | collective-permute-start | bytes 786440 | tf_op jit(solution)/shard_map/ppermute | solution.py:209
  86.1 1.5 %copy-start.7 = (bf16[8,2,32,128]{3,2,1,0:T(8,128)(2,1)S(1)}, bf16[8,2,32,128]{3,2,1,0:T(8,128)(2,1)}, u32[]{:S(2)}) copy-start(bf16[8,2,32,128]{3,2,1,0:T(8,128)(2,1)} %get-tuple-element.35) | copy-start | bytes 393220
  87.7 8.5 %collective-permute-start.11 = (bf16[8,2,32,128]{3,2,1,0:T(8,128)(2,1)S(1)}, bf16[8,2,32,128]{3,2,1,0:T(8,128)(2,1)S(1)}, u32[]{:S(2)}, u32[]{:S(2)}) collective-permute-start(bf16[8,2,32,128]{3,2,1,0:T(8,128)(2,1)S(1)} %copy-done.7), channel_id=1, source_target_pairs={{0,2},{2,0},{1,3},{3,1},{4,6},{6,4},{5,7},{7,5},{8,10},{10,8},{9,1... | collective-permute-start | bytes 393224 | tf_op jit(solution)/shard_map/ppermute | solution.py:211
  93.7 8.9 %copy-start.5 = (bf16[8,2,32,128]{3,2,1,0:T(8,128)(2,1)S(1)}, bf16[8,2,32,128]{3,2,1,0:T(8,128)(2,1)}, u32[]{:S(2)}) copy-start(bf16[8,2,32,128]{3,2,1,0:T(8,128)(2,1)} %copy-done.4) | copy-start | bytes 393220
  96.2 0.6 copy-start.14
  98.1 6.3 %copy-start.13 = (bf16[8,2,32,128]{3,2,1,0:T(8,128)(2,1)S(1)}, bf16[8,2,32,128]{3,2,1,0:T(8,128)(2,1)}, u32[]{:S(2)}) copy-start(bf16[8,2,32,128]{3,2,1,0:T(8,128)(2,1)} %copy-done.12) | copy-start | bytes 393220
  98.1 6.3 %copy-start.15 = (bf16[8,2,32,128]{3,2,1,0:T(8,128)(2,1)S(1)}, bf16[8,2,32,128]{3,2,1,0:T(8,128)(2,1)}, u32[]{:S(2)}) copy-start(bf16[8,2,32,128]{3,2,1,0:T(8,128)(2,1)} %copy-done.14) | copy-start | bytes 393220
  98.1 26.3 %all-to-all-start.1 = ((f16[16,4,2,32,128]{4,3,2,1,0:T(8,128)(2,1)}), f16[16,4,2,32,128]{4,3,2,1,0:T(8,128)(2,1)}, u32[]{:S(2)}, u32[]{:S(2)}) async-start(f16[16,4,2,32,128]{4,3,2,1,0:T(8,128)(2,1)} %convert_element_type.37), calls=%async_computation.1 | async-start | bytes 2097152 | tf_op jit(solution)/shard_map/all_to_all | solution.py:365
  102.6 17.6 %collective-permute-start.13 = (bf16[16,2,32,128]{3,2,1,0:T(8,128)(2,1)S(1)}, bf16[16,2,32,128]{3,2,1,0:T(8,128)(2,1)S(1)}, u32[]{:S(2)}, u32[]{:S(2)}) collective-permute-start(bf16[16,2,32,128]{3,2,1,0:T(8,128)(2,1)S(1)} %pad_maximum_fusion.1), channel_id=1, source_target_pairs={{0,2},{2,0},{1,3},{3,1},{4,6},{6,4},{5,7},{7,5},{8,10},{10,8},{9,1... | collective-permute-start | bytes 786440 | tf_op jit(solution)/shard_map/ppermute | solution.py:211
  125.7 2.0 %copy-start.2 = (bf16[16,2,128,128]{3,2,1,0:T(8,128)(2,1)S(1)}, bf16[16,2,128,128]{3,2,1,0:T(8,128)(2,1)}, u32[]{:S(2)}) copy-start(bf16[16,2,128,128]{3,2,1,0:T(8,128)(2,1)} %copy-done.1) | copy-start | bytes 3145732
  127.7 9.4 %collective-permute-start.14 = (f16[16,2,32,128]{3,2,1,0:T(8,128)(2,1)}, f16[16,2,32,128]{3,2,1,0:T(8,128)(2,1)S(1)}, u32[]{:S(2)}, u32[]{:S(2)}) collective-permute-start(f16[16,2,32,128]{3,2,1,0:T(8,128)(2,1)} %convert_element_type.40), channel_id=1, source_target_pairs={{0,1},{1,0},{2,3},{3,2},{4,5},{5,4},{6,7},{7,6},{8,9},{9,8},{10,11... | collective-permute-start | bytes 786440 | tf_op jit(solution)/shard_map/ppermute | solution.py:209
  129.7 11.8 %collective-permute-start.12 = (f16[16,2,32,128]{3,2,1,0:T(8,128)(2,1)}, f16[16,2,32,128]{3,2,1,0:T(8,128)(2,1)}, u32[]{:S(2)}, u32[]{:S(2)}) collective-permute-start(f16[16,2,32,128]{3,2,1,0:T(8,128)(2,1)} %convert_element_type.38), channel_id=1, source_target_pairs={{0,1},{1,0},{2,3},{3,2},{4,5},{5,4},{6,7},{7,6},{8,9},{9,8},{10,11... | collective-permute-start | bytes 786440 | tf_op jit(solution)/shard_map/ppermute | solution.py:209
  131.7 1.2 copy-start.3

commit v5 on v3

--- a/solution.py
+++ b/solution.py
@@ -51,7 +51,8 @@
         out_ref[..., pl.ds(start, rows), :] = panel[...]
 
 
-def newton_kernel(member_ref, scale_ref, own_ref, one_ref, two_ref, three_ref, out_ref, psi_ref):
+def newton_kernel(member_ref, scale_ref, own_ref, one_ref, two_ref, three_ref, *refs):
+    out_ref, psi_ref = refs[-2:]
     bins, _, size, _ = psi_ref.shape
     place_rows(member_ref[0], [own_ref.at[0], one_ref, two_ref, three_ref], psi_ref)
     identity = eye(size)
@@ -160,13 +161,11 @@
         out_ref[:, item, 1] = result[:, size:].reshape(shape)
 
 
-def projection_table(lag_limit, count, freq_size, pairs, chunks):
+def projection_table(lag_limit, count, freq_size, pairs):
     own = count // (freq_size * 2 * pairs)
 
     def bins(index):
-        part = own // chunks
-        group, holder, inner = index // own % freq_size, index // (own * freq_size), index % own
-        return (group * chunks + inner // part) * (part * 2 * pairs) + holder * part + inner % part
+        return index // own % freq_size * (own * 2 * pairs) + index // (own * freq_size) * own + index % own
 
     row = lax.broadcasted_iota(jnp.int32, (count, 1), 0)
     column = lax.broadcasted_iota(jnp.int32, (1, count), 1)
@@ -206,7 +205,7 @@
     return lax.ppermute(value, ("side", "pair"), FLIP)
 
 
-def call(kernel, steps, in_specs, out_specs, out_shape, scratch, flops, moved):
+def call(kernel, steps, in_specs, out_specs, out_shape, scratch, flops, moved, aliases={}):
     return pl.pallas_call(
         kernel,
         grid_spec=pltpu.PrefetchScalarGridSpec(
@@ -217,6 +216,7 @@
             scratch_shapes=scratch,
         ),
         out_shape=out_shape,
+        input_output_aliases=aliases,
         compiler_params=params(16),
         cost_estimate=cost(flops, moved),
     )
@@ -241,82 +241,80 @@
     devices = chan_size * freq_size
     distances = range(1, chan_size)
 
-    factors = factor.reshape(chunks, chan_size, part, 2, rows, size)
+    factors = factor.reshape(chan_size, own, 2, rows, size)
+
+    def rows_for(owner, first, length):
+        return lax.dynamic_slice(
+            factors, (owner, first, 0, 0, 0), (1, length, 2, rows, size)
+        ).reshape(length, 2, rows, size)
 
     arrived = []
     for chunk in range(chunks):
-        pieces = [
-            lax.dynamic_index_in_dim(factors[chunk], member ^ d, 0, keepdims=False)
-            for d in distances
-        ]
+        pieces = [rows_for(member ^ d, chunk * part, part) for d in distances]
         if arrived:
             pieces = lax.optimization_barrier(tuple(pieces) + tuple(arrived[-1]))[: len(pieces)]
         arrived.append([swap(piece, d) for piece, d in zip(pieces, distances)])
     row_index = lax.broadcasted_iota(jnp.int32, (rows, size), 0) + member * rows
     column_index = lax.broadcasted_iota(jnp.int32, (rows, size), 1)
     packed = jnp.where(column_index >= row_index, spectrum[:, 0], spectrum[:, 1])
-    packed = packed.reshape(chunks, chan_size, part, rows, size)
-    pieces = [
-        lax.dynamic_index_in_dim(packed, member ^ d, 1, keepdims=False).reshape(own, rows, size)
-        for d in distances
-    ]
+    packed = packed.reshape(chan_size, own, rows, size)
+    pieces = [lax.dynamic_index_in_dim(packed, member ^ d, 0, keepdims=False) for d in distances]
     pieces = lax.optimization_barrier(tuple(pieces) + tuple(arrived[-1]))[: len(pieces)]
     packed_arrived = [swap(piece, d) for piece, d in zip(pieces, distances)]
-    table_re, table_im = projection_table(lag_cutoff[0], count, freq_size, pairs, chunks)
-
-    local_block = lambda chunk: pl.BlockSpec(
-        (pl.squeezed, 1, step, 2, rows, size), lambda i, m: (chunk, m[0], i, 0, 0, 0)
+    table_re, table_im = projection_table(lag_cutoff[0], count, freq_size, pairs)
+
+    local_block = lambda first: pl.BlockSpec(
+        (1, step, 2, rows, size), lambda i, m: (m[0], i + first, 0, 0, 0)
     )
     other_block = pl.BlockSpec((step, 2, rows, size), lambda i, m: (i, 0, 0, 0))
-    whole_block = pl.BlockSpec((step, 2, size, size), lambda i, m: (i, 0, 0, 0))
     inverse_block = pl.BlockSpec((step, 2, size, 2 * size), lambda i, m: (i, 0, 0, 0))
-    inverses, psis, middles = [], [], []
+    state = []
     for chunk in range(chunks):
-        scale = lax.dynamic_slice_in_dim(guess_scale, (chunk * chan_size + member) * part, part, 0)
-        inverse, psi = call(
+        scale = lax.dynamic_slice_in_dim(guess_scale, member * own + chunk * part, part, 0)
+        offset = chunk * part // step
+        state = call(
             newton_kernel,
             part // step,
-            [pl.BlockSpec(memory_space=pltpu.SMEM), local_block(chunk)] + [other_block] * 3,
-            [inverse_block, whole_block],
+            [pl.BlockSpec(memory_space=pltpu.SMEM), local_block(offset)]
+            + [other_block] * 3
+            + [pl.BlockSpec(memory_space=pl.ANY)] * len(state),
             [
-                jax.ShapeDtypeStruct((part, 2, size, 2 * size), BF16),
-                jax.ShapeDtypeStruct((part, 2, size, size), BF16),
+                pl.BlockSpec(
+                    (step, 2, size, 2 * size), lambda i, m, offset=offset: (i + offset, 0, 0, 0)
+                ),
+                pl.BlockSpec(
+                    (step, 2, size, size), lambda i, m, offset=offset: (i + offset, 0, 0, 0)
+                ),
+            ],
+            [
+                jax.ShapeDtypeStruct((own, 2, size, 2 * size), BF16),
+                jax.ShapeDtypeStruct((own, 2, size, size), BF16),
             ],
             [],
             part * 64 * 2 * 4 * size**3,
             part * 6 * 4 * size * size,
-        )(members, scale, factors, *arrived[chunk])
-        inverses.append(inverse)
-        psis.append(psi)
-    for chunk in range(chunks):
-        first = chunk * part // step
-        other = pl.BlockSpec((step, rows, size), lambda i, m, first=first: (i + first, 0, 0))
-        middles.append(
-            call(
-                middle_kernel,
-                part // step,
-                [
-                    inverse_block,
-                    pl.BlockSpec(
-                        (pl.squeezed, 1, step, rows, size),
-                        lambda i, m, chunk=chunk: (chunk, m[0], i, 0, 0),
-                    ),
-                ]
-                + [other] * 3,
-                pl.BlockSpec((size * part, size), lambda i, m: (0, 0)),
-                jax.ShapeDtypeStruct((size * part, size), F32),
-                [pltpu.VMEM((step, size, size), BF16)],
-                part * 10 * 2 * 4 * size**3,
-                part * 6 * 4 * size * size,
-            )(members, inverses[chunk], packed, *packed_arrived)
-        )
-    middles = [value.astype(jnp.float16).reshape(size, part, size) for value in middles]
-    sent = cat(middles, 1) if chunks > 1 else middles[0]
+            {6 + index: index for index in range(len(state))},
+        )(members, scale, factors, *arrived[chunk], *state)
+    inverse, psi = state
+
+    other = pl.BlockSpec((step, rows, size), lambda i, m: (i, 0, 0))
+    middle = call(
+        middle_kernel,
+        own // step,
+        [inverse_block, pl.BlockSpec((1, step, rows, size), lambda i, m: (m[0], i, 0, 0))]
+        + [other] * 3,
+        pl.BlockSpec((size * own, size), lambda i, m: (0, 0)),
+        jax.ShapeDtypeStruct((size * own, size), F32),
+        [pltpu.VMEM((step, size, size), BF16)],
+        own * 10 * 2 * 4 * size**3,
+        own * 6 * 4 * size * size,
+    )(members, inverse, packed, *packed_arrived)
+    sent = middle.astype(jnp.float16)
     if lane_parts > 1:
         sent = sent.reshape(size, own, lane_parts, lanes).transpose(0, 2, 1, 3)
     sent = sent.reshape(devices, kept, own, lanes)
     values = lax.all_to_all(sent, chan + ("freq",), 0, 0, tiled=True).astype(F32)
-    sources, own_rows, parts = devices, own, chunks
+    sources, own_rows = devices, own
     if own % 8:
         values = values.transpose(1, 0, 2, 3).reshape(1, kept, count, lanes)
         sources, own_rows = 1, count
@@ -330,61 +328,34 @@
             table_block,
             pl.BlockSpec((sources, twice, own_rows, lanes), lambda i: (0, i, 0, 0)),
         ],
-        out_specs=[
-            pl.BlockSpec((sources, twice, 2, own_rows // chunks, lanes), lambda i: (0, i, 0, 0, 0))
-        ]
-        * chunks,
-        out_shape=[jax.ShapeDtypeStruct((sources, kept, 2, own_rows // chunks, lanes), F32)] * chunks,
+        out_specs=[pl.BlockSpec((sources, twice, 2, own_rows, lanes), lambda i: (0, i, 0, 0, 0))],
+        out_shape=[jax.ShapeDtypeStruct((sources, kept, 2, own_rows, lanes), F32)],
         scratch_shapes=[pltpu.VMEM((2 * count, count), BF16), pltpu.VMEM((2 * count, count), BF16)],
         compiler_params=params(24),
         cost_estimate=cost(kept * 12 * count * count * lanes, 12 * kept * count * lanes),
-    )(table_re, table_im, values)
-
-    blocks = []
-    for chunk in range(chunks):
-        back = causal[chunk].astype(jnp.float16)
-        if own % 8:
-            back = back.reshape(kept, 2, devices, own, lanes).transpose(2, 0, 1, 3, 4)
-        if blocks:
-            back = after(back, backs)
-        back = lax.all_to_all(back, chan + ("freq",), 0, 0, tiled=True)
-        backs = back
-        if blocks:
-            back = after(back, *blocks[-1][1:])
-        back = back.astype(F32)
-        if lane_parts > 1:
-            back = back.reshape(chan_size * column_parts, lane_parts, kept, 2, part, lanes)
-            back = back.transpose(0, 2, 3, 4, 1, 5)
-        back = back.reshape(size * 2 * part, size)
-        result = pl.pallas_call(
-            product_kernel,
-            grid=(part // step,),
-            in_specs=[
-                pl.BlockSpec(back.shape, lambda i: (0, 0)),
-                pl.BlockSpec((step, 2, size, size), lambda i: (i, 0, 0, 0)),
-            ],
-            out_specs=pl.BlockSpec((chan_size, step, 2, rows, size), lambda i: (0, i, 0, 0, 0)),
-            out_shape=jax.ShapeDtypeStruct((chan_size, part, 2, rows, size), F32),
-            compiler_params=params(16),
-            cost_estimate=cost(part * 4 * 4 * size**3, part * 5 * 4 * size * size),
-        )(back, psis[chunk])
-        panels = [
-            lax.dynamic_index_in_dim(result, member ^ d, 0, keepdims=False) for d in range(chan_size)
-        ]
-        blocks.append(panels[:1] + [swap(panels[d].astype(jnp.float16), d) for d in distances])
-    ordered = []
-    for chunk in range(chunks):
-        pieces = [piece.astype(F32) for piece in blocks[chunk]]
-        owners = []
-        for owner in range(chan_size):
-            distance = member ^ owner
-            low = jnp.where(distance % 2 == 0, pieces[0], pieces[1])
-            high = jnp.where(distance % 2 == 0, pieces[2], pieces[3])
-            owners.append(jnp.where(distance < 2, low, high) * SCALE)
-        if chunk < chunks - 1:
-            owners = [lax.optimization_barrier(cat(owners, 0))]
-        ordered += owners
-    return jnp.swapaxes(cat(ordered, 0), 2, 3)
+    )(table_re, table_im, values)[0].astype(jnp.float16)
+    if own % 8:
+        causal = causal.reshape(kept, 2, devices, own, lanes).transpose(2, 0, 1, 3, 4)
+    back = lax.all_to_all(causal, chan + ("freq",), 0, 0, tiled=True).astype(F32)
+    if lane_parts > 1:
+        back = back.reshape(chan_size * column_parts, lane_parts, kept, 2, own, lanes)
+        back = back.transpose(0, 2, 3, 4, 1, 5)
+    back = back.reshape(size * 2 * own, size)
+    result = pl.pallas_call(
+        product_kernel,
+        grid=(own // step,),
+        in_specs=[
+            pl.BlockSpec(back.shape, lambda i: (0, 0)),
+            pl.BlockSpec((step, 2, size, size), lambda i: (i, 0, 0, 0)),
+        ],
+        out_specs=pl.BlockSpec((chan_size, step, 2, rows, size), lambda i: (0, i, 0, 0, 0)),
+        out_shape=jax.ShapeDtypeStruct((chan_size, own, 2, rows, size), F32),
+        compiler_params=params(16),
+        cost_estimate=cost(own * 4 * 4 * size**3, own * 5 * 4 * size * size),
+    )(back, psi)
+    result = lax.all_to_all(result.astype(jnp.float16), chan, 0, 0, tiled=True)
+    whole = result.reshape(group_bins, 2, rows, size).astype(F32) * SCALE
+    return jnp.swapaxes(whole, 2, 3)
 
 
 def solution(mesh):

time: 142 us -> 139 us (0.979)
  blocking collectives: 0 us -> 57.6 us
  waiting for transfers between devices: 63.2 us -> 21.8 us
  starting transfers between devices: 35.6 us -> 19.9 us
  local copies, waits for them, and re-layouts: 6.11 us -> 2.38 us
    all_to_all x0 -> x2, blocking collectives: none -> 57.6 us  [the longest x1 29.1 us: shards(): lax.all_to_all(causal, chan + ('freq',), 0, 0, tiled=True).astype(F32)]
    ppermute x5 -> x3, waiting for transfers between devices: 38.8 us -> 13.1 us  [swap(): return lax.ppermute(value, 'side', SWAP)]
    all_to_all x2 -> x0, waiting for transfers between devices: 14.6 us -> none  [shards(): back = lax.all_to_all(back, chan + ('freq',), 0, 0, tiled=True)]
    all_to_all x2 -> x0, starting transfers between devices: 6.37 us -> none  [shards(): back = lax.all_to_all(back, chan + ('freq',), 0, 0, tiled=True)]
    ppermute x5 -> x3, starting transfers between devices: 6.82 us -> 2.93 us  [swap(): return lax.ppermute(value, ('side', 'pair'), FLIP)]
    unnamed x23 -> x12, local copies, waits for them, and re-layouts: 3.05 us -> 0.02 us
    ppermute x5 -> x3, starting transfers between devices: 9.97 us -> 6.95 us  [swap(): return lax.ppermute(value, 'pair', SWAP)]
    ppermute x5 -> x3, starting transfers between devices: 7.17 us -> 4.65 us  [swap(): return lax.ppermute(value, 'side', SWAP)]
  transfers between devices with their start and end apart: 18 -> 10, of which waited for: 9 -> 5; matrix products, arithmetic and copies ran while one was open for 8% -> 6% of each run, Pallas kernels for 10% -> 10%
where the time goes in v5:
time: 139 us
  blocking collectives  57.6 us (41%)
  Pallas kernels  23.7 us (17%)
  waiting for transfers between devices  21.8 us (16%)
  starting transfers between devices  19.9 us (14%)
  other arithmetic  12.7 us (9%)
  local copies, waits for them, and re-layouts  2.38 us (2%)
    all_to_all x1, blocking collectives, shards(): lax.all_to_all(causal, chan + ('freq',), 0, 0, tiled=True).astype(F32)  29.1 us
    all_to_all x1, blocking collectives, shards(): result = lax.all_to_all(result.astype(jnp.float16), chan, 0, 0, tiled=True)  28.5 us
    pallas_call x2, Pallas kernels, shards(): call(newton_kernel, part // step, [pl.BlockSpec(memory_space=pltpu.SMEM),...  13.6 us
    ppermute x3, waiting for transfers between devices, swap(): return lax.ppermute(value, 'side', SWAP)  13.1 us
    select_n x1, other arithmetic, projection_table(): jnp.where(shift == 0, 0.0, (jnp.cos(half_angle) - jnp.cos(last_angle)) /...  8.24 us
    ppermute x3, starting transfers between devices, swap(): return lax.ppermute(value, 'pair', SWAP)  6.95 us
    all_to_all x1, waiting for transfers between devices, shards(): lax.all_to_all(sent, chan + ('freq',), 0, 0, tiled=True).astype(F32)  6.44 us
    all_to_all x1, starting transfers between devices, shards(): lax.all_to_all(sent, chan + ('freq',), 0, 0, tiled=True).astype(F32)  5.42 us
  transfers between devices with their start and end apart: 10, of which 5 were waited for; matrix products, arithmetic and copies ran while one was open for 6% of the time, Pallas kernels for 10%

profile of v5, /device:TPU:0, one launch (start us, length us, event | category | flops | bytes accessed | tf_op | source)
XLA Modules:
  0.0 138.9 jit_solution(6347135834266189906)
XLA Ops:
  0.0 0.0 copy-start.1
  0.0 2.2 %dynamic-slice_bitcast_fusion.3 = (bf16[8,2,32,128]{3,2,1,0:T(8,128)(2,1)}, bf16[8,2,32,128]{3,2,1,0:T(8,128)(2,1)}, bf16[8,2,32,128]{3,2,1,0:T(8,128)(2,1)}, bf...) fusion(bf16[4,16,2,32,128]{4,3,2,1,0:T(8,128)(2,1)} %bitcast.35, ...), kind=kLoop, calls=%fused_computation.28 | loop fusion | bytes 1572876 | tf_op jit(solution)/shard_map/reshape | solution.py:249
  2.2 0.0 copy-start.5
  2.2 3.0 %collective-permute-start = (bf16[8,2,32,128]{3,2,1,0:T(8,128)(2,1)}, bf16[8,2,32,128]{3,2,1,0:T(8,128)(2,1)S(1)}, u32[]{:S(2)}, u32[]{:S(2)}) collective-permute-start(bf16[8,2,32,128]{3,2,1,0:T(8,128)(2,1)} %get-tuple-element.29), channel_id=1, source_target_pairs={{0,1},{1,0},{2,3},{3,2},{4,5},{5,4},{6,7},{7,6},{8,9},{9,8},{10,11... | collective-permute-start | bytes 393224 | tf_op jit(solution)/shard_map/ppermute | solution.py:202
  5.2 2.6 %collective-permute-start.1 = (bf16[8,2,32,128]{3,2,1,0:T(8,128)(2,1)}, bf16[8,2,32,128]{3,2,1,0:T(8,128)(2,1)S(1)}, u32[]{:S(2)}, u32[]{:S(2)}) collective-permute-start(bf16[8,2,32,128]{3,2,1,0:T(8,128)(2,1)} %get-tuple-element.28), channel_id=1, source_target_pairs={{0,2},{2,0},{1,3},{3,1},{4,6},{6,4},{5,7},{7,5},{8,10},{10,8},{9,1... | collective-permute-start | bytes 393224 | tf_op jit(solution)/shard_map/ppermute | solution.py:204
  7.8 0.0 collective-permute-start.2
  7.8 0.1 iota_compare_fusion
  7.9 0.0 copy-done.1
  7.9 0.0 copy-start
  7.9 0.1 fusion.29
  8.0 0.0 copy-start.4
  8.0 0.0 copy-start.3
  8.0 0.0 copy-start.2
  8.0 0.1 bitcast_select_fusion.own_ref
  8.1 0.0 copy-done.5
  8.1 0.1 fusion.30
  8.2 2.3 %collective-permute-done.one_ref = bf16[8,2,32,128]{3,2,1,0:T(8,128)(2,1)S(1)} collective-permute-done((bf16[8,2,32,128]{3,2,1,0:T(8,128)(2,1)}, bf16[8,2,32,128]{3,2,1,0:T(8,128)(2,1)S(1)}, u32[]{:S(2)}, u32[]{:S(2)}) %collective-permute-start) | collective-permute-done | bytes 131104 | tf_op jit(solution)/shard_map/ppermute | solution.py:202
  10.4 7.9 %collective-permute-done.1.two_ref = bf16[8,2,32,128]{3,2,1,0:T(8,128)(2,1)S(1)} collective-permute-done((bf16[8,2,32,128]{3,2,1,0:T(8,128)(2,1)}, bf16[8,2,32,128]{3,2,1,0:T(8,128)(2,1)S(1)}, u32[]{:S(2)}, u32[]{:S(2)}) %collective-permute-start.1) | collective-permute-done | bytes 131104 | tf_op jit(solution)/shard_map/ppermute | solution.py:204
  18.3 0.0 collective-permute-done.2.three_ref
  18.3 0.0 copy-done.4
  18.3 2.0 %collective-permute-start.3 = (bf16[8,2,32,128]{3,2,1,0:T(8,128)(2,1)S(1)}, bf16[8,2,32,128]{3,2,1,0:T(8,128)(2,1)S(1)}, u32[]{:S(2)}, u32[]{:S(2)}) collective-permute-start(bf16[8,2,32,128]{3,2,1,0:T(8,128)(2,1)S(1)} %copy-done.4), channel_id=1, source_target_pairs={{0,1},{1,0},{2,3},{3,2},{4,5},{5,4},{6,7},{7,6},{8,9},{9,8},{10,11... | collective-permute-start | bytes 393224 | tf_op jit(solution)/shard_map/ppermute | solution.py:202
  20.3 0.0 copy-done.3
  20.3 1.1 collective-permute-start.4
  21.4 0.0 copy-done.2
  21.4 1.5 %collective-permute-start.5 = (bf16[8,2,32,128]{3,2,1,0:T(8,128)(2,1)S(1)}, bf16[8,2,32,128]{3,2,1,0:T(8,128)(2,1)S(1)}, u32[]{:S(2)}, u32[]{:S(2)}) collective-permute-start(bf16[8,2,32,128]{3,2,1,0:T(8,128)(2,1)S(1)} %copy-done.2), channel_id=1, source_target_pairs={{0,3},{1,2},{2,1},{3,0},{4,7},{5,6},{6,5},{7,4},{8,11},{9,10},{10,... | collective-permute-start | bytes 393224 | tf_op jit(solution)/shard_map/ppermute | solution.py:205
  22.9 0.0 copy-done
  22.9 6.8 %shard_map.46 = (bf16[16,2,128,256]{3,2,1,0:T(8,128)(2,1)S(1)}, bf16[16,2,128,128]{3,2,1,0:T(8,128)(2,1)S(1)}) custom-call(s32[1]{0:T(128)} %bitcast.2.member_ref, f32[8]{0:T(128)S(1)} %get-tuple-element.38.scale_ref, bf16[4,16,2,32,128]{4,3,2,1,0:T(8,128)(2,1)S(1)} %bitcast.36, bf16[8,2,32,128]{3,2,1,0:T(8,128)(2,1)S(1)} %collective-permute-done.one_ref, ...), custom_call_target="tpu_custom_call" | custom-call | flops 8589934592 | bytes 3145728 | tf_op jit(solution)/shard_map/pallas_call | solution.py:275
  29.7 0.0 collective-permute-done.3.one_ref
  29.7 2.4 %collective-permute-done.4.two_ref = bf16[8,2,32,128]{3,2,1,0:T(8,128)(2,1)S(1)} collective-permute-done((bf16[8,2,32,128]{3,2,1,0:T(8,128)(2,1)S(1)}, bf16[8,2,32,128]{3,2,1,0:T(8,128)(2,1)S(1)}, u32[]{:S(2)}, u32[]{:S(2)}) %collective-permute-start.4) | collective-permute-done | bytes 131104 | tf_op jit(solution)/shard_map/ppermute | solution.py:204
  32.1 0.0 collective-permute-done.5.three_ref
  32.1 2.0 %collective-permute-start.6 = (bf16[16,32,128]{2,1,0:T(8,128)(2,1)S(1)}, bf16[16,32,128]{2,1,0:T(8,128)(2,1)S(1)}, u32[]{:S(2)}, u32[]{:S(2)}) collective-permute-start(bf16[16,32,128]{2,1,0:T(8,128)(2,1)S(1)} %get-tuple-element.21), channel_id=1, source_target_pairs={{0,1},{1,0},{2,3},{3,2},{4,5},{5,4},{6,7},{7,6},{8,9},{9,8},{10,11... | collective-permute-start | bytes 393224 | tf_op jit(solution)/shard_map/ppermute | solution.py:202
  34.0 1.0 collective-permute-start.7
  35.0 1.5 %collective-permute-start.8 = (bf16[16,32,128]{2,1,0:T(8,128)(2,1)S(1)}, bf16[16,32,128]{2,1,0:T(8,128)(2,1)S(1)}, u32[]{:S(2)}, u32[]{:S(2)}) collective-permute-start(bf16[16,32,128]{2,1,0:T(8,128)(2,1)S(1)} %get-tuple-element.23), channel_id=1, source_target_pairs={{0,3},{1,2},{2,1},{3,0},{4,7},{5,6},{6,5},{7,4},{8,11},{9,10},{10,... | collective-permute-start | bytes 393224 | tf_op jit(solution)/shard_map/ppermute | solution.py:205
  36.5 6.8 %shard_map.47 = (bf16[16,2,128,256]{3,2,1,0:T(8,128)(2,1)S(1)}, bf16[16,2,128,128]{3,2,1,0:T(8,128)(2,1)S(1)}) custom-call(s32[1]{0:T(128)} %bitcast.2.member_ref, f32[8]{0:T(128)S(1)} %get-tuple-element.39.scale_ref, bf16[4,16,2,32,128]{4,3,2,1,0:T(8,128)(2,1)S(1)} %bitcast.37, ...), custom_call_target="tpu_custom_call", output_to_operand_aliasing={{0}: (6, {}), {1}: (7, {})} | custom-call | flops 8589934592 | bytes 3145728 | tf_op jit(solution)/shard_map/pallas_call | solution.py:275
  43.3 0.0 collective-permute-done.6.one_ref
  43.3 2.8 %collective-permute-done.7.two_ref = bf16[16,32,128]{2,1,0:T(8,128)(2,1)S(1)} collective-permute-done((bf16[16,32,128]{2,1,0:T(8,128)(2,1)S(1)}, bf16[16,32,128]{2,1,0:T(8,128)(2,1)S(1)}, u32[]{:S(2)}, u32[]{:S(2)}) %collective-permute-start.7) | collective-permute-done | bytes 131104 | tf_op jit(solution)/shard_map/ppermute | solution.py:204
  46.1 0.0 collective-permute-done.8.three_ref
  46.1 4.9 %shard_map.48 = f32[2048,128]{1,0:T(8,128)S(1)} custom-call(s32[1]{0:T(128)} %bitcast.2.member_ref, bf16[16,2,128,256]{3,2,1,0:T(8,128)(2,1)S(1)} %get-tuple-element.20.inverse_ref, bf16[4,16,32,128]{3,2,1,0:T(8,128)(2,1)S(1)} %bitcast_select_fusion.own_ref, bf16[16,32,128]{2,1,0:T(8,128)(2,1)S(1)} %collective-permute-done.6.one_ref, ...), custom_call_target="tpu_custom_call" | custom-call | flops 2684354560 | bytes 6291456 | tf_op jit(solution)/shard_map/pallas_call | solution.py:301
  51.1 0.9 convert_element_type.34
  51.9 5.4 %all-to-all-start = ((f16[32,4,16,128]{3,2,1,0:T(8,128)(2,1)}), f16[32,4,16,128]{3,2,1,0:T(8,128)(2,1)}, u32[]{:S(2)}, u32[]{:S(2)}) async-start(f16[32,4,16,128]{3,2,1,0:T(8,128)(2,1)} %bitcast.15), calls=%async_computation | async-start | bytes 1048576 | tf_op jit(solution)/shard_map/all_to_all | solution.py:316
  58.0 8.2 %fusion.3 = (f32[512,512]{1,0:T(8,128)S(1)}, f32[512,512]{1,0:T(8,128)S(1)}) fusion(s32[512]{0:T(512)S(1)} %fusion.23, s32[]{:T(128)} %bitcast.1, f32[]{:T(128)} %bitcast), kind=kLoop, calls=%fused_computation.10 | loop fusion | flops 7340032 | bytes 2099208 | tf_op jit(solution)/shard_map/jit(_where)/select_n | solution.py:180
  66.3 6.4 %all-to-all-done = f16[32,4,16,128]{3,2,1,0:T(8,128)(2,1)} async-done(((f16[32,4,16,128]{3,2,1,0:T(8,128)(2,1)}), f16[32,4,16,128]{3,2,1,0:T(8,128)(2,1)}, u32[]{:S(2)}, u32[]{:S(2)}) %all-to-all-start) | async-done | bytes 524320 | tf_op jit(solution)/shard_map/all_to_all | solution.py:316
  72.7 1.1 convert_element_type.35.values_ref
  73.8 2.5 %shard_map.49 = f32[32,4,2,16,128]{4,3,2,1,0:T(8,128)S(1)} custom-call(f32[512,512]{1,0:T(8,128)S(1)} %get-tuple-element.37.real_ref, f32[512,512]{1,0:T(8,128)S(1)} %get-tuple-element.36.imag_ref, f32[32,4,16,128]{3,2,1,0:T(8,128)S(1)} %convert_element_type.35.values_ref), custom_call_target="tpu_custom_call" | custom-call | flops 1610612736 | bytes 3145728 | tf_op jit(solution)/shard_map/pallas_call | solution.py:323
  76.3 0.3 convert_element_type.36
  76.6 29.1 %all_to_all.15 = f16[32,4,2,16,128]{4,3,2,1,0:T(8,128)(2,1)S(1)} all-to-all(f16[32,4,2,16,128]{4,3,2,1,0:T(8,128)(2,1)S(1)} %convert_element_type.36), channel_id=1, replica_groups=mesh['freq'=8,'side'=2,'pair'=2] {'side','pair','freq'}, dimensions={0} | all-to-all | bytes 2097152 | tf_op jit(solution)/shard_map/all_to_all | solution.py:339
  105.7 0.2 bitcast_convert_fusion.causal_ref
  105.9 2.6 %shard_map.50 = f32[4,16,2,32,128]{4,3,2,1,0:T(8,128)S(1)} custom-call(f32[4096,128]{1,0:T(8,128)S(1)} %bitcast_convert_fusion.causal_ref, bf16[16,2,128,128]{3,2,1,0:T(8,128)(2,1)S(1)} %get-tuple-element.24.psi_ref), custom_call_target="tpu_custom_call" | custom-call | flops 536870912 | bytes 5242880 | tf_op jit(solution)/shard_map/pallas_call | solution.py:344
  108.5 0.3 convert_element_type.37
  108.8 28.5 %all_to_all.16 = f16[4,16,2,32,128]{4,3,2,1,0:T(8,128)(2,1)S(1)} all-to-all(f16[4,16,2,32,128]{4,3,2,1,0:T(8,128)(2,1)S(1)} %convert_element_type.37), channel_id=1, replica_groups=mesh['freq'=8,'side'=2,'pair'=2] {'side','pair'}, dimensions={0} | all-to-all | bytes 2097152 | tf_op jit(solution)/shard_map/all_to_all | solution.py:356
  137.3 1.6 %convert_multiply_fusion = f32[4,16,2,32,128]{4,3,2,1,0:T(8,128)} fusion(f16[4,16,2,32,128]{4,3,2,1,0:T(8,128)(2,1)S(1)} %all_to_all.16), kind=kLoop, calls=%fused_computation.1 | loop fusion | flops 1048576 | bytes 3145728 | tf_op jit(solution)/shard_map/mul | solution.py:357
  (3 shorter events, 0.0 us)
Async XLA Ops:
  0.0 7.9 %copy-start.1 = (bf16[64,2,32,128]{3,2,1,0:T(8,128)(2,1)S(1)}, bf16[64,2,32,128]{3,2,1,0:T(8,128)(2,1)}, u32[]{:S(2)}) copy-start(bf16[64,2,32,128]{3,2,1,0:T(8,128)(2,1)} %param.5) | copy-start | bytes 3145732
  2.2 5.9 %copy-start.5 = (f32[64]{0:T(128)S(1)}, f32[64]{0:T(128)}, u32[]{:S(2)}) copy-start(f32[64]{0:T(128)} %param.6) | copy-start | bytes 772
  2.2 8.3 %collective-permute-start = (bf16[8,2,32,128]{3,2,1,0:T(8,128)(2,1)}, bf16[8,2,32,128]{3,2,1,0:T(8,128)(2,1)S(1)}, u32[]{:S(2)}, u32[]{:S(2)}) collective-permute-start(bf16[8,2,32,128]{3,2,1,0:T(8,128)(2,1)} %get-tuple-element.29), channel_id=1, source_target_pairs={{0,1},{1,0},{2,3},{3,2},{4,5},{5,4},{6,7},{7,6},{8,9},{9,8},{10,11... | collective-permute-start | bytes 393224 | tf_op jit(solution)/shard_map/ppermute | solution.py:202
  5.2 13.1 %collective-permute-start.1 = (bf16[8,2,32,128]{3,2,1,0:T(8,128)(2,1)}, bf16[8,2,32,128]{3,2,1,0:T(8,128)(2,1)S(1)}, u32[]{:S(2)}, u32[]{:S(2)}) collective-permute-start(bf16[8,2,32,128]{3,2,1,0:T(8,128)(2,1)} %get-tuple-element.28), channel_id=1, source_target_pairs={{0,2},{2,0},{1,3},{3,1},{4,6},{6,4},{5,7},{7,5},{8,10},{10,8},{9,1... | collective-permute-start | bytes 393224 | tf_op jit(solution)/shard_map/ppermute | solution.py:204
  7.8 10.5 %collective-permute-start.2 = (bf16[8,2,32,128]{3,2,1,0:T(8,128)(2,1)}, bf16[8,2,32,128]{3,2,1,0:T(8,128)(2,1)S(1)}, u32[]{:S(2)}, u32[]{:S(2)}) collective-permute-start(bf16[8,2,32,128]{3,2,1,0:T(8,128)(2,1)} %get-tuple-element.27), channel_id=1, source_target_pairs={{0,3},{1,2},{2,1},{3,0},{4,7},{5,6},{6,5},{7,4},{8,11},{9,10},{10,... | collective-permute-start | bytes 393224 | tf_op jit(solution)/shard_map/ppermute | solution.py:205
  7.9 15.0 %copy-start = (bf16[64,2,32,128]{3,2,1,0:T(8,128)(2,1)S(1)}, bf16[64,2,32,128]{3,2,1,0:T(8,128)(2,1)}, u32[]{:S(2)}) copy-start(bf16[64,2,32,128]{3,2,1,0:T(8,128)(2,1)} %param.4) | copy-start | bytes 3145732
  8.0 10.4 %copy-start.4 = (bf16[8,2,32,128]{3,2,1,0:T(8,128)(2,1)S(1)}, bf16[8,2,32,128]{3,2,1,0:T(8,128)(2,1)}, u32[]{:S(2)}) copy-start(bf16[8,2,32,128]{3,2,1,0:T(8,128)(2,1)} %get-tuple-element.15) | copy-start | bytes 393220
  8.0 12.3 %copy-start.3 = (bf16[8,2,32,128]{3,2,1,0:T(8,128)(2,1)S(1)}, bf16[8,2,32,128]{3,2,1,0:T(8,128)(2,1)}, u32[]{:S(2)}) copy-start(bf16[8,2,32,128]{3,2,1,0:T(8,128)(2,1)} %get-tuple-element.16) | copy-start | bytes 393220
  8.0 13.4 %copy-start.2 = (bf16[8,2,32,128]{3,2,1,0:T(8,128)(2,1)S(1)}, bf16[8,2,32,128]{3,2,1,0:T(8,128)(2,1)}, u32[]{:S(2)}) copy-start(bf16[8,2,32,128]{3,2,1,0:T(8,128)(2,1)} %get-tuple-element.17) | copy-start | bytes 393220
  18.3 11.3 %collective-permute-start.3 = (bf16[8,2,32,128]{3,2,1,0:T(8,128)(2,1)S(1)}, bf16[8,2,32,128]{3,2,1,0:T(8,128)(2,1)S(1)}, u32[]{:S(2)}, u32[]{:S(2)}) collective-permute-start(bf16[8,2,32,128]{3,2,1,0:T(8,128)(2,1)S(1)} %copy-done.4), channel_id=1, source_target_pairs={{0,1},{1,0},{2,3},{3,2},{4,5},{5,4},{6,7},{7,6},{8,9},{9,8},{10,11... | collective-permute-start | bytes 393224 | tf_op jit(solution)/shard_map/ppermute | solution.py:202
  20.3 11.7 %collective-permute-start.4 = (bf16[8,2,32,128]{3,2,1,0:T(8,128)(2,1)S(1)}, bf16[8,2,32,128]{3,2,1,0:T(8,128)(2,1)S(1)}, u32[]{:S(2)}, u32[]{:S(2)}) collective-permute-start(bf16[8,2,32,128]{3,2,1,0:T(8,128)(2,1)S(1)} %copy-done.3), channel_id=1, source_target_pairs={{0,2},{2,0},{1,3},{3,1},{4,6},{6,4},{5,7},{7,5},{8,10},{10,8},{9,1... | collective-permute-start | bytes 393224 | tf_op jit(solution)/shard_map/ppermute | solution.py:204
  21.4 10.7 %collective-permute-start.5 = (bf16[8,2,32,128]{3,2,1,0:T(8,128)(2,1)S(1)}, bf16[8,2,32,128]{3,2,1,0:T(8,128)(2,1)S(1)}, u32[]{:S(2)}, u32[]{:S(2)}) collective-permute-start(bf16[8,2,32,128]{3,2,1,0:T(8,128)(2,1)S(1)} %copy-done.2), channel_id=1, source_target_pairs={{0,3},{1,2},{2,1},{3,0},{4,7},{5,6},{6,5},{7,4},{8,11},{9,10},{10,... | collective-permute-start | bytes 393224 | tf_op jit(solution)/shard_map/ppermute | solution.py:205
  32.1 11.2 %collective-permute-start.6 = (bf16[16,32,128]{2,1,0:T(8,128)(2,1)S(1)}, bf16[16,32,128]{2,1,0:T(8,128)(2,1)S(1)}, u32[]{:S(2)}, u32[]{:S(2)}) collective-permute-start(bf16[16,32,128]{2,1,0:T(8,128)(2,1)S(1)} %get-tuple-element.21), channel_id=1, source_target_pairs={{0,1},{1,0},{2,3},{3,2},{4,5},{5,4},{6,7},{7,6},{8,9},{9,8},{10,11... | collective-permute-start | bytes 393224 | tf_op jit(solution)/shard_map/ppermute | solution.py:202
  34.0 12.1 %collective-permute-start.7 = (bf16[16,32,128]{2,1,0:T(8,128)(2,1)S(1)}, bf16[16,32,128]{2,1,0:T(8,128)(2,1)S(1)}, u32[]{:S(2)}, u32[]{:S(2)}) collective-permute-start(bf16[16,32,128]{2,1,0:T(8,128)(2,1)S(1)} %get-tuple-element.22), channel_id=1, source_target_pairs={{0,2},{2,0},{1,3},{3,1},{4,6},{6,4},{5,7},{7,5},{8,10},{10,8},{9,1... | collective-permute-start | bytes 393224 | tf_op jit(solution)/shard_map/ppermute | solution.py:204
  35.0 11.1 %collective-permute-start.8 = (bf16[16,32,128]{2,1,0:T(8,128)(2,1)S(1)}, bf16[16,32,128]{2,1,0:T(8,128)(2,1)S(1)}, u32[]{:S(2)}, u32[]{:S(2)}) collective-permute-start(bf16[16,32,128]{2,1,0:T(8,128)(2,1)S(1)} %get-tuple-element.23), channel_id=1, source_target_pairs={{0,3},{1,2},{2,1},{3,0},{4,7},{5,6},{6,5},{7,4},{8,11},{9,10},{10,... | collective-permute-start | bytes 393224 | tf_op jit(solution)/shard_map/ppermute | solution.py:205
  51.9 20.8 %all-to-all-start = ((f16[32,4,16,128]{3,2,1,0:T(8,128)(2,1)}), f16[32,4,16,128]{3,2,1,0:T(8,128)(2,1)}, u32[]{:S(2)}, u32[]{:S(2)}) async-start(f16[32,4,16,128]{3,2,1,0:T(8,128)(2,1)} %bitcast.15), calls=%async_computation | async-start | bytes 1048576 | tf_op jit(solution)/shard_map/all_to_all | solution.py:316

commit v6 on v5

--- a/solution.py
+++ b/solution.py
@@ -105,6 +105,10 @@
     identity = eye(size)
     rows = lax.broadcasted_iota(jnp.int32, (size, size), 0)
     columns = lax.broadcasted_iota(jnp.int32, (size, size), 1)
+
+    def swapped(value):
+        return cat([value, cat([value[:, size:], -value[:, :size]], 1)], 0)
+
     for item in range(bins):
         packed = packed_ref[item].astype(F32)
         packed_t = packed.T
@@ -112,10 +116,9 @@
         im = jnp.where(columns == rows, 0.0, jnp.where(columns < rows, packed, -packed_t)).astype(BF16)
         high, low = inverse_ref[item, 0], inverse_ref[item, 1]
         both = dot(cat([high, low], 0), cat([cat([re, im], 1), cat([-im, re], 1)], 0))
-        left = both[:size] + both[size:]
-        left_re, left_im = left[:, :size], left[:, size:]
-        left_high, left_low = split(cat([left_re + left_im, left_im - left_re], 1))
-        middle = dot3(left_high, left_low, high, low, NT)
+        left_high, left_low = split(both[:size] + both[size:])
+        middle = dot3(left_high, left_low, swapped(high), swapped(low), NT)
+        middle = middle[:, :size] - middle[:, size:]
         place = pl.program_id(0) * bins + item
         out_ref[pl.ds(place, size, stride=total_bins), :] = (middle + identity) * (1.0 / SCALE)
 
@@ -251,15 +254,13 @@
     arrived = []
     for chunk in range(chunks):
         pieces = [rows_for(member ^ d, chunk * part, part) for d in distances]
-        if arrived:
-            pieces = lax.optimization_barrier(tuple(pieces) + tuple(arrived[-1]))[: len(pieces)]
         arrived.append([swap(piece, d) for piece, d in zip(pieces, distances)])
     row_index = lax.broadcasted_iota(jnp.int32, (rows, size), 0) + member * rows
     column_index = lax.broadcasted_iota(jnp.int32, (rows, size), 1)
     packed = jnp.where(column_index >= row_index, spectrum[:, 0], spectrum[:, 1])
     packed = packed.reshape(chan_size, own, rows, size)
     pieces = [lax.dynamic_index_in_dim(packed, member ^ d, 0, keepdims=False) for d in distances]
-    pieces = lax.optimization_barrier(tuple(pieces) + tuple(arrived[-1]))[: len(pieces)]
+    pieces = lax.optimization_barrier(tuple(pieces) + tuple(arrived[0]))[: len(pieces)]
     packed_arrived = [swap(piece, d) for piece, d in zip(pieces, distances)]
     table_re, table_im = projection_table(lag_cutoff[0], count, freq_size, pairs)
 

time: 139 us -> 135 us (0.971)
  waiting for transfers between devices: 21.8 us -> 9.19 us
  starting transfers between devices: 19.9 us -> 29.4 us
  Pallas kernels: 23.7 us -> 22.3 us
    ppermute x3, waiting for transfers between devices: 13.1 us -> 2.74 us  [swap(): return lax.ppermute(value, 'side', SWAP)]
    ppermute x3, starting transfers between devices: 6.95 us -> 14.4 us  [swap(): return lax.ppermute(value, 'pair', SWAP)]
    ppermute x3, starting transfers between devices: 4.65 us -> 6.97 us  [swap(): return lax.ppermute(value, 'side', SWAP)]
    ppermute x3, waiting for transfers between devices: 2.26 us -> 0.01 us  [swap(): return lax.ppermute(value, 'pair', SWAP)]
  transfers between devices with their start and end apart: 10 -> 10, of which waited for: 5 -> 2; matrix products, arithmetic and copies ran while one was open for 6% -> 7% of each run, Pallas kernels for 10% -> 10%
where the time goes in v6:
time: 135 us
  blocking collectives  57.6 us (43%)
  starting transfers between devices  29.4 us (22%)
  Pallas kernels  22.3 us (17%)
  other arithmetic  12.7 us (9%)
  waiting for transfers between devices  9.19 us (7%)
  local copies, waits for them, and re-layouts  2.74 us (2%)
    all_to_all x1, blocking collectives, shards(): lax.all_to_all(causal, chan + ('freq',), 0, 0, tiled=True).astype(F32)  29.1 us
    all_to_all x1, blocking collectives, shards(): result = lax.all_to_all(result.astype(jnp.float16), chan, 0, 0, tiled=True)  28.5 us
    ppermute x3, starting transfers between devices, swap(): return lax.ppermute(value, 'pair', SWAP)  14.4 us
    pallas_call x2, Pallas kernels, shards(): call(newton_kernel, part // step, [pl.BlockSpec(memory_space=pltpu.SMEM),...  13.6 us
    select_n x1, other arithmetic, projection_table(): jnp.where(shift == 0, 0.0, (jnp.cos(half_angle) - jnp.cos(last_angle)) /...  8.24 us
    ppermute x3, starting transfers between devices, swap(): return lax.ppermute(value, 'side', SWAP)  6.97 us
    all_to_all x1, waiting for transfers between devices, shards(): lax.all_to_all(sent, chan + ('freq',), 0, 0, tiled=True).astype(F32)  6.44 us
    all_to_all x1, starting transfers between devices, shards(): lax.all_to_all(sent, chan + ('freq',), 0, 0, tiled=True).astype(F32)  4.9 us
  transfers between devices with their start and end apart: 10, of which 2 were waited for; matrix products, arithmetic and copies ran while one was open for 7% of the time, Pallas kernels for 10%

profile of v6, /device:TPU:0, one launch (start us, length us, event | category | flops | bytes accessed | tf_op | source)
XLA Modules:
  0.0 134.7 jit_solution(10692073048860881593)
XLA Ops:
  0.0 1.3 dynamic-slice_bitcast_fusion.3
  1.3 0.0 copy-start.1
  1.3 3.1 %collective-permute-start.3 = (bf16[8,2,32,128]{3,2,1,0:T(8,128)(2,1)S(1)}, bf16[8,2,32,128]{3,2,1,0:T(8,128)(2,1)S(1)}, u32[]{:S(2)}, u32[]{:S(2)}) collective-permute-start(bf16[8,2,32,128]{3,2,1,0:T(8,128)(2,1)S(1)} %get-tuple-element.23), channel_id=1, source_target_pairs={{0,1},{1,0},{2,3},{3,2},{4,5},{5,4},{6,7},{7,6},{8,9},{9,8},{10,11... | collective-permute-start | bytes 393224 | tf_op jit(solution)/shard_map/ppermute | solution.py:205
  4.4 2.6 %collective-permute-start.4 = (bf16[8,2,32,128]{3,2,1,0:T(8,128)(2,1)S(1)}, bf16[8,2,32,128]{3,2,1,0:T(8,128)(2,1)S(1)}, u32[]{:S(2)}, u32[]{:S(2)}) collective-permute-start(bf16[8,2,32,128]{3,2,1,0:T(8,128)(2,1)S(1)} %get-tuple-element.22), channel_id=1, source_target_pairs={{0,2},{2,0},{1,3},{3,1},{4,6},{6,4},{5,7},{7,5},{8,10},{10,8},{9,1... | collective-permute-start | bytes 393224 | tf_op jit(solution)/shard_map/ppermute | solution.py:207
  6.9 0.0 collective-permute-start.5
  7.0 0.9 collective-permute-start
  7.8 3.5 %collective-permute-start.1 = (bf16[8,2,32,128]{3,2,1,0:T(8,128)(2,1)S(1)}, bf16[8,2,32,128]{3,2,1,0:T(8,128)(2,1)S(1)}, u32[]{:S(2)}, u32[]{:S(2)}) collective-permute-start(bf16[8,2,32,128]{3,2,1,0:T(8,128)(2,1)S(1)} %get-tuple-element.25), channel_id=1, source_target_pairs={{0,2},{2,0},{1,3},{3,1},{4,6},{6,4},{5,7},{7,5},{8,10},{10,8},{9,1... | collective-permute-start | bytes 393224 | tf_op jit(solution)/shard_map/ppermute | solution.py:207
  11.3 0.1 iota_compare_fusion
  11.4 0.0 copy-start
  11.4 1.4 %fusion.29 = (bf16[64,1,32,128]{3,2,1,0:T(8,128)(2,1)S(1)}, bf16[64,1,32,128]{3,2,1,0:T(8,128)(2,1)S(1)}) fusion(bf16[64,2,32,128]{3,2,1,0:T(8,128)(2,1)} %param.5), kind=kLoop, calls=%fused_computation.59 | loop fusion | bytes 2097152 | tf_op jit(solution)/shard_map/slice | solution.py:260
  12.8 0.1 bitcast_select_fusion.own_ref
  12.9 0.0 copy-done.1
  12.9 0.1 fusion.30
  13.0 0.0 collective-permute-done.3.one_ref
  13.0 1.6 %collective-permute-start.2 = (bf16[8,2,32,128]{3,2,1,0:T(8,128)(2,1)S(1)}, bf16[8,2,32,128]{3,2,1,0:T(8,128)(2,1)S(1)}, u32[]{:S(2)}, u32[]{:S(2)}) collective-permute-start(bf16[8,2,32,128]{3,2,1,0:T(8,128)(2,1)S(1)} %get-tuple-element.24), channel_id=1, source_target_pairs={{0,3},{1,2},{2,1},{3,0},{4,7},{5,6},{6,5},{7,4},{8,11},{9,10},{10,... | collective-permute-start | bytes 393224 | tf_op jit(solution)/shard_map/ppermute | solution.py:208
  14.6 2.7 %collective-permute-done.4.two_ref = bf16[8,2,32,128]{3,2,1,0:T(8,128)(2,1)S(1)} collective-permute-done((bf16[8,2,32,128]{3,2,1,0:T(8,128)(2,1)S(1)}, bf16[8,2,32,128]{3,2,1,0:T(8,128)(2,1)S(1)}, u32[]{:S(2)}, u32[]{:S(2)}) %collective-permute-start.4) | collective-permute-done | bytes 131104 | tf_op jit(solution)/shard_map/ppermute | solution.py:207
  17.3 0.0 collective-permute-done.5.three_ref
  17.3 10.4 %collective-permute-start.6 = (bf16[16,32,128]{2,1,0:T(8,128)(2,1)S(1)}, bf16[16,32,128]{2,1,0:T(8,128)(2,1)S(1)}, u32[]{:S(2)}, u32[]{:S(2)}) collective-permute-start(bf16[16,32,128]{2,1,0:T(8,128)(2,1)S(1)} %get-tuple-element.15), channel_id=1, source_target_pairs={{0,1},{1,0},{2,3},{3,2},{4,5},{5,4},{6,7},{7,6},{8,9},{9,8},{10,11... | collective-permute-start | bytes 393224 | tf_op jit(solution)/shard_map/ppermute | solution.py:205
  27.7 0.9 collective-permute-start.7
  28.6 0.0 copy-done
  28.6 6.8 %shard_map.46 = (bf16[16,2,128,256]{3,2,1,0:T(8,128)(2,1)S(1)}, bf16[16,2,128,128]{3,2,1,0:T(8,128)(2,1)S(1)}) custom-call(s32[1]{0:T(128)} %bitcast.2.member_ref, f32[8]{0:T(128)S(1)} %get-tuple-element.32.scale_ref, bf16[4,16,2,32,128]{4,3,2,1,0:T(8,128)(2,1)S(1)} %bitcast.36, bf16[8,2,32,128]{3,2,1,0:T(8,128)(2,1)S(1)} %collective-permute-done.3.one_ref, ...), custom_call_target="tpu_custom_call" | custom-call | flops 8589934592 | bytes 3145728 | tf_op jit(solution)/shard_map/pallas_call | solution.py:276
  35.4 0.0 collective-permute-done.one_ref
  35.4 1.5 %collective-permute-start.8 = (bf16[16,32,128]{2,1,0:T(8,128)(2,1)S(1)}, bf16[16,32,128]{2,1,0:T(8,128)(2,1)S(1)}, u32[]{:S(2)}, u32[]{:S(2)}) collective-permute-start(bf16[16,32,128]{2,1,0:T(8,128)(2,1)S(1)} %get-tuple-element.17), channel_id=1, source_target_pairs={{0,3},{1,2},{2,1},{3,0},{4,7},{5,6},{6,5},{7,4},{8,11},{9,10},{10,... | collective-permute-start | bytes 393224 | tf_op jit(solution)/shard_map/ppermute | solution.py:208
  37.0 0.0 collective-permute-done.1.two_ref
  37.0 0.0 collective-permute-done.2.three_ref
  37.0 6.8 %shard_map.47 = (bf16[16,2,128,256]{3,2,1,0:T(8,128)(2,1)S(1)}, bf16[16,2,128,128]{3,2,1,0:T(8,128)(2,1)S(1)}) custom-call(s32[1]{0:T(128)} %bitcast.2.member_ref, f32[8]{0:T(128)S(1)} %get-tuple-element.33.scale_ref, bf16[4,16,2,32,128]{4,3,2,1,0:T(8,128)(2,1)S(1)} %bitcast.37, ...), custom_call_target="tpu_custom_call", output_to_operand_aliasing={{0}: (6, {}), {1}: (7, {})} | custom-call | flops 8589934592 | bytes 3145728 | tf_op jit(solution)/shard_map/pallas_call | solution.py:276
  43.8 0.0 collective-permute-done.6.one_ref
  43.8 0.0 collective-permute-done.7.two_ref
  43.8 0.0 collective-permute-done.8.three_ref
  43.8 3.5 %shard_map.48 = f32[2048,128]{1,0:T(8,128)S(1)} custom-call(s32[1]{0:T(128)} %bitcast.2.member_ref, bf16[16,2,128,256]{3,2,1,0:T(8,128)(2,1)S(1)} %get-tuple-element.14.inverse_ref, bf16[4,16,32,128]{3,2,1,0:T(8,128)(2,1)S(1)} %bitcast_select_fusion.own_ref, bf16[16,32,128]{2,1,0:T(8,128)(2,1)S(1)} %collective-permute-done.6.one_ref, ...), custom_call_target="tpu_custom_call" | custom-call | flops 2684354560 | bytes 6291456 | tf_op jit(solution)/shard_map/pallas_call | solution.py:302
  47.4 0.9 convert_element_type.34
  48.2 4.9 %all-to-all-start = ((f16[32,4,16,128]{3,2,1,0:T(8,128)(2,1)}), f16[32,4,16,128]{3,2,1,0:T(8,128)(2,1)}, u32[]{:S(2)}, u32[]{:S(2)}) async-start(f16[32,4,16,128]{3,2,1,0:T(8,128)(2,1)} %bitcast.15), calls=%async_computation | async-start | bytes 1048576 | tf_op jit(solution)/shard_map/all_to_all | solution.py:317
  53.8 8.2 %fusion.3 = (f32[512,512]{1,0:T(8,128)S(1)}, f32[512,512]{1,0:T(8,128)S(1)}) fusion(s32[512]{0:T(512)S(1)} %fusion.23, s32[]{:T(128)} %bitcast.1, f32[]{:T(128)} %bitcast), kind=kLoop, calls=%fused_computation.10 | loop fusion | flops 7340032 | bytes 2099208 | tf_op jit(solution)/shard_map/jit(_where)/select_n | solution.py:183
  62.0 6.4 %all-to-all-done = f16[32,4,16,128]{3,2,1,0:T(8,128)(2,1)} async-done(((f16[32,4,16,128]{3,2,1,0:T(8,128)(2,1)}), f16[32,4,16,128]{3,2,1,0:T(8,128)(2,1)}, u32[]{:S(2)}, u32[]{:S(2)}) %all-to-all-start) | async-done | bytes 524320 | tf_op jit(solution)/shard_map/all_to_all | solution.py:317
  68.5 1.1 convert_element_type.35.values_ref
  69.6 2.5 %shard_map.49 = f32[32,4,2,16,128]{4,3,2,1,0:T(8,128)S(1)} custom-call(f32[512,512]{1,0:T(8,128)S(1)} %get-tuple-element.31.real_ref, f32[512,512]{1,0:T(8,128)S(1)} %get-tuple-element.30.imag_ref, f32[32,4,16,128]{3,2,1,0:T(8,128)S(1)} %convert_element_type.35.values_ref), custom_call_target="tpu_custom_call" | custom-call | flops 1610612736 | bytes 3145728 | tf_op jit(solution)/shard_map/pallas_call | solution.py:324
  72.1 0.3 convert_element_type.36
  72.4 29.1 %all_to_all.15 = f16[32,4,2,16,128]{4,3,2,1,0:T(8,128)(2,1)S(1)} all-to-all(f16[32,4,2,16,128]{4,3,2,1,0:T(8,128)(2,1)S(1)} %convert_element_type.36), channel_id=1, replica_groups=mesh['freq'=8,'side'=2,'pair'=2] {'side','pair','freq'}, dimensions={0} | all-to-all | bytes 2097152 | tf_op jit(solution)/shard_map/all_to_all | solution.py:340
  101.5 0.2 bitcast_convert_fusion.causal_ref
  101.7 2.6 %shard_map.50 = f32[4,16,2,32,128]{4,3,2,1,0:T(8,128)S(1)} custom-call(f32[4096,128]{1,0:T(8,128)S(1)} %bitcast_convert_fusion.causal_ref, bf16[16,2,128,128]{3,2,1,0:T(8,128)(2,1)S(1)} %get-tuple-element.18.psi_ref), custom_call_target="tpu_custom_call" | custom-call | flops 536870912 | bytes 5242880 | tf_op jit(solution)/shard_map/pallas_call | solution.py:345
  104.3 0.3 convert_element_type.37
  104.6 28.5 %all_to_all.16 = f16[4,16,2,32,128]{4,3,2,1,0:T(8,128)(2,1)S(1)} all-to-all(f16[4,16,2,32,128]{4,3,2,1,0:T(8,128)(2,1)S(1)} %convert_element_type.37), channel_id=1, replica_groups=mesh['freq'=8,'side'=2,'pair'=2] {'side','pair'}, dimensions={0} | all-to-all | bytes 2097152 | tf_op jit(solution)/shard_map/all_to_all | solution.py:357
  133.1 1.6 %convert_multiply_fusion = f32[4,16,2,32,128]{4,3,2,1,0:T(8,128)} fusion(f16[4,16,2,32,128]{4,3,2,1,0:T(8,128)(2,1)S(1)} %all_to_all.16), kind=kLoop, calls=%fused_computation.1 | loop fusion | flops 1048576 | bytes 3145728 | tf_op jit(solution)/shard_map/mul | solution.py:358
  (3 shorter events, 0.0 us)
Async XLA Ops:
  1.3 11.6 %copy-start.1 = (f32[64]{0:T(128)S(1)}, f32[64]{0:T(128)}, u32[]{:S(2)}) copy-start(f32[64]{0:T(128)} %param.6) | copy-start | bytes 772
  1.3 11.7 %collective-permute-start.3 = (bf16[8,2,32,128]{3,2,1,0:T(8,128)(2,1)S(1)}, bf16[8,2,32,128]{3,2,1,0:T(8,128)(2,1)S(1)}, u32[]{:S(2)}, u32[]{:S(2)}) collective-permute-start(bf16[8,2,32,128]{3,2,1,0:T(8,128)(2,1)S(1)} %get-tuple-element.23), channel_id=1, source_target_pairs={{0,1},{1,0},{2,3},{3,2},{4,5},{5,4},{6,7},{7,6},{8,9},{9,8},{10,11... | collective-permute-start | bytes 393224 | tf_op jit(solution)/shard_map/ppermute | solution.py:205
  4.4 12.9 %collective-permute-start.4 = (bf16[8,2,32,128]{3,2,1,0:T(8,128)(2,1)S(1)}, bf16[8,2,32,128]{3,2,1,0:T(8,128)(2,1)S(1)}, u32[]{:S(2)}, u32[]{:S(2)}) collective-permute-start(bf16[8,2,32,128]{3,2,1,0:T(8,128)(2,1)S(1)} %get-tuple-element.22), channel_id=1, source_target_pairs={{0,2},{2,0},{1,3},{3,1},{4,6},{6,4},{5,7},{7,5},{8,10},{10,8},{9,1... | collective-permute-start | bytes 393224 | tf_op jit(solution)/shard_map/ppermute | solution.py:207
  6.9 10.4 %collective-permute-start.5 = (bf16[8,2,32,128]{3,2,1,0:T(8,128)(2,1)S(1)}, bf16[8,2,32,128]{3,2,1,0:T(8,128)(2,1)S(1)}, u32[]{:S(2)}, u32[]{:S(2)}) collective-permute-start(bf16[8,2,32,128]{3,2,1,0:T(8,128)(2,1)S(1)} %get-tuple-element.21), channel_id=1, source_target_pairs={{0,3},{1,2},{2,1},{3,0},{4,7},{5,6},{6,5},{7,4},{8,11},{9,10},{10,... | collective-permute-start | bytes 393224 | tf_op jit(solution)/shard_map/ppermute | solution.py:208
  7.0 28.5 %collective-permute-start = (bf16[8,2,32,128]{3,2,1,0:T(8,128)(2,1)S(1)}, bf16[8,2,32,128]{3,2,1,0:T(8,128)(2,1)S(1)}, u32[]{:S(2)}, u32[]{:S(2)}) collective-permute-start(bf16[8,2,32,128]{3,2,1,0:T(8,128)(2,1)S(1)} %get-tuple-element.26), channel_id=1, source_target_pairs={{0,1},{1,0},{2,3},{3,2},{4,5},{5,4},{6,7},{7,6},{8,9},{9,8},{10,11... | collective-permute-start | bytes 393224 | tf_op jit(solution)/shard_map/ppermute | solution.py:205
  7.8 29.1 %collective-permute-start.1 = (bf16[8,2,32,128]{3,2,1,0:T(8,128)(2,1)S(1)}, bf16[8,2,32,128]{3,2,1,0:T(8,128)(2,1)S(1)}, u32[]{:S(2)}, u32[]{:S(2)}) collective-permute-start(bf16[8,2,32,128]{3,2,1,0:T(8,128)(2,1)S(1)} %get-tuple-element.25), channel_id=1, source_target_pairs={{0,2},{2,0},{1,3},{3,1},{4,6},{6,4},{5,7},{7,5},{8,10},{10,8},{9,1... | collective-permute-start | bytes 393224 | tf_op jit(solution)/shard_map/ppermute | solution.py:207
  11.4 17.2 %copy-start = (bf16[64,2,32,128]{3,2,1,0:T(8,128)(2,1)S(1)}, bf16[64,2,32,128]{3,2,1,0:T(8,128)(2,1)}, u32[]{:S(2)}) copy-start(bf16[64,2,32,128]{3,2,1,0:T(8,128)(2,1)} %param.4) | copy-start | bytes 3145732
  13.0 24.0 %collective-permute-start.2 = (bf16[8,2,32,128]{3,2,1,0:T(8,128)(2,1)S(1)}, bf16[8,2,32,128]{3,2,1,0:T(8,128)(2,1)S(1)}, u32[]{:S(2)}, u32[]{:S(2)}) collective-permute-start(bf16[8,2,32,128]{3,2,1,0:T(8,128)(2,1)S(1)} %get-tuple-element.24), channel_id=1, source_target_pairs={{0,3},{1,2},{2,1},{3,0},{4,7},{5,6},{6,5},{7,4},{8,11},{9,10},{10,... | collective-permute-start | bytes 393224 | tf_op jit(solution)/shard_map/ppermute | solution.py:208
  17.3 26.5 %collective-permute-start.6 = (bf16[16,32,128]{2,1,0:T(8,128)(2,1)S(1)}, bf16[16,32,128]{2,1,0:T(8,128)(2,1)S(1)}, u32[]{:S(2)}, u32[]{:S(2)}) collective-permute-start(bf16[16,32,128]{2,1,0:T(8,128)(2,1)S(1)} %get-tuple-element.15), channel_id=1, source_target_pairs={{0,1},{1,0},{2,3},{3,2},{4,5},{5,4},{6,7},{7,6},{8,9},{9,8},{10,11... | collective-permute-start | bytes 393224 | tf_op jit(solution)/shard_map/ppermute | solution.py:205
  27.7 16.1 %collective-permute-start.7 = (bf16[16,32,128]{2,1,0:T(8,128)(2,1)S(1)}, bf16[16,32,128]{2,1,0:T(8,128)(2,1)S(1)}, u32[]{:S(2)}, u32[]{:S(2)}) collective-permute-start(bf16[16,32,128]{2,1,0:T(8,128)(2,1)S(1)} %get-tuple-element.16), channel_id=1, source_target_pairs={{0,2},{2,0},{1,3},{3,1},{4,6},{6,4},{5,7},{7,5},{8,10},{10,8},{9,1... | collective-permute-start | bytes 393224 | tf_op jit(solution)/shard_map/ppermute | solution.py:207
  35.4 8.4 %collective-permute-start.8 = (bf16[16,32,128]{2,1,0:T(8,128)(2,1)S(1)}, bf16[16,32,128]{2,1,0:T(8,128)(2,1)S(1)}, u32[]{:S(2)}, u32[]{:S(2)}) collective-permute-start(bf16[16,32,128]{2,1,0:T(8,128)(2,1)S(1)} %get-tuple-element.17), channel_id=1, source_target_pairs={{0,3},{1,2},{2,1},{3,0},{4,7},{5,6},{6,5},{7,4},{8,11},{9,10},{10,... | collective-permute-start | bytes 393224 | tf_op jit(solution)/shard_map/ppermute | solution.py:208
  48.2 20.2 %all-to-all-start = ((f16[32,4,16,128]{3,2,1,0:T(8,128)(2,1)}), f16[32,4,16,128]{3,2,1,0:T(8,128)(2,1)}, u32[]{:S(2)}, u32[]{:S(2)}) async-start(f16[32,4,16,128]{3,2,1,0:T(8,128)(2,1)} %bitcast.15), calls=%async_computation | async-start | bytes 1048576 | tf_op jit(solution)/shard_map/all_to_all | solution.py:317

commit v7 on v6

--- a/solution.py
+++ b/solution.py
@@ -260,8 +260,6 @@
     packed = jnp.where(column_index >= row_index, spectrum[:, 0], spectrum[:, 1])
     packed = packed.reshape(chan_size, own, rows, size)
     pieces = [lax.dynamic_index_in_dim(packed, member ^ d, 0, keepdims=False) for d in distances]
-    pieces = lax.optimization_barrier(tuple(pieces) + tuple(arrived[0]))[: len(pieces)]
-    packed_arrived = [swap(piece, d) for piece, d in zip(pieces, distances)]
     table_re, table_im = projection_table(lag_cutoff[0], count, freq_size, pairs)
 
     local_block = lambda first: pl.BlockSpec(
@@ -269,7 +267,7 @@
     )
     other_block = pl.BlockSpec((step, 2, rows, size), lambda i, m: (i, 0, 0, 0))
     inverse_block = pl.BlockSpec((step, 2, size, 2 * size), lambda i, m: (i, 0, 0, 0))
-    state = []
+    state, packed_arrived = [], []
     for chunk in range(chunks):
         scale = lax.dynamic_slice_in_dim(guess_scale, member * own + chunk * part, part, 0)
         offset = chunk * part // step
@@ -296,6 +294,10 @@
             part * 6 * 4 * size * size,
             {6 + index: index for index in range(len(state))},
         )(members, scale, factors, *arrived[chunk], *state)
+        if chunk == 0:
+            held = lax.optimization_barrier(tuple(pieces) + tuple(state))
+            state = held[len(pieces) :]
+            packed_arrived = [swap(piece, d) for piece, d in zip(held, distances)]
     inverse, psi = state
 
     other = pl.BlockSpec((step, rows, size), lambda i, m: (i, 0, 0))

time: 135 us -> 134 us (level)
  starting transfers between devices: 29.4 us -> 28 us
where the time goes in v7:
time: 134 us; the launch traced here: 133 us
  blocking collectives  57.6 us (43%)
  starting transfers between devices  28 us (21%)
  Pallas kernels  22.2 us (17%)
  other arithmetic  12.7 us (9%)
  waiting for transfers between devices  9.19 us (7%)
  local copies, waits for them, and re-layouts  2.74 us (2%)
    all_to_all x1, blocking collectives, shards(): lax.all_to_all(causal, chan + ('freq',), 0, 0, tiled=True).astype(F32)  29.1 us
    all_to_all x1, blocking collectives, shards(): result = lax.all_to_all(result.astype(jnp.float16), chan, 0, 0, tiled=True)  28.5 us
    pallas_call x2, Pallas kernels, shards(): call(newton_kernel, part // step, [pl.BlockSpec(memory_space=pltpu.SMEM),...  13.6 us
    ppermute x3, starting transfers between devices, swap(): return lax.ppermute(value, 'pair', SWAP)  13.1 us
    select_n x1, other arithmetic, projection_table(): jnp.where(shift == 0, 0.0, (jnp.cos(half_angle) - jnp.cos(last_angle)) /...  8.24 us
    ppermute x3, starting transfers between devices, swap(): return lax.ppermute(value, 'side', SWAP)  6.97 us
    all_to_all x1, waiting for transfers between devices, shards(): lax.all_to_all(sent, chan + ('freq',), 0, 0, tiled=True).astype(F32)  6.44 us
    all_to_all x1, starting transfers between devices, shards(): lax.all_to_all(sent, chan + ('freq',), 0, 0, tiled=True).astype(F32)  4.86 us
  transfers between devices with their start and end apart: 10, of which 2 were waited for; matrix products, arithmetic and copies ran while one was open for 7% of the time, Pallas kernels for 10%

profile of v7, /device:TPU:0, one launch (start us, length us, event | category | flops | bytes accessed | tf_op | source)
XLA Modules:
  0.0 133.3 jit_solution(4027621438299327928)
XLA Ops:
  0.0 1.3 dynamic-slice_bitcast_fusion
  1.3 0.0 copy-start.1
  1.3 3.1 %collective-permute-start.3 = (bf16[8,2,32,128]{3,2,1,0:T(8,128)(2,1)S(1)}, bf16[8,2,32,128]{3,2,1,0:T(8,128)(2,1)S(1)}, u32[]{:S(2)}, u32[]{:S(2)}) collective-permute-start(bf16[8,2,32,128]{3,2,1,0:T(8,128)(2,1)S(1)} %get-tuple-element.25), channel_id=1, source_target_pairs={{0,1},{1,0},{2,3},{3,2},{4,5},{5,4},{6,7},{7,6},{8,9},{9,8},{10,11... | collective-permute-start | bytes 393224 | tf_op jit(solution)/shard_map/ppermute | solution.py:205
  4.4 2.6 %collective-permute-start.4 = (bf16[8,2,32,128]{3,2,1,0:T(8,128)(2,1)S(1)}, bf16[8,2,32,128]{3,2,1,0:T(8,128)(2,1)S(1)}, u32[]{:S(2)}, u32[]{:S(2)}) collective-permute-start(bf16[8,2,32,128]{3,2,1,0:T(8,128)(2,1)S(1)} %get-tuple-element.24), channel_id=1, source_target_pairs={{0,2},{2,0},{1,3},{3,1},{4,6},{6,4},{5,7},{7,5},{8,10},{10,8},{9,1... | collective-permute-start | bytes 393224 | tf_op jit(solution)/shard_map/ppermute | solution.py:207
  6.9 0.0 collective-permute-start.5
  7.0 0.9 collective-permute-start
  7.8 3.5 %collective-permute-start.1 = (bf16[8,2,32,128]{3,2,1,0:T(8,128)(2,1)S(1)}, bf16[8,2,32,128]{3,2,1,0:T(8,128)(2,1)S(1)}, u32[]{:S(2)}, u32[]{:S(2)}) collective-permute-start(bf16[8,2,32,128]{3,2,1,0:T(8,128)(2,1)S(1)} %get-tuple-element.27), channel_id=1, source_target_pairs={{0,2},{2,0},{1,3},{3,1},{4,6},{6,4},{5,7},{7,5},{8,10},{10,8},{9,1... | collective-permute-start | bytes 393224 | tf_op jit(solution)/shard_map/ppermute | solution.py:207
  11.3 0.1 iota_compare_fusion
  11.4 0.0 copy-start
  11.4 1.4 %fusion.29 = (bf16[64,1,32,128]{3,2,1,0:T(8,128)(2,1)S(1)}, bf16[64,1,32,128]{3,2,1,0:T(8,128)(2,1)S(1)}) fusion(bf16[64,2,32,128]{3,2,1,0:T(8,128)(2,1)} %param.5), kind=kLoop, calls=%fused_computation.59 | loop fusion | bytes 2097152 | tf_op jit(solution)/shard_map/slice | solution.py:260
  12.8 0.1 bitcast_select_fusion.own_ref
  12.9 0.0 copy-done.1
  12.9 0.1 fusion.30
  13.0 0.0 collective-permute-done.3.one_ref
  13.0 1.6 %collective-permute-start.2 = (bf16[8,2,32,128]{3,2,1,0:T(8,128)(2,1)S(1)}, bf16[8,2,32,128]{3,2,1,0:T(8,128)(2,1)S(1)}, u32[]{:S(2)}, u32[]{:S(2)}) collective-permute-start(bf16[8,2,32,128]{3,2,1,0:T(8,128)(2,1)S(1)} %get-tuple-element.26), channel_id=1, source_target_pairs={{0,3},{1,2},{2,1},{3,0},{4,7},{5,6},{6,5},{7,4},{8,11},{9,10},{10,... | collective-permute-start | bytes 393224 | tf_op jit(solution)/shard_map/ppermute | solution.py:208
  14.6 2.7 %collective-permute-done.4.two_ref = bf16[8,2,32,128]{3,2,1,0:T(8,128)(2,1)S(1)} collective-permute-done((bf16[8,2,32,128]{3,2,1,0:T(8,128)(2,1)S(1)}, bf16[8,2,32,128]{3,2,1,0:T(8,128)(2,1)S(1)}, u32[]{:S(2)}, u32[]{:S(2)}) %collective-permute-start.4) | collective-permute-done | bytes 131104 | tf_op jit(solution)/shard_map/ppermute | solution.py:207
  17.3 0.0 collective-permute-done.5.three_ref
  17.3 0.0 copy-done
  17.3 6.8 %shard_map.46 = (bf16[16,2,128,256]{3,2,1,0:T(8,128)(2,1)S(1)}, bf16[16,2,128,128]{3,2,1,0:T(8,128)(2,1)S(1)}) custom-call(s32[1]{0:T(128)} %bitcast.2.member_ref, f32[8]{0:T(128)S(1)} %get-tuple-element.36.scale_ref, bf16[4,16,2,32,128]{4,3,2,1,0:T(8,128)(2,1)S(1)} %bitcast.36, bf16[8,2,32,128]{3,2,1,0:T(8,128)(2,1)S(1)} %collective-permute-done.3.one_ref, ...), custom_call_target="tpu_custom_call" | custom-call | flops 8589934592 | bytes 3145728 | tf_op jit(solution)/shard_map/pallas_call | solution.py:274
  24.1 9.1 %collective-permute-start.6 = (bf16[16,32,128]{2,1,0:T(8,128)(2,1)S(1)}, bf16[16,32,128]{2,1,0:T(8,128)(2,1)S(1)}, u32[]{:S(2)}, u32[]{:S(2)}) collective-permute-start(bf16[16,32,128]{2,1,0:T(8,128)(2,1)S(1)} %get-tuple-element.19), channel_id=1, source_target_pairs={{0,1},{1,0},{2,3},{3,2},{4,5},{5,4},{6,7},{7,6},{8,9},{9,8},{10,11... | collective-permute-start | bytes 393224 | tf_op jit(solution)/shard_map/ppermute | solution.py:205
  33.2 0.9 collective-permute-start.7
  34.1 0.0 collective-permute-done.one_ref
  34.1 1.5 %collective-permute-start.8 = (bf16[16,32,128]{2,1,0:T(8,128)(2,1)S(1)}, bf16[16,32,128]{2,1,0:T(8,128)(2,1)S(1)}, u32[]{:S(2)}, u32[]{:S(2)}) collective-permute-start(bf16[16,32,128]{2,1,0:T(8,128)(2,1)S(1)} %get-tuple-element.21), channel_id=1, source_target_pairs={{0,3},{1,2},{2,1},{3,0},{4,7},{5,6},{6,5},{7,4},{8,11},{9,10},{10,... | collective-permute-start | bytes 393224 | tf_op jit(solution)/shard_map/ppermute | solution.py:208
  35.6 0.0 collective-permute-done.1.two_ref
  35.7 0.0 collective-permute-done.2.three_ref
  35.7 6.8 %shard_map.47 = (bf16[16,2,128,256]{3,2,1,0:T(8,128)(2,1)S(1)}, bf16[16,2,128,128]{3,2,1,0:T(8,128)(2,1)S(1)}) custom-call(s32[1]{0:T(128)} %bitcast.2.member_ref, f32[8]{0:T(128)S(1)} %get-tuple-element.37.scale_ref, bf16[4,16,2,32,128]{4,3,2,1,0:T(8,128)(2,1)S(1)} %bitcast.37, ...), custom_call_target="tpu_custom_call", output_to_operand_aliasing={{0}: (6, {}), {1}: (7, {})} | custom-call | flops 8589934592 | bytes 3145728 | tf_op jit(solution)/shard_map/pallas_call | solution.py:274
  42.5 0.0 collective-permute-done.6.one_ref
  42.5 0.0 collective-permute-done.7.two_ref
  42.5 0.0 collective-permute-done.8.three_ref
  42.5 3.5 %shard_map.48 = f32[2048,128]{1,0:T(8,128)S(1)} custom-call(s32[1]{0:T(128)} %bitcast.2.member_ref, bf16[16,2,128,256]{3,2,1,0:T(8,128)(2,1)S(1)} %get-tuple-element.18.inverse_ref, bf16[4,16,32,128]{3,2,1,0:T(8,128)(2,1)S(1)} %bitcast_select_fusion.own_ref, bf16[16,32,128]{2,1,0:T(8,128)(2,1)S(1)} %collective-permute-done.6.one_ref, ...), custom_call_target="tpu_custom_call" | custom-call | flops 2684354560 | bytes 6291456 | tf_op jit(solution)/shard_map/pallas_call | solution.py:304
  46.0 0.9 convert_element_type.34
  46.9 4.9 %all-to-all-start = ((f16[32,4,16,128]{3,2,1,0:T(8,128)(2,1)}), f16[32,4,16,128]{3,2,1,0:T(8,128)(2,1)}, u32[]{:S(2)}, u32[]{:S(2)}) async-start(f16[32,4,16,128]{3,2,1,0:T(8,128)(2,1)} %bitcast.15), calls=%async_computation | async-start | bytes 1048576 | tf_op jit(solution)/shard_map/all_to_all | solution.py:319
  52.4 8.2 %fusion.3 = (f32[512,512]{1,0:T(8,128)S(1)}, f32[512,512]{1,0:T(8,128)S(1)}) fusion(s32[512]{0:T(512)S(1)} %fusion.23, s32[]{:T(128)} %bitcast.1, f32[]{:T(128)} %bitcast), kind=kLoop, calls=%fused_computation.10 | loop fusion | flops 7340032 | bytes 2099208 | tf_op jit(solution)/shard_map/jit(_where)/select_n | solution.py:183
  60.6 6.4 %all-to-all-done = f16[32,4,16,128]{3,2,1,0:T(8,128)(2,1)} async-done(((f16[32,4,16,128]{3,2,1,0:T(8,128)(2,1)}), f16[32,4,16,128]{3,2,1,0:T(8,128)(2,1)}, u32[]{:S(2)}, u32[]{:S(2)}) %all-to-all-start) | async-done | bytes 524320 | tf_op jit(solution)/shard_map/all_to_all | solution.py:319
  67.1 1.1 convert_element_type.35.values_ref
  68.2 2.5 %shard_map.49 = f32[32,4,2,16,128]{4,3,2,1,0:T(8,128)S(1)} custom-call(f32[512,512]{1,0:T(8,128)S(1)} %get-tuple-element.35.real_ref, f32[512,512]{1,0:T(8,128)S(1)} %get-tuple-element.34.imag_ref, f32[32,4,16,128]{3,2,1,0:T(8,128)S(1)} %convert_element_type.35.values_ref), custom_call_target="tpu_custom_call" | custom-call | flops 1610612736 | bytes 3145728 | tf_op jit(solution)/shard_map/pallas_call | solution.py:326
  70.7 0.3 convert_element_type.36
  71.0 29.1 %all_to_all.15 = f16[32,4,2,16,128]{4,3,2,1,0:T(8,128)(2,1)S(1)} all-to-all(f16[32,4,2,16,128]{4,3,2,1,0:T(8,128)(2,1)S(1)} %convert_element_type.36), channel_id=1, replica_groups=mesh['freq'=8,'side'=2,'pair'=2] {'side','pair','freq'}, dimensions={0} | all-to-all | bytes 2097152 | tf_op jit(solution)/shard_map/all_to_all | solution.py:342
  100.1 0.2 bitcast_convert_fusion.causal_ref
  100.3 2.6 %shard_map.50 = f32[4,16,2,32,128]{4,3,2,1,0:T(8,128)S(1)} custom-call(f32[4096,128]{1,0:T(8,128)S(1)} %bitcast_convert_fusion.causal_ref, bf16[16,2,128,128]{3,2,1,0:T(8,128)(2,1)S(1)} %get-tuple-element.22.psi_ref), custom_call_target="tpu_custom_call" | custom-call | flops 536870912 | bytes 5242880 | tf_op jit(solution)/shard_map/pallas_call | solution.py:347
  102.9 0.3 convert_element_type.37
  103.2 28.5 %all_to_all.16 = f16[4,16,2,32,128]{4,3,2,1,0:T(8,128)(2,1)S(1)} all-to-all(f16[4,16,2,32,128]{4,3,2,1,0:T(8,128)(2,1)S(1)} %convert_element_type.37), channel_id=1, replica_groups=mesh['freq'=8,'side'=2,'pair'=2] {'side','pair'}, dimensions={0} | all-to-all | bytes 2097152 | tf_op jit(solution)/shard_map/all_to_all | solution.py:359
  131.7 1.6 %convert_multiply_fusion = f32[4,16,2,32,128]{4,3,2,1,0:T(8,128)} fusion(f16[4,16,2,32,128]{4,3,2,1,0:T(8,128)(2,1)S(1)} %all_to_all.16), kind=kLoop, calls=%fused_computation.1 | loop fusion | flops 1048576 | bytes 3145728 | tf_op jit(solution)/shard_map/mul | solution.py:360
  (3 shorter events, 0.0 us)
Async XLA Ops:
  1.3 11.6 %copy-start.1 = (f32[64]{0:T(128)S(1)}, f32[64]{0:T(128)}, u32[]{:S(2)}) copy-start(f32[64]{0:T(128)} %param.6) | copy-start | bytes 772
  1.3 11.7 %collective-permute-start.3 = (bf16[8,2,32,128]{3,2,1,0:T(8,128)(2,1)S(1)}, bf16[8,2,32,128]{3,2,1,0:T(8,128)(2,1)S(1)}, u32[]{:S(2)}, u32[]{:S(2)}) collective-permute-start(bf16[8,2,32,128]{3,2,1,0:T(8,128)(2,1)S(1)} %get-tuple-element.25), channel_id=1, source_target_pairs={{0,1},{1,0},{2,3},{3,2},{4,5},{5,4},{6,7},{7,6},{8,9},{9,8},{10,11... | collective-permute-start | bytes 393224 | tf_op jit(solution)/shard_map/ppermute | solution.py:205
  4.4 12.9 %collective-permute-start.4 = (bf16[8,2,32,128]{3,2,1,0:T(8,128)(2,1)S(1)}, bf16[8,2,32,128]{3,2,1,0:T(8,128)(2,1)S(1)}, u32[]{:S(2)}, u32[]{:S(2)}) collective-permute-start(bf16[8,2,32,128]{3,2,1,0:T(8,128)(2,1)S(1)} %get-tuple-element.24), channel_id=1, source_target_pairs={{0,2},{2,0},{1,3},{3,1},{4,6},{6,4},{5,7},{7,5},{8,10},{10,8},{9,1... | collective-permute-start | bytes 393224 | tf_op jit(solution)/shard_map/ppermute | solution.py:207
  6.9 10.4 %collective-permute-start.5 = (bf16[8,2,32,128]{3,2,1,0:T(8,128)(2,1)S(1)}, bf16[8,2,32,128]{3,2,1,0:T(8,128)(2,1)S(1)}, u32[]{:S(2)}, u32[]{:S(2)}) collective-permute-start(bf16[8,2,32,128]{3,2,1,0:T(8,128)(2,1)S(1)} %get-tuple-element.23), channel_id=1, source_target_pairs={{0,3},{1,2},{2,1},{3,0},{4,7},{5,6},{6,5},{7,4},{8,11},{9,10},{10,... | collective-permute-start | bytes 393224 | tf_op jit(solution)/shard_map/ppermute | solution.py:208
  7.0 27.2 %collective-permute-start = (bf16[8,2,32,128]{3,2,1,0:T(8,128)(2,1)S(1)}, bf16[8,2,32,128]{3,2,1,0:T(8,128)(2,1)S(1)}, u32[]{:S(2)}, u32[]{:S(2)}) collective-permute-start(bf16[8,2,32,128]{3,2,1,0:T(8,128)(2,1)S(1)} %get-tuple-element.28), channel_id=1, source_target_pairs={{0,1},{1,0},{2,3},{3,2},{4,5},{5,4},{6,7},{7,6},{8,9},{9,8},{10,11... | collective-permute-start | bytes 393224 | tf_op jit(solution)/shard_map/ppermute | solution.py:205
  7.8 27.8 %collective-permute-start.1 = (bf16[8,2,32,128]{3,2,1,0:T(8,128)(2,1)S(1)}, bf16[8,2,32,128]{3,2,1,0:T(8,128)(2,1)S(1)}, u32[]{:S(2)}, u32[]{:S(2)}) collective-permute-start(bf16[8,2,32,128]{3,2,1,0:T(8,128)(2,1)S(1)} %get-tuple-element.27), channel_id=1, source_target_pairs={{0,2},{2,0},{1,3},{3,1},{4,6},{6,4},{5,7},{7,5},{8,10},{10,8},{9,1... | collective-permute-start | bytes 393224 | tf_op jit(solution)/shard_map/ppermute | solution.py:207
  11.4 5.9 %copy-start = (bf16[64,2,32,128]{3,2,1,0:T(8,128)(2,1)S(1)}, bf16[64,2,32,128]{3,2,1,0:T(8,128)(2,1)}, u32[]{:S(2)}) copy-start(bf16[64,2,32,128]{3,2,1,0:T(8,128)(2,1)} %param.4) | copy-start | bytes 3145732
  13.0 22.7 %collective-permute-start.2 = (bf16[8,2,32,128]{3,2,1,0:T(8,128)(2,1)S(1)}, bf16[8,2,32,128]{3,2,1,0:T(8,128)(2,1)S(1)}, u32[]{:S(2)}, u32[]{:S(2)}) collective-permute-start(bf16[8,2,32,128]{3,2,1,0:T(8,128)(2,1)S(1)} %get-tuple-element.26), channel_id=1, source_target_pairs={{0,3},{1,2},{2,1},{3,0},{4,7},{5,6},{6,5},{7,4},{8,11},{9,10},{10,... | collective-permute-start | bytes 393224 | tf_op jit(solution)/shard_map/ppermute | solution.py:208
  24.1 18.4 %collective-permute-start.6 = (bf16[16,32,128]{2,1,0:T(8,128)(2,1)S(1)}, bf16[16,32,128]{2,1,0:T(8,128)(2,1)S(1)}, u32[]{:S(2)}, u32[]{:S(2)}) collective-permute-start(bf16[16,32,128]{2,1,0:T(8,128)(2,1)S(1)} %get-tuple-element.19), channel_id=1, source_target_pairs={{0,1},{1,0},{2,3},{3,2},{4,5},{5,4},{6,7},{7,6},{8,9},{9,8},{10,11... | collective-permute-start | bytes 393224 | tf_op jit(solution)/shard_map/ppermute | solution.py:205
  33.2 9.3 %collective-permute-start.7 = (bf16[16,32,128]{2,1,0:T(8,128)(2,1)S(1)}, bf16[16,32,128]{2,1,0:T(8,128)(2,1)S(1)}, u32[]{:S(2)}, u32[]{:S(2)}) collective-permute-start(bf16[16,32,128]{2,1,0:T(8,128)(2,1)S(1)} %get-tuple-element.20), channel_id=1, source_target_pairs={{0,2},{2,0},{1,3},{3,1},{4,6},{6,4},{5,7},{7,5},{8,10},{10,8},{9,1... | collective-permute-start | bytes 393224 | tf_op jit(solution)/shard_map/ppermute | solution.py:207
  34.1 8.4 %collective-permute-start.8 = (bf16[16,32,128]{2,1,0:T(8,128)(2,1)S(1)}, bf16[16,32,128]{2,1,0:T(8,128)(2,1)S(1)}, u32[]{:S(2)}, u32[]{:S(2)}) collective-permute-start(bf16[16,32,128]{2,1,0:T(8,128)(2,1)S(1)} %get-tuple-element.21), channel_id=1, source_target_pairs={{0,3},{1,2},{2,1},{3,0},{4,7},{5,6},{6,5},{7,4},{8,11},{9,10},{10,... | collective-permute-start | bytes 393224 | tf_op jit(solution)/shard_map/ppermute | solution.py:208
  46.9 20.2 %all-to-all-start = ((f16[32,4,16,128]{3,2,1,0:T(8,128)(2,1)}), f16[32,4,16,128]{3,2,1,0:T(8,128)(2,1)}, u32[]{:S(2)}, u32[]{:S(2)}) async-start(f16[32,4,16,128]{3,2,1,0:T(8,128)(2,1)} %bitcast.15), calls=%async_computation | async-start | bytes 1048576 | tf_op jit(solution)/shard_map/all_to_all | solution.py:319

commit v8 on v7

--- a/solution.py
+++ b/solution.py
@@ -254,6 +254,8 @@
     arrived = []
     for chunk in range(chunks):
         pieces = [rows_for(member ^ d, chunk * part, part) for d in distances]
+        if arrived:
+            pieces = lax.optimization_barrier((*pieces, arrived[-1][0]))[: len(pieces)]
         arrived.append([swap(piece, d) for piece, d in zip(pieces, distances)])
     row_index = lax.broadcasted_iota(jnp.int32, (rows, size), 0) + member * rows
     column_index = lax.broadcasted_iota(jnp.int32, (rows, size), 1)
@@ -356,9 +358,17 @@
         compiler_params=params(16),
         cost_estimate=cost(own * 4 * 4 * size**3, own * 5 * 4 * size * size),
     )(back, psi)
-    result = lax.all_to_all(result.astype(jnp.float16), chan, 0, 0, tiled=True)
-    whole = result.reshape(group_bins, 2, rows, size).astype(F32) * SCALE
-    return jnp.swapaxes(whole, 2, 3)
+    panels = [
+        lax.dynamic_index_in_dim(result, member ^ d, 0, keepdims=False) for d in range(chan_size)
+    ]
+    panels[1:] = [swap(panels[d].astype(jnp.float16), d).astype(F32) for d in distances]
+    owners = []
+    for owner in range(chan_size):
+        distance = member ^ owner
+        low = jnp.where(distance % 2 == 0, panels[0], panels[1])
+        high = jnp.where(distance % 2 == 0, panels[2], panels[3])
+        owners.append(jnp.where(distance < 2, low, high))
+    return jnp.swapaxes(cat(owners, 0) * SCALE, 2, 3)
 
 
 def solution(mesh):

time: 134 us -> 131 us (0.978)
  the two profiles are of different devices: /device:TPU:0 before, /device:TPU:10 now
where the time goes in v8:
time: 131 us; the launch traced here: 130 us
  waiting for transfers between devices  41.2 us (31%)
  blocking collectives  29.3 us (22%)
  Pallas kernels  22.2 us (17%)
  starting transfers between devices  20.8 us (16%)
  other arithmetic  13.6 us (10%)
  local copies, waits for them, and re-layouts  2.38 us (2%)
    all_to_all x1, blocking collectives, shards(): lax.all_to_all(causal, chan + ('freq',), 0, 0, tiled=True).astype(F32)  29.3 us
    ppermute x4, waiting for transfers between devices, swap(): return lax.ppermute(value, ('side', 'pair'), FLIP)  17.1 us
    ppermute x4, waiting for transfers between devices, swap(): return lax.ppermute(value, 'side', SWAP)  17 us
    pallas_call x2, Pallas kernels, shards(): call(newton_kernel, part // step, [pl.BlockSpec(memory_space=pltpu.SMEM),...  13.6 us
    ppermute x4, starting transfers between devices, swap(): return lax.ppermute(value, 'side', SWAP)  9.37 us
    select_n x1, other arithmetic, projection_table(): jnp.where(shift == 0, 0.0, (jnp.cos(half_angle) - jnp.cos(last_angle)) /...  8.24 us
    all_to_all x1, starting transfers between devices, shards(): lax.all_to_all(sent, chan + ('freq',), 0, 0, tiled=True).astype(F32)  5.06 us
    all_to_all x1, waiting for transfers between devices, shards(): lax.all_to_all(sent, chan + ('freq',), 0, 0, tiled=True).astype(F32)  5.01 us
  transfers between devices with their start and end apart: 13, of which 7 were waited for; matrix products, arithmetic and copies ran while one was open for 7% of the time, Pallas kernels for 10%

profile of v8, /device:TPU:10, one launch (start us, length us, event | category | flops | bytes accessed | tf_op | source)
XLA Modules:
  0.0 130.4 jit_solution(2681786790177165824)
XLA Ops:
  0.0 0.0 copy-start.1
  0.0 2.2 %dynamic-slice_bitcast_fusion = (bf16[8,2,32,128]{3,2,1,0:T(8,128)(2,1)}, bf16[8,2,32,128]{3,2,1,0:T(8,128)(2,1)}, bf16[8,2,32,128]{3,2,1,0:T(8,128)(2,1)}, bf16...) fusion(bf16[4,16,2,32,128]{4,3,2,1,0:T(8,128)(2,1)} %bitcast.45, ...), kind=kLoop, calls=%fused_computation.44 | loop fusion | bytes 1572876 | tf_op jit(solution)/shard_map/reshape | solution.py:252
  2.2 0.0 copy-start.5
  2.2 0.4 collective-permute-start
  2.6 2.6 %collective-permute-start.4 = (bf16[8,2,32,128]{3,2,1,0:T(8,128)(2,1)}, bf16[8,2,32,128]{3,2,1,0:T(8,128)(2,1)S(1)}, u32[]{:S(2)}, u32[]{:S(2)}) collective-permute-start(bf16[8,2,32,128]{3,2,1,0:T(8,128)(2,1)} %get-tuple-element.37), channel_id=1, source_target_pairs={{0,2},{2,0},{1,3},{3,1},{4,6},{6,4},{5,7},{7,5},{8,10},{10,8},{9,1... | collective-permute-start | bytes 393224 | tf_op jit(solution)/shard_map/ppermute | solution.py:207
  5.2 0.5 collective-permute-start.5
  5.7 0.1 iota_compare_fusion
  5.7 0.0 copy-done.1
  5.7 0.0 copy-start
  5.8 0.1 fusion.37
  5.8 0.0 copy-start.4
  5.8 0.0 copy-start.3
  5.9 0.0 copy-start.2
  5.9 0.1 bitcast_select_fusion.own_ref
  5.9 0.0 copy-done.5
  5.9 0.1 fusion.38
  6.1 2.0 %collective-permute-done.one_ref = bf16[8,2,32,128]{3,2,1,0:T(8,128)(2,1)S(1)} collective-permute-done((bf16[8,2,32,128]{3,2,1,0:T(8,128)(2,1)}, bf16[8,2,32,128]{3,2,1,0:T(8,128)(2,1)S(1)}, u32[]{:S(2)}, u32[]{:S(2)}) %collective-permute-start) | collective-permute-done | bytes 131104 | tf_op jit(solution)/shard_map/ppermute | solution.py:205
  8.1 0.0 copy-done.4
  8.1 1.6 %collective-permute-start.1 = (bf16[8,2,32,128]{3,2,1,0:T(8,128)(2,1)S(1)}, bf16[8,2,32,128]{3,2,1,0:T(8,128)(2,1)S(1)}, u32[]{:S(2)}, u32[]{:S(2)}) collective-permute-start(bf16[8,2,32,128]{3,2,1,0:T(8,128)(2,1)S(1)} %copy-done.4), channel_id=1, source_target_pairs={{0,1},{1,0},{2,3},{3,2},{4,5},{5,4},{6,7},{7,6},{8,9},{9,8},{10,11... | collective-permute-start | bytes 393224 | tf_op jit(solution)/shard_map/ppermute | solution.py:205
  9.7 0.0 copy-done.3
  9.7 2.2 %collective-permute-start.2 = (bf16[8,2,32,128]{3,2,1,0:T(8,128)(2,1)S(1)}, bf16[8,2,32,128]{3,2,1,0:T(8,128)(2,1)S(1)}, u32[]{:S(2)}, u32[]{:S(2)}) collective-permute-start(bf16[8,2,32,128]{3,2,1,0:T(8,128)(2,1)S(1)} %copy-done.3), channel_id=1, source_target_pairs={{0,2},{2,0},{1,3},{3,1},{4,6},{6,4},{5,7},{7,5},{8,10},{10,8},{9,1... | collective-permute-start | bytes 393224 | tf_op jit(solution)/shard_map/ppermute | solution.py:207
  11.9 0.0 copy-done.2
  11.9 0.6 collective-permute-start.3
  12.4 2.7 %collective-permute-done.4.two_ref = bf16[8,2,32,128]{3,2,1,0:T(8,128)(2,1)S(1)} collective-permute-done((bf16[8,2,32,128]{3,2,1,0:T(8,128)(2,1)}, bf16[8,2,32,128]{3,2,1,0:T(8,128)(2,1)S(1)}, u32[]{:S(2)}, u32[]{:S(2)}) %collective-permute-start.4) | collective-permute-done | bytes 131104 | tf_op jit(solution)/shard_map/ppermute | solution.py:207
  15.2 9.2 %collective-permute-done.5.three_ref = bf16[8,2,32,128]{3,2,1,0:T(8,128)(2,1)S(1)} collective-permute-done((bf16[8,2,32,128]{3,2,1,0:T(8,128)(2,1)}, bf16[8,2,32,128]{3,2,1,0:T(8,128)(2,1)S(1)}, u32[]{:S(2)}, u32[]{:S(2)}) %collective-permute-start.5) | collective-permute-done | bytes 131104 | tf_op jit(solution)/shard_map/ppermute | solution.py:208
  24.3 0.0 copy-done
  24.3 6.8 %shard_map.46 = (bf16[16,2,128,256]{3,2,1,0:T(8,128)(2,1)S(1)}, bf16[16,2,128,128]{3,2,1,0:T(8,128)(2,1)S(1)}) custom-call(s32[1]{0:T(128)} %bitcast.2.member_ref, f32[8]{0:T(128)S(1)} %get-tuple-element.49.scale_ref, bf16[4,16,2,32,128]{4,3,2,1,0:T(8,128)(2,1)S(1)} %bitcast.46, bf16[8,2,32,128]{3,2,1,0:T(8,128)(2,1)S(1)} %collective-permute-done.one_ref, ...), custom_call_target="tpu_custom_call" | custom-call | flops 8589934592 | bytes 3145728 | tf_op jit(solution)/shard_map/pallas_call | solution.py:276
  31.1 0.1 collective-permute-start.6
  31.2 2.9 %collective-permute-start.7 = (bf16[16,32,128]{2,1,0:T(8,128)(2,1)S(1)}, bf16[16,32,128]{2,1,0:T(8,128)(2,1)S(1)}, u32[]{:S(2)}, u32[]{:S(2)}) collective-permute-start(bf16[16,32,128]{2,1,0:T(8,128)(2,1)S(1)} %get-tuple-element.26), channel_id=1, source_target_pairs={{0,2},{2,0},{1,3},{3,1},{4,6},{6,4},{5,7},{7,5},{8,10},{10,8},{9,1... | collective-permute-start | bytes 393224 | tf_op jit(solution)/shard_map/ppermute | solution.py:207
  34.1 0.0 collective-permute-done.1.one_ref
  34.1 0.6 collective-permute-start.8
  34.7 0.0 collective-permute-done.2.two_ref
  34.7 0.0 collective-permute-done.3.three_ref
  34.7 6.8 %shard_map.47 = (bf16[16,2,128,256]{3,2,1,0:T(8,128)(2,1)S(1)}, bf16[16,2,128,128]{3,2,1,0:T(8,128)(2,1)S(1)}) custom-call(s32[1]{0:T(128)} %bitcast.2.member_ref, f32[8]{0:T(128)S(1)} %get-tuple-element.50.scale_ref, bf16[4,16,2,32,128]{4,3,2,1,0:T(8,128)(2,1)S(1)} %bitcast.47, ...), custom_call_target="tpu_custom_call", output_to_operand_aliasing={{0}: (6, {}), {1}: (7, {})} | custom-call | flops 8589934592 | bytes 3145728 | tf_op jit(solution)/shard_map/pallas_call | solution.py:276
  41.5 0.0 collective-permute-done.6.one_ref
  41.5 0.0 collective-permute-done.7.two_ref
  41.5 0.3 collective-permute-done.8.three_ref
  41.8 3.5 %shard_map.48 = f32[2048,128]{1,0:T(8,128)S(1)} custom-call(s32[1]{0:T(128)} %bitcast.2.member_ref, bf16[16,2,128,256]{3,2,1,0:T(8,128)(2,1)S(1)} %get-tuple-element.24.inverse_ref, bf16[4,16,32,128]{3,2,1,0:T(8,128)(2,1)S(1)} %bitcast_select_fusion.own_ref, bf16[16,32,128]{2,1,0:T(8,128)(2,1)S(1)} %collective-permute-done.6.one_ref, ...), custom_call_target="tpu_custom_call" | custom-call | flops 2684354560 | bytes 6291456 | tf_op jit(solution)/shard_map/pallas_call | solution.py:306
  45.4 0.9 convert_element_type.54
  46.2 5.1 %all-to-all-start = ((f16[32,4,16,128]{3,2,1,0:T(8,128)(2,1)}), f16[32,4,16,128]{3,2,1,0:T(8,128)(2,1)}, u32[]{:S(2)}, u32[]{:S(2)}) async-start(f16[32,4,16,128]{3,2,1,0:T(8,128)(2,1)} %bitcast.15), calls=%async_computation | async-start | bytes 1048576 | tf_op jit(solution)/shard_map/all_to_all | solution.py:321
  52.0 8.2 %fusion.4 = (f32[512,512]{1,0:T(8,128)S(1)}, f32[512,512]{1,0:T(8,128)S(1)}) fusion(s32[512]{0:T(512)S(1)} %fusion.31, s32[]{:T(128)} %bitcast.1, f32[]{:T(128)} %bitcast), kind=kLoop, calls=%fused_computation.11 | loop fusion | flops 7340032 | bytes 2099208 | tf_op jit(solution)/shard_map/jit(_where)/select_n | solution.py:183
  60.2 5.0 %all-to-all-done = f16[32,4,16,128]{3,2,1,0:T(8,128)(2,1)} async-done(((f16[32,4,16,128]{3,2,1,0:T(8,128)(2,1)}), f16[32,4,16,128]{3,2,1,0:T(8,128)(2,1)}, u32[]{:S(2)}, u32[]{:S(2)}) %all-to-all-start) | async-done | bytes 524320 | tf_op jit(solution)/shard_map/all_to_all | solution.py:321
  65.2 1.1 convert_element_type.55.values_ref
  66.3 2.5 %shard_map.49 = f32[32,4,2,16,128]{4,3,2,1,0:T(8,128)S(1)} custom-call(f32[512,512]{1,0:T(8,128)S(1)} %get-tuple-element.48.real_ref, f32[512,512]{1,0:T(8,128)S(1)} %get-tuple-element.47.imag_ref, f32[32,4,16,128]{3,2,1,0:T(8,128)S(1)} %convert_element_type.55.values_ref), custom_call_target="tpu_custom_call" | custom-call | flops 1610612736 | bytes 3145728 | tf_op jit(solution)/shard_map/pallas_call | solution.py:328
  68.8 0.3 convert_element_type.56
  69.1 29.3 %all_to_all.10 = f16[32,4,2,16,128]{4,3,2,1,0:T(8,128)(2,1)S(1)} all-to-all(f16[32,4,2,16,128]{4,3,2,1,0:T(8,128)(2,1)S(1)} %convert_element_type.56), channel_id=1, replica_groups=mesh['freq'=8,'side'=2,'pair'=2] {'side','pair','freq'}, dimensions={0} | all-to-all | bytes 2097152 | tf_op jit(solution)/shard_map/all_to_all | solution.py:344
  98.4 0.2 bitcast_convert_fusion.causal_ref
  98.6 2.6 %shard_map.50 = f32[4,16,2,32,128]{4,3,2,1,0:T(8,128)S(1)} custom-call(f32[4096,128]{1,0:T(8,128)S(1)} %bitcast_convert_fusion.causal_ref, bf16[16,2,128,128]{3,2,1,0:T(8,128)(2,1)S(1)} %get-tuple-element.28.psi_ref), custom_call_target="tpu_custom_call" | custom-call | flops 536870912 | bytes 5242880 | tf_op jit(solution)/shard_map/pallas_call | solution.py:349
  101.3 0.9 fusion.22
  102.2 1.7 %collective-permute-start.10 = (f16[16,2,32,128]{3,2,1,0:T(8,128)(2,1)}, f16[16,2,32,128]{3,2,1,0:T(8,128)(2,1)S(1)}, u32[]{:S(2)}, u32[]{:S(2)}) collective-permute-start(f16[16,2,32,128]{3,2,1,0:T(8,128)(2,1)} %get-tuple-element.33), channel_id=1, source_target_pairs={{0,2},{2,0},{1,3},{3,1},{4,6},{6,4},{5,7},{7,5},{8,10},{10,8},{9,1... | collective-permute-start | bytes 786440 | tf_op jit(solution)/shard_map/ppermute | solution.py:207
  103.9 1.5 %collective-permute-start.11 = (f16[16,2,32,128]{3,2,1,0:T(8,128)(2,1)S(1)}, f16[16,2,32,128]{3,2,1,0:T(8,128)(2,1)S(1)}, u32[]{:S(2)}, u32[]{:S(2)}) collective-permute-start(f16[16,2,32,128]{3,2,1,0:T(8,128)(2,1)S(1)} %get-tuple-element.34), channel_id=1, source_target_pairs={{0,3},{1,2},{2,1},{3,0},{4,7},{5,6},{6,5},{7,4},{8,11},{9,10},{10,... | collective-permute-start | bytes 786440 | tf_op jit(solution)/shard_map/ppermute | solution.py:208
  105.4 1.2 collective-permute-start.9
  106.6 14.3 %collective-permute-done.10 = f16[16,2,32,128]{3,2,1,0:T(8,128)(2,1)S(1)} collective-permute-done((f16[16,2,32,128]{3,2,1,0:T(8,128)(2,1)}, f16[16,2,32,128]{3,2,1,0:T(8,128)(2,1)S(1)}, u32[]{:S(2)}, u32[]{:S(2)}) %collective-permute-start.10) | collective-permute-done | bytes 262176 | tf_op jit(solution)/shard_map/ppermute | solution.py:207
  120.9 7.6 %collective-permute-done.11 = f16[16,2,32,128]{3,2,1,0:T(8,128)(2,1)S(1)} collective-permute-done((f16[16,2,32,128]{3,2,1,0:T(8,128)(2,1)S(1)}, f16[16,2,32,128]{3,2,1,0:T(8,128)(2,1)S(1)}, u32[]{:S(2)}, u32[]{:S(2)}) %collective-permute-start.11) | collective-permute-done | bytes 262176 | tf_op jit(solution)/shard_map/ppermute | solution.py:208
  128.5 0.0 collective-permute-done.9
  128.5 0.3 fusion.17
  128.8 1.6 %fusion = f32[64,2,128,32]{2,3,1,0:T(8,128)} fusion(f32[16,2,32,128]{3,2,1,0:T(8,128)S(1)} %get-tuple-element.32, f32[16,2,32,128]{3,2,1,0:T(8,128)S(1)} %get-tuple-element.31, f32[16,2,32,128]{3,2,1,0:T(8,128)S(1)} %get-tuple-element.30, f32[16,2,32,128]{3,2,1,0:T(8,128)S(1)} %get-tuple-element.29), kind=kLoop, calls=%fused_computation.2 | loop fusion | flops 2097152 | bytes 4194304 | tf_op jit(solution)/shard_map/transpose | solution.py:371
  (3 shorter events, 0.0 us)
Async XLA Ops:
  0.0 5.7 %copy-start.1 = (bf16[64,2,32,128]{3,2,1,0:T(8,128)(2,1)S(1)}, bf16[64,2,32,128]{3,2,1,0:T(8,128)(2,1)}, u32[]{:S(2)}) copy-start(bf16[64,2,32,128]{3,2,1,0:T(8,128)(2,1)} %param.5) | copy-start | bytes 3145732
  2.2 3.8 %copy-start.5 = (f32[64]{0:T(128)S(1)}, f32[64]{0:T(128)}, u32[]{:S(2)}) copy-start(f32[64]{0:T(128)} %param.6) | copy-start | bytes 772
  2.2 5.9 %collective-permute-start = (bf16[8,2,32,128]{3,2,1,0:T(8,128)(2,1)}, bf16[8,2,32,128]{3,2,1,0:T(8,128)(2,1)S(1)}, u32[]{:S(2)}, u32[]{:S(2)}) collective-permute-start(bf16[8,2,32,128]{3,2,1,0:T(8,128)(2,1)} %get-tuple-element.38), channel_id=1, source_target_pairs={{0,1},{1,0},{2,3},{3,2},{4,5},{5,4},{6,7},{7,6},{8,9},{9,8},{10,11... | collective-permute-start | bytes 393224 | tf_op jit(solution)/shard_map/ppermute | solution.py:205
  2.6 12.5 %collective-permute-start.4 = (bf16[8,2,32,128]{3,2,1,0:T(8,128)(2,1)}, bf16[8,2,32,128]{3,2,1,0:T(8,128)(2,1)S(1)}, u32[]{:S(2)}, u32[]{:S(2)}) collective-permute-start(bf16[8,2,32,128]{3,2,1,0:T(8,128)(2,1)} %get-tuple-element.37), channel_id=1, source_target_pairs={{0,2},{2,0},{1,3},{3,1},{4,6},{6,4},{5,7},{7,5},{8,10},{10,8},{9,1... | collective-permute-start | bytes 393224 | tf_op jit(solution)/shard_map/ppermute | solution.py:207
  5.2 19.1 %collective-permute-start.5 = (bf16[8,2,32,128]{3,2,1,0:T(8,128)(2,1)}, bf16[8,2,32,128]{3,2,1,0:T(8,128)(2,1)S(1)}, u32[]{:S(2)}, u32[]{:S(2)}) collective-permute-start(bf16[8,2,32,128]{3,2,1,0:T(8,128)(2,1)} %get-tuple-element.36), channel_id=1, source_target_pairs={{0,3},{1,2},{2,1},{3,0},{4,7},{5,6},{6,5},{7,4},{8,11},{9,10},{10,... | collective-permute-start | bytes 393224 | tf_op jit(solution)/shard_map/ppermute | solution.py:208
  5.7 18.6 %copy-start = (bf16[64,2,32,128]{3,2,1,0:T(8,128)(2,1)S(1)}, bf16[64,2,32,128]{3,2,1,0:T(8,128)(2,1)}, u32[]{:S(2)}) copy-start(bf16[64,2,32,128]{3,2,1,0:T(8,128)(2,1)} %param.4) | copy-start | bytes 3145732
  5.8 2.3 %copy-start.4 = (bf16[8,2,32,128]{3,2,1,0:T(8,128)(2,1)S(1)}, bf16[8,2,32,128]{3,2,1,0:T(8,128)(2,1)}, u32[]{:S(2)}) copy-start(bf16[8,2,32,128]{3,2,1,0:T(8,128)(2,1)} %get-tuple-element.17) | copy-start | bytes 393220
  5.8 3.8 %copy-start.3 = (bf16[8,2,32,128]{3,2,1,0:T(8,128)(2,1)S(1)}, bf16[8,2,32,128]{3,2,1,0:T(8,128)(2,1)}, u32[]{:S(2)}) copy-start(bf16[8,2,32,128]{3,2,1,0:T(8,128)(2,1)} %get-tuple-element.18) | copy-start | bytes 393220
  5.9 6.0 %copy-start.2 = (bf16[8,2,32,128]{3,2,1,0:T(8,128)(2,1)S(1)}, bf16[8,2,32,128]{3,2,1,0:T(8,128)(2,1)}, u32[]{:S(2)}) copy-start(bf16[8,2,32,128]{3,2,1,0:T(8,128)(2,1)} %get-tuple-element.19) | copy-start | bytes 393220
  8.1 26.0 %collective-permute-start.1 = (bf16[8,2,32,128]{3,2,1,0:T(8,128)(2,1)S(1)}, bf16[8,2,32,128]{3,2,1,0:T(8,128)(2,1)S(1)}, u32[]{:S(2)}, u32[]{:S(2)}) collective-permute-start(bf16[8,2,32,128]{3,2,1,0:T(8,128)(2,1)S(1)} %copy-done.4), channel_id=1, source_target_pairs={{0,1},{1,0},{2,3},{3,2},{4,5},{5,4},{6,7},{7,6},{8,9},{9,8},{10,11... | collective-permute-start | bytes 393224 | tf_op jit(solution)/shard_map/ppermute | solution.py:205
  9.7 25.0 %collective-permute-start.2 = (bf16[8,2,32,128]{3,2,1,0:T(8,128)(2,1)S(1)}, bf16[8,2,32,128]{3,2,1,0:T(8,128)(2,1)S(1)}, u32[]{:S(2)}, u32[]{:S(2)}) collective-permute-start(bf16[8,2,32,128]{3,2,1,0:T(8,128)(2,1)S(1)} %copy-done.3), channel_id=1, source_target_pairs={{0,2},{2,0},{1,3},{3,1},{4,6},{6,4},{5,7},{7,5},{8,10},{10,8},{9,1... | collective-permute-start | bytes 393224 | tf_op jit(solution)/shard_map/ppermute | solution.py:207
  11.9 22.8 %collective-permute-start.3 = (bf16[8,2,32,128]{3,2,1,0:T(8,128)(2,1)S(1)}, bf16[8,2,32,128]{3,2,1,0:T(8,128)(2,1)S(1)}, u32[]{:S(2)}, u32[]{:S(2)}) collective-permute-start(bf16[8,2,32,128]{3,2,1,0:T(8,128)(2,1)S(1)} %copy-done.2), channel_id=1, source_target_pairs={{0,3},{1,2},{2,1},{3,0},{4,7},{5,6},{6,5},{7,4},{8,11},{9,10},{10,... | collective-permute-start | bytes 393224 | tf_op jit(solution)/shard_map/ppermute | solution.py:208
  31.1 10.4 %collective-permute-start.6 = (bf16[16,32,128]{2,1,0:T(8,128)(2,1)S(1)}, bf16[16,32,128]{2,1,0:T(8,128)(2,1)S(1)}, u32[]{:S(2)}, u32[]{:S(2)}) collective-permute-start(bf16[16,32,128]{2,1,0:T(8,128)(2,1)S(1)} %get-tuple-element.25), channel_id=1, source_target_pairs={{0,1},{1,0},{2,3},{3,2},{4,5},{5,4},{6,7},{7,6},{8,9},{9,8},{10,11... | collective-permute-start | bytes 393224 | tf_op jit(solution)/shard_map/ppermute | solution.py:205
  31.2 10.3 %collective-permute-start.7 = (bf16[16,32,128]{2,1,0:T(8,128)(2,1)S(1)}, bf16[16,32,128]{2,1,0:T(8,128)(2,1)S(1)}, u32[]{:S(2)}, u32[]{:S(2)}) collective-permute-start(bf16[16,32,128]{2,1,0:T(8,128)(2,1)S(1)} %get-tuple-element.26), channel_id=1, source_target_pairs={{0,2},{2,0},{1,3},{3,1},{4,6},{6,4},{5,7},{7,5},{8,10},{10,8},{9,1... | collective-permute-start | bytes 393224 | tf_op jit(solution)/shard_map/ppermute | solution.py:207
  34.1 7.8 %collective-permute-start.8 = (bf16[16,32,128]{2,1,0:T(8,128)(2,1)S(1)}, bf16[16,32,128]{2,1,0:T(8,128)(2,1)S(1)}, u32[]{:S(2)}, u32[]{:S(2)}) collective-permute-start(bf16[16,32,128]{2,1,0:T(8,128)(2,1)S(1)} %get-tuple-element.27), channel_id=1, source_target_pairs={{0,3},{1,2},{2,1},{3,0},{4,7},{5,6},{6,5},{7,4},{8,11},{9,10},{10,... | collective-permute-start | bytes 393224 | tf_op jit(solution)/shard_map/ppermute | solution.py:208
  46.2 19.0 %all-to-all-start = ((f16[32,4,16,128]{3,2,1,0:T(8,128)(2,1)}), f16[32,4,16,128]{3,2,1,0:T(8,128)(2,1)}, u32[]{:S(2)}, u32[]{:S(2)}) async-start(f16[32,4,16,128]{3,2,1,0:T(8,128)(2,1)} %bitcast.15), calls=%async_computation | async-start | bytes 1048576 | tf_op jit(solution)/shard_map/all_to_all | solution.py:321
  102.2 18.7 %collective-permute-start.10 = (f16[16,2,32,128]{3,2,1,0:T(8,128)(2,1)}, f16[16,2,32,128]{3,2,1,0:T(8,128)(2,1)S(1)}, u32[]{:S(2)}, u32[]{:S(2)}) collective-permute-start(f16[16,2,32,128]{3,2,1,0:T(8,128)(2,1)} %get-tuple-element.33), channel_id=1, source_target_pairs={{0,2},{2,0},{1,3},{3,1},{4,6},{6,4},{5,7},{7,5},{8,10},{10,8},{9,1... | collective-permute-start | bytes 786440 | tf_op jit(solution)/shard_map/ppermute | solution.py:207
  103.9 24.6 %collective-permute-start.11 = (f16[16,2,32,128]{3,2,1,0:T(8,128)(2,1)S(1)}, f16[16,2,32,128]{3,2,1,0:T(8,128)(2,1)S(1)}, u32[]{:S(2)}, u32[]{:S(2)}) collective-permute-start(f16[16,2,32,128]{3,2,1,0:T(8,128)(2,1)S(1)} %get-tuple-element.34), channel_id=1, source_target_pairs={{0,3},{1,2},{2,1},{3,0},{4,7},{5,6},{6,5},{7,4},{8,11},{9,10},{10,... | collective-permute-start | bytes 786440 | tf_op jit(solution)/shard_map/ppermute | solution.py:208
  105.4 23.1 %collective-permute-start.9 = (f16[16,2,32,128]{3,2,1,0:T(8,128)(2,1)S(1)}, f16[16,2,32,128]{3,2,1,0:T(8,128)(2,1)S(1)}, u32[]{:S(2)}, u32[]{:S(2)}) collective-permute-start(f16[16,2,32,128]{3,2,1,0:T(8,128)(2,1)S(1)} %get-tuple-element.35), channel_id=1, source_target_pairs={{0,1},{1,0},{2,3},{3,2},{4,5},{5,4},{6,7},{7,6},{8,9},{9,8},{10,11... | collective-permute-start | bytes 786440 | tf_op jit(solution)/shard_map/ppermute | solution.py:205

commit v9 on v8

--- a/solution.py
+++ b/solution.py
@@ -147,10 +147,10 @@
                 out_ref[:, item, part] = piece[:, chunk * step : (chunk + 1) * step]
 
 
-def product_kernel(causal_ref, psi_ref, out_ref):
+def product_kernel(member_ref, causal_ref, psi_ref, out_ref):
     bins, _, size, _ = psi_ref.shape
     total_bins = causal_ref.shape[0] // (2 * size)
-    shape = (out_ref.shape[0], out_ref.shape[3], size)
+    rows = out_ref.shape[3]
     for item in range(bins):
         re, im = psi_ref[item, 0], psi_ref[item, 1]
         place = pl.program_id(0) * bins + item
@@ -160,8 +160,10 @@
         high, low = split(0.5 * cat([taken.T + added, added.T - taken], 1))
         both = dot(cat([high, low], 0), cat([cat([re, -im], 1), cat([im, re], 1)], 0), NT)
         result = both[:size] + both[size:]
-        out_ref[:, item, 0] = result[:, :size].reshape(shape)
-        out_ref[:, item, 1] = result[:, size:].reshape(shape)
+        for panel in range(out_ref.shape[0]):
+            piece = result[panel * rows : (panel + 1) * rows]
+            out_ref[member_ref[0] ^ panel, item, 0] = piece[:, :size]
+            out_ref[member_ref[0] ^ panel, item, 1] = piece[:, size:]
 
 
 def projection_table(lag_limit, count, freq_size, pairs):
@@ -254,8 +256,6 @@
     arrived = []
     for chunk in range(chunks):
         pieces = [rows_for(member ^ d, chunk * part, part) for d in distances]
-        if arrived:
-            pieces = lax.optimization_barrier((*pieces, arrived[-1][0]))[: len(pieces)]
         arrived.append([swap(piece, d) for piece, d in zip(pieces, distances)])
     row_index = lax.broadcasted_iota(jnp.int32, (rows, size), 0) + member * rows
     column_index = lax.broadcasted_iota(jnp.int32, (rows, size), 1)
@@ -346,22 +346,21 @@
         back = back.reshape(chan_size * column_parts, lane_parts, kept, 2, own, lanes)
         back = back.transpose(0, 2, 3, 4, 1, 5)
     back = back.reshape(size * 2 * own, size)
-    result = pl.pallas_call(
+    result = call(
         product_kernel,
-        grid=(own // step,),
-        in_specs=[
-            pl.BlockSpec(back.shape, lambda i: (0, 0)),
-            pl.BlockSpec((step, 2, size, size), lambda i: (i, 0, 0, 0)),
+        own // step,
+        [
+            pl.BlockSpec(back.shape, lambda i, m: (0, 0)),
+            pl.BlockSpec((step, 2, size, size), lambda i, m: (i, 0, 0, 0)),
         ],
-        out_specs=pl.BlockSpec((chan_size, step, 2, rows, size), lambda i: (0, i, 0, 0, 0)),
-        out_shape=jax.ShapeDtypeStruct((chan_size, own, 2, rows, size), F32),
-        compiler_params=params(16),
-        cost_estimate=cost(own * 4 * 4 * size**3, own * 5 * 4 * size * size),
-    )(back, psi)
-    panels = [
-        lax.dynamic_index_in_dim(result, member ^ d, 0, keepdims=False) for d in range(chan_size)
-    ]
-    panels[1:] = [swap(panels[d].astype(jnp.float16), d).astype(F32) for d in distances]
+        pl.BlockSpec((chan_size, step, 2, rows, size), lambda i, m: (0, i, 0, 0, 0)),
+        jax.ShapeDtypeStruct((chan_size, own, 2, rows, size), F32),
+        [],
+        own * 4 * 4 * size**3,
+        own * 5 * 4 * size * size,
+    )(members, back, psi)
+    panels = [result[0]]
+    panels += [swap(result[d].astype(jnp.float16), d).astype(F32) for d in distances]
     owners = []
     for owner in range(chan_size):
         distance = member ^ owner

time: 131 us -> 130 us (level)
  the two profiles are of different devices: /device:TPU:10 before, /device:TPU:0 now
where the time goes in v9:
time: 130 us; the launch traced here: 127 us
  starting transfers between devices  31.6 us (24%)
  blocking collectives  29.1 us (22%)
  waiting for transfers between devices  26.9 us (21%)
  Pallas kernels  22.2 us (17%)
  other arithmetic  13.9 us (11%)
  local copies, waits for them, and re-layouts  2.94 us (2%)
    all_to_all x1, blocking collectives, shards(): lax.all_to_all(causal, chan + ('freq',), 0, 0, tiled=True).astype(F32)  29.1 us
    ppermute x4, waiting for transfers between devices, swap(): return lax.ppermute(value, 'side', SWAP)  20.2 us
    pallas_call x2, Pallas kernels, shards(): call(newton_kernel, part // step, [pl.BlockSpec(memory_space=pltpu.SMEM),...  13.6 us
    ppermute x4, starting transfers between devices, swap(): return lax.ppermute(value, 'pair', SWAP)  13.4 us
    select_n x1, other arithmetic, projection_table(): jnp.where(shift == 0, 0.0, (jnp.cos(half_angle) - jnp.cos(last_angle)) /...  8.24 us
    ppermute x4, starting transfers between devices, swap(): return lax.ppermute(value, 'side', SWAP)  7.79 us
    all_to_all x1, waiting for transfers between devices, shards(): lax.all_to_all(sent, chan + ('freq',), 0, 0, tiled=True).astype(F32)  6.44 us
    ppermute x4, starting transfers between devices, swap(): return lax.ppermute(value, ('side', 'pair'), FLIP)  5.49 us
  transfers between devices with their start and end apart: 13, of which 4 were waited for; matrix products, arithmetic and copies ran while one was open for 8% of the time, Pallas kernels for 11%

profile of v9, /device:TPU:0, one launch (start us, length us, event | category | flops | bytes accessed | tf_op | source)
XLA Modules:
  0.0 127.4 jit_solution(16429165965900689062)
XLA Ops:
  0.0 1.3 dynamic-slice_bitcast_fusion
  1.3 0.0 copy-start.1
  1.3 3.1 %collective-permute-start.3 = (bf16[8,2,32,128]{3,2,1,0:T(8,128)(2,1)S(1)}, bf16[8,2,32,128]{3,2,1,0:T(8,128)(2,1)S(1)}, u32[]{:S(2)}, u32[]{:S(2)}) collective-permute-start(bf16[8,2,32,128]{3,2,1,0:T(8,128)(2,1)S(1)} %get-tuple-element.32), channel_id=1, source_target_pairs={{0,1},{1,0},{2,3},{3,2},{4,5},{5,4},{6,7},{7,6},{8,9},{9,8},{10,11... | collective-permute-start | bytes 393224 | tf_op jit(solution)/shard_map/ppermute | solution.py:207
  4.4 2.6 %collective-permute-start.4 = (bf16[8,2,32,128]{3,2,1,0:T(8,128)(2,1)S(1)}, bf16[8,2,32,128]{3,2,1,0:T(8,128)(2,1)S(1)}, u32[]{:S(2)}, u32[]{:S(2)}) collective-permute-start(bf16[8,2,32,128]{3,2,1,0:T(8,128)(2,1)S(1)} %get-tuple-element.31), channel_id=1, source_target_pairs={{0,2},{2,0},{1,3},{3,1},{4,6},{6,4},{5,7},{7,5},{8,10},{10,8},{9,1... | collective-permute-start | bytes 393224 | tf_op jit(solution)/shard_map/ppermute | solution.py:209
  6.9 0.0 collective-permute-start.5
  7.0 0.9 collective-permute-start
  7.8 3.5 %collective-permute-start.1 = (bf16[8,2,32,128]{3,2,1,0:T(8,128)(2,1)S(1)}, bf16[8,2,32,128]{3,2,1,0:T(8,128)(2,1)S(1)}, u32[]{:S(2)}, u32[]{:S(2)}) collective-permute-start(bf16[8,2,32,128]{3,2,1,0:T(8,128)(2,1)S(1)} %get-tuple-element.34), channel_id=1, source_target_pairs={{0,2},{2,0},{1,3},{3,1},{4,6},{6,4},{5,7},{7,5},{8,10},{10,8},{9,1... | collective-permute-start | bytes 393224 | tf_op jit(solution)/shard_map/ppermute | solution.py:209
  11.3 0.1 iota_compare_fusion
  11.4 0.0 copy-start
  11.4 1.4 %fusion.34 = (bf16[64,1,32,128]{3,2,1,0:T(8,128)(2,1)S(1)}, bf16[64,1,32,128]{3,2,1,0:T(8,128)(2,1)S(1)}) fusion(bf16[64,2,32,128]{3,2,1,0:T(8,128)(2,1)} %param.5), kind=kLoop, calls=%fused_computation.76 | loop fusion | bytes 2097152 | tf_op jit(solution)/shard_map/slice | solution.py:262
  12.8 0.1 bitcast_select_fusion.own_ref
  12.9 0.0 copy-done.1
  12.9 0.1 fusion.35
  13.0 0.0 collective-permute-done.3.one_ref
  13.0 1.6 %collective-permute-start.2 = (bf16[8,2,32,128]{3,2,1,0:T(8,128)(2,1)S(1)}, bf16[8,2,32,128]{3,2,1,0:T(8,128)(2,1)S(1)}, u32[]{:S(2)}, u32[]{:S(2)}) collective-permute-start(bf16[8,2,32,128]{3,2,1,0:T(8,128)(2,1)S(1)} %get-tuple-element.33), channel_id=1, source_target_pairs={{0,3},{1,2},{2,1},{3,0},{4,7},{5,6},{6,5},{7,4},{8,11},{9,10},{10,... | collective-permute-start | bytes 393224 | tf_op jit(solution)/shard_map/ppermute | solution.py:210
  14.6 2.7 %collective-permute-done.4.two_ref = bf16[8,2,32,128]{3,2,1,0:T(8,128)(2,1)S(1)} collective-permute-done((bf16[8,2,32,128]{3,2,1,0:T(8,128)(2,1)S(1)}, bf16[8,2,32,128]{3,2,1,0:T(8,128)(2,1)S(1)}, u32[]{:S(2)}, u32[]{:S(2)}) %collective-permute-start.4) | collective-permute-done | bytes 131104 | tf_op jit(solution)/shard_map/ppermute | solution.py:209
  17.3 0.0 collective-permute-done.5.three_ref
  17.3 0.0 copy-done
  17.3 6.8 %shard_map.46 = (bf16[16,2,128,256]{3,2,1,0:T(8,128)(2,1)S(1)}, bf16[16,2,128,128]{3,2,1,0:T(8,128)(2,1)S(1)}) custom-call(s32[1]{0:T(128)} %bitcast.member_ref, f32[8]{0:T(128)S(1)} %get-tuple-element.43.scale_ref, bf16[4,16,2,32,128]{4,3,2,1,0:T(8,128)(2,1)S(1)} %bitcast.51, bf16[8,2,32,128]{3,2,1,0:T(8,128)(2,1)S(1)} %collective-permute-done.3.one_ref, ...), custom_call_target="tpu_custom_call" | custom-call | flops 8589934592 | bytes 3145728 | tf_op jit(solution)/shard_map/pallas_call | solution.py:276
  24.1 9.1 %collective-permute-start.6 = (bf16[16,32,128]{2,1,0:T(8,128)(2,1)S(1)}, bf16[16,32,128]{2,1,0:T(8,128)(2,1)S(1)}, u32[]{:S(2)}, u32[]{:S(2)}) collective-permute-start(bf16[16,32,128]{2,1,0:T(8,128)(2,1)S(1)} %get-tuple-element.19), channel_id=1, source_target_pairs={{0,1},{1,0},{2,3},{3,2},{4,5},{5,4},{6,7},{7,6},{8,9},{9,8},{10,11... | collective-permute-start | bytes 393224 | tf_op jit(solution)/shard_map/ppermute | solution.py:207
  33.2 0.9 collective-permute-start.7
  34.1 0.0 collective-permute-done.one_ref
  34.1 1.5 %collective-permute-start.8 = (bf16[16,32,128]{2,1,0:T(8,128)(2,1)S(1)}, bf16[16,32,128]{2,1,0:T(8,128)(2,1)S(1)}, u32[]{:S(2)}, u32[]{:S(2)}) collective-permute-start(bf16[16,32,128]{2,1,0:T(8,128)(2,1)S(1)} %get-tuple-element.21), channel_id=1, source_target_pairs={{0,3},{1,2},{2,1},{3,0},{4,7},{5,6},{6,5},{7,4},{8,11},{9,10},{10,... | collective-permute-start | bytes 393224 | tf_op jit(solution)/shard_map/ppermute | solution.py:210
  35.6 0.0 collective-permute-done.1.two_ref
  35.7 0.0 collective-permute-done.2.three_ref
  35.7 6.8 %shard_map.47 = (bf16[16,2,128,256]{3,2,1,0:T(8,128)(2,1)S(1)}, bf16[16,2,128,128]{3,2,1,0:T(8,128)(2,1)S(1)}) custom-call(s32[1]{0:T(128)} %bitcast.member_ref, f32[8]{0:T(128)S(1)} %get-tuple-element.44.scale_ref, bf16[4,16,2,32,128]{4,3,2,1,0:T(8,128)(2,1)S(1)} %bitcast.52, ...), custom_call_target="tpu_custom_call", output_to_operand_aliasing={{0}: (6, {}), {1}: (7, {})} | custom-call | flops 8589934592 | bytes 3145728 | tf_op jit(solution)/shard_map/pallas_call | solution.py:276
  42.5 0.0 collective-permute-done.6.one_ref
  42.5 0.0 collective-permute-done.7.two_ref
  42.5 0.0 collective-permute-done.8.three_ref
  42.5 3.5 %shard_map.48 = f32[2048,128]{1,0:T(8,128)S(1)} custom-call(s32[1]{0:T(128)} %bitcast.member_ref, bf16[16,2,128,256]{3,2,1,0:T(8,128)(2,1)S(1)} %get-tuple-element.18.inverse_ref, bf16[4,16,32,128]{3,2,1,0:T(8,128)(2,1)S(1)} %bitcast_select_fusion.own_ref, bf16[16,32,128]{2,1,0:T(8,128)(2,1)S(1)} %collective-permute-done.6.one_ref, ...), custom_call_target="tpu_custom_call" | custom-call | flops 2684354560 | bytes 6291456 | tf_op jit(solution)/shard_map/pallas_call | solution.py:306
  46.0 0.9 convert_element_type.48
  46.9 4.9 %all-to-all-start = ((f16[32,4,16,128]{3,2,1,0:T(8,128)(2,1)}), f16[32,4,16,128]{3,2,1,0:T(8,128)(2,1)}, u32[]{:S(2)}, u32[]{:S(2)}) async-start(f16[32,4,16,128]{3,2,1,0:T(8,128)(2,1)} %bitcast.15), calls=%async_computation | async-start | bytes 1048576 | tf_op jit(solution)/shard_map/all_to_all | solution.py:321
  52.4 8.2 %fusion.4 = (f32[512,512]{1,0:T(8,128)S(1)}, f32[512,512]{1,0:T(8,128)S(1)}) fusion(s32[512]{0:T(512)S(1)} %fusion.28, s32[]{:T(128)} %bitcast.2, f32[]{:T(128)} %bitcast.1), kind=kLoop, calls=%fused_computation.11 | loop fusion | flops 7340032 | bytes 2099208 | tf_op jit(solution)/shard_map/jit(_where)/select_n | solution.py:185
  60.6 6.4 %all-to-all-done = f16[32,4,16,128]{3,2,1,0:T(8,128)(2,1)} async-done(((f16[32,4,16,128]{3,2,1,0:T(8,128)(2,1)}), f16[32,4,16,128]{3,2,1,0:T(8,128)(2,1)}, u32[]{:S(2)}, u32[]{:S(2)}) %all-to-all-start) | async-done | bytes 524320 | tf_op jit(solution)/shard_map/all_to_all | solution.py:321
  67.1 1.1 convert_element_type.49.values_ref
  68.2 2.5 %shard_map.49 = f32[32,4,2,16,128]{4,3,2,1,0:T(8,128)S(1)} custom-call(f32[512,512]{1,0:T(8,128)S(1)} %get-tuple-element.42.real_ref, f32[512,512]{1,0:T(8,128)S(1)} %get-tuple-element.41.imag_ref, f32[32,4,16,128]{3,2,1,0:T(8,128)S(1)} %convert_element_type.49.values_ref), custom_call_target="tpu_custom_call" | custom-call | flops 1610612736 | bytes 3145728 | tf_op jit(solution)/shard_map/pallas_call | solution.py:328
  70.7 0.3 convert_element_type.50
  71.0 29.1 %all_to_all.10 = f16[32,4,2,16,128]{4,3,2,1,0:T(8,128)(2,1)S(1)} all-to-all(f16[32,4,2,16,128]{4,3,2,1,0:T(8,128)(2,1)S(1)} %convert_element_type.50), channel_id=1, replica_groups=mesh['freq'=8,'side'=2,'pair'=2] {'side','pair','freq'}, dimensions={0} | all-to-all | bytes 2097152 | tf_op jit(solution)/shard_map/all_to_all | solution.py:344
  100.1 0.2 bitcast_convert_fusion.causal_ref
  100.3 2.6 %shard_map.50 = f32[4,16,2,32,128]{4,3,2,1,0:T(8,128)S(1)} custom-call(s32[1]{0:T(128)} %bitcast.member_ref, f32[4096,128]{1,0:T(8,128)S(1)} %bitcast_convert_fusion.causal_ref, bf16[16,2,128,128]{3,2,1,0:T(8,128)(2,1)S(1)} %get-tuple-element.22.psi_ref), custom_call_target="tpu_custom_call" | custom-call | flops 536870912 | bytes 5242880 | tf_op jit(solution)/shard_map/pallas_call | solution.py:349
  102.9 0.3 convert.6
  103.2 0.2 slice_bitcast_fusion.2
  103.4 0.8 collective-permute-start.10
  104.2 2.4 %collective-permute-start.11 = (f16[16,2,32,128]{3,2,1,0:T(8,128)(2,1)S(1)}, f16[16,2,32,128]{3,2,1,0:T(8,128)(2,1)S(1)}, u32[]{:S(2)}, u32[]{:S(2)}) collective-permute-start(f16[16,2,32,128]{3,2,1,0:T(8,128)(2,1)S(1)} %get-tuple-element.28), channel_id=1, source_target_pairs={{0,3},{1,2},{2,1},{3,0},{4,7},{5,6},{6,5},{7,4},{8,11},{9,10},{10,... | collective-permute-start | bytes 786440 | tf_op jit(solution)/shard_map/ppermute | solution.py:210
  106.6 0.4 collective-permute-start.9
  106.9 17.4 %collective-permute-done.10 = f16[16,2,32,128]{3,2,1,0:T(8,128)(2,1)S(1)} collective-permute-done((f16[16,2,32,128]{3,2,1,0:T(8,128)(2,1)S(1)}, f16[16,2,32,128]{3,2,1,0:T(8,128)(2,1)S(1)}, u32[]{:S(2)}, u32[]{:S(2)}) %collective-permute-start.10) | collective-permute-done | bytes 262176 | tf_op jit(solution)/shard_map/ppermute | solution.py:209
  124.4 0.0 collective-permute-done.11
  124.4 0.2 collective-permute-done.9
  124.6 1.3 fusion.17
  125.9 1.6 %fusion = f32[64,2,128,32]{2,3,1,0:T(8,128)} fusion(f32[16,2,32,128]{3,2,1,0:T(8,128)S(1)} %get-tuple-element.26, f32[16,2,32,128]{3,2,1,0:T(8,128)S(1)} %get-tuple-element.25, f32[16,2,32,128]{3,2,1,0:T(8,128)S(1)} %get-tuple-element.24, f32[16,2,32,128]{3,2,1,0:T(8,128)S(1)} %get-tuple-element.23), kind=kLoop, calls=%fused_computation.2 | loop fusion | flops 2097152 | bytes 4194304 | tf_op jit(solution)/shard_map/transpose | solution.py:370
  (3 shorter events, 0.0 us)
Async XLA Ops:
  1.3 11.6 %copy-start.1 = (f32[64]{0:T(128)S(1)}, f32[64]{0:T(128)}, u32[]{:S(2)}) copy-start(f32[64]{0:T(128)} %param.6) | copy-start | bytes 772
  1.3 11.7 %collective-permute-start.3 = (bf16[8,2,32,128]{3,2,1,0:T(8,128)(2,1)S(1)}, bf16[8,2,32,128]{3,2,1,0:T(8,128)(2,1)S(1)}, u32[]{:S(2)}, u32[]{:S(2)}) collective-permute-start(bf16[8,2,32,128]{3,2,1,0:T(8,128)(2,1)S(1)} %get-tuple-element.32), channel_id=1, source_target_pairs={{0,1},{1,0},{2,3},{3,2},{4,5},{5,4},{6,7},{7,6},{8,9},{9,8},{10,11... | collective-permute-start | bytes 393224 | tf_op jit(solution)/shard_map/ppermute | solution.py:207
  4.4 12.9 %collective-permute-start.4 = (bf16[8,2,32,128]{3,2,1,0:T(8,128)(2,1)S(1)}, bf16[8,2,32,128]{3,2,1,0:T(8,128)(2,1)S(1)}, u32[]{:S(2)}, u32[]{:S(2)}) collective-permute-start(bf16[8,2,32,128]{3,2,1,0:T(8,128)(2,1)S(1)} %get-tuple-element.31), channel_id=1, source_target_pairs={{0,2},{2,0},{1,3},{3,1},{4,6},{6,4},{5,7},{7,5},{8,10},{10,8},{9,1... | collective-permute-start | bytes 393224 | tf_op jit(solution)/shard_map/ppermute | solution.py:209
  6.9 10.4 %collective-permute-start.5 = (bf16[8,2,32,128]{3,2,1,0:T(8,128)(2,1)S(1)}, bf16[8,2,32,128]{3,2,1,0:T(8,128)(2,1)S(1)}, u32[]{:S(2)}, u32[]{:S(2)}) collective-permute-start(bf16[8,2,32,128]{3,2,1,0:T(8,128)(2,1)S(1)} %get-tuple-element.30), channel_id=1, source_target_pairs={{0,3},{1,2},{2,1},{3,0},{4,7},{5,6},{6,5},{7,4},{8,11},{9,10},{10,... | collective-permute-start | bytes 393224 | tf_op jit(solution)/shard_map/ppermute | solution.py:210
  7.0 27.2 %collective-permute-start = (bf16[8,2,32,128]{3,2,1,0:T(8,128)(2,1)S(1)}, bf16[8,2,32,128]{3,2,1,0:T(8,128)(2,1)S(1)}, u32[]{:S(2)}, u32[]{:S(2)}) collective-permute-start(bf16[8,2,32,128]{3,2,1,0:T(8,128)(2,1)S(1)} %get-tuple-element.35), channel_id=1, source_target_pairs={{0,1},{1,0},{2,3},{3,2},{4,5},{5,4},{6,7},{7,6},{8,9},{9,8},{10,11... | collective-permute-start | bytes 393224 | tf_op jit(solution)/shard_map/ppermute | solution.py:207
  7.8 27.8 %collective-permute-start.1 = (bf16[8,2,32,128]{3,2,1,0:T(8,128)(2,1)S(1)}, bf16[8,2,32,128]{3,2,1,0:T(8,128)(2,1)S(1)}, u32[]{:S(2)}, u32[]{:S(2)}) collective-permute-start(bf16[8,2,32,128]{3,2,1,0:T(8,128)(2,1)S(1)} %get-tuple-element.34), channel_id=1, source_target_pairs={{0,2},{2,0},{1,3},{3,1},{4,6},{6,4},{5,7},{7,5},{8,10},{10,8},{9,1... | collective-permute-start | bytes 393224 | tf_op jit(solution)/shard_map/ppermute | solution.py:209
  11.4 5.9 %copy-start = (bf16[64,2,32,128]{3,2,1,0:T(8,128)(2,1)S(1)}, bf16[64,2,32,128]{3,2,1,0:T(8,128)(2,1)}, u32[]{:S(2)}) copy-start(bf16[64,2,32,128]{3,2,1,0:T(8,128)(2,1)} %param.4) | copy-start | bytes 3145732
  13.0 22.7 %collective-permute-start.2 = (bf16[8,2,32,128]{3,2,1,0:T(8,128)(2,1)S(1)}, bf16[8,2,32,128]{3,2,1,0:T(8,128)(2,1)S(1)}, u32[]{:S(2)}, u32[]{:S(2)}) collective-permute-start(bf16[8,2,32,128]{3,2,1,0:T(8,128)(2,1)S(1)} %get-tuple-element.33), channel_id=1, source_target_pairs={{0,3},{1,2},{2,1},{3,0},{4,7},{5,6},{6,5},{7,4},{8,11},{9,10},{10,... | collective-permute-start | bytes 393224 | tf_op jit(solution)/shard_map/ppermute | solution.py:210
  24.1 18.4 %collective-permute-start.6 = (bf16[16,32,128]{2,1,0:T(8,128)(2,1)S(1)}, bf16[16,32,128]{2,1,0:T(8,128)(2,1)S(1)}, u32[]{:S(2)}, u32[]{:S(2)}) collective-permute-start(bf16[16,32,128]{2,1,0:T(8,128)(2,1)S(1)} %get-tuple-element.19), channel_id=1, source_target_pairs={{0,1},{1,0},{2,3},{3,2},{4,5},{5,4},{6,7},{7,6},{8,9},{9,8},{10,11... | collective-permute-start | bytes 393224 | tf_op jit(solution)/shard_map/ppermute | solution.py:207
  33.2 9.3 %collective-permute-start.7 = (bf16[16,32,128]{2,1,0:T(8,128)(2,1)S(1)}, bf16[16,32,128]{2,1,0:T(8,128)(2,1)S(1)}, u32[]{:S(2)}, u32[]{:S(2)}) collective-permute-start(bf16[16,32,128]{2,1,0:T(8,128)(2,1)S(1)} %get-tuple-element.20), channel_id=1, source_target_pairs={{0,2},{2,0},{1,3},{3,1},{4,6},{6,4},{5,7},{7,5},{8,10},{10,8},{9,1... | collective-permute-start | bytes 393224 | tf_op jit(solution)/shard_map/ppermute | solution.py:209
  34.1 8.4 %collective-permute-start.8 = (bf16[16,32,128]{2,1,0:T(8,128)(2,1)S(1)}, bf16[16,32,128]{2,1,0:T(8,128)(2,1)S(1)}, u32[]{:S(2)}, u32[]{:S(2)}) collective-permute-start(bf16[16,32,128]{2,1,0:T(8,128)(2,1)S(1)} %get-tuple-element.21), channel_id=1, source_target_pairs={{0,3},{1,2},{2,1},{3,0},{4,7},{5,6},{6,5},{7,4},{8,11},{9,10},{10,... | collective-permute-start | bytes 393224 | tf_op jit(solution)/shard_map/ppermute | solution.py:210
  46.9 20.2 %all-to-all-start = ((f16[32,4,16,128]{3,2,1,0:T(8,128)(2,1)}), f16[32,4,16,128]{3,2,1,0:T(8,128)(2,1)}, u32[]{:S(2)}, u32[]{:S(2)}) async-start(f16[32,4,16,128]{3,2,1,0:T(8,128)(2,1)} %bitcast.15), calls=%async_computation | async-start | bytes 1048576 | tf_op jit(solution)/shard_map/all_to_all | solution.py:321
  103.4 21.0 %collective-permute-start.10 = (f16[16,2,32,128]{3,2,1,0:T(8,128)(2,1)S(1)}, f16[16,2,32,128]{3,2,1,0:T(8,128)(2,1)S(1)}, u32[]{:S(2)}, u32[]{:S(2)}) collective-permute-start(f16[16,2,32,128]{3,2,1,0:T(8,128)(2,1)S(1)} %get-tuple-element.27), channel_id=1, source_target_pairs={{0,2},{2,0},{1,3},{3,1},{4,6},{6,4},{5,7},{7,5},{8,10},{10,8},{9,1... | collective-permute-start | bytes 786440 | tf_op jit(solution)/shard_map/ppermute | solution.py:209
  104.2 20.2 %collective-permute-start.11 = (f16[16,2,32,128]{3,2,1,0:T(8,128)(2,1)S(1)}, f16[16,2,32,128]{3,2,1,0:T(8,128)(2,1)S(1)}, u32[]{:S(2)}, u32[]{:S(2)}) collective-permute-start(f16[16,2,32,128]{3,2,1,0:T(8,128)(2,1)S(1)} %get-tuple-element.28), channel_id=1, source_target_pairs={{0,3},{1,2},{2,1},{3,0},{4,7},{5,6},{6,5},{7,4},{8,11},{9,10},{10,... | collective-permute-start | bytes 786440 | tf_op jit(solution)/shard_map/ppermute | solution.py:210
  106.6 18.0 %collective-permute-start.9 = (f16[16,2,32,128]{3,2,1,0:T(8,128)(2,1)S(1)}, f16[16,2,32,128]{3,2,1,0:T(8,128)(2,1)}, u32[]{:S(2)}, u32[]{:S(2)}) collective-permute-start(f16[16,2,32,128]{3,2,1,0:T(8,128)(2,1)S(1)} %get-tuple-element.29), channel_id=1, source_target_pairs={{0,1},{1,0},{2,3},{3,2},{4,5},{5,4},{6,7},{7,6},{8,9},{9,8},{10,11... | collective-permute-start | bytes 786440 | tf_op jit(solution)/shard_map/ppermute | solution.py:207

commit v10 on v9

--- a/solution.py
+++ b/solution.py
@@ -256,6 +256,8 @@
     arrived = []
     for chunk in range(chunks):
         pieces = [rows_for(member ^ d, chunk * part, part) for d in distances]
+        if arrived:
+            pieces = lax.optimization_barrier((*pieces, *arrived[-1]))[: len(pieces)]
         arrived.append([swap(piece, d) for piece, d in zip(pieces, distances)])
     row_index = lax.broadcasted_iota(jnp.int32, (rows, size), 0) + member * rows
     column_index = lax.broadcasted_iota(jnp.int32, (rows, size), 1)
@@ -359,7 +361,7 @@
         own * 4 * 4 * size**3,
         own * 5 * 4 * size * size,
     )(members, back, psi)
-    panels = [result[0]]
+    panels = [lax.optimization_barrier(result[0])]
     panels += [swap(result[d].astype(jnp.float16), d).astype(F32) for d in distances]
     owners = []
     for owner in range(chan_size):

time: 130 us -> 134 us (1.031)
  waiting for transfers between devices: 26.9 us -> 36.5 us
  starting transfers between devices: 31.6 us -> 25.7 us
    ppermute x4, waiting for transfers between devices: 20.2 us -> 27.6 us  [swap(): return lax.ppermute(value, 'side', SWAP)]
    ppermute x4, starting transfers between devices: 13.4 us -> 6.37 us  [swap(): return lax.ppermute(value, 'pair', SWAP)]
    all_to_all x1, starting transfers between devices: 4.87 us -> 7.6 us  [shards(): lax.all_to_all(sent, chan + ('freq',), 0, 0, tiled=True).astype(F32)]
    ppermute x4, waiting for transfers between devices: 0.22 us -> 2.48 us  [swap(): return lax.ppermute(value, 'pair', SWAP)]
  transfers between devices with their start and end apart: 13 -> 13, of which waited for: 4 -> 6; matrix products, arithmetic and copies ran while one was open for 8% -> 7% of each run, Pallas kernels for 11% -> 10%
where the time goes in v10:
time: 134 us; the launch traced here: 131 us
  waiting for transfers between devices  36.5 us (27%)
  blocking collectives  29.1 us (22%)
  starting transfers between devices  25.7 us (19%)
  Pallas kernels  22.2 us (17%)
  other arithmetic  13.9 us (10%)
  local copies, waits for them, and re-layouts  2.61 us (2%)
    all_to_all x1, blocking collectives, shards(): lax.all_to_all(causal, chan + ('freq',), 0, 0, tiled=True).astype(F32)  29.1 us
    ppermute x4, waiting for transfers between devices, swap(): return lax.ppermute(value, 'side', SWAP)  27.6 us
    pallas_call x2, Pallas kernels, shards(): call(newton_kernel, part // step, [pl.BlockSpec(memory_space=pltpu.SMEM),...  13.6 us
    select_n x1, other arithmetic, projection_table(): jnp.where(shift == 0, 0.0, (jnp.cos(half_angle) - jnp.cos(last_angle)) /...  8.24 us
    all_to_all x1, starting transfers between devices, shards(): lax.all_to_all(sent, chan + ('freq',), 0, 0, tiled=True).astype(F32)  7.6 us
    ppermute x4, starting transfers between devices, swap(): return lax.ppermute(value, 'side', SWAP)  6.47 us
    all_to_all x1, waiting for transfers between devices, shards(): lax.all_to_all(sent, chan + ('freq',), 0, 0, tiled=True).astype(F32)  6.44 us
    ppermute x4, starting transfers between devices, swap(): return lax.ppermute(value, 'pair', SWAP)  6.37 us
  transfers between devices with their start and end apart: 13, of which 6 were waited for; matrix products, arithmetic and copies ran while one was open for 7% of the time, Pallas kernels for 10%

profile of v10, /device:TPU:0, one launch (start us, length us, event | category | flops | bytes accessed | tf_op | source)
XLA Modules:
  0.0 131.0 jit_solution(9309438647637165008)
XLA Ops:
  0.0 0.0 copy-start.1
  0.0 2.2 %dynamic-slice_bitcast_fusion.3 = (bf16[8,2,32,128]{3,2,1,0:T(8,128)(2,1)}, bf16[8,2,32,128]{3,2,1,0:T(8,128)(2,1)}, bf16[8,2,32,128]{3,2,1,0:T(8,128)(2,1)}, bf...) fusion(bf16[4,16,2,32,128]{4,3,2,1,0:T(8,128)(2,1)} %bitcast.42, ...), kind=kLoop, calls=%fused_computation.45 | loop fusion | bytes 1572876 | tf_op jit(solution)/shard_map/reshape | solution.py:254
  2.2 0.0 copy-start.5
  2.2 3.0 %collective-permute-start = (bf16[8,2,32,128]{3,2,1,0:T(8,128)(2,1)}, bf16[8,2,32,128]{3,2,1,0:T(8,128)(2,1)S(1)}, u32[]{:S(2)}, u32[]{:S(2)}) collective-permute-start(bf16[8,2,32,128]{3,2,1,0:T(8,128)(2,1)} %get-tuple-element.40), channel_id=1, source_target_pairs={{0,1},{1,0},{2,3},{3,2},{4,5},{5,4},{6,7},{7,6},{8,9},{9,8},{10,11... | collective-permute-start | bytes 393224 | tf_op jit(solution)/shard_map/ppermute | solution.py:207
  5.2 2.6 %collective-permute-start.1 = (bf16[8,2,32,128]{3,2,1,0:T(8,128)(2,1)}, bf16[8,2,32,128]{3,2,1,0:T(8,128)(2,1)S(1)}, u32[]{:S(2)}, u32[]{:S(2)}) collective-permute-start(bf16[8,2,32,128]{3,2,1,0:T(8,128)(2,1)} %get-tuple-element.39), channel_id=1, source_target_pairs={{0,2},{2,0},{1,3},{3,1},{4,6},{6,4},{5,7},{7,5},{8,10},{10,8},{9,1... | collective-permute-start | bytes 393224 | tf_op jit(solution)/shard_map/ppermute | solution.py:209
  7.8 0.0 collective-permute-start.2
  7.8 0.1 iota_compare_fusion
  7.9 0.0 copy-done.1
  7.9 0.0 copy-start
  7.9 0.1 fusion.34
  8.0 0.0 copy-start.4
  8.0 0.0 copy-start.3
  8.0 0.0 copy-start.2
  8.0 0.1 bitcast_select_fusion.own_ref
  8.1 0.0 copy-done.5
  8.1 0.1 fusion.35
  8.2 2.3 %collective-permute-done.one_ref = bf16[8,2,32,128]{3,2,1,0:T(8,128)(2,1)S(1)} collective-permute-done((bf16[8,2,32,128]{3,2,1,0:T(8,128)(2,1)}, bf16[8,2,32,128]{3,2,1,0:T(8,128)(2,1)S(1)}, u32[]{:S(2)}, u32[]{:S(2)}) %collective-permute-start) | collective-permute-done | bytes 131104 | tf_op jit(solution)/shard_map/ppermute | solution.py:207
  10.4 7.9 %collective-permute-done.1.two_ref = bf16[8,2,32,128]{3,2,1,0:T(8,128)(2,1)S(1)} collective-permute-done((bf16[8,2,32,128]{3,2,1,0:T(8,128)(2,1)}, bf16[8,2,32,128]{3,2,1,0:T(8,128)(2,1)S(1)}, u32[]{:S(2)}, u32[]{:S(2)}) %collective-permute-start.1) | collective-permute-done | bytes 131104 | tf_op jit(solution)/shard_map/ppermute | solution.py:209
  18.3 0.0 collective-permute-done.2.three_ref
  18.3 0.0 copy-done.4
  18.3 2.0 %collective-permute-start.3 = (bf16[8,2,32,128]{3,2,1,0:T(8,128)(2,1)S(1)}, bf16[8,2,32,128]{3,2,1,0:T(8,128)(2,1)S(1)}, u32[]{:S(2)}, u32[]{:S(2)}) collective-permute-start(bf16[8,2,32,128]{3,2,1,0:T(8,128)(2,1)S(1)} %copy-done.4), channel_id=1, source_target_pairs={{0,1},{1,0},{2,3},{3,2},{4,5},{5,4},{6,7},{7,6},{8,9},{9,8},{10,11... | collective-permute-start | bytes 393224 | tf_op jit(solution)/shard_map/ppermute | solution.py:207
  20.3 0.0 copy-done.3
  20.3 1.1 collective-permute-start.4
  21.4 0.0 copy-done.2
  21.4 1.5 %collective-permute-start.5 = (bf16[8,2,32,128]{3,2,1,0:T(8,128)(2,1)S(1)}, bf16[8,2,32,128]{3,2,1,0:T(8,128)(2,1)S(1)}, u32[]{:S(2)}, u32[]{:S(2)}) collective-permute-start(bf16[8,2,32,128]{3,2,1,0:T(8,128)(2,1)S(1)} %copy-done.2), channel_id=1, source_target_pairs={{0,3},{1,2},{2,1},{3,0},{4,7},{5,6},{6,5},{7,4},{8,11},{9,10},{10,... | collective-permute-start | bytes 393224 | tf_op jit(solution)/shard_map/ppermute | solution.py:210
  22.9 0.0 copy-done
  22.9 6.8 %shard_map.46 = (bf16[16,2,128,256]{3,2,1,0:T(8,128)(2,1)S(1)}, bf16[16,2,128,128]{3,2,1,0:T(8,128)(2,1)S(1)}) custom-call(s32[1]{0:T(128)} %bitcast.member_ref, f32[8]{0:T(128)S(1)} %get-tuple-element.49.scale_ref, bf16[4,16,2,32,128]{4,3,2,1,0:T(8,128)(2,1)S(1)} %bitcast.43, bf16[8,2,32,128]{3,2,1,0:T(8,128)(2,1)S(1)} %collective-permute-done.one_ref, ...), custom_call_target="tpu_custom_call" | custom-call | flops 8589934592 | bytes 3145728 | tf_op jit(solution)/shard_map/pallas_call | solution.py:278
  29.7 1.0 collective-permute-start.6
  30.7 2.0 %collective-permute-start.7 = (bf16[16,32,128]{2,1,0:T(8,128)(2,1)S(1)}, bf16[16,32,128]{2,1,0:T(8,128)(2,1)S(1)}, u32[]{:S(2)}, u32[]{:S(2)}) collective-permute-start(bf16[16,32,128]{2,1,0:T(8,128)(2,1)S(1)} %get-tuple-element.26), channel_id=1, source_target_pairs={{0,2},{2,0},{1,3},{3,1},{4,6},{6,4},{5,7},{7,5},{8,10},{10,8},{9,1... | collective-permute-start | bytes 393224 | tf_op jit(solution)/shard_map/ppermute | solution.py:209
  32.7 0.0 collective-permute-done.3.one_ref
  32.7 1.5 %collective-permute-start.8 = (bf16[16,32,128]{2,1,0:T(8,128)(2,1)S(1)}, bf16[16,32,128]{2,1,0:T(8,128)(2,1)S(1)}, u32[]{:S(2)}, u32[]{:S(2)}) collective-permute-start(bf16[16,32,128]{2,1,0:T(8,128)(2,1)S(1)} %get-tuple-element.27), channel_id=1, source_target_pairs={{0,3},{1,2},{2,1},{3,0},{4,7},{5,6},{6,5},{7,4},{8,11},{9,10},{10,... | collective-permute-start | bytes 393224 | tf_op jit(solution)/shard_map/ppermute | solution.py:210
  34.1 0.0 collective-permute-done.4.two_ref
  34.1 0.0 collective-permute-done.5.three_ref
  34.1 6.8 %shard_map.47 = (bf16[16,2,128,256]{3,2,1,0:T(8,128)(2,1)S(1)}, bf16[16,2,128,128]{3,2,1,0:T(8,128)(2,1)S(1)}) custom-call(s32[1]{0:T(128)} %bitcast.member_ref, f32[8]{0:T(128)S(1)} %get-tuple-element.50.scale_ref, bf16[4,16,2,32,128]{4,3,2,1,0:T(8,128)(2,1)S(1)} %bitcast.44, ...), custom_call_target="tpu_custom_call", output_to_operand_aliasing={{0}: (6, {}), {1}: (7, {})} | custom-call | flops 8589934592 | bytes 3145728 | tf_op jit(solution)/shard_map/pallas_call | solution.py:278
  41.0 0.0 collective-permute-done.6.one_ref
  41.0 2.3 %collective-permute-done.7.two_ref = bf16[16,32,128]{2,1,0:T(8,128)(2,1)S(1)} collective-permute-done((bf16[16,32,128]{2,1,0:T(8,128)(2,1)S(1)}, bf16[16,32,128]{2,1,0:T(8,128)(2,1)S(1)}, u32[]{:S(2)}, u32[]{:S(2)}) %collective-permute-start.7) | collective-permute-done | bytes 131104 | tf_op jit(solution)/shard_map/ppermute | solution.py:209
  43.3 0.0 collective-permute-done.8.three_ref
  43.3 3.5 %shard_map.48 = f32[2048,128]{1,0:T(8,128)S(1)} custom-call(s32[1]{0:T(128)} %bitcast.member_ref, bf16[16,2,128,256]{3,2,1,0:T(8,128)(2,1)S(1)} %get-tuple-element.24.inverse_ref, bf16[4,16,32,128]{3,2,1,0:T(8,128)(2,1)S(1)} %bitcast_select_fusion.own_ref, bf16[16,32,128]{2,1,0:T(8,128)(2,1)S(1)} %collective-permute-done.6.one_ref, ...), custom_call_target="tpu_custom_call" | custom-call | flops 2684354560 | bytes 6291456 | tf_op jit(solution)/shard_map/pallas_call | solution.py:308
  46.8 0.9 convert_element_type.48
  47.7 7.6 %all-to-all-start = ((f16[32,4,16,128]{3,2,1,0:T(8,128)(2,1)}), f16[32,4,16,128]{3,2,1,0:T(8,128)(2,1)}, u32[]{:S(2)}, u32[]{:S(2)}) async-start(f16[32,4,16,128]{3,2,1,0:T(8,128)(2,1)} %bitcast.15), calls=%async_computation | async-start | bytes 1048576 | tf_op jit(solution)/shard_map/all_to_all | solution.py:323
  55.9 8.2 %fusion.4 = (f32[512,512]{1,0:T(8,128)S(1)}, f32[512,512]{1,0:T(8,128)S(1)}) fusion(s32[512]{0:T(512)S(1)} %fusion.28, s32[]{:T(128)} %bitcast.2, f32[]{:T(128)} %bitcast.1), kind=kLoop, calls=%fused_computation.11 | loop fusion | flops 7340032 | bytes 2099208 | tf_op jit(solution)/shard_map/jit(_where)/select_n | solution.py:185
  64.2 6.4 %all-to-all-done = f16[32,4,16,128]{3,2,1,0:T(8,128)(2,1)} async-done(((f16[32,4,16,128]{3,2,1,0:T(8,128)(2,1)}), f16[32,4,16,128]{3,2,1,0:T(8,128)(2,1)}, u32[]{:S(2)}, u32[]{:S(2)}) %all-to-all-start) | async-done | bytes 524320 | tf_op jit(solution)/shard_map/all_to_all | solution.py:323
  70.6 1.1 convert_element_type.49.values_ref
  71.7 2.5 %shard_map.49 = f32[32,4,2,16,128]{4,3,2,1,0:T(8,128)S(1)} custom-call(f32[512,512]{1,0:T(8,128)S(1)} %get-tuple-element.48.real_ref, f32[512,512]{1,0:T(8,128)S(1)} %get-tuple-element.47.imag_ref, f32[32,4,16,128]{3,2,1,0:T(8,128)S(1)} %convert_element_type.49.values_ref), custom_call_target="tpu_custom_call" | custom-call | flops 1610612736 | bytes 3145728 | tf_op jit(solution)/shard_map/pallas_call | solution.py:330
  74.2 0.3 convert_element_type.50
  74.5 29.1 %all_to_all.10 = f16[32,4,2,16,128]{4,3,2,1,0:T(8,128)(2,1)S(1)} all-to-all(f16[32,4,2,16,128]{4,3,2,1,0:T(8,128)(2,1)S(1)} %convert_element_type.50), channel_id=1, replica_groups=mesh['freq'=8,'side'=2,'pair'=2] {'side','pair','freq'}, dimensions={0} | all-to-all | bytes 2097152 | tf_op jit(solution)/shard_map/all_to_all | solution.py:346
  103.6 0.2 bitcast_convert_fusion.causal_ref
  103.8 2.6 %shard_map.50 = f32[4,16,2,32,128]{4,3,2,1,0:T(8,128)S(1)} custom-call(s32[1]{0:T(128)} %bitcast.member_ref, f32[4096,128]{1,0:T(8,128)S(1)} %bitcast_convert_fusion.causal_ref, bf16[16,2,128,128]{3,2,1,0:T(8,128)(2,1)S(1)} %get-tuple-element.28.psi_ref), custom_call_target="tpu_custom_call" | custom-call | flops 536870912 | bytes 5242880 | tf_op jit(solution)/shard_map/pallas_call | solution.py:351
  106.5 0.3 convert.6
  106.8 0.2 slice_bitcast_fusion.2
  107.0 0.8 collective-permute-start.10
  107.8 2.4 %collective-permute-start.11 = (f16[16,2,32,128]{3,2,1,0:T(8,128)(2,1)S(1)}, f16[16,2,32,128]{3,2,1,0:T(8,128)(2,1)S(1)}, u32[]{:S(2)}, u32[]{:S(2)}) collective-permute-start(f16[16,2,32,128]{3,2,1,0:T(8,128)(2,1)S(1)} %get-tuple-element.34), channel_id=1, source_target_pairs={{0,3},{1,2},{2,1},{3,0},{4,7},{5,6},{6,5},{7,4},{8,11},{9,10},{10,... | collective-permute-start | bytes 786440 | tf_op jit(solution)/shard_map/ppermute | solution.py:210
  110.2 0.4 collective-permute-start.9
  110.6 17.4 %collective-permute-done.10 = f16[16,2,32,128]{3,2,1,0:T(8,128)(2,1)S(1)} collective-permute-done((f16[16,2,32,128]{3,2,1,0:T(8,128)(2,1)S(1)}, f16[16,2,32,128]{3,2,1,0:T(8,128)(2,1)S(1)}, u32[]{:S(2)}, u32[]{:S(2)}) %collective-permute-start.10) | collective-permute-done | bytes 262176 | tf_op jit(solution)/shard_map/ppermute | solution.py:209
  128.0 0.0 collective-permute-done.11
  128.0 0.2 collective-permute-done.9
  128.2 1.3 fusion.17
  129.5 1.6 %fusion = f32[64,2,128,32]{2,3,1,0:T(8,128)} fusion(f32[16,2,32,128]{3,2,1,0:T(8,128)S(1)} %get-tuple-element.30, f32[16,2,32,128]{3,2,1,0:T(8,128)S(1)} %get-tuple-element.31, f32[16,2,32,128]{3,2,1,0:T(8,128)S(1)} %get-tuple-element.32, f32[16,2,32,128]{3,2,1,0:T(8,128)S(1)} %get-tuple-element.29), kind=kLoop, calls=%fused_computation.2 | loop fusion | flops 2097152 | bytes 4194304 | tf_op jit(solution)/shard_map/transpose | solution.py:372
  (4 shorter events, 0.1 us)
Async XLA Ops:
  0.0 7.9 %copy-start.1 = (bf16[64,2,32,128]{3,2,1,0:T(8,128)(2,1)S(1)}, bf16[64,2,32,128]{3,2,1,0:T(8,128)(2,1)}, u32[]{:S(2)}) copy-start(bf16[64,2,32,128]{3,2,1,0:T(8,128)(2,1)} %param.5) | copy-start | bytes 3145732
  2.2 5.9 %copy-start.5 = (f32[64]{0:T(128)S(1)}, f32[64]{0:T(128)}, u32[]{:S(2)}) copy-start(f32[64]{0:T(128)} %param.6) | copy-start | bytes 772
  2.2 8.3 %collective-permute-start = (bf16[8,2,32,128]{3,2,1,0:T(8,128)(2,1)}, bf16[8,2,32,128]{3,2,1,0:T(8,128)(2,1)S(1)}, u32[]{:S(2)}, u32[]{:S(2)}) collective-permute-start(bf16[8,2,32,128]{3,2,1,0:T(8,128)(2,1)} %get-tuple-element.40), channel_id=1, source_target_pairs={{0,1},{1,0},{2,3},{3,2},{4,5},{5,4},{6,7},{7,6},{8,9},{9,8},{10,11... | collective-permute-start | bytes 393224 | tf_op jit(solution)/shard_map/ppermute | solution.py:207
  5.2 13.1 %collective-permute-start.1 = (bf16[8,2,32,128]{3,2,1,0:T(8,128)(2,1)}, bf16[8,2,32,128]{3,2,1,0:T(8,128)(2,1)S(1)}, u32[]{:S(2)}, u32[]{:S(2)}) collective-permute-start(bf16[8,2,32,128]{3,2,1,0:T(8,128)(2,1)} %get-tuple-element.39), channel_id=1, source_target_pairs={{0,2},{2,0},{1,3},{3,1},{4,6},{6,4},{5,7},{7,5},{8,10},{10,8},{9,1... | collective-permute-start | bytes 393224 | tf_op jit(solution)/shard_map/ppermute | solution.py:209
  7.8 10.5 %collective-permute-start.2 = (bf16[8,2,32,128]{3,2,1,0:T(8,128)(2,1)}, bf16[8,2,32,128]{3,2,1,0:T(8,128)(2,1)S(1)}, u32[]{:S(2)}, u32[]{:S(2)}) collective-permute-start(bf16[8,2,32,128]{3,2,1,0:T(8,128)(2,1)} %get-tuple-element.38), channel_id=1, source_target_pairs={{0,3},{1,2},{2,1},{3,0},{4,7},{5,6},{6,5},{7,4},{8,11},{9,10},{10,... | collective-permute-start | bytes 393224 | tf_op jit(solution)/shard_map/ppermute | solution.py:210
  7.9 15.0 %copy-start = (bf16[64,2,32,128]{3,2,1,0:T(8,128)(2,1)S(1)}, bf16[64,2,32,128]{3,2,1,0:T(8,128)(2,1)}, u32[]{:S(2)}) copy-start(bf16[64,2,32,128]{3,2,1,0:T(8,128)(2,1)} %param.4) | copy-start | bytes 3145732
  8.0 10.4 %copy-start.4 = (bf16[8,2,32,128]{3,2,1,0:T(8,128)(2,1)S(1)}, bf16[8,2,32,128]{3,2,1,0:T(8,128)(2,1)}, u32[]{:S(2)}) copy-start(bf16[8,2,32,128]{3,2,1,0:T(8,128)(2,1)} %get-tuple-element.17) | copy-start | bytes 393220
  8.0 12.3 %copy-start.3 = (bf16[8,2,32,128]{3,2,1,0:T(8,128)(2,1)S(1)}, bf16[8,2,32,128]{3,2,1,0:T(8,128)(2,1)}, u32[]{:S(2)}) copy-start(bf16[8,2,32,128]{3,2,1,0:T(8,128)(2,1)} %get-tuple-element.18) | copy-start | bytes 393220
  8.0 13.4 %copy-start.2 = (bf16[8,2,32,128]{3,2,1,0:T(8,128)(2,1)S(1)}, bf16[8,2,32,128]{3,2,1,0:T(8,128)(2,1)}, u32[]{:S(2)}) copy-start(bf16[8,2,32,128]{3,2,1,0:T(8,128)(2,1)} %get-tuple-element.19) | copy-start | bytes 393220
  18.3 14.3 %collective-permute-start.3 = (bf16[8,2,32,128]{3,2,1,0:T(8,128)(2,1)S(1)}, bf16[8,2,32,128]{3,2,1,0:T(8,128)(2,1)S(1)}, u32[]{:S(2)}, u32[]{:S(2)}) collective-permute-start(bf16[8,2,32,128]{3,2,1,0:T(8,128)(2,1)S(1)} %copy-done.4), channel_id=1, source_target_pairs={{0,1},{1,0},{2,3},{3,2},{4,5},{5,4},{6,7},{7,6},{8,9},{9,8},{10,11... | collective-permute-start | bytes 393224 | tf_op jit(solution)/shard_map/ppermute | solution.py:207
  20.3 13.8 %collective-permute-start.4 = (bf16[8,2,32,128]{3,2,1,0:T(8,128)(2,1)S(1)}, bf16[8,2,32,128]{3,2,1,0:T(8,128)(2,1)S(1)}, u32[]{:S(2)}, u32[]{:S(2)}) collective-permute-start(bf16[8,2,32,128]{3,2,1,0:T(8,128)(2,1)S(1)} %copy-done.3), channel_id=1, source_target_pairs={{0,2},{2,0},{1,3},{3,1},{4,6},{6,4},{5,7},{7,5},{8,10},{10,8},{9,1... | collective-permute-start | bytes 393224 | tf_op jit(solution)/shard_map/ppermute | solution.py:209
  21.4 12.7 %collective-permute-start.5 = (bf16[8,2,32,128]{3,2,1,0:T(8,128)(2,1)S(1)}, bf16[8,2,32,128]{3,2,1,0:T(8,128)(2,1)S(1)}, u32[]{:S(2)}, u32[]{:S(2)}) collective-permute-start(bf16[8,2,32,128]{3,2,1,0:T(8,128)(2,1)S(1)} %copy-done.2), channel_id=1, source_target_pairs={{0,3},{1,2},{2,1},{3,0},{4,7},{5,6},{6,5},{7,4},{8,11},{9,10},{10,... | collective-permute-start | bytes 393224 | tf_op jit(solution)/shard_map/ppermute | solution.py:210
  29.7 11.3 %collective-permute-start.6 = (bf16[16,32,128]{2,1,0:T(8,128)(2,1)S(1)}, bf16[16,32,128]{2,1,0:T(8,128)(2,1)S(1)}, u32[]{:S(2)}, u32[]{:S(2)}) collective-permute-start(bf16[16,32,128]{2,1,0:T(8,128)(2,1)S(1)} %get-tuple-element.25), channel_id=1, source_target_pairs={{0,1},{1,0},{2,3},{3,2},{4,5},{5,4},{6,7},{7,6},{8,9},{9,8},{10,11... | collective-permute-start | bytes 393224 | tf_op jit(solution)/shard_map/ppermute | solution.py:207
  30.7 12.6 %collective-permute-start.7 = (bf16[16,32,128]{2,1,0:T(8,128)(2,1)S(1)}, bf16[16,32,128]{2,1,0:T(8,128)(2,1)S(1)}, u32[]{:S(2)}, u32[]{:S(2)}) collective-permute-start(bf16[16,32,128]{2,1,0:T(8,128)(2,1)S(1)} %get-tuple-element.26), channel_id=1, source_target_pairs={{0,2},{2,0},{1,3},{3,1},{4,6},{6,4},{5,7},{7,5},{8,10},{10,8},{9,1... | collective-permute-start | bytes 393224 | tf_op jit(solution)/shard_map/ppermute | solution.py:209
  32.7 10.6 %collective-permute-start.8 = (bf16[16,32,128]{2,1,0:T(8,128)(2,1)S(1)}, bf16[16,32,128]{2,1,0:T(8,128)(2,1)S(1)}, u32[]{:S(2)}, u32[]{:S(2)}) collective-permute-start(bf16[16,32,128]{2,1,0:T(8,128)(2,1)S(1)} %get-tuple-element.27), channel_id=1, source_target_pairs={{0,3},{1,2},{2,1},{3,0},{4,7},{5,6},{6,5},{7,4},{8,11},{9,10},{10,... | collective-permute-start | bytes 393224 | tf_op jit(solution)/shard_map/ppermute | solution.py:210
  47.7 22.9 %all-to-all-start = ((f16[32,4,16,128]{3,2,1,0:T(8,128)(2,1)}), f16[32,4,16,128]{3,2,1,0:T(8,128)(2,1)}, u32[]{:S(2)}, u32[]{:S(2)}) async-start(f16[32,4,16,128]{3,2,1,0:T(8,128)(2,1)} %bitcast.15), calls=%async_computation | async-start | bytes 1048576 | tf_op jit(solution)/shard_map/all_to_all | solution.py:323
  107.0 21.0 %collective-permute-start.10 = (f16[16,2,32,128]{3,2,1,0:T(8,128)(2,1)S(1)}, f16[16,2,32,128]{3,2,1,0:T(8,128)(2,1)S(1)}, u32[]{:S(2)}, u32[]{:S(2)}) collective-permute-start(f16[16,2,32,128]{3,2,1,0:T(8,128)(2,1)S(1)} %get-tuple-element.33), channel_id=1, source_target_pairs={{0,2},{2,0},{1,3},{3,1},{4,6},{6,4},{5,7},{7,5},{8,10},{10,8},{9,1... | collective-permute-start | bytes 786440 | tf_op jit(solution)/shard_map/ppermute | solution.py:209
  107.8 20.2 %collective-permute-start.11 = (f16[16,2,32,128]{3,2,1,0:T(8,128)(2,1)S(1)}, f16[16,2,32,128]{3,2,1,0:T(8,128)(2,1)S(1)}, u32[]{:S(2)}, u32[]{:S(2)}) collective-permute-start(f16[16,2,32,128]{3,2,1,0:T(8,128)(2,1)S(1)} %get-tuple-element.34), channel_id=1, source_target_pairs={{0,3},{1,2},{2,1},{3,0},{4,7},{5,6},{6,5},{7,4},{8,11},{9,10},{10,... | collective-permute-start | bytes 786440 | tf_op jit(solution)/shard_map/ppermute | solution.py:210
  110.2 18.0 %collective-permute-start.9 = (f16[16,2,32,128]{3,2,1,0:T(8,128)(2,1)S(1)}, f16[16,2,32,128]{3,2,1,0:T(8,128)(2,1)}, u32[]{:S(2)}, u32[]{:S(2)}) collective-permute-start(f16[16,2,32,128]{3,2,1,0:T(8,128)(2,1)S(1)} %get-tuple-element.35), channel_id=1, source_target_pairs={{0,1},{1,0},{2,3},{3,2},{4,5},{5,4},{6,7},{7,6},{8,9},{9,8},{10,11... | collective-permute-start | bytes 786440 | tf_op jit(solution)/shard_map/ppermute | solution.py:207

commit v11 on v9

--- a/solution.py
+++ b/solution.py
@@ -264,27 +264,28 @@
     pieces = [lax.dynamic_index_in_dim(packed, member ^ d, 0, keepdims=False) for d in distances]
     table_re, table_im = projection_table(lag_cutoff[0], count, freq_size, pairs)
 
+    wide = math.gcd(part, 8)
     local_block = lambda first: pl.BlockSpec(
-        (1, step, 2, rows, size), lambda i, m: (m[0], i + first, 0, 0, 0)
-    )
-    other_block = pl.BlockSpec((step, 2, rows, size), lambda i, m: (i, 0, 0, 0))
+        (1, wide, 2, rows, size), lambda i, m: (m[0], i + first, 0, 0, 0)
+    )
+    other_block = pl.BlockSpec((wide, 2, rows, size), lambda i, m: (i, 0, 0, 0))
     inverse_block = pl.BlockSpec((step, 2, size, 2 * size), lambda i, m: (i, 0, 0, 0))
     state, packed_arrived = [], []
     for chunk in range(chunks):
         scale = lax.dynamic_slice_in_dim(guess_scale, member * own + chunk * part, part, 0)
-        offset = chunk * part // step
+        offset = chunk * part // wide
         state = call(
             newton_kernel,
-            part // step,
+            part // wide,
             [pl.BlockSpec(memory_space=pltpu.SMEM), local_block(offset)]
             + [other_block] * 3
             + [pl.BlockSpec(memory_space=pl.ANY)] * len(state),
             [
                 pl.BlockSpec(
-                    (step, 2, size, 2 * size), lambda i, m, offset=offset: (i + offset, 0, 0, 0)
+                    (wide, 2, size, 2 * size), lambda i, m, offset=offset: (i + offset, 0, 0, 0)
                 ),
                 pl.BlockSpec(
-                    (step, 2, size, size), lambda i, m, offset=offset: (i + offset, 0, 0, 0)
+                    (wide, 2, size, size), lambda i, m, offset=offset: (i + offset, 0, 0, 0)
                 ),
             ],
             [
@@ -359,15 +360,11 @@
         own * 4 * 4 * size**3,
         own * 5 * 4 * size * size,
     )(members, back, psi)
-    panels = [result[0]]
-    panels += [swap(result[d].astype(jnp.float16), d).astype(F32) for d in distances]
-    owners = []
-    for owner in range(chan_size):
-        distance = member ^ owner
-        low = jnp.where(distance % 2 == 0, panels[0], panels[1])
-        high = jnp.where(distance % 2 == 0, panels[2], panels[3])
-        owners.append(jnp.where(distance < 2, low, high))
-    return jnp.swapaxes(cat(owners, 0) * SCALE, 2, 3)
+    panels = [result[0]] + [swap(result[d].astype(jnp.float16), d).astype(F32) for d in distances]
+    whole = jnp.zeros((group_bins, 2, rows, size), F32)
+    for d in range(chan_size):
+        whole = lax.dynamic_update_slice(whole, panels[d] * SCALE, ((member ^ d) * own, 0, 0, 0))
+    return jnp.swapaxes(whole, 2, 3)
 
 
 def solution(mesh):

time: 130 us -> 128 us (0.985)
  other arithmetic: 13.9 us -> 11.4 us
  Pallas kernels: 22.2 us -> 20 us
  local copies, waits for them, and re-layouts: 2.94 us -> 4.5 us
    ppermute x4, waiting for transfers between devices: 0.22 us -> 7.62 us  [swap(): return lax.ppermute(value, 'pair', SWAP)]
    ppermute x4, waiting for transfers between devices: 20.2 us -> 12.8 us  [swap(): return lax.ppermute(value, 'side', SWAP)]
    pallas_call x2, Pallas kernels: 13.6 us -> 11.4 us  [shards(): call(newton_kernel, part // wide, [pl.BlockSpec(memory_space=pltpu.SMEM),...]
    transpose x1 -> x0, other arithmetic: 1.55 us -> none  [shards(): return jnp.swapaxes(cat(owners, 0) * SCALE, 2, 3)]
    unnamed x4 -> x6, local copies, waits for them, and re-layouts: 0.01 us -> 1.32 us
  transfers between devices with their start and end apart: 13 -> 13, of which waited for: 4 -> 5; matrix products, arithmetic and copies ran while one was open for 8% -> 8% of each run, Pallas kernels for 11% -> 9%
where the time goes in v11:
time: 128 us; the launch traced here: 126 us
  starting transfers between devices  32.8 us (26%)
  blocking collectives  29.1 us (23%)
  waiting for transfers between devices  27.1 us (21%)
  Pallas kernels  20 us (16%)
  other arithmetic  11.4 us (9%)
  local copies, waits for them, and re-layouts  4.5 us (4%)
    all_to_all x1, blocking collectives, shards(): lax.all_to_all(causal, chan + ('freq',), 0, 0, tiled=True).astype(F32)  29.1 us
    ppermute x4, starting transfers between devices, swap(): return lax.ppermute(value, 'pair', SWAP)  13.9 us
    ppermute x4, waiting for transfers between devices, swap(): return lax.ppermute(value, 'side', SWAP)  12.8 us
    pallas_call x2, Pallas kernels, shards(): call(newton_kernel, part // wide, [pl.BlockSpec(memory_space=pltpu.SMEM),...  11.4 us
    select_n x1, other arithmetic, projection_table(): jnp.where(shift == 0, 0.0, (jnp.cos(half_angle) - jnp.cos(last_angle)) /...  8.24 us
    ppermute x4, starting transfers between devices, swap(): return lax.ppermute(value, 'side', SWAP)  8.11 us
    ppermute x4, waiting for transfers between devices, swap(): return lax.ppermute(value, 'pair', SWAP)  7.62 us
    all_to_all x1, waiting for transfers between devices, shards(): lax.all_to_all(sent, chan + ('freq',), 0, 0, tiled=True).astype(F32)  6.62 us
  transfers between devices with their start and end apart: 13, of which 5 were waited for; matrix products, arithmetic and copies ran while one was open for 8% of the time, Pallas kernels for 9%

profile of v11, /device:TPU:0, one launch (start us, length us, event | category | flops | bytes accessed | tf_op | source)
XLA Modules:
  0.0 125.7 jit_solution(7280654822009988287)
XLA Ops:
  0.0 1.3 dynamic-slice_bitcast_fusion
  1.3 0.0 copy-start.2
  1.3 3.1 %collective-permute-start.3 = (bf16[8,2,32,128]{3,2,1,0:T(8,128)(2,1)S(1)}, bf16[8,2,32,128]{3,2,1,0:T(8,128)(2,1)S(1)}, u32[]{:S(2)}, u32[]{:S(2)}) collective-permute-start(bf16[8,2,32,128]{3,2,1,0:T(8,128)(2,1)S(1)} %get-tuple-element.28), channel_id=1, source_target_pairs={{0,1},{1,0},{2,3},{3,2},{4,5},{5,4},{6,7},{7,6},{8,9},{9,8},{10,11... | collective-permute-start | bytes 393224 | tf_op jit(solution)/shard_map/ppermute | solution.py:207
  4.4 2.6 %collective-permute-start.4 = (bf16[8,2,32,128]{3,2,1,0:T(8,128)(2,1)S(1)}, bf16[8,2,32,128]{3,2,1,0:T(8,128)(2,1)S(1)}, u32[]{:S(2)}, u32[]{:S(2)}) collective-permute-start(bf16[8,2,32,128]{3,2,1,0:T(8,128)(2,1)S(1)} %get-tuple-element.27), channel_id=1, source_target_pairs={{0,2},{2,0},{1,3},{3,1},{4,6},{6,4},{5,7},{7,5},{8,10},{10,8},{9,1... | collective-permute-start | bytes 393224 | tf_op jit(solution)/shard_map/ppermute | solution.py:209
  6.9 0.0 collective-permute-start.5
  7.0 0.9 collective-permute-start
  7.8 3.5 %collective-permute-start.1 = (bf16[8,2,32,128]{3,2,1,0:T(8,128)(2,1)S(1)}, bf16[8,2,32,128]{3,2,1,0:T(8,128)(2,1)S(1)}, u32[]{:S(2)}, u32[]{:S(2)}) collective-permute-start(bf16[8,2,32,128]{3,2,1,0:T(8,128)(2,1)S(1)} %get-tuple-element.30), channel_id=1, source_target_pairs={{0,2},{2,0},{1,3},{3,1},{4,6},{6,4},{5,7},{7,5},{8,10},{10,8},{9,1... | collective-permute-start | bytes 393224 | tf_op jit(solution)/shard_map/ppermute | solution.py:209
  11.3 0.1 iota_compare_fusion
  11.4 0.0 copy-start
  11.4 1.4 %fusion.31 = (bf16[64,1,32,128]{3,2,1,0:T(8,128)(2,1)S(1)}, bf16[64,1,32,128]{3,2,1,0:T(8,128)(2,1)S(1)}) fusion(bf16[64,2,32,128]{3,2,1,0:T(8,128)(2,1)} %param.5), kind=kLoop, calls=%fused_computation.67 | loop fusion | bytes 2097152 | tf_op jit(solution)/shard_map/slice | solution.py:262
  12.8 0.1 bitcast_select_fusion.own_ref
  12.9 0.0 copy-done.2
  12.9 0.1 fusion.32
  13.0 0.0 collective-permute-done.3.one_ref
  13.0 1.6 %collective-permute-start.2 = (bf16[8,2,32,128]{3,2,1,0:T(8,128)(2,1)S(1)}, bf16[8,2,32,128]{3,2,1,0:T(8,128)(2,1)S(1)}, u32[]{:S(2)}, u32[]{:S(2)}) collective-permute-start(bf16[8,2,32,128]{3,2,1,0:T(8,128)(2,1)S(1)} %get-tuple-element.29), channel_id=1, source_target_pairs={{0,3},{1,2},{2,1},{3,0},{4,7},{5,6},{6,5},{7,4},{8,11},{9,10},{10,... | collective-permute-start | bytes 393224 | tf_op jit(solution)/shard_map/ppermute | solution.py:210
  14.6 2.7 %collective-permute-done.4.two_ref = bf16[8,2,32,128]{3,2,1,0:T(8,128)(2,1)S(1)} collective-permute-done((bf16[8,2,32,128]{3,2,1,0:T(8,128)(2,1)S(1)}, bf16[8,2,32,128]{3,2,1,0:T(8,128)(2,1)S(1)}, u32[]{:S(2)}, u32[]{:S(2)}) %collective-permute-start.4) | collective-permute-done | bytes 131104 | tf_op jit(solution)/shard_map/ppermute | solution.py:209
  17.3 0.0 collective-permute-done.5.three_ref
  17.3 0.0 copy-done
  17.3 5.7 %shard_map.46 = (bf16[16,2,128,256]{3,2,1,0:T(8,128)(2,1)S(1)}, bf16[16,2,128,128]{3,2,1,0:T(8,128)(2,1)S(1)}) custom-call(s32[1]{0:T(128)} %bitcast.member_ref, f32[8]{0:T(128)S(1)} %get-tuple-element.39.scale_ref, bf16[4,16,2,32,128]{4,3,2,1,0:T(8,128)(2,1)S(1)} %bitcast.44, bf16[8,2,32,128]{3,2,1,0:T(8,128)(2,1)S(1)} %collective-permute-done.3.one_ref, ...), custom_call_target="tpu_custom_call" | custom-call | flops 8589934592 | bytes 3145728 | tf_op jit(solution)/shard_map/pallas_call | solution.py:277
  23.0 9.1 %collective-permute-start.6 = (bf16[16,32,128]{2,1,0:T(8,128)(2,1)S(1)}, bf16[16,32,128]{2,1,0:T(8,128)(2,1)S(1)}, u32[]{:S(2)}, u32[]{:S(2)}) collective-permute-start(bf16[16,32,128]{2,1,0:T(8,128)(2,1)S(1)} %get-tuple-element.19), channel_id=1, source_target_pairs={{0,1},{1,0},{2,3},{3,2},{4,5},{5,4},{6,7},{7,6},{8,9},{9,8},{10,11... | collective-permute-start | bytes 393224 | tf_op jit(solution)/shard_map/ppermute | solution.py:207
  32.1 0.9 collective-permute-start.7
  33.0 0.0 collective-permute-done.one_ref
  33.0 1.5 %collective-permute-start.8 = (bf16[16,32,128]{2,1,0:T(8,128)(2,1)S(1)}, bf16[16,32,128]{2,1,0:T(8,128)(2,1)S(1)}, u32[]{:S(2)}, u32[]{:S(2)}) collective-permute-start(bf16[16,32,128]{2,1,0:T(8,128)(2,1)S(1)} %get-tuple-element.21), channel_id=1, source_target_pairs={{0,3},{1,2},{2,1},{3,0},{4,7},{5,6},{6,5},{7,4},{8,11},{9,10},{10,... | collective-permute-start | bytes 393224 | tf_op jit(solution)/shard_map/ppermute | solution.py:210
  34.5 0.0 collective-permute-done.1.two_ref
  34.5 0.0 collective-permute-done.2.three_ref
  34.5 5.7 %shard_map.47 = (bf16[16,2,128,256]{3,2,1,0:T(8,128)(2,1)S(1)}, bf16[16,2,128,128]{3,2,1,0:T(8,128)(2,1)S(1)}) custom-call(s32[1]{0:T(128)} %bitcast.member_ref, f32[8]{0:T(128)S(1)} %get-tuple-element.40.scale_ref, bf16[4,16,2,32,128]{4,3,2,1,0:T(8,128)(2,1)S(1)} %bitcast.45, ...), custom_call_target="tpu_custom_call", output_to_operand_aliasing={{0}: (6, {}), {1}: (7, {})} | custom-call | flops 8589934592 | bytes 3145728 | tf_op jit(solution)/shard_map/pallas_call | solution.py:277
  40.3 0.0 collective-permute-done.6.one_ref
  40.3 0.5 collective-permute-done.7.two_ref
  40.8 0.0 collective-permute-done.8.three_ref
  40.8 3.5 %shard_map.48 = f32[2048,128]{1,0:T(8,128)S(1)} custom-call(s32[1]{0:T(128)} %bitcast.member_ref, bf16[16,2,128,256]{3,2,1,0:T(8,128)(2,1)S(1)} %get-tuple-element.18.inverse_ref, bf16[4,16,32,128]{3,2,1,0:T(8,128)(2,1)S(1)} %bitcast_select_fusion.own_ref, bf16[16,32,128]{2,1,0:T(8,128)(2,1)S(1)} %collective-permute-done.6.one_ref, ...), custom_call_target="tpu_custom_call" | custom-call | flops 2684354560 | bytes 6291456 | tf_op jit(solution)/shard_map/pallas_call | solution.py:307
  44.3 0.9 convert_element_type.48
  45.1 5.2 %all-to-all-start = ((f16[32,4,16,128]{3,2,1,0:T(8,128)(2,1)}), f16[32,4,16,128]{3,2,1,0:T(8,128)(2,1)}, u32[]{:S(2)}, u32[]{:S(2)}) async-start(f16[32,4,16,128]{3,2,1,0:T(8,128)(2,1)} %bitcast.15), calls=%async_computation | async-start | bytes 1048576 | tf_op jit(solution)/shard_map/all_to_all | solution.py:322
  51.0 8.2 %fusion.3 = (f32[512,512]{1,0:T(8,128)S(1)}, f32[512,512]{1,0:T(8,128)S(1)}) fusion(s32[512]{0:T(512)S(1)} %fusion.25, s32[]{:T(128)} %bitcast.2, f32[]{:T(128)} %bitcast.1), kind=kLoop, calls=%fused_computation.9 | loop fusion | flops 7340032 | bytes 2099208 | tf_op jit(solution)/shard_map/jit(_where)/select_n | solution.py:185
  59.2 6.6 %all-to-all-done = f16[32,4,16,128]{3,2,1,0:T(8,128)(2,1)} async-done(((f16[32,4,16,128]{3,2,1,0:T(8,128)(2,1)}), f16[32,4,16,128]{3,2,1,0:T(8,128)(2,1)}, u32[]{:S(2)}, u32[]{:S(2)}) %all-to-all-start) | async-done | bytes 524320 | tf_op jit(solution)/shard_map/all_to_all | solution.py:322
  65.8 1.1 convert_element_type.49.values_ref
  67.0 2.5 %shard_map.49 = f32[32,4,2,16,128]{4,3,2,1,0:T(8,128)S(1)} custom-call(f32[512,512]{1,0:T(8,128)S(1)} %get-tuple-element.38.real_ref, f32[512,512]{1,0:T(8,128)S(1)} %get-tuple-element.37.imag_ref, f32[32,4,16,128]{3,2,1,0:T(8,128)S(1)} %convert_element_type.49.values_ref), custom_call_target="tpu_custom_call" | custom-call | flops 1610612736 | bytes 3145728 | tf_op jit(solution)/shard_map/pallas_call | solution.py:329
  69.5 0.3 convert_element_type.50
  69.7 29.1 %all_to_all.10 = f16[32,4,2,16,128]{4,3,2,1,0:T(8,128)(2,1)S(1)} all-to-all(f16[32,4,2,16,128]{4,3,2,1,0:T(8,128)(2,1)S(1)} %convert_element_type.50), channel_id=1, replica_groups=mesh['freq'=8,'side'=2,'pair'=2] {'side','pair','freq'}, dimensions={0} | all-to-all | bytes 2097152 | tf_op jit(solution)/shard_map/all_to_all | solution.py:345
  98.9 0.2 bitcast_convert_fusion.causal_ref
  99.1 2.6 %shard_map.50 = f32[4,16,2,32,128]{4,3,2,1,0:T(8,128)S(1)} custom-call(s32[1]{0:T(128)} %bitcast.member_ref, f32[4096,128]{1,0:T(8,128)S(1)} %bitcast_convert_fusion.causal_ref, bf16[16,2,128,128]{3,2,1,0:T(8,128)(2,1)S(1)} %get-tuple-element.22.psi_ref), custom_call_target="tpu_custom_call" | custom-call | flops 536870912 | bytes 5242880 | tf_op jit(solution)/shard_map/pallas_call | solution.py:350
  101.6 0.3 convert.6
  101.9 0.2 slice_bitcast_fusion
  102.1 0.8 collective-permute-start.9
  102.9 1.1 collective-permute-start.10
  104.1 0.2 broadcast_in_dim.18
  104.3 0.1 fusion.17
  104.4 2.6 %collective-permute-start.11 = (f16[16,2,32,128]{3,2,1,0:T(8,128)(2,1)S(1)}, f16[16,2,32,128]{3,2,1,0:T(8,128)(2,1)S(1)}, u32[]{:S(2)}, u32[]{:S(2)}) collective-permute-start(f16[16,2,32,128]{3,2,1,0:T(8,128)(2,1)S(1)} %get-tuple-element.23), channel_id=1, source_target_pairs={{0,3},{1,2},{2,1},{3,0},{4,7},{5,6},{6,5},{7,4},{8,11},{9,10},{10,... | collective-permute-start | bytes 786440 | tf_op jit(solution)/shard_map/ppermute | solution.py:210
  107.0 7.6 %collective-permute-done.9 = f16[16,2,32,128]{3,2,1,0:T(8,128)(2,1)S(1)} collective-permute-done((f16[16,2,32,128]{3,2,1,0:T(8,128)(2,1)S(1)}, f16[16,2,32,128]{3,2,1,0:T(8,128)(2,1)S(1)}, u32[]{:S(2)}, u32[]{:S(2)}) %collective-permute-start.9) | collective-permute-done | bytes 262176 | tf_op jit(solution)/shard_map/ppermute | solution.py:207
  114.6 0.1 multiply_dynamic-update-slice_fusion.2
  114.7 9.6 %collective-permute-done.10 = f16[16,2,32,128]{3,2,1,0:T(8,128)(2,1)S(1)} collective-permute-done((f16[16,2,32,128]{3,2,1,0:T(8,128)(2,1)S(1)}, f16[16,2,32,128]{3,2,1,0:T(8,128)(2,1)S(1)}, u32[]{:S(2)}, u32[]{:S(2)}) %collective-permute-start.10) | collective-permute-done | bytes 262176 | tf_op jit(solution)/shard_map/ppermute | solution.py:209
  124.3 0.1 multiply_dynamic-update-slice_fusion.1
  124.3 0.0 collective-permute-done.11
  124.3 0.1 multiply_dynamic-update-slice_fusion
  124.4 0.0 copy-start.1
  124.4 1.3 %copy-done.1 = f32[64,2,32,128]{3,2,1,0:T(8,128)} copy-done((f32[64,2,32,128]{3,2,1,0:T(8,128)}, f32[64,2,32,128]{3,2,1,0:T(8,128)S(1)}, u32[]{:S(2)}) %copy-start.1) | copy-done | bytes 2097176
  (3 shorter events, 0.0 us)
Async XLA Ops:
  1.3 11.6 %copy-start.2 = (f32[64]{0:T(128)S(1)}, f32[64]{0:T(128)}, u32[]{:S(2)}) copy-start(f32[64]{0:T(128)} %param.6) | copy-start | bytes 772
  1.3 11.7 %collective-permute-start.3 = (bf16[8,2,32,128]{3,2,1,0:T(8,128)(2,1)S(1)}, bf16[8,2,32,128]{3,2,1,0:T(8,128)(2,1)S(1)}, u32[]{:S(2)}, u32[]{:S(2)}) collective-permute-start(bf16[8,2,32,128]{3,2,1,0:T(8,128)(2,1)S(1)} %get-tuple-element.28), channel_id=1, source_target_pairs={{0,1},{1,0},{2,3},{3,2},{4,5},{5,4},{6,7},{7,6},{8,9},{9,8},{10,11... | collective-permute-start | bytes 393224 | tf_op jit(solution)/shard_map/ppermute | solution.py:207
  4.4 12.9 %collective-permute-start.4 = (bf16[8,2,32,128]{3,2,1,0:T(8,128)(2,1)S(1)}, bf16[8,2,32,128]{3,2,1,0:T(8,128)(2,1)S(1)}, u32[]{:S(2)}, u32[]{:S(2)}) collective-permute-start(bf16[8,2,32,128]{3,2,1,0:T(8,128)(2,1)S(1)} %get-tuple-element.27), channel_id=1, source_target_pairs={{0,2},{2,0},{1,3},{3,1},{4,6},{6,4},{5,7},{7,5},{8,10},{10,8},{9,1... | collective-permute-start | bytes 393224 | tf_op jit(solution)/shard_map/ppermute | solution.py:209
  6.9 10.4 %collective-permute-start.5 = (bf16[8,2,32,128]{3,2,1,0:T(8,128)(2,1)S(1)}, bf16[8,2,32,128]{3,2,1,0:T(8,128)(2,1)S(1)}, u32[]{:S(2)}, u32[]{:S(2)}) collective-permute-start(bf16[8,2,32,128]{3,2,1,0:T(8,128)(2,1)S(1)} %get-tuple-element.26), channel_id=1, source_target_pairs={{0,3},{1,2},{2,1},{3,0},{4,7},{5,6},{6,5},{7,4},{8,11},{9,10},{10,... | collective-permute-start | bytes 393224 | tf_op jit(solution)/shard_map/ppermute | solution.py:210
  7.0 26.1 %collective-permute-start = (bf16[8,2,32,128]{3,2,1,0:T(8,128)(2,1)S(1)}, bf16[8,2,32,128]{3,2,1,0:T(8,128)(2,1)S(1)}, u32[]{:S(2)}, u32[]{:S(2)}) collective-permute-start(bf16[8,2,32,128]{3,2,1,0:T(8,128)(2,1)S(1)} %get-tuple-element.31), channel_id=1, source_target_pairs={{0,1},{1,0},{2,3},{3,2},{4,5},{5,4},{6,7},{7,6},{8,9},{9,8},{10,11... | collective-permute-start | bytes 393224 | tf_op jit(solution)/shard_map/ppermute | solution.py:207
  7.8 26.7 %collective-permute-start.1 = (bf16[8,2,32,128]{3,2,1,0:T(8,128)(2,1)S(1)}, bf16[8,2,32,128]{3,2,1,0:T(8,128)(2,1)S(1)}, u32[]{:S(2)}, u32[]{:S(2)}) collective-permute-start(bf16[8,2,32,128]{3,2,1,0:T(8,128)(2,1)S(1)} %get-tuple-element.30), channel_id=1, source_target_pairs={{0,2},{2,0},{1,3},{3,1},{4,6},{6,4},{5,7},{7,5},{8,10},{10,8},{9,1... | collective-permute-start | bytes 393224 | tf_op jit(solution)/shard_map/ppermute | solution.py:209
  11.4 5.9 %copy-start = (bf16[64,2,32,128]{3,2,1,0:T(8,128)(2,1)S(1)}, bf16[64,2,32,128]{3,2,1,0:T(8,128)(2,1)}, u32[]{:S(2)}) copy-start(bf16[64,2,32,128]{3,2,1,0:T(8,128)(2,1)} %param.4) | copy-start | bytes 3145732
  13.0 21.5 %collective-permute-start.2 = (bf16[8,2,32,128]{3,2,1,0:T(8,128)(2,1)S(1)}, bf16[8,2,32,128]{3,2,1,0:T(8,128)(2,1)S(1)}, u32[]{:S(2)}, u32[]{:S(2)}) collective-permute-start(bf16[8,2,32,128]{3,2,1,0:T(8,128)(2,1)S(1)} %get-tuple-element.29), channel_id=1, source_target_pairs={{0,3},{1,2},{2,1},{3,0},{4,7},{5,6},{6,5},{7,4},{8,11},{9,10},{10,... | collective-permute-start | bytes 393224 | tf_op jit(solution)/shard_map/ppermute | solution.py:210
  23.0 17.2 %collective-permute-start.6 = (bf16[16,32,128]{2,1,0:T(8,128)(2,1)S(1)}, bf16[16,32,128]{2,1,0:T(8,128)(2,1)S(1)}, u32[]{:S(2)}, u32[]{:S(2)}) collective-permute-start(bf16[16,32,128]{2,1,0:T(8,128)(2,1)S(1)} %get-tuple-element.19), channel_id=1, source_target_pairs={{0,1},{1,0},{2,3},{3,2},{4,5},{5,4},{6,7},{7,6},{8,9},{9,8},{10,11... | collective-permute-start | bytes 393224 | tf_op jit(solution)/shard_map/ppermute | solution.py:207
  32.1 8.7 %collective-permute-start.7 = (bf16[16,32,128]{2,1,0:T(8,128)(2,1)S(1)}, bf16[16,32,128]{2,1,0:T(8,128)(2,1)S(1)}, u32[]{:S(2)}, u32[]{:S(2)}) collective-permute-start(bf16[16,32,128]{2,1,0:T(8,128)(2,1)S(1)} %get-tuple-element.20), channel_id=1, source_target_pairs={{0,2},{2,0},{1,3},{3,1},{4,6},{6,4},{5,7},{7,5},{8,10},{10,8},{9,1... | collective-permute-start | bytes 393224 | tf_op jit(solution)/shard_map/ppermute | solution.py:209
  33.0 7.7 %collective-permute-start.8 = (bf16[16,32,128]{2,1,0:T(8,128)(2,1)S(1)}, bf16[16,32,128]{2,1,0:T(8,128)(2,1)S(1)}, u32[]{:S(2)}, u32[]{:S(2)}) collective-permute-start(bf16[16,32,128]{2,1,0:T(8,128)(2,1)S(1)} %get-tuple-element.21), channel_id=1, source_target_pairs={{0,3},{1,2},{2,1},{3,0},{4,7},{5,6},{6,5},{7,4},{8,11},{9,10},{10,... | collective-permute-start | bytes 393224 | tf_op jit(solution)/shard_map/ppermute | solution.py:210
  45.1 20.7 %all-to-all-start = ((f16[32,4,16,128]{3,2,1,0:T(8,128)(2,1)}), f16[32,4,16,128]{3,2,1,0:T(8,128)(2,1)}, u32[]{:S(2)}, u32[]{:S(2)}) async-start(f16[32,4,16,128]{3,2,1,0:T(8,128)(2,1)} %bitcast.15), calls=%async_computation | async-start | bytes 1048576 | tf_op jit(solution)/shard_map/all_to_all | solution.py:322
  102.1 12.4 %collective-permute-start.9 = (f16[16,2,32,128]{3,2,1,0:T(8,128)(2,1)S(1)}, f16[16,2,32,128]{3,2,1,0:T(8,128)(2,1)S(1)}, u32[]{:S(2)}, u32[]{:S(2)}) collective-permute-start(f16[16,2,32,128]{3,2,1,0:T(8,128)(2,1)S(1)} %get-tuple-element.25), channel_id=1, source_target_pairs={{0,1},{1,0},{2,3},{3,2},{4,5},{5,4},{6,7},{7,6},{8,9},{9,8},{10,11... | collective-permute-start | bytes 786440 | tf_op jit(solution)/shard_map/ppermute | solution.py:207
  102.9 21.3 %collective-permute-start.10 = (f16[16,2,32,128]{3,2,1,0:T(8,128)(2,1)S(1)}, f16[16,2,32,128]{3,2,1,0:T(8,128)(2,1)S(1)}, u32[]{:S(2)}, u32[]{:S(2)}) collective-permute-start(f16[16,2,32,128]{3,2,1,0:T(8,128)(2,1)S(1)} %get-tuple-element.24), channel_id=1, source_target_pairs={{0,2},{2,0},{1,3},{3,1},{4,6},{6,4},{5,7},{7,5},{8,10},{10,8},{9,1... | collective-permute-start | bytes 786440 | tf_op jit(solution)/shard_map/ppermute | solution.py:209
  104.4 20.0 %collective-permute-start.11 = (f16[16,2,32,128]{3,2,1,0:T(8,128)(2,1)S(1)}, f16[16,2,32,128]{3,2,1,0:T(8,128)(2,1)S(1)}, u32[]{:S(2)}, u32[]{:S(2)}) collective-permute-start(f16[16,2,32,128]{3,2,1,0:T(8,128)(2,1)S(1)} %get-tuple-element.23), channel_id=1, source_target_pairs={{0,3},{1,2},{2,1},{3,0},{4,7},{5,6},{6,5},{7,4},{8,11},{9,10},{10,... | collective-permute-start | bytes 786440 | tf_op jit(solution)/shard_map/ppermute | solution.py:210
  124.4 1.3 %copy-start.1 = (f32[64,2,32,128]{3,2,1,0:T(8,128)}, f32[64,2,32,128]{3,2,1,0:T(8,128)S(1)}, u32[]{:S(2)}) copy-start(f32[64,2,32,128]{3,2,1,0:T(8,128)S(1)} %multiply_dynamic-update-slice_fusion) | copy-start | bytes 6291460

commit v12 on v11

--- a/solution.py
+++ b/solution.py
@@ -235,7 +235,7 @@
     count = group_bins * freq_size
     chunks = CHUNKS if own % (4 * CHUNKS) == 0 else 1
     part = own // chunks
-    step = math.gcd(part, 4)
+    step = math.gcd(part, 8)
     column_parts = min(freq_size, rows)
     lane_parts = freq_size // column_parts
     kept = rows // column_parts
@@ -264,7 +264,7 @@
     pieces = [lax.dynamic_index_in_dim(packed, member ^ d, 0, keepdims=False) for d in distances]
     table_re, table_im = projection_table(lag_cutoff[0], count, freq_size, pairs)
 
-    wide = math.gcd(part, 8)
+    wide = step
     local_block = lambda first: pl.BlockSpec(
         (1, wide, 2, rows, size), lambda i, m: (m[0], i + first, 0, 0, 0)
     )

time: 128 us -> 127 us (level)
  no operation moved by 1% of the time
where the time goes in v12:
time: 127 us; the launch traced here: 125 us
  starting transfers between devices  32.8 us (26%)
  blocking collectives  29.1 us (23%)
  waiting for transfers between devices  27.1 us (21%)
  Pallas kernels  19 us (15%)
  other arithmetic  11.4 us (9%)
  local copies, waits for them, and re-layouts  4.5 us (4%)
    all_to_all x1, blocking collectives, shards(): lax.all_to_all(causal, chan + ('freq',), 0, 0, tiled=True).astype(F32)  29.1 us
    ppermute x4, starting transfers between devices, swap(): return lax.ppermute(value, 'pair', SWAP)  13.9 us
    ppermute x4, waiting for transfers between devices, swap(): return lax.ppermute(value, 'side', SWAP)  12.8 us
    pallas_call x2, Pallas kernels, shards(): call(newton_kernel, part // wide, [pl.BlockSpec(memory_space=pltpu.SMEM),...  11.4 us
    select_n x1, other arithmetic, projection_table(): jnp.where(shift == 0, 0.0, (jnp.cos(half_angle) - jnp.cos(last_angle)) /...  8.24 us
    ppermute x4, starting transfers between devices, swap(): return lax.ppermute(value, 'side', SWAP)  8.11 us
    ppermute x4, waiting for transfers between devices, swap(): return lax.ppermute(value, 'pair', SWAP)  7.63 us
    all_to_all x1, waiting for transfers between devices, shards(): lax.all_to_all(sent, chan + ('freq',), 0, 0, tiled=True).astype(F32)  6.62 us
  transfers between devices with their start and end apart: 13, of which 5 were waited for; matrix products, arithmetic and copies ran while one was open for 8% of the time, Pallas kernels for 9%

profile of v12, /device:TPU:0, one launch (start us, length us, event | category | flops | bytes accessed | tf_op | source)
XLA Modules:
  0.0 124.7 jit_solution(11162345877521874129)
XLA Ops:
  0.0 1.3 %dynamic-slice_bitcast_fusion = (bf16[8,2,32,128]{3,2,1,0:T(8,128)(2,1)S(1)}, bf16[8,2,32,128]{3,2,1,0:T(8,128)(2,1)S(1)}, bf16[8,2,32,128]{3,2,1,0:T(8,128)(2,1...) fusion(bf16[4,16,2,32,128]{4,3,2,1,0:T(8,128)(2,1)} %bitcast.43, ...), kind=kLoop, calls=%fused_computation.33 | loop fusion | bytes 1572876 | tf_op jit(solution)/shard_map/reshape | solution.py:254
  1.3 0.0 copy-start.2
  1.3 3.1 %collective-permute-start.3 = (bf16[8,2,32,128]{3,2,1,0:T(8,128)(2,1)S(1)}, bf16[8,2,32,128]{3,2,1,0:T(8,128)(2,1)S(1)}, u32[]{:S(2)}, u32[]{:S(2)}) collective-permute-start(bf16[8,2,32,128]{3,2,1,0:T(8,128)(2,1)S(1)} %get-tuple-element.28), channel_id=1, source_target_pairs={{0,1},{1,0},{2,3},{3,2},{4,5},{5,4},{6,7},{7,6},{8,9},{9,8},{10,11... | collective-permute-start | bytes 393224 | tf_op jit(solution)/shard_map/ppermute | solution.py:207
  4.4 2.6 %collective-permute-start.4 = (bf16[8,2,32,128]{3,2,1,0:T(8,128)(2,1)S(1)}, bf16[8,2,32,128]{3,2,1,0:T(8,128)(2,1)S(1)}, u32[]{:S(2)}, u32[]{:S(2)}) collective-permute-start(bf16[8,2,32,128]{3,2,1,0:T(8,128)(2,1)S(1)} %get-tuple-element.27), channel_id=1, source_target_pairs={{0,2},{2,0},{1,3},{3,1},{4,6},{6,4},{5,7},{7,5},{8,10},{10,8},{9,1... | collective-permute-start | bytes 393224 | tf_op jit(solution)/shard_map/ppermute | solution.py:209
  6.9 0.0 collective-permute-start.5
  7.0 0.9 collective-permute-start
  7.8 3.5 %collective-permute-start.1 = (bf16[8,2,32,128]{3,2,1,0:T(8,128)(2,1)S(1)}, bf16[8,2,32,128]{3,2,1,0:T(8,128)(2,1)S(1)}, u32[]{:S(2)}, u32[]{:S(2)}) collective-permute-start(bf16[8,2,32,128]{3,2,1,0:T(8,128)(2,1)S(1)} %get-tuple-element.30), channel_id=1, source_target_pairs={{0,2},{2,0},{1,3},{3,1},{4,6},{6,4},{5,7},{7,5},{8,10},{10,8},{9,1... | collective-permute-start | bytes 393224 | tf_op jit(solution)/shard_map/ppermute | solution.py:209
  11.3 0.1 iota_compare_fusion
  11.4 0.0 copy-start
  11.4 1.4 %fusion.31 = (bf16[64,1,32,128]{3,2,1,0:T(8,128)(2,1)S(1)}, bf16[64,1,32,128]{3,2,1,0:T(8,128)(2,1)S(1)}) fusion(bf16[64,2,32,128]{3,2,1,0:T(8,128)(2,1)} %param.5), kind=kLoop, calls=%fused_computation.67 | loop fusion | bytes 2097152 | tf_op jit(solution)/shard_map/slice | solution.py:262
  12.8 0.1 bitcast_select_fusion.own_ref
  12.9 0.0 copy-done.2
  12.9 0.1 fusion.32
  13.0 0.0 collective-permute-done.3.one_ref
  13.0 1.6 %collective-permute-start.2 = (bf16[8,2,32,128]{3,2,1,0:T(8,128)(2,1)S(1)}, bf16[8,2,32,128]{3,2,1,0:T(8,128)(2,1)S(1)}, u32[]{:S(2)}, u32[]{:S(2)}) collective-permute-start(bf16[8,2,32,128]{3,2,1,0:T(8,128)(2,1)S(1)} %get-tuple-element.29), channel_id=1, source_target_pairs={{0,3},{1,2},{2,1},{3,0},{4,7},{5,6},{6,5},{7,4},{8,11},{9,10},{10,... | collective-permute-start | bytes 393224 | tf_op jit(solution)/shard_map/ppermute | solution.py:210
  14.6 2.7 %collective-permute-done.4.two_ref = bf16[8,2,32,128]{3,2,1,0:T(8,128)(2,1)S(1)} collective-permute-done((bf16[8,2,32,128]{3,2,1,0:T(8,128)(2,1)S(1)}, bf16[8,2,32,128]{3,2,1,0:T(8,128)(2,1)S(1)}, u32[]{:S(2)}, u32[]{:S(2)}) %collective-permute-start.4) | collective-permute-done | bytes 131104 | tf_op jit(solution)/shard_map/ppermute | solution.py:209
  17.3 0.0 collective-permute-done.5.three_ref
  17.3 0.0 copy-done
  17.3 5.7 %shard_map.46 = (bf16[16,2,128,256]{3,2,1,0:T(8,128)(2,1)S(1)}, bf16[16,2,128,128]{3,2,1,0:T(8,128)(2,1)S(1)}) custom-call(s32[1]{0:T(128)} %bitcast.member_ref, f32[8]{0:T(128)S(1)} %get-tuple-element.39.scale_ref, bf16[4,16,2,32,128]{4,3,2,1,0:T(8,128)(2,1)S(1)} %bitcast.44, bf16[8,2,32,128]{3,2,1,0:T(8,128)(2,1)S(1)} %collective-permute-done.3.one_ref, ...), custom_call_target="tpu_custom_call" | custom-call | flops 8589934592 | bytes 3145728 | tf_op jit(solution)/shard_map/pallas_call | solution.py:277
  23.0 9.1 %collective-permute-start.6 = (bf16[16,32,128]{2,1,0:T(8,128)(2,1)S(1)}, bf16[16,32,128]{2,1,0:T(8,128)(2,1)S(1)}, u32[]{:S(2)}, u32[]{:S(2)}) collective-permute-start(bf16[16,32,128]{2,1,0:T(8,128)(2,1)S(1)} %get-tuple-element.19), channel_id=1, source_target_pairs={{0,1},{1,0},{2,3},{3,2},{4,5},{5,4},{6,7},{7,6},{8,9},{9,8},{10,11... | collective-permute-start | bytes 393224 | tf_op jit(solution)/shard_map/ppermute | solution.py:207
  32.1 0.9 collective-permute-start.7
  33.0 0.0 collective-permute-done.one_ref
  33.0 1.5 %collective-permute-start.8 = (bf16[16,32,128]{2,1,0:T(8,128)(2,1)S(1)}, bf16[16,32,128]{2,1,0:T(8,128)(2,1)S(1)}, u32[]{:S(2)}, u32[]{:S(2)}) collective-permute-start(bf16[16,32,128]{2,1,0:T(8,128)(2,1)S(1)} %get-tuple-element.21), channel_id=1, source_target_pairs={{0,3},{1,2},{2,1},{3,0},{4,7},{5,6},{6,5},{7,4},{8,11},{9,10},{10,... | collective-permute-start | bytes 393224 | tf_op jit(solution)/shard_map/ppermute | solution.py:210
  34.5 0.0 collective-permute-done.1.two_ref
  34.5 0.0 collective-permute-done.2.three_ref
  34.5 5.7 %shard_map.47 = (bf16[16,2,128,256]{3,2,1,0:T(8,128)(2,1)S(1)}, bf16[16,2,128,128]{3,2,1,0:T(8,128)(2,1)S(1)}) custom-call(s32[1]{0:T(128)} %bitcast.member_ref, f32[8]{0:T(128)S(1)} %get-tuple-element.40.scale_ref, bf16[4,16,2,32,128]{4,3,2,1,0:T(8,128)(2,1)S(1)} %bitcast.45, ...), custom_call_target="tpu_custom_call", output_to_operand_aliasing={{0}: (6, {}), {1}: (7, {})} | custom-call | flops 8589934592 | bytes 3145728 | tf_op jit(solution)/shard_map/pallas_call | solution.py:277
  40.3 0.0 collective-permute-done.6.one_ref
  40.3 0.5 collective-permute-done.7.two_ref
  40.8 0.0 collective-permute-done.8.three_ref
  40.8 2.9 %shard_map.48 = f32[2048,128]{1,0:T(8,128)S(1)} custom-call(s32[1]{0:T(128)} %bitcast.member_ref, bf16[16,2,128,256]{3,2,1,0:T(8,128)(2,1)S(1)} %get-tuple-element.18.inverse_ref, bf16[4,16,32,128]{3,2,1,0:T(8,128)(2,1)S(1)} %bitcast_select_fusion.own_ref, bf16[16,32,128]{2,1,0:T(8,128)(2,1)S(1)} %collective-permute-done.6.one_ref, ...), custom_call_target="tpu_custom_call" | custom-call | flops 2684354560 | bytes 6291456 | tf_op jit(solution)/shard_map/pallas_call | solution.py:307
  43.7 0.9 convert_element_type.48
  44.5 5.2 %all-to-all-start = ((f16[32,4,16,128]{3,2,1,0:T(8,128)(2,1)}), f16[32,4,16,128]{3,2,1,0:T(8,128)(2,1)}, u32[]{:S(2)}, u32[]{:S(2)}) async-start(f16[32,4,16,128]{3,2,1,0:T(8,128)(2,1)} %bitcast.15), calls=%async_computation | async-start | bytes 1048576 | tf_op jit(solution)/shard_map/all_to_all | solution.py:322
  50.4 8.2 %fusion.3 = (f32[512,512]{1,0:T(8,128)S(1)}, f32[512,512]{1,0:T(8,128)S(1)}) fusion(s32[512]{0:T(512)S(1)} %fusion.25, s32[]{:T(128)} %bitcast.2, f32[]{:T(128)} %bitcast.1), kind=kLoop, calls=%fused_computation.9 | loop fusion | flops 7340032 | bytes 2099208 | tf_op jit(solution)/shard_map/jit(_where)/select_n | solution.py:185
  58.6 6.6 %all-to-all-done = f16[32,4,16,128]{3,2,1,0:T(8,128)(2,1)} async-done(((f16[32,4,16,128]{3,2,1,0:T(8,128)(2,1)}), f16[32,4,16,128]{3,2,1,0:T(8,128)(2,1)}, u32[]{:S(2)}, u32[]{:S(2)}) %all-to-all-start) | async-done | bytes 524320 | tf_op jit(solution)/shard_map/all_to_all | solution.py:322
  65.3 1.1 convert_element_type.49.values_ref
  66.4 2.5 %shard_map.49 = f32[32,4,2,16,128]{4,3,2,1,0:T(8,128)S(1)} custom-call(f32[512,512]{1,0:T(8,128)S(1)} %get-tuple-element.38.real_ref, f32[512,512]{1,0:T(8,128)S(1)} %get-tuple-element.37.imag_ref, f32[32,4,16,128]{3,2,1,0:T(8,128)S(1)} %convert_element_type.49.values_ref), custom_call_target="tpu_custom_call" | custom-call | flops 1610612736 | bytes 3145728 | tf_op jit(solution)/shard_map/pallas_call | solution.py:329
  68.9 0.3 convert_element_type.50
  69.2 29.1 %all_to_all.10 = f16[32,4,2,16,128]{4,3,2,1,0:T(8,128)(2,1)S(1)} all-to-all(f16[32,4,2,16,128]{4,3,2,1,0:T(8,128)(2,1)S(1)} %convert_element_type.50), channel_id=1, replica_groups=mesh['freq'=8,'side'=2,'pair'=2] {'side','pair','freq'}, dimensions={0} | all-to-all | bytes 2097152 | tf_op jit(solution)/shard_map/all_to_all | solution.py:345
  98.3 0.2 bitcast_convert_fusion.causal_ref
  98.5 2.1 %shard_map.50 = f32[4,16,2,32,128]{4,3,2,1,0:T(8,128)S(1)} custom-call(s32[1]{0:T(128)} %bitcast.member_ref, f32[4096,128]{1,0:T(8,128)S(1)} %bitcast_convert_fusion.causal_ref, bf16[16,2,128,128]{3,2,1,0:T(8,128)(2,1)S(1)} %get-tuple-element.22.psi_ref), custom_call_target="tpu_custom_call" | custom-call | flops 536870912 | bytes 5242880 | tf_op jit(solution)/shard_map/pallas_call | solution.py:350
  100.6 0.3 convert.6
  100.9 0.2 slice_bitcast_fusion
  101.1 0.8 collective-permute-start.9
  101.9 1.1 collective-permute-start.10
  103.0 0.2 broadcast_in_dim.18
  103.3 0.1 fusion.17
  103.4 2.6 %collective-permute-start.11 = (f16[16,2,32,128]{3,2,1,0:T(8,128)(2,1)S(1)}, f16[16,2,32,128]{3,2,1,0:T(8,128)(2,1)S(1)}, u32[]{:S(2)}, u32[]{:S(2)}) collective-permute-start(f16[16,2,32,128]{3,2,1,0:T(8,128)(2,1)S(1)} %get-tuple-element.23), channel_id=1, source_target_pairs={{0,3},{1,2},{2,1},{3,0},{4,7},{5,6},{6,5},{7,4},{8,11},{9,10},{10,... | collective-permute-start | bytes 786440 | tf_op jit(solution)/shard_map/ppermute | solution.py:210
  106.0 7.6 %collective-permute-done.9 = f16[16,2,32,128]{3,2,1,0:T(8,128)(2,1)S(1)} collective-permute-done((f16[16,2,32,128]{3,2,1,0:T(8,128)(2,1)S(1)}, f16[16,2,32,128]{3,2,1,0:T(8,128)(2,1)S(1)}, u32[]{:S(2)}, u32[]{:S(2)}) %collective-permute-start.9) | collective-permute-done | bytes 262176 | tf_op jit(solution)/shard_map/ppermute | solution.py:207
  113.6 0.1 multiply_dynamic-update-slice_fusion.2
  113.7 9.6 %collective-permute-done.10 = f16[16,2,32,128]{3,2,1,0:T(8,128)(2,1)S(1)} collective-permute-done((f16[16,2,32,128]{3,2,1,0:T(8,128)(2,1)S(1)}, f16[16,2,32,128]{3,2,1,0:T(8,128)(2,1)S(1)}, u32[]{:S(2)}, u32[]{:S(2)}) %collective-permute-start.10) | collective-permute-done | bytes 262176 | tf_op jit(solution)/shard_map/ppermute | solution.py:209
  123.3 0.1 multiply_dynamic-update-slice_fusion.1
  123.3 0.0 collective-permute-done.11
  123.3 0.1 multiply_dynamic-update-slice_fusion
  123.4 0.0 copy-start.1
  123.4 1.3 %copy-done.1 = f32[64,2,32,128]{3,2,1,0:T(8,128)} copy-done((f32[64,2,32,128]{3,2,1,0:T(8,128)}, f32[64,2,32,128]{3,2,1,0:T(8,128)S(1)}, u32[]{:S(2)}) %copy-start.1) | copy-done | bytes 2097176
  (3 shorter events, 0.0 us)
Async XLA Ops:
  1.3 11.6 %copy-start.2 = (f32[64]{0:T(128)S(1)}, f32[64]{0:T(128)}, u32[]{:S(2)}) copy-start(f32[64]{0:T(128)} %param.6) | copy-start | bytes 772
  1.3 11.7 %collective-permute-start.3 = (bf16[8,2,32,128]{3,2,1,0:T(8,128)(2,1)S(1)}, bf16[8,2,32,128]{3,2,1,0:T(8,128)(2,1)S(1)}, u32[]{:S(2)}, u32[]{:S(2)}) collective-permute-start(bf16[8,2,32,128]{3,2,1,0:T(8,128)(2,1)S(1)} %get-tuple-element.28), channel_id=1, source_target_pairs={{0,1},{1,0},{2,3},{3,2},{4,5},{5,4},{6,7},{7,6},{8,9},{9,8},{10,11... | collective-permute-start | bytes 393224 | tf_op jit(solution)/shard_map/ppermute | solution.py:207
  4.4 12.9 %collective-permute-start.4 = (bf16[8,2,32,128]{3,2,1,0:T(8,128)(2,1)S(1)}, bf16[8,2,32,128]{3,2,1,0:T(8,128)(2,1)S(1)}, u32[]{:S(2)}, u32[]{:S(2)}) collective-permute-start(bf16[8,2,32,128]{3,2,1,0:T(8,128)(2,1)S(1)} %get-tuple-element.27), channel_id=1, source_target_pairs={{0,2},{2,0},{1,3},{3,1},{4,6},{6,4},{5,7},{7,5},{8,10},{10,8},{9,1... | collective-permute-start | bytes 393224 | tf_op jit(solution)/shard_map/ppermute | solution.py:209
  6.9 10.4 %collective-permute-start.5 = (bf16[8,2,32,128]{3,2,1,0:T(8,128)(2,1)S(1)}, bf16[8,2,32,128]{3,2,1,0:T(8,128)(2,1)S(1)}, u32[]{:S(2)}, u32[]{:S(2)}) collective-permute-start(bf16[8,2,32,128]{3,2,1,0:T(8,128)(2,1)S(1)} %get-tuple-element.26), channel_id=1, source_target_pairs={{0,3},{1,2},{2,1},{3,0},{4,7},{5,6},{6,5},{7,4},{8,11},{9,10},{10,... | collective-permute-start | bytes 393224 | tf_op jit(solution)/shard_map/ppermute | solution.py:210
  7.0 26.1 %collective-permute-start = (bf16[8,2,32,128]{3,2,1,0:T(8,128)(2,1)S(1)}, bf16[8,2,32,128]{3,2,1,0:T(8,128)(2,1)S(1)}, u32[]{:S(2)}, u32[]{:S(2)}) collective-permute-start(bf16[8,2,32,128]{3,2,1,0:T(8,128)(2,1)S(1)} %get-tuple-element.31), channel_id=1, source_target_pairs={{0,1},{1,0},{2,3},{3,2},{4,5},{5,4},{6,7},{7,6},{8,9},{9,8},{10,11... | collective-permute-start | bytes 393224 | tf_op jit(solution)/shard_map/ppermute | solution.py:207
  7.8 26.7 %collective-permute-start.1 = (bf16[8,2,32,128]{3,2,1,0:T(8,128)(2,1)S(1)}, bf16[8,2,32,128]{3,2,1,0:T(8,128)(2,1)S(1)}, u32[]{:S(2)}, u32[]{:S(2)}) collective-permute-start(bf16[8,2,32,128]{3,2,1,0:T(8,128)(2,1)S(1)} %get-tuple-element.30), channel_id=1, source_target_pairs={{0,2},{2,0},{1,3},{3,1},{4,6},{6,4},{5,7},{7,5},{8,10},{10,8},{9,1... | collective-permute-start | bytes 393224 | tf_op jit(solution)/shard_map/ppermute | solution.py:209
  11.4 5.9 %copy-start = (bf16[64,2,32,128]{3,2,1,0:T(8,128)(2,1)S(1)}, bf16[64,2,32,128]{3,2,1,0:T(8,128)(2,1)}, u32[]{:S(2)}) copy-start(bf16[64,2,32,128]{3,2,1,0:T(8,128)(2,1)} %param.4) | copy-start | bytes 3145732
  13.0 21.5 %collective-permute-start.2 = (bf16[8,2,32,128]{3,2,1,0:T(8,128)(2,1)S(1)}, bf16[8,2,32,128]{3,2,1,0:T(8,128)(2,1)S(1)}, u32[]{:S(2)}, u32[]{:S(2)}) collective-permute-start(bf16[8,2,32,128]{3,2,1,0:T(8,128)(2,1)S(1)} %get-tuple-element.29), channel_id=1, source_target_pairs={{0,3},{1,2},{2,1},{3,0},{4,7},{5,6},{6,5},{7,4},{8,11},{9,10},{10,... | collective-permute-start | bytes 393224 | tf_op jit(solution)/shard_map/ppermute | solution.py:210
  23.0 17.2 %collective-permute-start.6 = (bf16[16,32,128]{2,1,0:T(8,128)(2,1)S(1)}, bf16[16,32,128]{2,1,0:T(8,128)(2,1)S(1)}, u32[]{:S(2)}, u32[]{:S(2)}) collective-permute-start(bf16[16,32,128]{2,1,0:T(8,128)(2,1)S(1)} %get-tuple-element.19), channel_id=1, source_target_pairs={{0,1},{1,0},{2,3},{3,2},{4,5},{5,4},{6,7},{7,6},{8,9},{9,8},{10,11... | collective-permute-start | bytes 393224 | tf_op jit(solution)/shard_map/ppermute | solution.py:207
  32.1 8.7 %collective-permute-start.7 = (bf16[16,32,128]{2,1,0:T(8,128)(2,1)S(1)}, bf16[16,32,128]{2,1,0:T(8,128)(2,1)S(1)}, u32[]{:S(2)}, u32[]{:S(2)}) collective-permute-start(bf16[16,32,128]{2,1,0:T(8,128)(2,1)S(1)} %get-tuple-element.20), channel_id=1, source_target_pairs={{0,2},{2,0},{1,3},{3,1},{4,6},{6,4},{5,7},{7,5},{8,10},{10,8},{9,1... | collective-permute-start | bytes 393224 | tf_op jit(solution)/shard_map/ppermute | solution.py:209
  33.0 7.7 %collective-permute-start.8 = (bf16[16,32,128]{2,1,0:T(8,128)(2,1)S(1)}, bf16[16,32,128]{2,1,0:T(8,128)(2,1)S(1)}, u32[]{:S(2)}, u32[]{:S(2)}) collective-permute-start(bf16[16,32,128]{2,1,0:T(8,128)(2,1)S(1)} %get-tuple-element.21), channel_id=1, source_target_pairs={{0,3},{1,2},{2,1},{3,0},{4,7},{5,6},{6,5},{7,4},{8,11},{9,10},{10,... | collective-permute-start | bytes 393224 | tf_op jit(solution)/shard_map/ppermute | solution.py:210
  44.5 20.7 %all-to-all-start = ((f16[32,4,16,128]{3,2,1,0:T(8,128)(2,1)}), f16[32,4,16,128]{3,2,1,0:T(8,128)(2,1)}, u32[]{:S(2)}, u32[]{:S(2)}) async-start(f16[32,4,16,128]{3,2,1,0:T(8,128)(2,1)} %bitcast.15), calls=%async_computation | async-start | bytes 1048576 | tf_op jit(solution)/shard_map/all_to_all | solution.py:322
  101.1 12.5 %collective-permute-start.9 = (f16[16,2,32,128]{3,2,1,0:T(8,128)(2,1)S(1)}, f16[16,2,32,128]{3,2,1,0:T(8,128)(2,1)S(1)}, u32[]{:S(2)}, u32[]{:S(2)}) collective-permute-start(f16[16,2,32,128]{3,2,1,0:T(8,128)(2,1)S(1)} %get-tuple-element.25), channel_id=1, source_target_pairs={{0,1},{1,0},{2,3},{3,2},{4,5},{5,4},{6,7},{7,6},{8,9},{9,8},{10,11... | collective-permute-start | bytes 786440 | tf_op jit(solution)/shard_map/ppermute | solution.py:207
  101.9 21.3 %collective-permute-start.10 = (f16[16,2,32,128]{3,2,1,0:T(8,128)(2,1)S(1)}, f16[16,2,32,128]{3,2,1,0:T(8,128)(2,1)S(1)}, u32[]{:S(2)}, u32[]{:S(2)}) collective-permute-start(f16[16,2,32,128]{3,2,1,0:T(8,128)(2,1)S(1)} %get-tuple-element.24), channel_id=1, source_target_pairs={{0,2},{2,0},{1,3},{3,1},{4,6},{6,4},{5,7},{7,5},{8,10},{10,8},{9,1... | collective-permute-start | bytes 786440 | tf_op jit(solution)/shard_map/ppermute | solution.py:209
  103.4 20.0 %collective-permute-start.11 = (f16[16,2,32,128]{3,2,1,0:T(8,128)(2,1)S(1)}, f16[16,2,32,128]{3,2,1,0:T(8,128)(2,1)S(1)}, u32[]{:S(2)}, u32[]{:S(2)}) collective-permute-start(f16[16,2,32,128]{3,2,1,0:T(8,128)(2,1)S(1)} %get-tuple-element.23), channel_id=1, source_target_pairs={{0,3},{1,2},{2,1},{3,0},{4,7},{5,6},{6,5},{7,4},{8,11},{9,10},{10,... | collective-permute-start | bytes 786440 | tf_op jit(solution)/shard_map/ppermute | solution.py:210
  123.4 1.3 %copy-start.1 = (f32[64,2,32,128]{3,2,1,0:T(8,128)}, f32[64,2,32,128]{3,2,1,0:T(8,128)S(1)}, u32[]{:S(2)}) copy-start(f32[64,2,32,128]{3,2,1,0:T(8,128)S(1)} %multiply_dynamic-update-slice_fusion) | copy-start | bytes 6291460

commit v13 on v12

--- a/solution.py
+++ b/solution.py
@@ -324,7 +324,7 @@
     if own % 8:
         values = values.transpose(1, 0, 2, 3).reshape(1, kept, count, lanes)
         sources, own_rows = 1, count
-    twice = math.gcd(kept, 2)
+    twice = math.gcd(kept, 4)
     table_block = pl.BlockSpec((count, count), lambda i: (0, 0))
     causal = pl.pallas_call(
         causal_kernel,

time: 127 us -> 126 us (level)
  no operation moved by 1% of the time
where the time goes in v13:
time: 126 us; the launch traced here: 124 us
  starting transfers between devices  32.8 us (26%)
  blocking collectives  29.1 us (23%)
  waiting for transfers between devices  27.1 us (22%)
  Pallas kernels  18.3 us (15%)
  other arithmetic  11.4 us (9%)
  local copies, waits for them, and re-layouts  4.5 us (4%)
    all_to_all x1, blocking collectives, shards(): lax.all_to_all(causal, chan + ('freq',), 0, 0, tiled=True).astype(F32)  29.1 us
    ppermute x4, starting transfers between devices, swap(): return lax.ppermute(value, 'pair', SWAP)  13.9 us
    ppermute x4, waiting for transfers between devices, swap(): return lax.ppermute(value, 'side', SWAP)  12.8 us
    pallas_call x2, Pallas kernels, shards(): call(newton_kernel, part // wide, [pl.BlockSpec(memory_space=pltpu.SMEM),...  11.4 us
    select_n x1, other arithmetic, projection_table(): jnp.where(shift == 0, 0.0, (jnp.cos(half_angle) - jnp.cos(last_angle)) /...  8.24 us
    ppermute x4, starting transfers between devices, swap(): return lax.ppermute(value, 'side', SWAP)  8.11 us
    ppermute x4, waiting for transfers between devices, swap(): return lax.ppermute(value, 'pair', SWAP)  7.62 us
    all_to_all x1, waiting for transfers between devices, shards(): lax.all_to_all(sent, chan + ('freq',), 0, 0, tiled=True).astype(F32)  6.62 us
  transfers between devices with their start and end apart: 13, of which 5 were waited for; matrix products, arithmetic and copies ran while one was open for 8% of the time, Pallas kernels for 9%

profile of v13, /device:TPU:0, one launch (start us, length us, event | category | flops | bytes accessed | tf_op | source)
XLA Modules:
  0.0 124.0 jit_solution(14918176556352199242)
XLA Ops:
  0.0 1.3 %dynamic-slice_bitcast_fusion = (bf16[8,2,32,128]{3,2,1,0:T(8,128)(2,1)S(1)}, bf16[8,2,32,128]{3,2,1,0:T(8,128)(2,1)S(1)}, bf16[8,2,32,128]{3,2,1,0:T(8,128)(2,1...) fusion(bf16[4,16,2,32,128]{4,3,2,1,0:T(8,128)(2,1)} %bitcast.43, ...), kind=kLoop, calls=%fused_computation.33 | loop fusion | bytes 1572876 | tf_op jit(solution)/shard_map/reshape | solution.py:254
  1.3 0.0 copy-start.2
  1.3 3.1 %collective-permute-start.3 = (bf16[8,2,32,128]{3,2,1,0:T(8,128)(2,1)S(1)}, bf16[8,2,32,128]{3,2,1,0:T(8,128)(2,1)S(1)}, u32[]{:S(2)}, u32[]{:S(2)}) collective-permute-start(bf16[8,2,32,128]{3,2,1,0:T(8,128)(2,1)S(1)} %get-tuple-element.28), channel_id=1, source_target_pairs={{0,1},{1,0},{2,3},{3,2},{4,5},{5,4},{6,7},{7,6},{8,9},{9,8},{10,11... | collective-permute-start | bytes 393224 | tf_op jit(solution)/shard_map/ppermute | solution.py:207
  4.4 2.6 %collective-permute-start.4 = (bf16[8,2,32,128]{3,2,1,0:T(8,128)(2,1)S(1)}, bf16[8,2,32,128]{3,2,1,0:T(8,128)(2,1)S(1)}, u32[]{:S(2)}, u32[]{:S(2)}) collective-permute-start(bf16[8,2,32,128]{3,2,1,0:T(8,128)(2,1)S(1)} %get-tuple-element.27), channel_id=1, source_target_pairs={{0,2},{2,0},{1,3},{3,1},{4,6},{6,4},{5,7},{7,5},{8,10},{10,8},{9,1... | collective-permute-start | bytes 393224 | tf_op jit(solution)/shard_map/ppermute | solution.py:209
  6.9 0.0 collective-permute-start.5
  7.0 0.9 collective-permute-start
  7.8 3.5 %collective-permute-start.1 = (bf16[8,2,32,128]{3,2,1,0:T(8,128)(2,1)S(1)}, bf16[8,2,32,128]{3,2,1,0:T(8,128)(2,1)S(1)}, u32[]{:S(2)}, u32[]{:S(2)}) collective-permute-start(bf16[8,2,32,128]{3,2,1,0:T(8,128)(2,1)S(1)} %get-tuple-element.30), channel_id=1, source_target_pairs={{0,2},{2,0},{1,3},{3,1},{4,6},{6,4},{5,7},{7,5},{8,10},{10,8},{9,1... | collective-permute-start | bytes 393224 | tf_op jit(solution)/shard_map/ppermute | solution.py:209
  11.3 0.1 iota_compare_fusion
  11.4 0.0 copy-start
  11.4 1.4 %fusion.31 = (bf16[64,1,32,128]{3,2,1,0:T(8,128)(2,1)S(1)}, bf16[64,1,32,128]{3,2,1,0:T(8,128)(2,1)S(1)}) fusion(bf16[64,2,32,128]{3,2,1,0:T(8,128)(2,1)} %param.5), kind=kLoop, calls=%fused_computation.67 | loop fusion | bytes 2097152 | tf_op jit(solution)/shard_map/slice | solution.py:262
  12.8 0.1 bitcast_select_fusion.own_ref
  12.9 0.0 copy-done.2
  12.9 0.1 fusion.32
  13.0 0.0 collective-permute-done.3.one_ref
  13.0 1.6 %collective-permute-start.2 = (bf16[8,2,32,128]{3,2,1,0:T(8,128)(2,1)S(1)}, bf16[8,2,32,128]{3,2,1,0:T(8,128)(2,1)S(1)}, u32[]{:S(2)}, u32[]{:S(2)}) collective-permute-start(bf16[8,2,32,128]{3,2,1,0:T(8,128)(2,1)S(1)} %get-tuple-element.29), channel_id=1, source_target_pairs={{0,3},{1,2},{2,1},{3,0},{4,7},{5,6},{6,5},{7,4},{8,11},{9,10},{10,... | collective-permute-start | bytes 393224 | tf_op jit(solution)/shard_map/ppermute | solution.py:210
  14.6 2.7 %collective-permute-done.4.two_ref = bf16[8,2,32,128]{3,2,1,0:T(8,128)(2,1)S(1)} collective-permute-done((bf16[8,2,32,128]{3,2,1,0:T(8,128)(2,1)S(1)}, bf16[8,2,32,128]{3,2,1,0:T(8,128)(2,1)S(1)}, u32[]{:S(2)}, u32[]{:S(2)}) %collective-permute-start.4) | collective-permute-done | bytes 131104 | tf_op jit(solution)/shard_map/ppermute | solution.py:209
  17.3 0.0 collective-permute-done.5.three_ref
  17.3 0.0 copy-done
  17.3 5.7 %shard_map.46 = (bf16[16,2,128,256]{3,2,1,0:T(8,128)(2,1)S(1)}, bf16[16,2,128,128]{3,2,1,0:T(8,128)(2,1)S(1)}) custom-call(s32[1]{0:T(128)} %bitcast.member_ref, f32[8]{0:T(128)S(1)} %get-tuple-element.39.scale_ref, bf16[4,16,2,32,128]{4,3,2,1,0:T(8,128)(2,1)S(1)} %bitcast.44, bf16[8,2,32,128]{3,2,1,0:T(8,128)(2,1)S(1)} %collective-permute-done.3.one_ref, ...), custom_call_target="tpu_custom_call" | custom-call | flops 8589934592 | bytes 3145728 | tf_op jit(solution)/shard_map/pallas_call | solution.py:277
  23.0 9.1 %collective-permute-start.6 = (bf16[16,32,128]{2,1,0:T(8,128)(2,1)S(1)}, bf16[16,32,128]{2,1,0:T(8,128)(2,1)S(1)}, u32[]{:S(2)}, u32[]{:S(2)}) collective-permute-start(bf16[16,32,128]{2,1,0:T(8,128)(2,1)S(1)} %get-tuple-element.19), channel_id=1, source_target_pairs={{0,1},{1,0},{2,3},{3,2},{4,5},{5,4},{6,7},{7,6},{8,9},{9,8},{10,11... | collective-permute-start | bytes 393224 | tf_op jit(solution)/shard_map/ppermute | solution.py:207
  32.1 0.9 collective-permute-start.7
  33.0 0.0 collective-permute-done.one_ref
  33.0 1.5 %collective-permute-start.8 = (bf16[16,32,128]{2,1,0:T(8,128)(2,1)S(1)}, bf16[16,32,128]{2,1,0:T(8,128)(2,1)S(1)}, u32[]{:S(2)}, u32[]{:S(2)}) collective-permute-start(bf16[16,32,128]{2,1,0:T(8,128)(2,1)S(1)} %get-tuple-element.21), channel_id=1, source_target_pairs={{0,3},{1,2},{2,1},{3,0},{4,7},{5,6},{6,5},{7,4},{8,11},{9,10},{10,... | collective-permute-start | bytes 393224 | tf_op jit(solution)/shard_map/ppermute | solution.py:210
  34.5 0.0 collective-permute-done.1.two_ref
  34.5 0.0 collective-permute-done.2.three_ref
  34.5 5.7 %shard_map.47 = (bf16[16,2,128,256]{3,2,1,0:T(8,128)(2,1)S(1)}, bf16[16,2,128,128]{3,2,1,0:T(8,128)(2,1)S(1)}) custom-call(s32[1]{0:T(128)} %bitcast.member_ref, f32[8]{0:T(128)S(1)} %get-tuple-element.40.scale_ref, bf16[4,16,2,32,128]{4,3,2,1,0:T(8,128)(2,1)S(1)} %bitcast.45, ...), custom_call_target="tpu_custom_call", output_to_operand_aliasing={{0}: (6, {}), {1}: (7, {})} | custom-call | flops 8589934592 | bytes 3145728 | tf_op jit(solution)/shard_map/pallas_call | solution.py:277
  40.3 0.0 collective-permute-done.6.one_ref
  40.3 0.5 collective-permute-done.7.two_ref
  40.8 0.0 collective-permute-done.8.three_ref
  40.8 2.9 %shard_map.48 = f32[2048,128]{1,0:T(8,128)S(1)} custom-call(s32[1]{0:T(128)} %bitcast.member_ref, bf16[16,2,128,256]{3,2,1,0:T(8,128)(2,1)S(1)} %get-tuple-element.18.inverse_ref, bf16[4,16,32,128]{3,2,1,0:T(8,128)(2,1)S(1)} %bitcast_select_fusion.own_ref, bf16[16,32,128]{2,1,0:T(8,128)(2,1)S(1)} %collective-permute-done.6.one_ref, ...), custom_call_target="tpu_custom_call" | custom-call | flops 2684354560 | bytes 6291456 | tf_op jit(solution)/shard_map/pallas_call | solution.py:307
  43.7 0.9 convert_element_type.48
  44.5 5.2 %all-to-all-start = ((f16[32,4,16,128]{3,2,1,0:T(8,128)(2,1)}), f16[32,4,16,128]{3,2,1,0:T(8,128)(2,1)}, u32[]{:S(2)}, u32[]{:S(2)}) async-start(f16[32,4,16,128]{3,2,1,0:T(8,128)(2,1)} %bitcast.15), calls=%async_computation | async-start | bytes 1048576 | tf_op jit(solution)/shard_map/all_to_all | solution.py:322
  50.4 8.2 %fusion.3 = (f32[512,512]{1,0:T(8,128)S(1)}, f32[512,512]{1,0:T(8,128)S(1)}) fusion(s32[512]{0:T(512)S(1)} %fusion.25, s32[]{:T(128)} %bitcast.2, f32[]{:T(128)} %bitcast.1), kind=kLoop, calls=%fused_computation.9 | loop fusion | flops 7340032 | bytes 2099208 | tf_op jit(solution)/shard_map/jit(_where)/select_n | solution.py:185
  58.6 6.6 %all-to-all-done = f16[32,4,16,128]{3,2,1,0:T(8,128)(2,1)} async-done(((f16[32,4,16,128]{3,2,1,0:T(8,128)(2,1)}), f16[32,4,16,128]{3,2,1,0:T(8,128)(2,1)}, u32[]{:S(2)}, u32[]{:S(2)}) %all-to-all-start) | async-done | bytes 524320 | tf_op jit(solution)/shard_map/all_to_all | solution.py:322
  65.3 1.1 convert_element_type.49.values_ref
  66.4 1.8 %shard_map.49 = f32[32,4,2,16,128]{4,3,2,1,0:T(8,128)S(1)} custom-call(f32[512,512]{1,0:T(8,128)S(1)} %get-tuple-element.38.real_ref, f32[512,512]{1,0:T(8,128)S(1)} %get-tuple-element.37.imag_ref, f32[32,4,16,128]{3,2,1,0:T(8,128)S(1)} %convert_element_type.49.values_ref), custom_call_target="tpu_custom_call" | custom-call | flops 1610612736 | bytes 3145728 | tf_op jit(solution)/shard_map/pallas_call | solution.py:329
  68.2 0.3 convert_element_type.50
  68.5 29.1 %all_to_all.10 = f16[32,4,2,16,128]{4,3,2,1,0:T(8,128)(2,1)S(1)} all-to-all(f16[32,4,2,16,128]{4,3,2,1,0:T(8,128)(2,1)S(1)} %convert_element_type.50), channel_id=1, replica_groups=mesh['freq'=8,'side'=2,'pair'=2] {'side','pair','freq'}, dimensions={0} | all-to-all | bytes 2097152 | tf_op jit(solution)/shard_map/all_to_all | solution.py:345
  97.6 0.2 bitcast_convert_fusion.causal_ref
  97.8 2.1 %shard_map.50 = f32[4,16,2,32,128]{4,3,2,1,0:T(8,128)S(1)} custom-call(s32[1]{0:T(128)} %bitcast.member_ref, f32[4096,128]{1,0:T(8,128)S(1)} %bitcast_convert_fusion.causal_ref, bf16[16,2,128,128]{3,2,1,0:T(8,128)(2,1)S(1)} %get-tuple-element.22.psi_ref), custom_call_target="tpu_custom_call" | custom-call | flops 536870912 | bytes 5242880 | tf_op jit(solution)/shard_map/pallas_call | solution.py:350
  99.9 0.3 convert.6
  100.2 0.2 slice_bitcast_fusion
  100.4 0.8 collective-permute-start.9
  101.2 1.1 collective-permute-start.10
  102.3 0.2 broadcast_in_dim.18
  102.6 0.1 fusion.17
  102.7 2.6 %collective-permute-start.11 = (f16[16,2,32,128]{3,2,1,0:T(8,128)(2,1)S(1)}, f16[16,2,32,128]{3,2,1,0:T(8,128)(2,1)S(1)}, u32[]{:S(2)}, u32[]{:S(2)}) collective-permute-start(f16[16,2,32,128]{3,2,1,0:T(8,128)(2,1)S(1)} %get-tuple-element.23), channel_id=1, source_target_pairs={{0,3},{1,2},{2,1},{3,0},{4,7},{5,6},{6,5},{7,4},{8,11},{9,10},{10,... | collective-permute-start | bytes 786440 | tf_op jit(solution)/shard_map/ppermute | solution.py:210
  105.3 7.6 %collective-permute-done.9 = f16[16,2,32,128]{3,2,1,0:T(8,128)(2,1)S(1)} collective-permute-done((f16[16,2,32,128]{3,2,1,0:T(8,128)(2,1)S(1)}, f16[16,2,32,128]{3,2,1,0:T(8,128)(2,1)S(1)}, u32[]{:S(2)}, u32[]{:S(2)}) %collective-permute-start.9) | collective-permute-done | bytes 262176 | tf_op jit(solution)/shard_map/ppermute | solution.py:207
  112.9 0.1 multiply_dynamic-update-slice_fusion.2
  113.0 9.6 %collective-permute-done.10 = f16[16,2,32,128]{3,2,1,0:T(8,128)(2,1)S(1)} collective-permute-done((f16[16,2,32,128]{3,2,1,0:T(8,128)(2,1)S(1)}, f16[16,2,32,128]{3,2,1,0:T(8,128)(2,1)S(1)}, u32[]{:S(2)}, u32[]{:S(2)}) %collective-permute-start.10) | collective-permute-done | bytes 262176 | tf_op jit(solution)/shard_map/ppermute | solution.py:209
  122.6 0.1 multiply_dynamic-update-slice_fusion.1
  122.6 0.0 collective-permute-done.11
  122.6 0.1 multiply_dynamic-update-slice_fusion
  122.7 0.0 copy-start.1
  122.7 1.3 %copy-done.1 = f32[64,2,32,128]{3,2,1,0:T(8,128)} copy-done((f32[64,2,32,128]{3,2,1,0:T(8,128)}, f32[64,2,32,128]{3,2,1,0:T(8,128)S(1)}, u32[]{:S(2)}) %copy-start.1) | copy-done | bytes 2097176
  (3 shorter events, 0.0 us)
Async XLA Ops:
  1.3 11.6 %copy-start.2 = (f32[64]{0:T(128)S(1)}, f32[64]{0:T(128)}, u32[]{:S(2)}) copy-start(f32[64]{0:T(128)} %param.6) | copy-start | bytes 772
  1.3 11.7 %collective-permute-start.3 = (bf16[8,2,32,128]{3,2,1,0:T(8,128)(2,1)S(1)}, bf16[8,2,32,128]{3,2,1,0:T(8,128)(2,1)S(1)}, u32[]{:S(2)}, u32[]{:S(2)}) collective-permute-start(bf16[8,2,32,128]{3,2,1,0:T(8,128)(2,1)S(1)} %get-tuple-element.28), channel_id=1, source_target_pairs={{0,1},{1,0},{2,3},{3,2},{4,5},{5,4},{6,7},{7,6},{8,9},{9,8},{10,11... | collective-permute-start | bytes 393224 | tf_op jit(solution)/shard_map/ppermute | solution.py:207
  4.4 12.9 %collective-permute-start.4 = (bf16[8,2,32,128]{3,2,1,0:T(8,128)(2,1)S(1)}, bf16[8,2,32,128]{3,2,1,0:T(8,128)(2,1)S(1)}, u32[]{:S(2)}, u32[]{:S(2)}) collective-permute-start(bf16[8,2,32,128]{3,2,1,0:T(8,128)(2,1)S(1)} %get-tuple-element.27), channel_id=1, source_target_pairs={{0,2},{2,0},{1,3},{3,1},{4,6},{6,4},{5,7},{7,5},{8,10},{10,8},{9,1... | collective-permute-start | bytes 393224 | tf_op jit(solution)/shard_map/ppermute | solution.py:209
  6.9 10.4 %collective-permute-start.5 = (bf16[8,2,32,128]{3,2,1,0:T(8,128)(2,1)S(1)}, bf16[8,2,32,128]{3,2,1,0:T(8,128)(2,1)S(1)}, u32[]{:S(2)}, u32[]{:S(2)}) collective-permute-start(bf16[8,2,32,128]{3,2,1,0:T(8,128)(2,1)S(1)} %get-tuple-element.26), channel_id=1, source_target_pairs={{0,3},{1,2},{2,1},{3,0},{4,7},{5,6},{6,5},{7,4},{8,11},{9,10},{10,... | collective-permute-start | bytes 393224 | tf_op jit(solution)/shard_map/ppermute | solution.py:210
  7.0 26.1 %collective-permute-start = (bf16[8,2,32,128]{3,2,1,0:T(8,128)(2,1)S(1)}, bf16[8,2,32,128]{3,2,1,0:T(8,128)(2,1)S(1)}, u32[]{:S(2)}, u32[]{:S(2)}) collective-permute-start(bf16[8,2,32,128]{3,2,1,0:T(8,128)(2,1)S(1)} %get-tuple-element.31), channel_id=1, source_target_pairs={{0,1},{1,0},{2,3},{3,2},{4,5},{5,4},{6,7},{7,6},{8,9},{9,8},{10,11... | collective-permute-start | bytes 393224 | tf_op jit(solution)/shard_map/ppermute | solution.py:207
  7.8 26.7 %collective-permute-start.1 = (bf16[8,2,32,128]{3,2,1,0:T(8,128)(2,1)S(1)}, bf16[8,2,32,128]{3,2,1,0:T(8,128)(2,1)S(1)}, u32[]{:S(2)}, u32[]{:S(2)}) collective-permute-start(bf16[8,2,32,128]{3,2,1,0:T(8,128)(2,1)S(1)} %get-tuple-element.30), channel_id=1, source_target_pairs={{0,2},{2,0},{1,3},{3,1},{4,6},{6,4},{5,7},{7,5},{8,10},{10,8},{9,1... | collective-permute-start | bytes 393224 | tf_op jit(solution)/shard_map/ppermute | solution.py:209
  11.4 5.9 %copy-start = (bf16[64,2,32,128]{3,2,1,0:T(8,128)(2,1)S(1)}, bf16[64,2,32,128]{3,2,1,0:T(8,128)(2,1)}, u32[]{:S(2)}) copy-start(bf16[64,2,32,128]{3,2,1,0:T(8,128)(2,1)} %param.4) | copy-start | bytes 3145732
  13.0 21.5 %collective-permute-start.2 = (bf16[8,2,32,128]{3,2,1,0:T(8,128)(2,1)S(1)}, bf16[8,2,32,128]{3,2,1,0:T(8,128)(2,1)S(1)}, u32[]{:S(2)}, u32[]{:S(2)}) collective-permute-start(bf16[8,2,32,128]{3,2,1,0:T(8,128)(2,1)S(1)} %get-tuple-element.29), channel_id=1, source_target_pairs={{0,3},{1,2},{2,1},{3,0},{4,7},{5,6},{6,5},{7,4},{8,11},{9,10},{10,... | collective-permute-start | bytes 393224 | tf_op jit(solution)/shard_map/ppermute | solution.py:210
  23.0 17.2 %collective-permute-start.6 = (bf16[16,32,128]{2,1,0:T(8,128)(2,1)S(1)}, bf16[16,32,128]{2,1,0:T(8,128)(2,1)S(1)}, u32[]{:S(2)}, u32[]{:S(2)}) collective-permute-start(bf16[16,32,128]{2,1,0:T(8,128)(2,1)S(1)} %get-tuple-element.19), channel_id=1, source_target_pairs={{0,1},{1,0},{2,3},{3,2},{4,5},{5,4},{6,7},{7,6},{8,9},{9,8},{10,11... | collective-permute-start | bytes 393224 | tf_op jit(solution)/shard_map/ppermute | solution.py:207
  32.1 8.7 %collective-permute-start.7 = (bf16[16,32,128]{2,1,0:T(8,128)(2,1)S(1)}, bf16[16,32,128]{2,1,0:T(8,128)(2,1)S(1)}, u32[]{:S(2)}, u32[]{:S(2)}) collective-permute-start(bf16[16,32,128]{2,1,0:T(8,128)(2,1)S(1)} %get-tuple-element.20), channel_id=1, source_target_pairs={{0,2},{2,0},{1,3},{3,1},{4,6},{6,4},{5,7},{7,5},{8,10},{10,8},{9,1... | collective-permute-start | bytes 393224 | tf_op jit(solution)/shard_map/ppermute | solution.py:209
  33.0 7.7 %collective-permute-start.8 = (bf16[16,32,128]{2,1,0:T(8,128)(2,1)S(1)}, bf16[16,32,128]{2,1,0:T(8,128)(2,1)S(1)}, u32[]{:S(2)}, u32[]{:S(2)}) collective-permute-start(bf16[16,32,128]{2,1,0:T(8,128)(2,1)S(1)} %get-tuple-element.21), channel_id=1, source_target_pairs={{0,3},{1,2},{2,1},{3,0},{4,7},{5,6},{6,5},{7,4},{8,11},{9,10},{10,... | collective-permute-start | bytes 393224 | tf_op jit(solution)/shard_map/ppermute | solution.py:210
  44.5 20.7 %all-to-all-start = ((f16[32,4,16,128]{3,2,1,0:T(8,128)(2,1)}), f16[32,4,16,128]{3,2,1,0:T(8,128)(2,1)}, u32[]{:S(2)}, u32[]{:S(2)}) async-start(f16[32,4,16,128]{3,2,1,0:T(8,128)(2,1)} %bitcast.15), calls=%async_computation | async-start | bytes 1048576 | tf_op jit(solution)/shard_map/all_to_all | solution.py:322
  100.4 12.5 %collective-permute-start.9 = (f16[16,2,32,128]{3,2,1,0:T(8,128)(2,1)S(1)}, f16[16,2,32,128]{3,2,1,0:T(8,128)(2,1)S(1)}, u32[]{:S(2)}, u32[]{:S(2)}) collective-permute-start(f16[16,2,32,128]{3,2,1,0:T(8,128)(2,1)S(1)} %get-tuple-element.25), channel_id=1, source_target_pairs={{0,1},{1,0},{2,3},{3,2},{4,5},{5,4},{6,7},{7,6},{8,9},{9,8},{10,11... | collective-permute-start | bytes 786440 | tf_op jit(solution)/shard_map/ppermute | solution.py:207
  101.2 21.3 %collective-permute-start.10 = (f16[16,2,32,128]{3,2,1,0:T(8,128)(2,1)S(1)}, f16[16,2,32,128]{3,2,1,0:T(8,128)(2,1)S(1)}, u32[]{:S(2)}, u32[]{:S(2)}) collective-permute-start(f16[16,2,32,128]{3,2,1,0:T(8,128)(2,1)S(1)} %get-tuple-element.24), channel_id=1, source_target_pairs={{0,2},{2,0},{1,3},{3,1},{4,6},{6,4},{5,7},{7,5},{8,10},{10,8},{9,1... | collective-permute-start | bytes 786440 | tf_op jit(solution)/shard_map/ppermute | solution.py:209
  102.7 20.0 %collective-permute-start.11 = (f16[16,2,32,128]{3,2,1,0:T(8,128)(2,1)S(1)}, f16[16,2,32,128]{3,2,1,0:T(8,128)(2,1)S(1)}, u32[]{:S(2)}, u32[]{:S(2)}) collective-permute-start(f16[16,2,32,128]{3,2,1,0:T(8,128)(2,1)S(1)} %get-tuple-element.23), channel_id=1, source_target_pairs={{0,3},{1,2},{2,1},{3,0},{4,7},{5,6},{6,5},{7,4},{8,11},{9,10},{10,... | collective-permute-start | bytes 786440 | tf_op jit(solution)/shard_map/ppermute | solution.py:210
  122.7 1.3 %copy-start.1 = (f32[64,2,32,128]{3,2,1,0:T(8,128)}, f32[64,2,32,128]{3,2,1,0:T(8,128)S(1)}, u32[]{:S(2)}) copy-start(f32[64,2,32,128]{3,2,1,0:T(8,128)S(1)} %multiply_dynamic-update-slice_fusion) | copy-start | bytes 6291460

commit v14 on v13

--- a/solution.py
+++ b/solution.py
@@ -235,7 +235,7 @@
     count = group_bins * freq_size
     chunks = CHUNKS if own % (4 * CHUNKS) == 0 else 1
     part = own // chunks
-    step = math.gcd(part, 8)
+    step = math.gcd(own, 16)
     column_parts = min(freq_size, rows)
     lane_parts = freq_size // column_parts
     kept = rows // column_parts
@@ -264,7 +264,7 @@
     pieces = [lax.dynamic_index_in_dim(packed, member ^ d, 0, keepdims=False) for d in distances]
     table_re, table_im = projection_table(lag_cutoff[0], count, freq_size, pairs)
 
-    wide = step
+    wide = math.gcd(part, 8)
     local_block = lambda first: pl.BlockSpec(
         (1, wide, 2, rows, size), lambda i, m: (m[0], i + first, 0, 0, 0)
     )

time: 126 us -> 126 us (level)
  no operation moved by 1% of the time
where the time goes in v14:
time: 126 us; the launch traced here: 123 us
  starting transfers between devices  32.8 us (26%)
  blocking collectives  29.1 us (23%)
  waiting for transfers between devices  27.1 us (22%)
  Pallas kernels  17.7 us (14%)
  other arithmetic  11.4 us (9%)
  local copies, waits for them, and re-layouts  4.5 us (4%)
    all_to_all x1, blocking collectives, shards(): lax.all_to_all(causal, chan + ('freq',), 0, 0, tiled=True).astype(F32)  29.1 us
    ppermute x4, starting transfers between devices, swap(): return lax.ppermute(value, 'pair', SWAP)  13.9 us
    ppermute x4, waiting for transfers between devices, swap(): return lax.ppermute(value, 'side', SWAP)  12.8 us
    pallas_call x2, Pallas kernels, shards(): call(newton_kernel, part // wide, [pl.BlockSpec(memory_space=pltpu.SMEM),...  11.4 us
    select_n x1, other arithmetic, projection_table(): jnp.where(shift == 0, 0.0, (jnp.cos(half_angle) - jnp.cos(last_angle)) /...  8.24 us
    ppermute x4, starting transfers between devices, swap(): return lax.ppermute(value, 'side', SWAP)  8.11 us
    ppermute x4, waiting for transfers between devices, swap(): return lax.ppermute(value, 'pair', SWAP)  7.63 us
    all_to_all x1, waiting for transfers between devices, shards(): lax.all_to_all(sent, chan + ('freq',), 0, 0, tiled=True).astype(F32)  6.62 us
  transfers between devices with their start and end apart: 13, of which 5 were waited for; matrix products, arithmetic and copies ran while one was open for 8% of the time, Pallas kernels for 9%

profile of v14, /device:TPU:0, one launch (start us, length us, event | category | flops | bytes accessed | tf_op | source)
XLA Modules:
  0.0 123.5 jit_solution(18055628023138558645)
XLA Ops:
  0.0 1.3 %dynamic-slice_bitcast_fusion = (bf16[8,2,32,128]{3,2,1,0:T(8,128)(2,1)S(1)}, bf16[8,2,32,128]{3,2,1,0:T(8,128)(2,1)S(1)}, bf16[8,2,32,128]{3,2,1,0:T(8,128)(2,1...) fusion(bf16[4,16,2,32,128]{4,3,2,1,0:T(8,128)(2,1)} %bitcast.43, ...), kind=kLoop, calls=%fused_computation.33 | loop fusion | bytes 1572876 | tf_op jit(solution)/shard_map/reshape | solution.py:254
  1.3 0.0 copy-start.2
  1.3 3.1 %collective-permute-start.3 = (bf16[8,2,32,128]{3,2,1,0:T(8,128)(2,1)S(1)}, bf16[8,2,32,128]{3,2,1,0:T(8,128)(2,1)S(1)}, u32[]{:S(2)}, u32[]{:S(2)}) collective-permute-start(bf16[8,2,32,128]{3,2,1,0:T(8,128)(2,1)S(1)} %get-tuple-element.28), channel_id=1, source_target_pairs={{0,1},{1,0},{2,3},{3,2},{4,5},{5,4},{6,7},{7,6},{8,9},{9,8},{10,11... | collective-permute-start | bytes 393224 | tf_op jit(solution)/shard_map/ppermute | solution.py:207
  4.4 2.6 %collective-permute-start.4 = (bf16[8,2,32,128]{3,2,1,0:T(8,128)(2,1)S(1)}, bf16[8,2,32,128]{3,2,1,0:T(8,128)(2,1)S(1)}, u32[]{:S(2)}, u32[]{:S(2)}) collective-permute-start(bf16[8,2,32,128]{3,2,1,0:T(8,128)(2,1)S(1)} %get-tuple-element.27), channel_id=1, source_target_pairs={{0,2},{2,0},{1,3},{3,1},{4,6},{6,4},{5,7},{7,5},{8,10},{10,8},{9,1... | collective-permute-start | bytes 393224 | tf_op jit(solution)/shard_map/ppermute | solution.py:209
  6.9 0.0 collective-permute-start.5
  7.0 0.9 collective-permute-start
  7.8 3.5 %collective-permute-start.1 = (bf16[8,2,32,128]{3,2,1,0:T(8,128)(2,1)S(1)}, bf16[8,2,32,128]{3,2,1,0:T(8,128)(2,1)S(1)}, u32[]{:S(2)}, u32[]{:S(2)}) collective-permute-start(bf16[8,2,32,128]{3,2,1,0:T(8,128)(2,1)S(1)} %get-tuple-element.30), channel_id=1, source_target_pairs={{0,2},{2,0},{1,3},{3,1},{4,6},{6,4},{5,7},{7,5},{8,10},{10,8},{9,1... | collective-permute-start | bytes 393224 | tf_op jit(solution)/shard_map/ppermute | solution.py:209
  11.3 0.1 iota_compare_fusion
  11.4 0.0 copy-start
  11.4 1.4 %fusion.31 = (bf16[64,1,32,128]{3,2,1,0:T(8,128)(2,1)S(1)}, bf16[64,1,32,128]{3,2,1,0:T(8,128)(2,1)S(1)}) fusion(bf16[64,2,32,128]{3,2,1,0:T(8,128)(2,1)} %param.5), kind=kLoop, calls=%fused_computation.67 | loop fusion | bytes 2097152 | tf_op jit(solution)/shard_map/slice | solution.py:262
  12.8 0.1 bitcast_select_fusion.own_ref
  12.9 0.0 copy-done.2
  12.9 0.1 fusion.32
  13.0 0.0 collective-permute-done.3.one_ref
  13.0 1.6 %collective-permute-start.2 = (bf16[8,2,32,128]{3,2,1,0:T(8,128)(2,1)S(1)}, bf16[8,2,32,128]{3,2,1,0:T(8,128)(2,1)S(1)}, u32[]{:S(2)}, u32[]{:S(2)}) collective-permute-start(bf16[8,2,32,128]{3,2,1,0:T(8,128)(2,1)S(1)} %get-tuple-element.29), channel_id=1, source_target_pairs={{0,3},{1,2},{2,1},{3,0},{4,7},{5,6},{6,5},{7,4},{8,11},{9,10},{10,... | collective-permute-start | bytes 393224 | tf_op jit(solution)/shard_map/ppermute | solution.py:210
  14.6 2.7 %collective-permute-done.4.two_ref = bf16[8,2,32,128]{3,2,1,0:T(8,128)(2,1)S(1)} collective-permute-done((bf16[8,2,32,128]{3,2,1,0:T(8,128)(2,1)S(1)}, bf16[8,2,32,128]{3,2,1,0:T(8,128)(2,1)S(1)}, u32[]{:S(2)}, u32[]{:S(2)}) %collective-permute-start.4) | collective-permute-done | bytes 131104 | tf_op jit(solution)/shard_map/ppermute | solution.py:209
  17.3 0.0 collective-permute-done.5.three_ref
  17.3 0.0 copy-done
  17.3 5.7 %shard_map.46 = (bf16[16,2,128,256]{3,2,1,0:T(8,128)(2,1)S(1)}, bf16[16,2,128,128]{3,2,1,0:T(8,128)(2,1)S(1)}) custom-call(s32[1]{0:T(128)} %bitcast.member_ref, f32[8]{0:T(128)S(1)} %get-tuple-element.39.scale_ref, bf16[4,16,2,32,128]{4,3,2,1,0:T(8,128)(2,1)S(1)} %bitcast.44, bf16[8,2,32,128]{3,2,1,0:T(8,128)(2,1)S(1)} %collective-permute-done.3.one_ref, ...), custom_call_target="tpu_custom_call" | custom-call | flops 8589934592 | bytes 3145728 | tf_op jit(solution)/shard_map/pallas_call | solution.py:277
  23.0 9.1 %collective-permute-start.6 = (bf16[16,32,128]{2,1,0:T(8,128)(2,1)S(1)}, bf16[16,32,128]{2,1,0:T(8,128)(2,1)S(1)}, u32[]{:S(2)}, u32[]{:S(2)}) collective-permute-start(bf16[16,32,128]{2,1,0:T(8,128)(2,1)S(1)} %get-tuple-element.19), channel_id=1, source_target_pairs={{0,1},{1,0},{2,3},{3,2},{4,5},{5,4},{6,7},{7,6},{8,9},{9,8},{10,11... | collective-permute-start | bytes 393224 | tf_op jit(solution)/shard_map/ppermute | solution.py:207
  32.1 0.9 collective-permute-start.7
  33.0 0.0 collective-permute-done.one_ref
  33.0 1.5 %collective-permute-start.8 = (bf16[16,32,128]{2,1,0:T(8,128)(2,1)S(1)}, bf16[16,32,128]{2,1,0:T(8,128)(2,1)S(1)}, u32[]{:S(2)}, u32[]{:S(2)}) collective-permute-start(bf16[16,32,128]{2,1,0:T(8,128)(2,1)S(1)} %get-tuple-element.21), channel_id=1, source_target_pairs={{0,3},{1,2},{2,1},{3,0},{4,7},{5,6},{6,5},{7,4},{8,11},{9,10},{10,... | collective-permute-start | bytes 393224 | tf_op jit(solution)/shard_map/ppermute | solution.py:210
  34.5 0.0 collective-permute-done.1.two_ref
  34.5 0.0 collective-permute-done.2.three_ref
  34.5 5.7 %shard_map.47 = (bf16[16,2,128,256]{3,2,1,0:T(8,128)(2,1)S(1)}, bf16[16,2,128,128]{3,2,1,0:T(8,128)(2,1)S(1)}) custom-call(s32[1]{0:T(128)} %bitcast.member_ref, f32[8]{0:T(128)S(1)} %get-tuple-element.40.scale_ref, bf16[4,16,2,32,128]{4,3,2,1,0:T(8,128)(2,1)S(1)} %bitcast.45, ...), custom_call_target="tpu_custom_call", output_to_operand_aliasing={{0}: (6, {}), {1}: (7, {})} | custom-call | flops 8589934592 | bytes 3145728 | tf_op jit(solution)/shard_map/pallas_call | solution.py:277
  40.3 0.0 collective-permute-done.6.one_ref
  40.3 0.5 collective-permute-done.7.two_ref
  40.8 0.0 collective-permute-done.8.three_ref
  40.8 2.8 %shard_map.48 = f32[2048,128]{1,0:T(8,128)S(1)} custom-call(s32[1]{0:T(128)} %bitcast.member_ref, bf16[16,2,128,256]{3,2,1,0:T(8,128)(2,1)S(1)} %get-tuple-element.18.inverse_ref, bf16[4,16,32,128]{3,2,1,0:T(8,128)(2,1)S(1)} %bitcast_select_fusion.own_ref, bf16[16,32,128]{2,1,0:T(8,128)(2,1)S(1)} %collective-permute-done.6.one_ref, ...), custom_call_target="tpu_custom_call" | custom-call | flops 2684354560 | bytes 6291456 | tf_op jit(solution)/shard_map/pallas_call | solution.py:307
  43.6 0.9 convert_element_type.48
  44.4 5.2 %all-to-all-start = ((f16[32,4,16,128]{3,2,1,0:T(8,128)(2,1)}), f16[32,4,16,128]{3,2,1,0:T(8,128)(2,1)}, u32[]{:S(2)}, u32[]{:S(2)}) async-start(f16[32,4,16,128]{3,2,1,0:T(8,128)(2,1)} %bitcast.15), calls=%async_computation | async-start | bytes 1048576 | tf_op jit(solution)/shard_map/all_to_all | solution.py:322
  50.3 8.2 %fusion.3 = (f32[512,512]{1,0:T(8,128)S(1)}, f32[512,512]{1,0:T(8,128)S(1)}) fusion(s32[512]{0:T(512)S(1)} %fusion.25, s32[]{:T(128)} %bitcast.2, f32[]{:T(128)} %bitcast.1), kind=kLoop, calls=%fused_computation.9 | loop fusion | flops 7340032 | bytes 2099208 | tf_op jit(solution)/shard_map/jit(_where)/select_n | solution.py:185
  58.5 6.6 %all-to-all-done = f16[32,4,16,128]{3,2,1,0:T(8,128)(2,1)} async-done(((f16[32,4,16,128]{3,2,1,0:T(8,128)(2,1)}), f16[32,4,16,128]{3,2,1,0:T(8,128)(2,1)}, u32[]{:S(2)}, u32[]{:S(2)}) %all-to-all-start) | async-done | bytes 524320 | tf_op jit(solution)/shard_map/all_to_all | solution.py:322
  65.1 1.1 convert_element_type.49.values_ref
  66.3 1.8 %shard_map.49 = f32[32,4,2,16,128]{4,3,2,1,0:T(8,128)S(1)} custom-call(f32[512,512]{1,0:T(8,128)S(1)} %get-tuple-element.38.real_ref, f32[512,512]{1,0:T(8,128)S(1)} %get-tuple-element.37.imag_ref, f32[32,4,16,128]{3,2,1,0:T(8,128)S(1)} %convert_element_type.49.values_ref), custom_call_target="tpu_custom_call" | custom-call | flops 1610612736 | bytes 3145728 | tf_op jit(solution)/shard_map/pallas_call | solution.py:329
  68.1 0.3 convert_element_type.50
  68.3 29.1 %all_to_all.10 = f16[32,4,2,16,128]{4,3,2,1,0:T(8,128)(2,1)S(1)} all-to-all(f16[32,4,2,16,128]{4,3,2,1,0:T(8,128)(2,1)S(1)} %convert_element_type.50), channel_id=1, replica_groups=mesh['freq'=8,'side'=2,'pair'=2] {'side','pair','freq'}, dimensions={0} | all-to-all | bytes 2097152 | tf_op jit(solution)/shard_map/all_to_all | solution.py:345
  97.5 0.2 bitcast_convert_fusion.causal_ref
  97.7 1.7 %shard_map.50 = f32[4,16,2,32,128]{4,3,2,1,0:T(8,128)S(1)} custom-call(s32[1]{0:T(128)} %bitcast.member_ref, f32[4096,128]{1,0:T(8,128)S(1)} %bitcast_convert_fusion.causal_ref, bf16[16,2,128,128]{3,2,1,0:T(8,128)(2,1)S(1)} %get-tuple-element.22.psi_ref), custom_call_target="tpu_custom_call" | custom-call | flops 536870912 | bytes 5242880 | tf_op jit(solution)/shard_map/pallas_call | solution.py:350
  99.4 0.3 convert.6
  99.7 0.2 slice_bitcast_fusion
  99.9 0.8 collective-permute-start.9
  100.7 1.1 collective-permute-start.10
  101.8 0.2 broadcast_in_dim.18
  102.1 0.1 fusion.17
  102.1 2.6 %collective-permute-start.11 = (f16[16,2,32,128]{3,2,1,0:T(8,128)(2,1)S(1)}, f16[16,2,32,128]{3,2,1,0:T(8,128)(2,1)S(1)}, u32[]{:S(2)}, u32[]{:S(2)}) collective-permute-start(f16[16,2,32,128]{3,2,1,0:T(8,128)(2,1)S(1)} %get-tuple-element.23), channel_id=1, source_target_pairs={{0,3},{1,2},{2,1},{3,0},{4,7},{5,6},{6,5},{7,4},{8,11},{9,10},{10,... | collective-permute-start | bytes 786440 | tf_op jit(solution)/shard_map/ppermute | solution.py:210
  104.7 7.6 %collective-permute-done.9 = f16[16,2,32,128]{3,2,1,0:T(8,128)(2,1)S(1)} collective-permute-done((f16[16,2,32,128]{3,2,1,0:T(8,128)(2,1)S(1)}, f16[16,2,32,128]{3,2,1,0:T(8,128)(2,1)S(1)}, u32[]{:S(2)}, u32[]{:S(2)}) %collective-permute-start.9) | collective-permute-done | bytes 262176 | tf_op jit(solution)/shard_map/ppermute | solution.py:207
  112.3 0.1 multiply_dynamic-update-slice_fusion.2
  112.4 9.6 %collective-permute-done.10 = f16[16,2,32,128]{3,2,1,0:T(8,128)(2,1)S(1)} collective-permute-done((f16[16,2,32,128]{3,2,1,0:T(8,128)(2,1)S(1)}, f16[16,2,32,128]{3,2,1,0:T(8,128)(2,1)S(1)}, u32[]{:S(2)}, u32[]{:S(2)}) %collective-permute-start.10) | collective-permute-done | bytes 262176 | tf_op jit(solution)/shard_map/ppermute | solution.py:209
  122.0 0.1 multiply_dynamic-update-slice_fusion.1
  122.1 0.0 collective-permute-done.11
  122.1 0.1 multiply_dynamic-update-slice_fusion
  122.2 0.0 copy-start.1
  122.2 1.3 %copy-done.1 = f32[64,2,32,128]{3,2,1,0:T(8,128)} copy-done((f32[64,2,32,128]{3,2,1,0:T(8,128)}, f32[64,2,32,128]{3,2,1,0:T(8,128)S(1)}, u32[]{:S(2)}) %copy-start.1) | copy-done | bytes 2097176
  (3 shorter events, 0.0 us)
Async XLA Ops:
  1.3 11.6 %copy-start.2 = (f32[64]{0:T(128)S(1)}, f32[64]{0:T(128)}, u32[]{:S(2)}) copy-start(f32[64]{0:T(128)} %param.6) | copy-start | bytes 772
  1.3 11.7 %collective-permute-start.3 = (bf16[8,2,32,128]{3,2,1,0:T(8,128)(2,1)S(1)}, bf16[8,2,32,128]{3,2,1,0:T(8,128)(2,1)S(1)}, u32[]{:S(2)}, u32[]{:S(2)}) collective-permute-start(bf16[8,2,32,128]{3,2,1,0:T(8,128)(2,1)S(1)} %get-tuple-element.28), channel_id=1, source_target_pairs={{0,1},{1,0},{2,3},{3,2},{4,5},{5,4},{6,7},{7,6},{8,9},{9,8},{10,11... | collective-permute-start | bytes 393224 | tf_op jit(solution)/shard_map/ppermute | solution.py:207
  4.4 12.9 %collective-permute-start.4 = (bf16[8,2,32,128]{3,2,1,0:T(8,128)(2,1)S(1)}, bf16[8,2,32,128]{3,2,1,0:T(8,128)(2,1)S(1)}, u32[]{:S(2)}, u32[]{:S(2)}) collective-permute-start(bf16[8,2,32,128]{3,2,1,0:T(8,128)(2,1)S(1)} %get-tuple-element.27), channel_id=1, source_target_pairs={{0,2},{2,0},{1,3},{3,1},{4,6},{6,4},{5,7},{7,5},{8,10},{10,8},{9,1... | collective-permute-start | bytes 393224 | tf_op jit(solution)/shard_map/ppermute | solution.py:209
  6.9 10.4 %collective-permute-start.5 = (bf16[8,2,32,128]{3,2,1,0:T(8,128)(2,1)S(1)}, bf16[8,2,32,128]{3,2,1,0:T(8,128)(2,1)S(1)}, u32[]{:S(2)}, u32[]{:S(2)}) collective-permute-start(bf16[8,2,32,128]{3,2,1,0:T(8,128)(2,1)S(1)} %get-tuple-element.26), channel_id=1, source_target_pairs={{0,3},{1,2},{2,1},{3,0},{4,7},{5,6},{6,5},{7,4},{8,11},{9,10},{10,... | collective-permute-start | bytes 393224 | tf_op jit(solution)/shard_map/ppermute | solution.py:210
  7.0 26.1 %collective-permute-start = (bf16[8,2,32,128]{3,2,1,0:T(8,128)(2,1)S(1)}, bf16[8,2,32,128]{3,2,1,0:T(8,128)(2,1)S(1)}, u32[]{:S(2)}, u32[]{:S(2)}) collective-permute-start(bf16[8,2,32,128]{3,2,1,0:T(8,128)(2,1)S(1)} %get-tuple-element.31), channel_id=1, source_target_pairs={{0,1},{1,0},{2,3},{3,2},{4,5},{5,4},{6,7},{7,6},{8,9},{9,8},{10,11... | collective-permute-start | bytes 393224 | tf_op jit(solution)/shard_map/ppermute | solution.py:207
  7.8 26.7 %collective-permute-start.1 = (bf16[8,2,32,128]{3,2,1,0:T(8,128)(2,1)S(1)}, bf16[8,2,32,128]{3,2,1,0:T(8,128)(2,1)S(1)}, u32[]{:S(2)}, u32[]{:S(2)}) collective-permute-start(bf16[8,2,32,128]{3,2,1,0:T(8,128)(2,1)S(1)} %get-tuple-element.30), channel_id=1, source_target_pairs={{0,2},{2,0},{1,3},{3,1},{4,6},{6,4},{5,7},{7,5},{8,10},{10,8},{9,1... | collective-permute-start | bytes 393224 | tf_op jit(solution)/shard_map/ppermute | solution.py:209
  11.4 5.9 %copy-start = (bf16[64,2,32,128]{3,2,1,0:T(8,128)(2,1)S(1)}, bf16[64,2,32,128]{3,2,1,0:T(8,128)(2,1)}, u32[]{:S(2)}) copy-start(bf16[64,2,32,128]{3,2,1,0:T(8,128)(2,1)} %param.4) | copy-start | bytes 3145732
  13.0 21.5 %collective-permute-start.2 = (bf16[8,2,32,128]{3,2,1,0:T(8,128)(2,1)S(1)}, bf16[8,2,32,128]{3,2,1,0:T(8,128)(2,1)S(1)}, u32[]{:S(2)}, u32[]{:S(2)}) collective-permute-start(bf16[8,2,32,128]{3,2,1,0:T(8,128)(2,1)S(1)} %get-tuple-element.29), channel_id=1, source_target_pairs={{0,3},{1,2},{2,1},{3,0},{4,7},{5,6},{6,5},{7,4},{8,11},{9,10},{10,... | collective-permute-start | bytes 393224 | tf_op jit(solution)/shard_map/ppermute | solution.py:210
  23.0 17.2 %collective-permute-start.6 = (bf16[16,32,128]{2,1,0:T(8,128)(2,1)S(1)}, bf16[16,32,128]{2,1,0:T(8,128)(2,1)S(1)}, u32[]{:S(2)}, u32[]{:S(2)}) collective-permute-start(bf16[16,32,128]{2,1,0:T(8,128)(2,1)S(1)} %get-tuple-element.19), channel_id=1, source_target_pairs={{0,1},{1,0},{2,3},{3,2},{4,5},{5,4},{6,7},{7,6},{8,9},{9,8},{10,11... | collective-permute-start | bytes 393224 | tf_op jit(solution)/shard_map/ppermute | solution.py:207
  32.1 8.7 %collective-permute-start.7 = (bf16[16,32,128]{2,1,0:T(8,128)(2,1)S(1)}, bf16[16,32,128]{2,1,0:T(8,128)(2,1)S(1)}, u32[]{:S(2)}, u32[]{:S(2)}) collective-permute-start(bf16[16,32,128]{2,1,0:T(8,128)(2,1)S(1)} %get-tuple-element.20), channel_id=1, source_target_pairs={{0,2},{2,0},{1,3},{3,1},{4,6},{6,4},{5,7},{7,5},{8,10},{10,8},{9,1... | collective-permute-start | bytes 393224 | tf_op jit(solution)/shard_map/ppermute | solution.py:209
  33.0 7.7 %collective-permute-start.8 = (bf16[16,32,128]{2,1,0:T(8,128)(2,1)S(1)}, bf16[16,32,128]{2,1,0:T(8,128)(2,1)S(1)}, u32[]{:S(2)}, u32[]{:S(2)}) collective-permute-start(bf16[16,32,128]{2,1,0:T(8,128)(2,1)S(1)} %get-tuple-element.21), channel_id=1, source_target_pairs={{0,3},{1,2},{2,1},{3,0},{4,7},{5,6},{6,5},{7,4},{8,11},{9,10},{10,... | collective-permute-start | bytes 393224 | tf_op jit(solution)/shard_map/ppermute | solution.py:210
  44.4 20.7 %all-to-all-start = ((f16[32,4,16,128]{3,2,1,0:T(8,128)(2,1)}), f16[32,4,16,128]{3,2,1,0:T(8,128)(2,1)}, u32[]{:S(2)}, u32[]{:S(2)}) async-start(f16[32,4,16,128]{3,2,1,0:T(8,128)(2,1)} %bitcast.15), calls=%async_computation | async-start | bytes 1048576 | tf_op jit(solution)/shard_map/all_to_all | solution.py:322
  99.9 12.5 %collective-permute-start.9 = (f16[16,2,32,128]{3,2,1,0:T(8,128)(2,1)S(1)}, f16[16,2,32,128]{3,2,1,0:T(8,128)(2,1)S(1)}, u32[]{:S(2)}, u32[]{:S(2)}) collective-permute-start(f16[16,2,32,128]{3,2,1,0:T(8,128)(2,1)S(1)} %get-tuple-element.25), channel_id=1, source_target_pairs={{0,1},{1,0},{2,3},{3,2},{4,5},{5,4},{6,7},{7,6},{8,9},{9,8},{10,11... | collective-permute-start | bytes 786440 | tf_op jit(solution)/shard_map/ppermute | solution.py:207
  100.7 21.3 %collective-permute-start.10 = (f16[16,2,32,128]{3,2,1,0:T(8,128)(2,1)S(1)}, f16[16,2,32,128]{3,2,1,0:T(8,128)(2,1)S(1)}, u32[]{:S(2)}, u32[]{:S(2)}) collective-permute-start(f16[16,2,32,128]{3,2,1,0:T(8,128)(2,1)S(1)} %get-tuple-element.24), channel_id=1, source_target_pairs={{0,2},{2,0},{1,3},{3,1},{4,6},{6,4},{5,7},{7,5},{8,10},{10,8},{9,1... | collective-permute-start | bytes 786440 | tf_op jit(solution)/shard_map/ppermute | solution.py:209
  102.1 20.0 %collective-permute-start.11 = (f16[16,2,32,128]{3,2,1,0:T(8,128)(2,1)S(1)}, f16[16,2,32,128]{3,2,1,0:T(8,128)(2,1)S(1)}, u32[]{:S(2)}, u32[]{:S(2)}) collective-permute-start(f16[16,2,32,128]{3,2,1,0:T(8,128)(2,1)S(1)} %get-tuple-element.23), channel_id=1, source_target_pairs={{0,3},{1,2},{2,1},{3,0},{4,7},{5,6},{6,5},{7,4},{8,11},{9,10},{10,... | collective-permute-start | bytes 786440 | tf_op jit(solution)/shard_map/ppermute | solution.py:210
  122.2 1.3 %copy-start.1 = (f32[64,2,32,128]{3,2,1,0:T(8,128)}, f32[64,2,32,128]{3,2,1,0:T(8,128)S(1)}, u32[]{:S(2)}) copy-start(f32[64,2,32,128]{3,2,1,0:T(8,128)S(1)} %multiply_dynamic-update-slice_fusion) | copy-start | bytes 6291460

commit v15 on v14

--- a/solution.py
+++ b/solution.py
@@ -298,8 +298,7 @@
             {6 + index: index for index in range(len(state))},
         )(members, scale, factors, *arrived[chunk], *state)
         if chunk == 0:
-            held = lax.optimization_barrier(tuple(pieces) + tuple(state))
-            state = held[len(pieces) :]
+            held = lax.optimization_barrier(tuple(pieces) + tuple(arrived[0]))[: len(pieces)]
             packed_arrived = [swap(piece, d) for piece, d in zip(held, distances)]
     inverse, psi = state
 

time: 126 us -> 126 us (level)
    ppermute x4, starting transfers between devices: 13.9 us -> 15.2 us  [swap(): return lax.ppermute(value, 'pair', SWAP)]
  transfers between devices with their start and end apart: 13 -> 13, of which waited for: 5 -> 4; matrix products, arithmetic and copies ran while one was open for 8% -> 8% of each run, Pallas kernels for 9% -> 9%
where the time goes in v15:
time: 126 us; the launch traced here: 124 us
  starting transfers between devices  33.7 us (27%)
  blocking collectives  29.1 us (23%)
  waiting for transfers between devices  26.6 us (21%)
  Pallas kernels  17.7 us (14%)
  other arithmetic  11.4 us (9%)
  local copies, waits for them, and re-layouts  4.5 us (4%)
    all_to_all x1, blocking collectives, shards(): lax.all_to_all(causal, chan + ('freq',), 0, 0, tiled=True).astype(F32)  29.1 us
    ppermute x4, starting transfers between devices, swap(): return lax.ppermute(value, 'pair', SWAP)  15.2 us
    ppermute x4, waiting for transfers between devices, swap(): return lax.ppermute(value, 'side', SWAP)  12.4 us
    pallas_call x2, Pallas kernels, shards(): call(newton_kernel, part // wide, [pl.BlockSpec(memory_space=pltpu.SMEM),...  11.4 us
    select_n x1, other arithmetic, projection_table(): jnp.where(shift == 0, 0.0, (jnp.cos(half_angle) - jnp.cos(last_angle)) /...  8.24 us
    ppermute x4, starting transfers between devices, swap(): return lax.ppermute(value, 'side', SWAP)  8.07 us
    ppermute x4, waiting for transfers between devices, swap(): return lax.ppermute(value, 'pair', SWAP)  7.62 us
    all_to_all x1, waiting for transfers between devices, shards(): lax.all_to_all(sent, chan + ('freq',), 0, 0, tiled=True).astype(F32)  6.62 us
  transfers between devices with their start and end apart: 13, of which 4 were waited for; matrix products, arithmetic and copies ran while one was open for 8% of the time, Pallas kernels for 9%

profile of v15, /device:TPU:0, one launch (start us, length us, event | category | flops | bytes accessed | tf_op | source)
XLA Modules:
  0.0 123.9 jit_solution(749864847821272964)
XLA Ops:
  0.0 1.3 %dynamic-slice_bitcast_fusion.3 = (bf16[8,2,32,128]{3,2,1,0:T(8,128)(2,1)S(1)}, bf16[8,2,32,128]{3,2,1,0:T(8,128)(2,1)S(1)}, bf16[8,2,32,128]{3,2,1,0:T(8,128)(2...) fusion(bf16[4,16,2,32,128]{4,3,2,1,0:T(8,128)(2,1)} %bitcast.43, ...), kind=kLoop, calls=%fused_computation.36 | loop fusion | bytes 1572876 | tf_op jit(solution)/shard_map/reshape | solution.py:254
  1.3 0.0 copy-start.2
  1.3 3.1 %collective-permute-start.3 = (bf16[8,2,32,128]{3,2,1,0:T(8,128)(2,1)S(1)}, bf16[8,2,32,128]{3,2,1,0:T(8,128)(2,1)S(1)}, u32[]{:S(2)}, u32[]{:S(2)}) collective-permute-start(bf16[8,2,32,128]{3,2,1,0:T(8,128)(2,1)S(1)} %get-tuple-element.26), channel_id=1, source_target_pairs={{0,1},{1,0},{2,3},{3,2},{4,5},{5,4},{6,7},{7,6},{8,9},{9,8},{10,11... | collective-permute-start | bytes 393224 | tf_op jit(solution)/shard_map/ppermute | solution.py:207
  4.4 2.6 %collective-permute-start.4 = (bf16[8,2,32,128]{3,2,1,0:T(8,128)(2,1)S(1)}, bf16[8,2,32,128]{3,2,1,0:T(8,128)(2,1)S(1)}, u32[]{:S(2)}, u32[]{:S(2)}) collective-permute-start(bf16[8,2,32,128]{3,2,1,0:T(8,128)(2,1)S(1)} %get-tuple-element.25), channel_id=1, source_target_pairs={{0,2},{2,0},{1,3},{3,1},{4,6},{6,4},{5,7},{7,5},{8,10},{10,8},{9,1... | collective-permute-start | bytes 393224 | tf_op jit(solution)/shard_map/ppermute | solution.py:209
  6.9 0.0 collective-permute-start.5
  7.0 0.9 collective-permute-start
  7.8 3.5 %collective-permute-start.1 = (bf16[8,2,32,128]{3,2,1,0:T(8,128)(2,1)S(1)}, bf16[8,2,32,128]{3,2,1,0:T(8,128)(2,1)S(1)}, u32[]{:S(2)}, u32[]{:S(2)}) collective-permute-start(bf16[8,2,32,128]{3,2,1,0:T(8,128)(2,1)S(1)} %get-tuple-element.28), channel_id=1, source_target_pairs={{0,2},{2,0},{1,3},{3,1},{4,6},{6,4},{5,7},{7,5},{8,10},{10,8},{9,1... | collective-permute-start | bytes 393224 | tf_op jit(solution)/shard_map/ppermute | solution.py:209
  11.3 0.1 iota_compare_fusion
  11.4 0.0 copy-start
  11.4 1.4 %fusion.31 = (bf16[64,1,32,128]{3,2,1,0:T(8,128)(2,1)S(1)}, bf16[64,1,32,128]{3,2,1,0:T(8,128)(2,1)S(1)}) fusion(bf16[64,2,32,128]{3,2,1,0:T(8,128)(2,1)} %param.5), kind=kLoop, calls=%fused_computation.67 | loop fusion | bytes 2097152 | tf_op jit(solution)/shard_map/slice | solution.py:262
  12.8 0.1 bitcast_select_fusion.own_ref
  12.9 0.0 copy-done.2
  12.9 0.1 fusion.32
  13.0 0.0 collective-permute-done.3.one_ref
  13.0 1.6 %collective-permute-start.2 = (bf16[8,2,32,128]{3,2,1,0:T(8,128)(2,1)S(1)}, bf16[8,2,32,128]{3,2,1,0:T(8,128)(2,1)S(1)}, u32[]{:S(2)}, u32[]{:S(2)}) collective-permute-start(bf16[8,2,32,128]{3,2,1,0:T(8,128)(2,1)S(1)} %get-tuple-element.27), channel_id=1, source_target_pairs={{0,3},{1,2},{2,1},{3,0},{4,7},{5,6},{6,5},{7,4},{8,11},{9,10},{10,... | collective-permute-start | bytes 393224 | tf_op jit(solution)/shard_map/ppermute | solution.py:210
  14.6 2.7 %collective-permute-done.4.two_ref = bf16[8,2,32,128]{3,2,1,0:T(8,128)(2,1)S(1)} collective-permute-done((bf16[8,2,32,128]{3,2,1,0:T(8,128)(2,1)S(1)}, bf16[8,2,32,128]{3,2,1,0:T(8,128)(2,1)S(1)}, u32[]{:S(2)}, u32[]{:S(2)}) %collective-permute-start.4) | collective-permute-done | bytes 131104 | tf_op jit(solution)/shard_map/ppermute | solution.py:209
  17.3 0.0 collective-permute-done.5.three_ref
  17.3 10.4 %collective-permute-start.6 = (bf16[16,32,128]{2,1,0:T(8,128)(2,1)S(1)}, bf16[16,32,128]{2,1,0:T(8,128)(2,1)S(1)}, u32[]{:S(2)}, u32[]{:S(2)}) collective-permute-start(bf16[16,32,128]{2,1,0:T(8,128)(2,1)S(1)} %get-tuple-element.15), channel_id=1, source_target_pairs={{0,1},{1,0},{2,3},{3,2},{4,5},{5,4},{6,7},{7,6},{8,9},{9,8},{10,11... | collective-permute-start | bytes 393224 | tf_op jit(solution)/shard_map/ppermute | solution.py:207
  27.7 0.9 collective-permute-start.7
  28.6 0.0 copy-done
  28.6 5.7 %shard_map.46 = (bf16[16,2,128,256]{3,2,1,0:T(8,128)(2,1)S(1)}, bf16[16,2,128,128]{3,2,1,0:T(8,128)(2,1)S(1)}) custom-call(s32[1]{0:T(128)} %bitcast.member_ref, f32[8]{0:T(128)S(1)} %get-tuple-element.35.scale_ref, bf16[4,16,2,32,128]{4,3,2,1,0:T(8,128)(2,1)S(1)} %bitcast.44, bf16[8,2,32,128]{3,2,1,0:T(8,128)(2,1)S(1)} %collective-permute-done.3.one_ref, ...), custom_call_target="tpu_custom_call" | custom-call | flops 8589934592 | bytes 3145728 | tf_op jit(solution)/shard_map/pallas_call | solution.py:277
  34.3 0.0 collective-permute-done.one_ref
  34.3 1.5 %collective-permute-start.8 = (bf16[16,32,128]{2,1,0:T(8,128)(2,1)S(1)}, bf16[16,32,128]{2,1,0:T(8,128)(2,1)S(1)}, u32[]{:S(2)}, u32[]{:S(2)}) collective-permute-start(bf16[16,32,128]{2,1,0:T(8,128)(2,1)S(1)} %get-tuple-element.17), channel_id=1, source_target_pairs={{0,3},{1,2},{2,1},{3,0},{4,7},{5,6},{6,5},{7,4},{8,11},{9,10},{10,... | collective-permute-start | bytes 393224 | tf_op jit(solution)/shard_map/ppermute | solution.py:210
  35.9 0.0 collective-permute-done.1.two_ref
  35.9 0.0 collective-permute-done.2.three_ref
  35.9 5.7 %shard_map.47 = (bf16[16,2,128,256]{3,2,1,0:T(8,128)(2,1)S(1)}, bf16[16,2,128,128]{3,2,1,0:T(8,128)(2,1)S(1)}) custom-call(s32[1]{0:T(128)} %bitcast.member_ref, f32[8]{0:T(128)S(1)} %get-tuple-element.36.scale_ref, bf16[4,16,2,32,128]{4,3,2,1,0:T(8,128)(2,1)S(1)} %bitcast.45, ...), custom_call_target="tpu_custom_call", output_to_operand_aliasing={{0}: (6, {}), {1}: (7, {})} | custom-call | flops 8589934592 | bytes 3145728 | tf_op jit(solution)/shard_map/pallas_call | solution.py:277
  41.6 0.0 collective-permute-done.6.one_ref
  41.6 0.0 collective-permute-done.7.two_ref
  41.6 0.0 collective-permute-done.8.three_ref
  41.6 2.8 %shard_map.48 = f32[2048,128]{1,0:T(8,128)S(1)} custom-call(s32[1]{0:T(128)} %bitcast.member_ref, bf16[16,2,128,256]{3,2,1,0:T(8,128)(2,1)S(1)} %get-tuple-element.14.inverse_ref, bf16[4,16,32,128]{3,2,1,0:T(8,128)(2,1)S(1)} %bitcast_select_fusion.own_ref, bf16[16,32,128]{2,1,0:T(8,128)(2,1)S(1)} %collective-permute-done.6.one_ref, ...), custom_call_target="tpu_custom_call" | custom-call | flops 2684354560 | bytes 6291456 | tf_op jit(solution)/shard_map/pallas_call | solution.py:306
  44.4 0.9 convert_element_type.48
  45.3 4.7 %all-to-all-start = ((f16[32,4,16,128]{3,2,1,0:T(8,128)(2,1)}), f16[32,4,16,128]{3,2,1,0:T(8,128)(2,1)}, u32[]{:S(2)}, u32[]{:S(2)}) async-start(f16[32,4,16,128]{3,2,1,0:T(8,128)(2,1)} %bitcast.15), calls=%async_computation | async-start | bytes 1048576 | tf_op jit(solution)/shard_map/all_to_all | solution.py:321
  50.7 8.2 %fusion.3 = (f32[512,512]{1,0:T(8,128)S(1)}, f32[512,512]{1,0:T(8,128)S(1)}) fusion(s32[512]{0:T(512)S(1)} %fusion.25, s32[]{:T(128)} %bitcast.2, f32[]{:T(128)} %bitcast.1), kind=kLoop, calls=%fused_computation.9 | loop fusion | flops 7340032 | bytes 2099208 | tf_op jit(solution)/shard_map/jit(_where)/select_n | solution.py:185
  58.9 6.6 %all-to-all-done = f16[32,4,16,128]{3,2,1,0:T(8,128)(2,1)} async-done(((f16[32,4,16,128]{3,2,1,0:T(8,128)(2,1)}), f16[32,4,16,128]{3,2,1,0:T(8,128)(2,1)}, u32[]{:S(2)}, u32[]{:S(2)}) %all-to-all-start) | async-done | bytes 524320 | tf_op jit(solution)/shard_map/all_to_all | solution.py:321
  65.6 1.1 convert_element_type.49.values_ref
  66.7 1.8 %shard_map.49 = f32[32,4,2,16,128]{4,3,2,1,0:T(8,128)S(1)} custom-call(f32[512,512]{1,0:T(8,128)S(1)} %get-tuple-element.34.real_ref, f32[512,512]{1,0:T(8,128)S(1)} %get-tuple-element.33.imag_ref, f32[32,4,16,128]{3,2,1,0:T(8,128)S(1)} %convert_element_type.49.values_ref), custom_call_target="tpu_custom_call" | custom-call | flops 1610612736 | bytes 3145728 | tf_op jit(solution)/shard_map/pallas_call | solution.py:328
  68.5 0.3 convert_element_type.50
  68.8 29.1 %all_to_all.10 = f16[32,4,2,16,128]{4,3,2,1,0:T(8,128)(2,1)S(1)} all-to-all(f16[32,4,2,16,128]{4,3,2,1,0:T(8,128)(2,1)S(1)} %convert_element_type.50), channel_id=1, replica_groups=mesh['freq'=8,'side'=2,'pair'=2] {'side','pair','freq'}, dimensions={0} | all-to-all | bytes 2097152 | tf_op jit(solution)/shard_map/all_to_all | solution.py:344
  97.9 0.2 bitcast_convert_fusion.causal_ref
  98.1 1.7 %shard_map.50 = f32[4,16,2,32,128]{4,3,2,1,0:T(8,128)S(1)} custom-call(s32[1]{0:T(128)} %bitcast.member_ref, f32[4096,128]{1,0:T(8,128)S(1)} %bitcast_convert_fusion.causal_ref, bf16[16,2,128,128]{3,2,1,0:T(8,128)(2,1)S(1)} %get-tuple-element.18.psi_ref), custom_call_target="tpu_custom_call" | custom-call | flops 536870912 | bytes 5242880 | tf_op jit(solution)/shard_map/pallas_call | solution.py:349
  99.8 0.3 convert.6
  100.1 0.2 slice_bitcast_fusion
  100.3 0.8 collective-permute-start.9
  101.1 1.1 collective-permute-start.10
  102.2 0.2 broadcast_in_dim.18
  102.5 0.1 fusion.17
  102.5 2.6 %collective-permute-start.11 = (f16[16,2,32,128]{3,2,1,0:T(8,128)(2,1)S(1)}, f16[16,2,32,128]{3,2,1,0:T(8,128)(2,1)S(1)}, u32[]{:S(2)}, u32[]{:S(2)}) collective-permute-start(f16[16,2,32,128]{3,2,1,0:T(8,128)(2,1)S(1)} %get-tuple-element.19), channel_id=1, source_target_pairs={{0,3},{1,2},{2,1},{3,0},{4,7},{5,6},{6,5},{7,4},{8,11},{9,10},{10,... | collective-permute-start | bytes 786440 | tf_op jit(solution)/shard_map/ppermute | solution.py:210
  105.1 7.6 %collective-permute-done.9 = f16[16,2,32,128]{3,2,1,0:T(8,128)(2,1)S(1)} collective-permute-done((f16[16,2,32,128]{3,2,1,0:T(8,128)(2,1)S(1)}, f16[16,2,32,128]{3,2,1,0:T(8,128)(2,1)S(1)}, u32[]{:S(2)}, u32[]{:S(2)}) %collective-permute-start.9) | collective-permute-done | bytes 262176 | tf_op jit(solution)/shard_map/ppermute | solution.py:207
  112.7 0.1 multiply_dynamic-update-slice_fusion.2
  112.8 9.6 %collective-permute-done.10 = f16[16,2,32,128]{3,2,1,0:T(8,128)(2,1)S(1)} collective-permute-done((f16[16,2,32,128]{3,2,1,0:T(8,128)(2,1)S(1)}, f16[16,2,32,128]{3,2,1,0:T(8,128)(2,1)S(1)}, u32[]{:S(2)}, u32[]{:S(2)}) %collective-permute-start.10) | collective-permute-done | bytes 262176 | tf_op jit(solution)/shard_map/ppermute | solution.py:209
  122.4 0.1 multiply_dynamic-update-slice_fusion.1
  122.5 0.0 collective-permute-done.11
  122.5 0.1 multiply_dynamic-update-slice_fusion
  122.6 0.0 copy-start.1
  122.6 1.3 %copy-done.1 = f32[64,2,32,128]{3,2,1,0:T(8,128)} copy-done((f32[64,2,32,128]{3,2,1,0:T(8,128)}, f32[64,2,32,128]{3,2,1,0:T(8,128)S(1)}, u32[]{:S(2)}) %copy-start.1) | copy-done | bytes 2097176
  (3 shorter events, 0.0 us)
Async XLA Ops:
  1.3 11.6 %copy-start.2 = (f32[64]{0:T(128)S(1)}, f32[64]{0:T(128)}, u32[]{:S(2)}) copy-start(f32[64]{0:T(128)} %param.6) | copy-start | bytes 772
  1.3 11.7 %collective-permute-start.3 = (bf16[8,2,32,128]{3,2,1,0:T(8,128)(2,1)S(1)}, bf16[8,2,32,128]{3,2,1,0:T(8,128)(2,1)S(1)}, u32[]{:S(2)}, u32[]{:S(2)}) collective-permute-start(bf16[8,2,32,128]{3,2,1,0:T(8,128)(2,1)S(1)} %get-tuple-element.26), channel_id=1, source_target_pairs={{0,1},{1,0},{2,3},{3,2},{4,5},{5,4},{6,7},{7,6},{8,9},{9,8},{10,11... | collective-permute-start | bytes 393224 | tf_op jit(solution)/shard_map/ppermute | solution.py:207
  4.4 12.9 %collective-permute-start.4 = (bf16[8,2,32,128]{3,2,1,0:T(8,128)(2,1)S(1)}, bf16[8,2,32,128]{3,2,1,0:T(8,128)(2,1)S(1)}, u32[]{:S(2)}, u32[]{:S(2)}) collective-permute-start(bf16[8,2,32,128]{3,2,1,0:T(8,128)(2,1)S(1)} %get-tuple-element.25), channel_id=1, source_target_pairs={{0,2},{2,0},{1,3},{3,1},{4,6},{6,4},{5,7},{7,5},{8,10},{10,8},{9,1... | collective-permute-start | bytes 393224 | tf_op jit(solution)/shard_map/ppermute | solution.py:209
  6.9 10.4 %collective-permute-start.5 = (bf16[8,2,32,128]{3,2,1,0:T(8,128)(2,1)S(1)}, bf16[8,2,32,128]{3,2,1,0:T(8,128)(2,1)S(1)}, u32[]{:S(2)}, u32[]{:S(2)}) collective-permute-start(bf16[8,2,32,128]{3,2,1,0:T(8,128)(2,1)S(1)} %get-tuple-element.24), channel_id=1, source_target_pairs={{0,3},{1,2},{2,1},{3,0},{4,7},{5,6},{6,5},{7,4},{8,11},{9,10},{10,... | collective-permute-start | bytes 393224 | tf_op jit(solution)/shard_map/ppermute | solution.py:210
  7.0 27.4 %collective-permute-start = (bf16[8,2,32,128]{3,2,1,0:T(8,128)(2,1)S(1)}, bf16[8,2,32,128]{3,2,1,0:T(8,128)(2,1)S(1)}, u32[]{:S(2)}, u32[]{:S(2)}) collective-permute-start(bf16[8,2,32,128]{3,2,1,0:T(8,128)(2,1)S(1)} %get-tuple-element.29), channel_id=1, source_target_pairs={{0,1},{1,0},{2,3},{3,2},{4,5},{5,4},{6,7},{7,6},{8,9},{9,8},{10,11... | collective-permute-start | bytes 393224 | tf_op jit(solution)/shard_map/ppermute | solution.py:207
  7.8 28.0 %collective-permute-start.1 = (bf16[8,2,32,128]{3,2,1,0:T(8,128)(2,1)S(1)}, bf16[8,2,32,128]{3,2,1,0:T(8,128)(2,1)S(1)}, u32[]{:S(2)}, u32[]{:S(2)}) collective-permute-start(bf16[8,2,32,128]{3,2,1,0:T(8,128)(2,1)S(1)} %get-tuple-element.28), channel_id=1, source_target_pairs={{0,2},{2,0},{1,3},{3,1},{4,6},{6,4},{5,7},{7,5},{8,10},{10,8},{9,1... | collective-permute-start | bytes 393224 | tf_op jit(solution)/shard_map/ppermute | solution.py:209
  11.4 17.2 %copy-start = (bf16[64,2,32,128]{3,2,1,0:T(8,128)(2,1)S(1)}, bf16[64,2,32,128]{3,2,1,0:T(8,128)(2,1)}, u32[]{:S(2)}) copy-start(bf16[64,2,32,128]{3,2,1,0:T(8,128)(2,1)} %param.4) | copy-start | bytes 3145732
  13.0 22.9 %collective-permute-start.2 = (bf16[8,2,32,128]{3,2,1,0:T(8,128)(2,1)S(1)}, bf16[8,2,32,128]{3,2,1,0:T(8,128)(2,1)S(1)}, u32[]{:S(2)}, u32[]{:S(2)}) collective-permute-start(bf16[8,2,32,128]{3,2,1,0:T(8,128)(2,1)S(1)} %get-tuple-element.27), channel_id=1, source_target_pairs={{0,3},{1,2},{2,1},{3,0},{4,7},{5,6},{6,5},{7,4},{8,11},{9,10},{10,... | collective-permute-start | bytes 393224 | tf_op jit(solution)/shard_map/ppermute | solution.py:210
  17.3 24.3 %collective-permute-start.6 = (bf16[16,32,128]{2,1,0:T(8,128)(2,1)S(1)}, bf16[16,32,128]{2,1,0:T(8,128)(2,1)S(1)}, u32[]{:S(2)}, u32[]{:S(2)}) collective-permute-start(bf16[16,32,128]{2,1,0:T(8,128)(2,1)S(1)} %get-tuple-element.15), channel_id=1, source_target_pairs={{0,1},{1,0},{2,3},{3,2},{4,5},{5,4},{6,7},{7,6},{8,9},{9,8},{10,11... | collective-permute-start | bytes 393224 | tf_op jit(solution)/shard_map/ppermute | solution.py:207
  27.7 13.9 %collective-permute-start.7 = (bf16[16,32,128]{2,1,0:T(8,128)(2,1)S(1)}, bf16[16,32,128]{2,1,0:T(8,128)(2,1)S(1)}, u32[]{:S(2)}, u32[]{:S(2)}) collective-permute-start(bf16[16,32,128]{2,1,0:T(8,128)(2,1)S(1)} %get-tuple-element.16), channel_id=1, source_target_pairs={{0,2},{2,0},{1,3},{3,1},{4,6},{6,4},{5,7},{7,5},{8,10},{10,8},{9,1... | collective-permute-start | bytes 393224 | tf_op jit(solution)/shard_map/ppermute | solution.py:209
  34.3 7.3 %collective-permute-start.8 = (bf16[16,32,128]{2,1,0:T(8,128)(2,1)S(1)}, bf16[16,32,128]{2,1,0:T(8,128)(2,1)S(1)}, u32[]{:S(2)}, u32[]{:S(2)}) collective-permute-start(bf16[16,32,128]{2,1,0:T(8,128)(2,1)S(1)} %get-tuple-element.17), channel_id=1, source_target_pairs={{0,3},{1,2},{2,1},{3,0},{4,7},{5,6},{6,5},{7,4},{8,11},{9,10},{10,... | collective-permute-start | bytes 393224 | tf_op jit(solution)/shard_map/ppermute | solution.py:210
  45.3 20.3 %all-to-all-start = ((f16[32,4,16,128]{3,2,1,0:T(8,128)(2,1)}), f16[32,4,16,128]{3,2,1,0:T(8,128)(2,1)}, u32[]{:S(2)}, u32[]{:S(2)}) async-start(f16[32,4,16,128]{3,2,1,0:T(8,128)(2,1)} %bitcast.15), calls=%async_computation | async-start | bytes 1048576 | tf_op jit(solution)/shard_map/all_to_all | solution.py:321
  100.3 12.4 %collective-permute-start.9 = (f16[16,2,32,128]{3,2,1,0:T(8,128)(2,1)S(1)}, f16[16,2,32,128]{3,2,1,0:T(8,128)(2,1)S(1)}, u32[]{:S(2)}, u32[]{:S(2)}) collective-permute-start(f16[16,2,32,128]{3,2,1,0:T(8,128)(2,1)S(1)} %get-tuple-element.21), channel_id=1, source_target_pairs={{0,1},{1,0},{2,3},{3,2},{4,5},{5,4},{6,7},{7,6},{8,9},{9,8},{10,11... | collective-permute-start | bytes 786440 | tf_op jit(solution)/shard_map/ppermute | solution.py:207
  101.1 21.3 %collective-permute-start.10 = (f16[16,2,32,128]{3,2,1,0:T(8,128)(2,1)S(1)}, f16[16,2,32,128]{3,2,1,0:T(8,128)(2,1)S(1)}, u32[]{:S(2)}, u32[]{:S(2)}) collective-permute-start(f16[16,2,32,128]{3,2,1,0:T(8,128)(2,1)S(1)} %get-tuple-element.20), channel_id=1, source_target_pairs={{0,2},{2,0},{1,3},{3,1},{4,6},{6,4},{5,7},{7,5},{8,10},{10,8},{9,1... | collective-permute-start | bytes 786440 | tf_op jit(solution)/shard_map/ppermute | solution.py:209
  102.5 20.0 %collective-permute-start.11 = (f16[16,2,32,128]{3,2,1,0:T(8,128)(2,1)S(1)}, f16[16,2,32,128]{3,2,1,0:T(8,128)(2,1)S(1)}, u32[]{:S(2)}, u32[]{:S(2)}) collective-permute-start(f16[16,2,32,128]{3,2,1,0:T(8,128)(2,1)S(1)} %get-tuple-element.19), channel_id=1, source_target_pairs={{0,3},{1,2},{2,1},{3,0},{4,7},{5,6},{6,5},{7,4},{8,11},{9,10},{10,... | collective-permute-start | bytes 786440 | tf_op jit(solution)/shard_map/ppermute | solution.py:210
  122.6 1.3 %copy-start.1 = (f32[64,2,32,128]{3,2,1,0:T(8,128)}, f32[64,2,32,128]{3,2,1,0:T(8,128)S(1)}, u32[]{:S(2)}) copy-start(f32[64,2,32,128]{3,2,1,0:T(8,128)S(1)} %multiply_dynamic-update-slice_fusion) | copy-start | bytes 6291460
